TPU v7x, 32 devices: a whole 2x2x4 slice. The times are simulated.
32 devices in a mesh: wide: 16 (over z, x, core), narrow: 2 (over y).
Axes of the slice: x: 2, y: 2, z: 4, core: 2. Of those that a mesh axis runs over, the one named last changes fastest.
Arguments:
- inputs: bfloat16 [16, 2, 2, 1024, 1024], P('wide', None, 'narrow'), may hold values from -6 to 6
- cotangent: bfloat16 [16, 2, 2, 1024, 1024], P('wide', None, 'narrow'), may hold values from -6 to 6
- lengths: int32 [16], P('wide'), may hold values from 512 to 4096, as said below
- w_qkv: bfloat16 [1024, 3072], replicated, may hold values from -0.1875 to 0.1875
- b_qkv: float32 [3072], replicated, may hold values from -1.5 to 1.5
- w_out: bfloat16 [1024, 1024], replicated, may hold values from -0.1875 to 0.1875
- b_out: float32 [1024], replicated, may hold values from -1.5 to 1.5
- w_up: bfloat16 [1024, 4096], replicated, may hold values from -0.1875 to 0.1875
- b_up: float32 [4096], replicated, may hold values from -1.5 to 1.5
- w_down: bfloat16 [4096, 1024], replicated, may hold values from -0.09375 to 0.09375
- b_down: float32 [1024], replicated, may hold values from -1.5 to 1.5
- gain_one: float32 [1024], replicated, may hold values from 0.5 to 1.5
- shift_one: float32 [1024], replicated, may hold values from -1.5 to 1.5
- gain_two: float32 [1024], replicated, may hold values from 0.5 to 1.5
- shift_two: float32 [1024], replicated, may hold values from -1.5 to 1.5
- gain_three: float32 [1024], replicated, may hold values from 0.5 to 1.5
- shift_three: float32 [1024], replicated, may hold values from -1.5 to 1.5
- gain_four: float32 [1024], replicated, may hold values from 0.5 to 1.5
- shift_four: float32 [1024], replicated, may hold values from -1.5 to 1.5
Outputs:
- output: bfloat16 [16, 2, 2, 1024, 1024], P('wide', None, 'narrow')
- input_grad: bfloat16 [16, 2, 2, 1024, 1024], P('wide', None, 'narrow')
- grad_w_qkv: float32 [1024, 3072], P(None, ('wide', 'narrow'))
- grad_w_out: float32 [1024, 1024], P(None, ('wide', 'narrow'))
- grad_w_up: float32 [1024, 4096], P(None, ('wide', 'narrow'))
- grad_w_down: float32 [4096, 1024], P(None, ('wide', 'narrow'))
- grad_b_qkv: float32 [3072], replicated
- grad_b_out: float32 [1024], replicated
- grad_b_up: float32 [4096], replicated
- grad_b_down: float32 [1024], replicated
- grad_gain_one: float32 [1024], replicated
- grad_shift_one: float32 [1024], replicated
- grad_gain_two: float32 [1024], replicated
- grad_shift_two: float32 [1024], replicated
- grad_gain_three: float32 [1024], replicated
- grad_shift_three: float32 [1024], replicated
- grad_gain_four: float32 [1024], replicated
- grad_shift_four: float32 [1024], replicated
Inputs may be any that keep to these rules, and one draw needn't show every extreme that they name: `lengths`: in each aligned pair of sequences one, drawn from the seed, has length 4096.
All inputs are finite; a program needn't handle non-finite values.
Results may differ from a plain program's by a relative error of at most 0.018.
Values may be sent and summed in bfloat16 or wider, within the bound.
No kernel may reach another device: no remote copies, remote signals or barrier semaphores. Data moves between devices by JAX's collectives and lax.ppermute only.
A program may use at most 704 MiB of HBM per device.

v0:
```python
import jax
import jax.numpy as jnp
from jax import lax
from jax.sharding import PartitionSpec as P

HEAD_DIM = 64


EPS = 1e-05


def layer_norm(values, gain, shift):
    centre = values - jnp.mean(values, axis=-1, keepdims=True)
    spread = jnp.mean(centre * centre, axis=-1, keepdims=True)
    return centre * lax.rsqrt(spread + EPS) * gain + shift


def smooth(values):
    return jax.nn.gelu(values, approximate=True)


def turn(values, cosine, sine, sign):
    half = values.shape[-1] // 2
    first = values[..., :half]
    second = values[..., half:]
    return jnp.concatenate(
        [first * cosine - sign * second * sine, second * cosine + sign * first * sine], axis=-1
    )


def outer_product(left, right):
    return lax.dot_general(
        left, right, (((0,), (0,)), ((), ())), preferred_element_type=jnp.float32
    )


def back_product(left, right):
    return lax.dot_general(
        left, right, (((1,), (1,)), ((), ())), preferred_element_type=jnp.float32
    )


def body(
    inputs,
    cotangent,
    lengths,
    w_qkv,
    b_qkv,
    w_out,
    b_out,
    w_up,
    b_up,
    w_down,
    b_down,
    gain_one,
    shift_one,
    gain_two,
    shift_two,
    gain_three,
    shift_three,
    gain_four,
    shift_four,
):
    seq_dev = inputs.shape[0]
    group = inputs.shape[3]
    width = inputs.shape[4]
    heads = width // HEAD_DIM
    parts = lax.axis_size("narrow")
    place = lax.axis_index("narrow")
    span = 2 * group
    rows = seq_dev * span
    offsets = jnp.arange(group, dtype=jnp.int32)
    query_pos = jnp.concatenate(
        [place * group + offsets, (2 * parts - 1 - place) * group + offsets]
    )
    row_pos = jnp.tile(query_pos, seq_dev).astype(jnp.float32)
    half = HEAD_DIM // 2
    freqs = jnp.power(10000.0, -jnp.arange(half, dtype=jnp.float32) / half)
    theta = row_pos[:, None] * freqs[None, :]
    cosine = jnp.cos(theta)[:, None, :]
    sine = jnp.sin(theta)[:, None, :]

    def key_places(start, count):
        shard_ids = start + jnp.arange(count, dtype=jnp.int32)
        early = shard_ids[:, None] * group + offsets[None, :]
        late = (2 * parts - 1 - shard_ids)[:, None] * group + offsets[None, :]
        return jnp.concatenate([early.reshape(-1), late.reshape(-1)])

    def usable_pairs(query_places, places):
        causal = places[None, None, :] <= query_places[None, :, None]
        inside = places[None, None, :] < lengths[:, None, None]
        return (causal & inside)[:, None]

    def allowed(places):
        return usable_pairs(query_pos, places)

    tokens = inputs.astype(jnp.float32).reshape(rows, width)
    normed, pull_one = jax.vjp(layer_norm, tokens, gain_one, shift_one)
    normed_low = normed.astype(jnp.bfloat16)
    mixed = jnp.dot(normed_low, w_qkv, preferred_element_type=jnp.float32) + b_qkv
    query_turned = turn(mixed[:, :width].reshape(rows, heads, HEAD_DIM), cosine, sine, 1.0)
    keys_turned = turn(
        mixed[:, width : 2 * width].reshape(rows, heads, HEAD_DIM), cosine, sine, 1.0
    )
    query_low = query_turned.astype(jnp.bfloat16).reshape(seq_dev, span, heads, HEAD_DIM)
    keys_low = keys_turned.astype(jnp.bfloat16).reshape(seq_dev, 2, 1, group, width)
    values_low = mixed[:, 2 * width :].astype(jnp.bfloat16).reshape(seq_dev, 2, 1, group, width)

    def fold(carry, piece, start):
        running, total, acc, exact = carry
        key_piece, value_piece = piece
        count = key_piece.shape[2]
        key_heads = key_piece.reshape(seq_dev, 2 * count * group, heads, HEAD_DIM)
        value_heads = value_piece.reshape(seq_dev, 2 * count * group, heads, HEAD_DIM)
        scores = (
            jnp.einsum("sqhd,skhd->shqk", query_low, key_heads, preferred_element_type=jnp.float32)
            * 0.125
        )
        usable = allowed(key_places(start, count))
        peak = jnp.maximum(running, jnp.max(jnp.where(usable, scores, -1e30), axis=-1))
        weights = jnp.where(usable, jnp.exp(scores - peak[..., None]), 0.0)
        factor = jnp.exp(running - peak)
        total = total * factor + jnp.sum(weights, axis=-1)
        acc = acc * factor[..., None] + jnp.einsum(
            "shqk,skhd->shqd",
            weights.astype(jnp.bfloat16),
            value_heads,
            preferred_element_type=jnp.float32,
        )
        exact = exact * factor[..., None] + jnp.einsum(
            "shqk,skhd->shqd",
            weights,
            value_heads.astype(jnp.float32),
            preferred_element_type=jnp.float32,
        )
        return (peak, total, acc, exact)

    start_carry = (
        jnp.full((seq_dev, heads, span), -1e30, jnp.float32),
        jnp.zeros((seq_dev, heads, span), jnp.float32),
        jnp.zeros((seq_dev, heads, span, HEAD_DIM), jnp.float32),
        jnp.zeros((seq_dev, heads, span, HEAD_DIM), jnp.float32),
    )
    whole_keys, whole_values = (
        lax.all_gather(keys_low, "narrow", axis=2, tiled=True),
        lax.all_gather(values_low, "narrow", axis=2, tiled=True),
    )

    def walk(carry, shard):
        piece = (
            lax.dynamic_slice_in_dim(whole_keys, shard, 1, 2),
            lax.dynamic_slice_in_dim(whole_values, shard, 1, 2),
        )
        return (fold(carry, piece, shard), None)

    final_carry, unused = lax.scan(walk, start_carry, jnp.arange(parts, dtype=jnp.int32))
    running, total, acc, exact = final_carry
    log_total = running + jnp.log(total)
    attended = acc / total[..., None]
    exact_attended = exact / total[..., None]
    attended_rows = jnp.transpose(attended, (0, 2, 1, 3)).reshape(rows, width)
    attended_low = attended_rows.astype(jnp.bfloat16)
    branch = jnp.dot(attended_low, w_out, preferred_element_type=jnp.float32) + b_out
    post_one, pull_two = jax.vjp(layer_norm, branch, gain_two, shift_two)
    middle = tokens + post_one
    normed_two, pull_three = jax.vjp(layer_norm, middle, gain_three, shift_three)
    normed_two_low = normed_two.astype(jnp.bfloat16)
    inner = jnp.dot(normed_two_low, w_up, preferred_element_type=jnp.float32) + b_up
    hidden, pull_smooth = jax.vjp(smooth, inner)
    hidden_low = hidden.astype(jnp.bfloat16)
    outer = jnp.dot(hidden_low, w_down, preferred_element_type=jnp.float32) + b_down
    post_two, pull_four = jax.vjp(layer_norm, outer, gain_four, shift_four)
    result = middle + post_two
    grad_result = cotangent.astype(jnp.float32).reshape(rows, width)
    d_outer, grad_gain_four, grad_shift_four = pull_four(grad_result)
    d_outer_low = d_outer.astype(jnp.bfloat16)
    grad_w_down = outer_product(hidden_low, d_outer_low)
    grad_b_down = jnp.sum(d_outer_low.astype(jnp.float32), axis=0)
    d_hidden = back_product(d_outer_low, w_down)
    d_inner = pull_smooth(d_hidden)[0]
    d_inner_low = d_inner.astype(jnp.bfloat16)
    grad_w_up = outer_product(normed_two_low, d_inner_low)
    grad_b_up = jnp.sum(d_inner_low.astype(jnp.float32), axis=0)
    d_normed_two = back_product(d_inner_low, w_up)
    d_middle_part, grad_gain_three, grad_shift_three = pull_three(d_normed_two)
    d_middle = grad_result + d_middle_part
    d_branch, grad_gain_two, grad_shift_two = pull_two(d_middle)
    d_branch_low = d_branch.astype(jnp.bfloat16)
    grad_w_out = outer_product(attended_low, d_branch_low)
    grad_b_out = jnp.sum(d_branch_low.astype(jnp.float32), axis=0)
    d_attended = back_product(d_branch_low, w_out).astype(jnp.bfloat16)
    d_attended_heads = d_attended.reshape(seq_dev, span, heads, HEAD_DIM)
    delta = jnp.sum(
        jnp.transpose(d_attended_heads.astype(jnp.float32), (0, 2, 1, 3)) * exact_attended, axis=-1
    )
    back_keys, back_values = (whole_keys, whole_values)

    def block_scores(shard):
        key_heads = lax.dynamic_slice_in_dim(back_keys, shard, 1, 2).reshape(
            seq_dev, span, heads, HEAD_DIM
        )
        value_heads = lax.dynamic_slice_in_dim(back_values, shard, 1, 2).reshape(
            seq_dev, span, heads, HEAD_DIM
        )
        scores = (
            jnp.einsum("sqhd,skhd->shqk", query_low, key_heads, preferred_element_type=jnp.float32)
            * 0.125
        )
        usable = allowed(key_places(shard, 1))
        probs = jnp.where(usable, jnp.exp(scores - log_total[..., None]), 0.0)
        d_probs = jnp.einsum(
            "sqhd,skhd->shqk", d_attended_heads, value_heads, preferred_element_type=jnp.float32
        )
        d_scores = (probs * (d_probs - delta[..., None])).astype(jnp.bfloat16)
        return (key_heads, probs, d_scores)

    zero_query = jnp.zeros((seq_dev, span, heads, HEAD_DIM), jnp.float32)

    def query_block(grad_query, shard):
        key_heads, probs, d_scores = block_scores(shard)
        grad_query = grad_query + 0.125 * jnp.einsum(
            "shqk,skhd->sqhd", d_scores, key_heads, preferred_element_type=jnp.float32
        )
        return (grad_query, None)

    grad_query, unused_terms = lax.scan(query_block, zero_query, jnp.arange(parts, dtype=jnp.int32))
    all_query, all_d_attended = (
        lax.all_gather(query_low, "narrow", axis=1, tiled=True),
        lax.all_gather(d_attended_heads, "narrow", axis=1, tiled=True),
    )
    all_log_total, all_delta = (
        lax.all_gather(log_total, "narrow", axis=2, tiled=True),
        lax.all_gather(delta, "narrow", axis=2, tiled=True),
    )
    own_keys = keys_low.reshape(seq_dev, span, heads, HEAD_DIM)
    own_values = values_low.reshape(seq_dev, span, heads, HEAD_DIM)

    def owner_block(carry, shard):
        keys_acc, values_acc = carry
        query_piece = lax.dynamic_slice_in_dim(all_query, shard * span, span, 1)
        grad_piece = lax.dynamic_slice_in_dim(all_d_attended, shard * span, span, 1)
        lse_piece = lax.dynamic_slice_in_dim(all_log_total, shard * span, span, 2)
        delta_piece = lax.dynamic_slice_in_dim(all_delta, shard * span, span, 2)
        scores = (
            jnp.einsum("sqhd,skhd->shqk", query_piece, own_keys, preferred_element_type=jnp.float32)
            * 0.125
        )
        usable = usable_pairs(key_places(shard, 1), query_pos)
        probs = jnp.where(usable, jnp.exp(scores - lse_piece[..., None]), 0.0)
        values_acc = values_acc + jnp.einsum(
            "shqk,sqhd->skhd",
            probs.astype(jnp.bfloat16),
            grad_piece,
            preferred_element_type=jnp.float32,
        )
        d_probs = jnp.einsum(
            "sqhd,skhd->shqk", grad_piece, own_values, preferred_element_type=jnp.float32
        )
        d_scores = (probs * (d_probs - delta_piece[..., None])).astype(jnp.bfloat16)
        keys_acc = keys_acc + 0.125 * jnp.einsum(
            "shqk,sqhd->skhd", d_scores, query_piece, preferred_element_type=jnp.float32
        )
        return ((keys_acc, values_acc), None)

    (d_keys, d_values), unused_owner = lax.scan(
        owner_block, (zero_query, zero_query), jnp.arange(parts, dtype=jnp.int32)
    )
    d_query_low = grad_query.astype(jnp.bfloat16).astype(jnp.float32).reshape(rows, heads, HEAD_DIM)
    d_keys_low = d_keys.astype(jnp.bfloat16).astype(jnp.float32).reshape(rows, heads, HEAD_DIM)
    d_values_low = d_values.astype(jnp.bfloat16).astype(jnp.float32).reshape(rows, width)
    d_mixed = jnp.concatenate(
        [
            turn(d_query_low, cosine, sine, -1.0).reshape(rows, width),
            turn(d_keys_low, cosine, sine, -1.0).reshape(rows, width),
            d_values_low,
        ],
        axis=-1,
    ).astype(jnp.bfloat16)
    grad_w_qkv = outer_product(normed_low, d_mixed)
    grad_b_qkv = jnp.sum(d_mixed.astype(jnp.float32), axis=0)
    d_normed = back_product(d_mixed, w_qkv)
    d_tokens_part, grad_gain_one, grad_shift_one = pull_one(d_normed)
    d_tokens = d_middle + d_tokens_part
    summed = (
        lax.psum_scatter(grad_w_qkv, ("wide", "narrow"), scatter_dimension=1, tiled=True),
        lax.psum_scatter(grad_w_out, ("wide", "narrow"), scatter_dimension=1, tiled=True),
        lax.psum_scatter(grad_w_up, ("wide", "narrow"), scatter_dimension=1, tiled=True),
        lax.psum_scatter(grad_w_down, ("wide", "narrow"), scatter_dimension=1, tiled=True),
    )
    small = lax.psum(
        (
            grad_b_qkv,
            grad_b_out,
            grad_b_up,
            grad_b_down,
            grad_gain_one,
            grad_shift_one,
            grad_gain_two,
            grad_shift_two,
            grad_gain_three,
            grad_shift_three,
            grad_gain_four,
            grad_shift_four,
        ),
        ("wide", "narrow"),
    )
    output = result.astype(jnp.bfloat16).reshape(seq_dev, 2, 1, group, width)
    input_grad = d_tokens.astype(jnp.bfloat16).reshape(seq_dev, 2, 1, group, width)
    return (
        output,
        input_grad,
        summed[0],
        summed[1],
        summed[2],
        summed[3],
        small[0],
        small[1],
        small[2],
        small[3],
        small[4],
        small[5],
        small[6],
        small[7],
        small[8],
        small[9],
        small[10],
        small[11],
    )


def solution(mesh):
    in_specs = (
        P("wide", None, "narrow", None, None),
        P("wide", None, "narrow", None, None),
        P("wide"),
        P(),
        P(),
        P(),
        P(),
        P(),
        P(),
        P(),
        P(),
        P(),
        P(),
        P(),
        P(),
        P(),
        P(),
        P(),
        P(),
    )
    out_specs = (
        P("wide", None, "narrow", None, None),
        P("wide", None, "narrow", None, None),
        P(None, ("wide", "narrow")),
        P(None, ("wide", "narrow")),
        P(None, ("wide", "narrow")),
        P(None, ("wide", "narrow")),
        P(),
        P(),
        P(),
        P(),
        P(),
        P(),
        P(),
        P(),
        P(),
        P(),
        P(),
        P(),
    )
    return jax.shard_map(body, mesh=mesh, in_specs=in_specs, out_specs=out_specs, check_vma=False)
```

profile of v0, /device:TPU:0, one launch (start us, length us, event | category | flops | bytes accessed | tf_op | source)
XLA Modules:
  0.0 3508.8 jit_solution(3918070436543415068)
XLA Ops:
  170.4 84.3 %all-gather.6.cloned.1.call-done = bf16[1,2,2,1024,1024]{4,3,1,0,2:T(8,128)(2,1)} async-done(((bf16[1,2,1,1024,1024]{4,3,1,0,2:T(8,128)(2,1)}), bf16[1,2,2,1024,1024]{4,3,1,0,2:T(8,128)(2,1)}) %all-gather.6.cloned.1.call-update) | async-done | bytes 8388624 | tf_op jit(solution)/shard_map/all_gather | solution.py:145
  277.1 775.5 %while.44 = (s32[]{:T(128)}, f32[1,16,2048]{2,1,0:T(8,128)S(1)}, f32[1,16,2048]{2,1,0:T(8,128)}, f32[1,16,2048,64]{2,3,1,0:T(8,128)}, f32[1,16,2048,64]{2,3,1,0:...) while((s32[]{:T(128)}, f32[1,16,2048]{2,1,0:T(8,128)S(1)}, ...), condition=%wide.region_5.6_spmd.clone.clone, body=%wide.region_2.5_spmd.clone.clone.sunk | while | flops 26730504192 | bytes 1182585088 | solution.py:156
  311.6 89.5 %fusion.198 = (f32[16,2048]{1,0:T(8,128)S(1)}, f32[16,2048,2048]{2,1,0:T(8,128)}) fusion(pred[2048,2048]{0,1:T(8,128)(4,1)} %compare_and_fusion.6, bf16[2048,16,64]{0,2,1:T(8,128)(2,1)} %reshape.843, bf16[1,2048,16,64]{1,3,2,0:T(8,128)(2,1)} %get-tuple-element.988), kind=kOutput, calls=%fused_computation.5.clone.1 | convolution fusion | flops 8791228416 | bytes 281149440 | tf_op jit(solution)/shard_map/while/body/eval_jaxpr/sqhd,skhd->shqk/dot_general | solution.py:116
  401.1 81.9 %fusion.200 = f32[16,2048]{1,0:T(8,128)S(1)} fusion(f32[16,2048,2048]{2,1,0:T(8,128)} %get-tuple-element.913, f32[16,2048]{1,0:T(8,128)S(1)} %bitcast.372, pred[2048,2048]{0,1:T(8,128)(4,1)} %compare_and_fusion.6), kind=kLoop, calls=%fused_computation.10.clone.1 | loop fusion | flops 268402688 | bytes 272891904 | tf_op jit(solution)/shard_map/while/body/eval_jaxpr/reduce_sum | solution.py:123
  483.8 91.1 %bitcast_add_fusion.18 = f32[1,16,2048,64]{2,3,1,0:T(8,128)} fusion(f32[1,16,2048,64]{2,3,1,0:T(8,128)} %get-tuple-element.967, bf16[2048,16,64]{0,2,1:T(8,128)(2,1)} %reshape.844, f32[16,2048,2048]{2,1,0:T(8,128)} %get-tuple-element.913, f32[16,2048]{1,0:T(8,128)S(1)} %bitcast.373, pred[2048,2048]{0,1:T(8,128)(4,1)} %compare_and_fusion.6, ...), kind=kOutput, calls=%fused_computation.18.clone.1 | convolution fusion | flops 8797552640 | bytes 293863424 | tf_op jit(solution)/shard_map/while/body/eval_jaxpr/shqk,skhd->shqd/dot_general | solution.py:130
  574.9 87.5 %bitcast_add_fusion.17 = f32[1,16,2048,64]{2,3,1,0:T(8,128)} fusion(f32[1,16,2048,64]{2,3,1,0:T(8,128)} %get-tuple-element.966, bf16[2048,16,64]{0,2,1:T(8,128)(2,1)} %reshape.844, f32[16,2048,2048]{2,1,0:T(8,128)} %get-tuple-element.913, f32[16,2048]{1,0:T(8,128)S(1)} %bitcast.374, pred[2048,2048]{0,1:T(8,128)(4,1)} %compare_and_fusion.6, ...), kind=kOutput, calls=%fused_computation.19.clone.1 | convolution fusion | flops 8864661504 | bytes 293863424 | tf_op jit(solution)/shard_map/while/body/eval_jaxpr/shqk,skhd->shqd/dot_general | solution.py:124
  696.8 89.5 %fusion.198 = (f32[16,2048]{1,0:T(8,128)S(1)}, f32[16,2048,2048]{2,1,0:T(8,128)}) fusion(pred[2048,2048]{0,1:T(8,128)(4,1)} %compare_and_fusion.6, bf16[2048,16,64]{0,2,1:T(8,128)(2,1)} %reshape.843, bf16[1,2048,16,64]{1,3,2,0:T(8,128)(2,1)} %get-tuple-element.988), kind=kOutput, calls=%fused_computation.5.clone.1 | convolution fusion | flops 8791228416 | bytes 281149440 | tf_op jit(solution)/shard_map/while/body/eval_jaxpr/sqhd,skhd->shqk/dot_general | solution.py:116
  786.3 81.9 %fusion.200 = f32[16,2048]{1,0:T(8,128)S(1)} fusion(f32[16,2048,2048]{2,1,0:T(8,128)} %get-tuple-element.913, f32[16,2048]{1,0:T(8,128)S(1)} %bitcast.372, pred[2048,2048]{0,1:T(8,128)(4,1)} %compare_and_fusion.6), kind=kLoop, calls=%fused_computation.10.clone.1 | loop fusion | flops 268402688 | bytes 272891904 | tf_op jit(solution)/shard_map/while/body/eval_jaxpr/reduce_sum | solution.py:123
  869.0 93.4 %bitcast_add_fusion.18 = f32[1,16,2048,64]{2,3,1,0:T(8,128)} fusion(f32[1,16,2048,64]{2,3,1,0:T(8,128)} %get-tuple-element.967, bf16[2048,16,64]{0,2,1:T(8,128)(2,1)} %reshape.844, f32[16,2048,2048]{2,1,0:T(8,128)} %get-tuple-element.913, f32[16,2048]{1,0:T(8,128)S(1)} %bitcast.373, pred[2048,2048]{0,1:T(8,128)(4,1)} %compare_and_fusion.6, ...), kind=kOutput, calls=%fused_computation.18.clone.1 | convolution fusion | flops 8797552640 | bytes 293863424 | tf_op jit(solution)/shard_map/while/body/eval_jaxpr/shqk,skhd->shqd/dot_general | solution.py:130
  962.4 90.0 %bitcast_add_fusion.17 = f32[1,16,2048,64]{2,3,1,0:T(8,128)} fusion(f32[1,16,2048,64]{2,3,1,0:T(8,128)} %get-tuple-element.966, bf16[2048,16,64]{0,2,1:T(8,128)(2,1)} %reshape.844, f32[16,2048,2048]{2,1,0:T(8,128)} %get-tuple-element.913, f32[16,2048]{1,0:T(8,128)S(1)} %bitcast.374, pred[2048,2048]{0,1:T(8,128)(4,1)} %compare_and_fusion.6, ...), kind=kOutput, calls=%fused_computation.19.clone.1 | convolution fusion | flops 8864661504 | bytes 293863424 | tf_op jit(solution)/shard_map/while/body/eval_jaxpr/shqk,skhd->shqd/dot_general | solution.py:124
  1075.2 36.3 %multiply_convert_fusion.2 = (bf16[2048,4096]{1,0:T(8,128)(2,1)}, f32[2048,4096]{1,0:T(8,128)}) fusion(f32[4096]{0:T(1024)S(1)} %copy-done.66, bf16[1024,4096]{1,0:T(8,128)(2,1)} %param.32, f32[2048,1024]{1,0:T(8,128)} %copy-done.8, f32[1024]{0:T(1024)S(1)} %copy-done.68, f32[1024]{0:T(1024)S(1)} %copy-done.64, f32[2048]{0:T(1024)S(1)} %fusion.104, ...), kind=kOutput, calls=%fused_computation.103 | convolution fusion | flops 17274241024 | bytes 67149824 | tf_op jit(solution)/shard_map/dot_general | solution.py:168
  1111.5 23.0 add_reduce_fusion
  1154.0 48.0 %convert_reduce_fusion = (f32[4096]{0:T(1024)}, bf16[2048,4096]{1,0:T(8,128)(2,1)}) fusion(f32[2048,4096]{1,0:T(8,128)} %get-tuple-element.699, f32[4096]{0:T(1024)S(1)} %copy-done.66, bf16[2048,1024]{1,0:T(8,128)(2,1)S(1)} %get-tuple-element.648, bf16[4096,1024]{1,0:T(8,128)(2,1)} %param.34), kind=kOutput, calls=%fused_computation.102 | convolution fusion | flops 17372803072 | bytes 62947328 | tf_op jit(solution)/shard_map/dot_general | solution.py:38
  1202.0 27.3 multiply_reduce_fusion
  1271.9 481.9 %while.45 = (s32[]{:T(128)}, f32[1,2048,16,64]{1,3,2,0:T(8,128)}, s32[2]{0:T(128)S(1)}, bf16[1,2,2,1024,1024]{3,1,4,2,0:T(2,128)(2,1)}, s32[2048]{0:T(1024)}, /*...) while((s32[]{:T(128)}, f32[1,2048,16,64]{1,3,2,0:T(8,128)}, ...), condition=%wide.region_20.21_spmd.clone.clone, body=%wide.region_19.20_spmd.clone.clone.sunk | while | flops 26187145216 | bytes 616878336 | solution.py:226
  1306.4 87.4 %fusion.206 = f32[16,2048,2048]{2,1,0:T(8,128)} fusion(bf16[2048,16,64]{0,2,1:T(8,128)(2,1)} %reshape.845, bf16[1,2048,16,64]{1,3,2,0:T(8,128)(2,1)} %get-tuple-element.1087), kind=kOutput, calls=%fused_computation.48.clone.1 | convolution fusion | flops 8589934592 | bytes 276824064 | tf_op jit(solution)/shard_map/while/body/eval_jaxpr/sqhd,skhd->shqk/dot_general | solution.py:206
  1393.7 118.8 %bitcast_add_fusion.19 = f32[1,2048,16,64]{1,3,2,0:T(8,128)} fusion(f32[1,2048,16,64]{1,3,2,0:T(8,128)} %get-tuple-element.1066, pred[]{:T(512)S(6)} %compare.10, bf16[2048,16,64]{0,2,1:T(8,128)(2,1)} %reshape.845, f32[16,2048,2048]{2,1,0:T(8,128)} %fusion.206, f32[16,2048]{1,0:T(8,128)S(1)} %bitcast.403, f32[16,2048]{1,0:T(8,128)S(1)} %bitcast.405, ...), kind=kOutput, calls=%fused_computation.46.clone.2 | convolution fusion | flops 17588813824 | bytes 302252032 | tf_op jit(solution)/shard_map/while/body/eval_jaxpr/shqk,skhd->sqhd/dot_general | solution.py:221
  1546.5 87.4 %fusion.206 = f32[16,2048,2048]{2,1,0:T(8,128)} fusion(bf16[2048,16,64]{0,2,1:T(8,128)(2,1)} %reshape.845, bf16[1,2048,16,64]{1,3,2,0:T(8,128)(2,1)} %get-tuple-element.1087), kind=kOutput, calls=%fused_computation.48.clone.1 | convolution fusion | flops 8589934592 | bytes 276824064 | tf_op jit(solution)/shard_map/while/body/eval_jaxpr/sqhd,skhd->shqk/dot_general | solution.py:206
  1633.9 119.9 %bitcast_add_fusion.19 = f32[1,2048,16,64]{1,3,2,0:T(8,128)} fusion(f32[1,2048,16,64]{1,3,2,0:T(8,128)} %get-tuple-element.1066, pred[]{:T(512)S(6)} %compare.10, bf16[2048,16,64]{0,2,1:T(8,128)(2,1)} %reshape.845, f32[16,2048,2048]{2,1,0:T(8,128)} %fusion.206, f32[16,2048]{1,0:T(8,128)S(1)} %bitcast.403, f32[16,2048]{1,0:T(8,128)S(1)} %bitcast.405, ...), kind=kOutput, calls=%fused_computation.46.clone.2 | convolution fusion | flops 17588813824 | bytes 302252032 | tf_op jit(solution)/shard_map/while/body/eval_jaxpr/shqk,skhd->sqhd/dot_general | solution.py:221
  1780.2 637.5 %while.46 = (s32[]{:T(128)}, f32[1,2048,16,64]{1,3,2,0:T(8,128)}, f32[1,2048,16,64]{1,3,2,0:T(8,128)}, s32[2]{0:T(128)}, bf16[1,4096,16,64]{1,3,2,0:T(8,128)(2,1...) while((s32[]{:T(128)}, f32[1,2048,16,64]{1,3,2,0:T(8,128)}, ...), condition=%wide.region_22.23_spmd.clone.clone, body=%wide.region_21.22_spmd.clone.clone.sunk | while | flops 35049709568 | bytes 940495104 | solution.py:265
  1796.3 84.6 %fusion.214 = f32[16,2048,2048]{2,1,0:T(8,128)} fusion(bf16[1,2048,16,64]{1,3,2,0:T(8,128)(2,1)S(1)} %copy-done.3, bf16[1,4096,16,64]{1,3,2,0:T(8,128)(2,1)S(1)} %copy-done.2, s32[]{:T(128)S(6)} %select_n.101), kind=kOutput, calls=%fused_computation.72.clone.2 | convolution fusion | flops 8589934592 | bytes 276824064 | tf_op jit(solution)/shard_map/while/body/eval_jaxpr/sqhd,skhd->shqk/dot_general | solution.py:245
  1881.0 127.2 %bitcast_add_fusion.20 = f32[1,2048,16,64]{1,3,2,0:T(8,128)} fusion(f32[1,2048,16,64]{1,3,2,0:T(8,128)} %get-tuple-element.1014, pred[]{:T(512)S(6)} %compare.11, f32[16,2048,2048]{2,1,0:T(8,128)} %fusion.214, f32[16,2048]{1,0:T(8,128)S(1)} %get-tuple-element.943, f32[16,2048]{1,0:T(8,128)S(1)} %get-tuple-element.944, ...), kind=kOutput, calls=%fused_computation.68.clone.3 | convolution fusion | flops 17588813824 | bytes 302252032 | tf_op jit(solution)/shard_map/while/body/eval_jaxpr/shqk,sqhd->skhd/dot_general | solution.py:260
  2008.2 89.9 %bitcast_add_fusion.21 = f32[1,2048,16,64]{1,3,2,0:T(8,128)} fusion(f32[1,2048,16,64]{1,3,2,0:T(8,128)} %get-tuple-element.1015, f32[16,2048,2048]{2,1,0:T(8,128)} %fusion.214, f32[16,2048]{1,0:T(8,128)S(1)} %get-tuple-element.944, pred[2048,2048]{1,0:T(8,128)(4,1)} %compare_and_fusion.8, pred[]{:T(512)S(6)} %compare.11, ...), kind=kOutput, calls=%fused_computation.67.clone.2 | convolution fusion | flops 8862564352 | bytes 293732352 | tf_op jit(solution)/shard_map/while/body/eval_jaxpr/shqk,sqhd->skhd/dot_general | solution.py:250
  2114.0 83.6 %fusion.214 = f32[16,2048,2048]{2,1,0:T(8,128)} fusion(bf16[1,2048,16,64]{1,3,2,0:T(8,128)(2,1)S(1)} %copy-done.3, bf16[1,4096,16,64]{1,3,2,0:T(8,128)(2,1)S(1)} %copy-done.2, s32[]{:T(128)S(6)} %select_n.101), kind=kOutput, calls=%fused_computation.72.clone.2 | convolution fusion | flops 8589934592 | bytes 276824064 | tf_op jit(solution)/shard_map/while/body/eval_jaxpr/sqhd,skhd->shqk/dot_general | solution.py:245
  2197.6 128.4 %bitcast_add_fusion.20 = f32[1,2048,16,64]{1,3,2,0:T(8,128)} fusion(f32[1,2048,16,64]{1,3,2,0:T(8,128)} %get-tuple-element.1014, pred[]{:T(512)S(6)} %compare.11, f32[16,2048,2048]{2,1,0:T(8,128)} %fusion.214, f32[16,2048]{1,0:T(8,128)S(1)} %get-tuple-element.943, f32[16,2048]{1,0:T(8,128)S(1)} %get-tuple-element.944, ...), kind=kOutput, calls=%fused_computation.68.clone.3 | convolution fusion | flops 17588813824 | bytes 302252032 | tf_op jit(solution)/shard_map/while/body/eval_jaxpr/shqk,sqhd->skhd/dot_general | solution.py:260
  2326.0 91.7 %bitcast_add_fusion.21 = f32[1,2048,16,64]{1,3,2,0:T(8,128)} fusion(f32[1,2048,16,64]{1,3,2,0:T(8,128)} %get-tuple-element.1015, f32[16,2048,2048]{2,1,0:T(8,128)} %fusion.214, f32[16,2048]{1,0:T(8,128)S(1)} %get-tuple-element.944, pred[2048,2048]{1,0:T(8,128)(4,1)} %compare_and_fusion.8, pred[]{:T(512)S(6)} %compare.11, ...), kind=kOutput, calls=%fused_computation.67.clone.2 | convolution fusion | flops 8862564352 | bytes 293732352 | tf_op jit(solution)/shard_map/while/body/eval_jaxpr/shqk,sqhd->skhd/dot_general | solution.py:250
  2496.6 23.8 fusion.126
  2521.2 26.7 fusion.111
  2558.7 41.6 %all-reduce.3.cloned.1.call-done = (f32[3072]{0:T(1024)}, f32[1024]{0:T(1024)}, f32[4096]{0:T(1024)}, f32[1024]{0:T(1024)}, f32[1024]{0:T(1024)}, /*index=5*/f32...) async-done(((f32[3072]{0:T(1024)}, f32[1024]{0:T(1024)}, f32[4096]{0:T(1024)}, ...) | async-done | bytes 69648 | tf_op jit(solution)/shard_map/psum | solution.py:290
  2600.3 165.7 %reduce-scatter.5.cloned.1.call-done = f32[1024,96]{0,1:T(8,128)} async-done(((f32[1024,3072]{0,1:T(8,128)}), f32[1024,96]{0,1:T(8,128)}) %reduce-scatter.5.cloned.1.call-update) | async-done | bytes 393232 | tf_op jit(solution)/shard_map/reduce_scatter | solution.py:285
  2766.0 359.4 %reduce-scatter.11.cloned.1.call-done = f32[4096,32]{0,1:T(8,128)} async-done(((f32[4096,1024]{0,1:T(8,128)}), f32[4096,32]{0,1:T(8,128)}) %reduce-scatter.11.cloned.1.call-update) | async-done | bytes 524304 | tf_op jit(solution)/shard_map/reduce_scatter | solution.py:288
  3125.4 361.4 %reduce-scatter.9.cloned.1.call-done = f32[1024,128]{1,0:T(8,128)} async-done(((f32[1024,4096]{1,0:T(8,128)}), f32[1024,128]{1,0:T(8,128)}) %reduce-scatter.9.cloned.1.call-update) | async-done | bytes 524304 | tf_op jit(solution)/shard_map/reduce_scatter | solution.py:287
  (352 shorter events, 554.9 us)
Async XLA Ops:
  7.2 1050.1 %copy-start = (bf16[1024,1024]{1,0:T(8,128)(2,1)S(1)}, bf16[1024,1024]{1,0:T(8,128)(2,1)}, u32[]{:S(2)}) copy-start(bf16[1024,1024]{1,0:T(8,128)(2,1)} %param.30) | copy-start | bytes 6291460
  7.2 141.3 %all-gather.8.cloned.1.call-start = ((), (), s32[]{:S(2)}) async-start(), calls=%async_computation.5 | async-start | bytes 12582912 | tf_op jit(solution)/shard_map/all_gather | solution.py:146
  41.7 213.0 %all-gather.6.cloned.1.call-start = ((), (), s32[]{:S(2)}) async-start(), calls=%async_computation.4 | async-start | bytes 12582912 | tf_op jit(solution)/shard_map/all_gather | solution.py:145
  107.2 1672.5 %all-gather.10.cloned.1.call-start = ((), (), s32[]{:S(2)}) async-start(), calls=%async_computation.6 | async-start | bytes 12582912 | tf_op jit(solution)/shard_map/all_gather | solution.py:228
  112.1 1667.6 %all-gather.12.cloned.1.call-start = ((), (), s32[]{:S(2)}) async-start(), calls=%async_computation.7 | async-start | bytes 12582912 | tf_op jit(solution)/shard_map/all_gather | solution.py:229
  401.1 81.9 %copy-start.19 = (f32[1,16,2048]{2,1,0:T(8,128)S(1)}, f32[1,16,2048]{2,1,0:T(8,128)}, u32[]{:S(2)}) copy-start(f32[1,16,2048]{2,1,0:T(8,128)} %get-tuple-element.965) | copy-start | bytes 393220 | tf_op jit(solution)/shard_map/while
  483.1 91.8 %copy-start.20 = (f32[1,16,2048]{2,1,0:T(8,128)}, f32[1,16,2048]{2,1,0:T(8,128)S(1)}, u32[]{:S(2)}) copy-start(f32[1,16,2048]{2,1,0:T(8,128)S(1)} %bitcast_add_fusion.16) | copy-start | bytes 393220 | tf_op jit(solution)/shard_map/while
  574.9 87.5 %copy-start.16 = (f32[1,16,2048]{2,1,0:T(8,128)S(1)}, f32[1,16,2048]{2,1,0:T(8,128)}, u32[]{:S(2)}) copy-start(f32[1,16,2048]{2,1,0:T(8,128)} %copy.96) | copy-start | bytes 393220 | tf_op jit(solution)/shard_map/while
  786.3 81.9 %copy-start.19 = (f32[1,16,2048]{2,1,0:T(8,128)S(1)}, f32[1,16,2048]{2,1,0:T(8,128)}, u32[]{:S(2)}) copy-start(f32[1,16,2048]{2,1,0:T(8,128)} %get-tuple-element.965) | copy-start | bytes 393220 | tf_op jit(solution)/shard_map/while
  868.3 94.1 %copy-start.20 = (f32[1,16,2048]{2,1,0:T(8,128)}, f32[1,16,2048]{2,1,0:T(8,128)S(1)}, u32[]{:S(2)}) copy-start(f32[1,16,2048]{2,1,0:T(8,128)S(1)} %bitcast_add_fusion.16) | copy-start | bytes 393220 | tf_op jit(solution)/shard_map/while
  962.4 90.0 %copy-start.16 = (f32[1,16,2048]{2,1,0:T(8,128)S(1)}, f32[1,16,2048]{2,1,0:T(8,128)}, u32[]{:S(2)}) copy-start(f32[1,16,2048]{2,1,0:T(8,128)} %copy.96) | copy-start | bytes 393220 | tf_op jit(solution)/shard_map/while
  1070.3 159.1 %copy-start.45 = (f32[2048]{0:T(1024)}, f32[2048]{0:T(1024)S(1)}, u32[]{:S(2)}) copy-start(f32[2048]{0:T(1024)S(1)} %broadcast_multiply_fusion.2) | copy-start | bytes 24580
  1075.2 154.2 %copy-start.58 = (f32[2048]{0:T(1024)}, f32[2048]{0:T(1024)S(1)}, u32[]{:S(2)}) copy-start(f32[2048]{0:T(1024)S(1)} %fusion.104) | copy-start | bytes 24580
  1075.2 36.3 %copy-start.53 = (f32[1024]{0:T(1024)S(1)}, f32[1024]{0:T(1024)}, u32[]{:S(2)}) copy-start(f32[1024]{0:T(1024)} %param.35) | copy-start | bytes 12292
  1154.0 48.0 %copy-start.22 = (bf16[2048,1024]{1,0:T(8,128)(2,1)}, bf16[2048,1024]{1,0:T(8,128)(2,1)S(1)}, u32[]{:S(2)}) copy-start(bf16[2048,1024]{1,0:T(8,128)(2,1)S(1)} %get-tuple-element.648) | copy-start | bytes 12582916
  1202.0 27.3 copy-start.50
  1271.8 1286.9 %reduce-scatter.7.cloned.1.call-start = ((), (), s32[]{:S(2)}) async-start(), calls=%async_computation.9 | async-start | bytes 4325376 | tf_op jit(solution)/shard_map/reduce_scatter | solution.py:286
  1393.7 118.8 %copy-start.71 = (s32[2]{0:T(128)S(1)}, s32[2]{0:T(128)}, u32[]{:S(2)}) copy-start(s32[2]{0:T(128)} %copy-done.70) | copy-start | bytes 28 | tf_op jit(solution)/shard_map/while
  1633.9 119.9 %copy-start.71 = (s32[2]{0:T(128)S(1)}, s32[2]{0:T(128)}, u32[]{:S(2)}) copy-start(s32[2]{0:T(128)} %copy-done.70) | copy-start | bytes 28 | tf_op jit(solution)/shard_map/while
  1779.6 820.7 %all-reduce.3.cloned.1.call-start = ((), (), s32[]{:S(2)}) async-start(), calls=%async_computation.12 | async-start | bytes 139264 | tf_op jit(solution)/shard_map/psum | solution.py:290
  1780.4 100.6 %copy-start.28 = (f32[1,16,4096]{2,1,0:T(8,128)}, f32[1,16,4096]{2,1,0:T(8,128)S(1)}, u32[]{:S(2)}) copy-start(f32[1,16,4096]{2,1,0:T(8,128)S(1)} %get-tuple-element.1039) | copy-start | bytes 786436 | tf_op jit(solution)/shard_map/while
  1780.4 100.5 %copy-start.30 = (f32[1,16,4096]{2,1,0:T(8,128)}, f32[1,16,4096]{2,1,0:T(8,128)S(1)}, u32[]{:S(2)}) copy-start(f32[1,16,4096]{2,1,0:T(8,128)S(1)} %get-tuple-element.1042) | copy-start | bytes 786436 | tf_op jit(solution)/shard_map/while
  2008.2 89.9 %copy-start.29 = (f32[1,16,4096]{2,1,0:T(8,128)S(1)}, f32[1,16,4096]{2,1,0:T(8,128)}, u32[]{:S(2)}) copy-start(f32[1,16,4096]{2,1,0:T(8,128)} %copy-done.28) | copy-start | bytes 786436 | tf_op jit(solution)/shard_map/while
  2008.2 89.9 %copy-start.31 = (f32[1,16,4096]{2,1,0:T(8,128)S(1)}, f32[1,16,4096]{2,1,0:T(8,128)}, u32[]{:S(2)}) copy-start(f32[1,16,4096]{2,1,0:T(8,128)} %copy-done.30) | copy-start | bytes 786436 | tf_op jit(solution)/shard_map/while
  2098.2 99.5 %copy-start.28 = (f32[1,16,4096]{2,1,0:T(8,128)}, f32[1,16,4096]{2,1,0:T(8,128)S(1)}, u32[]{:S(2)}) copy-start(f32[1,16,4096]{2,1,0:T(8,128)S(1)} %get-tuple-element.1039) | copy-start | bytes 786436 | tf_op jit(solution)/shard_map/while
  2098.2 99.5 %copy-start.30 = (f32[1,16,4096]{2,1,0:T(8,128)}, f32[1,16,4096]{2,1,0:T(8,128)S(1)}, u32[]{:S(2)}) copy-start(f32[1,16,4096]{2,1,0:T(8,128)S(1)} %get-tuple-element.1042) | copy-start | bytes 786436 | tf_op jit(solution)/shard_map/while
  2326.0 91.7 %copy-start.29 = (f32[1,16,4096]{2,1,0:T(8,128)S(1)}, f32[1,16,4096]{2,1,0:T(8,128)}, u32[]{:S(2)}) copy-start(f32[1,16,4096]{2,1,0:T(8,128)} %copy-done.28) | copy-start | bytes 786436 | tf_op jit(solution)/shard_map/while
  2326.0 91.7 %copy-start.31 = (f32[1,16,4096]{2,1,0:T(8,128)S(1)}, f32[1,16,4096]{2,1,0:T(8,128)}, u32[]{:S(2)}) copy-start(f32[1,16,4096]{2,1,0:T(8,128)} %copy-done.30) | copy-start | bytes 786436 | tf_op jit(solution)/shard_map/while
  2474.1 291.9 %reduce-scatter.5.cloned.1.call-start = ((), (), s32[]{:S(2)}) async-start(), calls=%async_computation.8 | async-start | bytes 12976128 | tf_op jit(solution)/shard_map/reduce_scatter | solution.py:285
  2496.6 628.8 %reduce-scatter.11.cloned.1.call-start = ((), (), s32[]{:S(2)}) async-start(), calls=%async_computation.11 | async-start | bytes 17301504 | tf_op jit(solution)/shard_map/reduce_scatter | solution.py:288
  2520.5 966.2 %reduce-scatter.9.cloned.1.call-start = ((), (), s32[]{:S(2)}) async-start(), calls=%async_computation.10 | async-start | bytes 17301504 | tf_op jit(solution)/shard_map/reduce_scatter | solution.py:287
  2547.9 954.1 %copy-start.1 = (bf16[1024,1024]{1,0:T(8,128)(2,1)S(1)}, bf16[1024,1024]{1,0:T(8,128)(2,1)}, u32[]{:S(2)}) copy-start(bf16[1024,1024]{1,0:T(8,128)(2,1)} %param.30) | copy-start | bytes 6291460
  (68 other events, 446.6 us)
Sparse Core Ops, SparseCore 0:
  41.8 106.6 all-gather.7
  150.6 103.9 all-gather.5
  256.2 104.0 all-gather.9
  1271.9 103.9 all-gather.11
  1779.7 141.4 reduce-scatter.6
  2474.2 126.0 all-reduce.2
  2607.9 158.0 reduce-scatter.4
  2768.9 356.4 reduce-scatter.10
  3128.2 358.4 reduce-scatter.8
where the time goes:
time: 3520 us; the launch traced here: 3510 us
  matrix products  1820 us (52%)
  waiting for transfers between devices  1030 us (29%)
  other arithmetic  354 us (10%)
  local copies, waits for them, and re-layouts  253 us (7%)
    reduce_scatter x1, waiting for transfers between devices, body(): lax.psum_scatter(grad_w_up, ('wide', 'narrow'), scatter_dimension=1, tile...  361 us
    reduce_scatter x1, waiting for transfers between devices, body(): lax.psum_scatter(grad_w_down, ('wide', 'narrow'), scatter_dimension=1, ti...  359 us
    dot_general x2, matrix products, owner_block(): jnp.einsum('shqk,sqhd->skhd', d_scores, query_piece, preferred_element_ty...  256 us
    dot_general x2, matrix products, query_block(): jnp.einsum('shqk,skhd->sqhd', d_scores, key_heads, preferred_element_type...  239 us
    dot_general x2, matrix products, fold(): jnp.einsum('shqk,skhd->shqd', weights, value_heads.astype(jnp.float32), p...  185 us
    dot_general x2, matrix products, owner_block(): jnp.einsum('shqk,sqhd->skhd', probs.astype(jnp.bfloat16), grad_piece, pre...  182 us
    dot_general x2, matrix products, fold(): jnp.einsum('sqhd,skhd->shqk', query_low, key_heads, preferred_element_typ...  179 us
    dot_general x2, matrix products, fold(): jnp.einsum('shqk,skhd->shqd', weights.astype(jnp.bfloat16), value_heads,...  178 us
  transfers between devices with their start and end apart: 9, of which 6 were waited for; matrix products, arithmetic and copies ran while one was open for 67% of the time, Pallas kernels for 0%

commit v1 on v0

v1 whole, which is shorter than its diff:
```python
import functools

import jax
import jax.numpy as jnp
from jax import lax
from jax.experimental import pallas as pl
from jax.experimental.pallas import tpu as pltpu
from jax.sharding import PartitionSpec as P

HEAD_DIM = 64
PAIR = 2 * HEAD_DIM
EPS = 1e-05
LOG2E = 1.4426950408889634
LN2 = 0.6931471805599453
NEG = -1e30
VMEM = 62 * 1024 * 1024
SPAN = 1024

f32 = jnp.float32
bf16 = jnp.bfloat16


def layer_norm(values, gain, shift):
    centre = values - jnp.mean(values, axis=-1, keepdims=True)
    spread = jnp.mean(centre * centre, axis=-1, keepdims=True)
    return centre * lax.rsqrt(spread + EPS) * gain + shift


def dot(left, right, left_dim, right_dim):
    return lax.dot_general(
        left, right, (((left_dim,), (right_dim,)), ((), ())), preferred_element_type=f32
    )


def fwd_chunk(q0, k0, q_n, k_n, offset, limit, qT, kT, vT, m_ref, l_ref, acc):
    queries = pl.ds(q0, q_n)
    strip = min(256, k_n)
    for h in range(2):
        rows = slice(HEAD_DIM * h, HEAD_DIM * (h + 1))
        old = m_ref[h : h + 1, queries]
        new = old
        strips = []
        for j in range(k_n // strip):
            keys = pl.ds(k0 + j * strip, strip)
            scores = dot(kT[rows, keys], qT[rows, queries], 0, 0)
            if offset is not None or limit is not None:
                key_at = j * strip + lax.broadcasted_iota(jnp.int32, (strip, q_n), 0)
                query_at = lax.broadcasted_iota(jnp.int32, (1, q_n), 1)
                last = jnp.zeros((1, q_n), jnp.int32) + (limit - 1)
                if offset is not None:
                    last = jnp.minimum(query_at + offset, last)
                scores = jnp.where(key_at <= last, scores, NEG)
            strips.append(scores)
            new = jnp.maximum(new, jnp.max(scores, axis=0, keepdims=True))
        factor = jnp.exp2(old - new)
        total = l_ref[h : h + 1, queries] * factor
        value = acc[rows, queries] * factor
        for j in range(k_n // strip):
            keys = pl.ds(k0 + j * strip, strip)
            weights = jnp.exp2(strips[j] - new)
            total = total + jnp.sum(weights, axis=0, keepdims=True)
            value = value + dot(vT[rows, keys], weights.astype(bf16), 1, 0)
        m_ref[h : h + 1, queries] = new
        l_ref[h : h + 1, queries] = total
        acc[rows, queries] = value


def pad_left(values, count):
    if not count:
        return values
    return jnp.concatenate([jnp.zeros((values.shape[0], count), f32), values], axis=1)


def pad_right(values, count):
    if not count:
        return values
    return jnp.concatenate([values, jnp.zeros((values.shape[0], count), f32)], axis=1)


def fwd_diagonal(base, group, qT, kT, vT, m_ref, l_ref, acc):
    strip = min(256, group)
    count = group // strip
    for h in range(2):
        rows = slice(HEAD_DIM * h, HEAD_DIM * (h + 1))
        strips = []
        for j in range(count):
            wide = group - j * strip
            keys, queries = pl.ds(base + j * strip, strip), pl.ds(base + j * strip, wide)
            scores = dot(kT[rows, keys], qT[rows, queries], 0, 0)
            key_at = lax.broadcasted_iota(jnp.int32, scores.shape, 0)
            query_at = lax.broadcasted_iota(jnp.int32, scores.shape, 1)
            strips.append(jnp.where(key_at <= query_at, scores, NEG))
        peaks = []
        for g in range(count):
            peak = None
            for j in range(g + 1):
                part = strips[j][:, (g - j) * strip : (g - j + 1) * strip]
                part = jnp.max(part, axis=0, keepdims=True)
                peak = part if peak is None else jnp.maximum(peak, part)
            peaks.append(peak)
        peak = jnp.concatenate(peaks, axis=1) if count > 1 else peaks[0]
        total, value = None, None
        for j in range(count):
            keys = pl.ds(base + j * strip, strip)
            weights = jnp.exp2(strips[j] - peak[:, j * strip :])
            part = pad_left(jnp.sum(weights, axis=0, keepdims=True), j * strip)
            term = pad_left(dot(vT[rows, keys], weights.astype(bf16), 1, 0), j * strip)
            total = part if total is None else total + part
            value = term if value is None else value + term
        queries = pl.ds(base, group)
        m_ref[h : h + 1, queries] = peak
        l_ref[h : h + 1, queries] = total
        acc[rows, queries] = value


def fwd_local_kernel(group, info, qT, kT, vT, acc, m_ref, l_ref):
    length = info[1]
    m_ref[...] = jnp.full(m_ref.shape, NEG, f32)
    l_ref[...] = jnp.zeros(l_ref.shape, f32)
    acc[...] = jnp.zeros(acc.shape, f32)
    refs = (qT, kT, vT, m_ref.at[0], l_ref.at[0], acc)

    def own(i, carry):
        base = pl.multiple_of(i * group, group)
        start = info[2 + i]

        @pl.when(start + group <= length)
        def _():
            fwd_diagonal(base, group, *refs)

        @pl.when((start < length) & (start + group > length))
        def _():
            fwd_chunk(base, base, group, group, 0, length - start, *refs)

        return carry

    lax.fori_loop(0, 2, own, 0)
    early = info[2]

    @pl.when(early + group <= length)
    def _():
        fwd_chunk(group, 0, group, group, None, None, *refs)

    @pl.when((early < length) & (early + group > length))
    def _():
        fwd_chunk(group, 0, group, group, None, length - early, *refs)


def remote_steps(group, parts, kind, info, full, partial):
    place, length = info[0], info[1]

    def visit(q_block, k_slot, k_block, wanted):
        q0 = pl.multiple_of(q_block * group, group)
        k0 = pl.multiple_of(k_slot * group, group)
        start = k_block * group

        @pl.when(wanted & (start + group <= length))
        def _():
            full(q0, k0)

        @pl.when(wanted & (start < length) & (start + group > length))
        def _():
            partial(q0, k0, length - start)

    others = parts - 1

    def early(i, carry):
        j = i // 2
        other = lax.rem(place + 1 + j, parts)
        late_query = lax.rem(i, 2)
        visit(late_query, j, other, (late_query == 1) | (other < place))
        return carry

    def late(j, carry):
        other = lax.rem(place + 1 + j, parts)
        slot = j + (others if kind == 2 else 0)
        visit(1, slot, 2 * parts - 1 - other, other > place)
        return carry

    if kind == 2:

        def both(i, carry):
            is_early = i < 2 * others
            j = jnp.where(is_early, i // 2, i - 2 * others)
            other = lax.rem(place + 1 + j, parts)
            late_query = jnp.where(is_early, lax.rem(i, 2), 1)
            slot = jnp.where(is_early, j, j + others)
            block = jnp.where(is_early, other, 2 * parts - 1 - other)
            wanted = jnp.where(
                is_early,
                ((late_query == 1) | (other < place)).astype(jnp.int32),
                (other > place).astype(jnp.int32),
            )
            visit(late_query, slot, block, wanted == 1)
            return carry

        lax.fori_loop(0, 3 * others, both, 0)
    elif kind == 0:
        lax.fori_loop(0, 2 * others, early, 0)
    else:
        lax.fori_loop(0, others, late, 0)


def fwd_remote_kernel(
    group, parts, kind, last, info, qT, kT, vT, acc_in, m_in, l_in, out, m_out, l_out, *scratch
):
    acc = scratch[0] if last else out
    acc[...] = acc_in[...]
    m_out[...] = m_in[...]
    l_out[...] = l_in[...]
    refs = (qT, kT, vT, m_out.at[0], l_out.at[0], acc)

    def full(q0, k0):
        fwd_chunk(q0, k0, group, group, None, None, *refs)

    def partial(q0, k0, limit):
        fwd_chunk(q0, k0, group, group, None, limit, *refs)

    remote_steps(group, parts, kind, info, full, partial)
    if last:
        for h in range(2):
            rows = slice(HEAD_DIM * h, HEAD_DIM * (h + 1))
            total = l_out[0, h : h + 1, :]
            out[rows, :] = (acc[rows, :] / total).astype(bf16)
            m_out[0, h : h + 1, :] = m_out[0, h : h + 1, :] + jnp.log2(total)


def split_three(values):
    high = values.astype(bf16).astype(f32)
    rest = values - high
    middle = rest.astype(bf16).astype(f32)
    low = (rest - middle).astype(bf16).astype(f32)
    return [high, middle, low]


def bwd_prepare(qT, kT, vT, doT, oT, lse, qa, da, ka, va):
    n_q, n_k = qT.shape[1], kT.shape[1]
    extra = qa.shape[1] - HEAD_DIM
    pad = jnp.zeros((extra - 3, n_q), f32)
    row_at = lax.broadcasted_iota(jnp.int32, (extra, n_k), 0)
    tail = jnp.where(row_at < 3, 1.0, 0.0).astype(bf16)
    for h in range(2):
        rows = slice(HEAD_DIM * h, HEAD_DIM * (h + 1))
        grad = doT[rows, :].astype(f32)
        delta = jnp.sum(grad * oT[rows, :].astype(f32), axis=0, keepdims=True)
        qa[h, :HEAD_DIM, :] = qT[rows, :]
        parts = split_three(-lse[0, h : h + 1, :]) + [pad]
        qa[h, HEAD_DIM:, :] = jnp.concatenate(parts, axis=0).astype(bf16)
        da[h, :HEAD_DIM, :] = doT[rows, :]
        parts = split_three(-delta) + [pad]
        da[h, HEAD_DIM:, :] = jnp.concatenate(parts, axis=0).astype(bf16)
        ka[h, :HEAD_DIM, :] = kT[rows, :]
        ka[h, HEAD_DIM:, :] = tail
        va[h, :HEAD_DIM, :] = vT[rows, :]
        va[h, HEAD_DIM:, :] = tail


def bwd_chunk(q0, k0, q_n, k_n, offset, limit, qT, kT, doT, qa, da, ka, va, dq, dk, dv):
    queries, keys = pl.ds(q0, q_n), pl.ds(k0, k_n)
    for h in range(2):
        rows = slice(HEAD_DIM * h, HEAD_DIM * (h + 1))
        probs = jnp.exp2(dot(qa[h, :, queries], ka[h, :, keys], 0, 0))
        if offset is not None or limit is not None:
            key_at = lax.broadcasted_iota(jnp.int32, (q_n, k_n), 1)
            last = jnp.zeros((q_n, 1), jnp.int32) + (limit - 1)
            if offset is not None:
                query_at = lax.broadcasted_iota(jnp.int32, (q_n, 1), 0)
                last = jnp.minimum(query_at + offset, last)
            probs = jnp.where(key_at <= last, probs, 0.0)
        d_probs = dot(da[h, :, queries], va[h, :, keys], 0, 0)
        d_scores = (probs * d_probs).astype(bf16)
        dv[rows, keys] += dot(doT[rows, queries], probs.astype(bf16), 1, 0)
        dk[rows, keys] += dot(qT[rows, queries], d_scores, 1, 0)
        dq[rows, queries] += dot(kT[rows, keys], d_scores, 1, 1)


def bwd_diagonal(base, group, qT, kT, doT, qa, da, ka, va, dq, dk, dv):
    strip = min(256, group)
    count = group // strip
    for h in range(2):
        rows = slice(HEAD_DIM * h, HEAD_DIM * (h + 1))
        d_keys, d_values, d_queries = None, None, []
        for j in range(count):
            wide = (j + 1) * strip
            queries, keys = pl.ds(base + j * strip, strip), pl.ds(base, wide)
            probs = jnp.exp2(dot(qa[h, :, queries], ka[h, :, keys], 0, 0))
            query_at = lax.broadcasted_iota(jnp.int32, probs.shape, 0)
            key_at = lax.broadcasted_iota(jnp.int32, probs.shape, 1)
            probs = jnp.where(key_at <= query_at + j * strip, probs, 0.0)
            d_probs = dot(da[h, :, queries], va[h, :, keys], 0, 0)
            d_scores = (probs * d_probs).astype(bf16)
            value = pad_right(dot(doT[rows, queries], probs.astype(bf16), 1, 0), group - wide)
            key = pad_right(dot(qT[rows, queries], d_scores, 1, 0), group - wide)
            d_values = value if d_values is None else d_values + value
            d_keys = key if d_keys is None else d_keys + key
            d_queries.append(dot(kT[rows, keys], d_scores, 1, 1))
        here = pl.ds(base, group)
        dq[rows, here] += jnp.concatenate(d_queries, axis=1) if count > 1 else d_queries[0]
        dk[rows, here] += d_keys
        dv[rows, here] += d_values


def turn_back(values, cosine, sine):
    half = HEAD_DIM // 2
    first, second = values[:half], values[half:]
    return jnp.concatenate(
        [first * cosine + second * sine, second * cosine - first * sine], axis=0
    )


def bwd_remote_kernel(group, parts, info, qT, kT, vT, doT, oT, lse, cosine, sine, *rest):
    dq, dkv, *scratch = rest[-8:]
    qa, da, ka, va, dk, dv = scratch
    bwd_prepare(qT, kT, vT, doT, oT, lse, qa, da, ka, va)
    dq[...] = jnp.zeros(dq.shape, f32)
    dk[...] = jnp.zeros(dk.shape, f32)
    dv[...] = jnp.zeros(dv.shape, f32)
    refs = (qT, kT, doT, qa, da, ka, va, dq, dk, dv)

    def full(q0, k0):
        bwd_chunk(q0, k0, group, group, None, None, *refs)

    def partial(q0, k0, limit):
        bwd_chunk(q0, k0, group, group, None, limit, *refs)

    remote_steps(group, parts, 2, info, full, partial)
    for h in range(2):
        rows = slice(HEAD_DIM * h, HEAD_DIM * (h + 1))
        dkv[0, rows, :] = turn_back(dk[rows, :] * LN2, cosine[...], sine[...]).astype(bf16)
    dkv[1] = dv[...].astype(bf16)


def bwd_local_kernel(group, info, qT, kT, vT, doT, oT, lse, cosine, sine, dq_in, *rest):
    dqkv, *scratch = rest[-8:]
    qa, da, ka, va, dq, dk, dv = scratch
    length = info[1]
    bwd_prepare(qT, kT, vT, doT, oT, lse, qa, da, ka, va)
    dq[...] = dq_in[...]
    dk[...] = jnp.zeros(dk.shape, f32)
    dv[...] = jnp.zeros(dv.shape, f32)
    refs = (qT, kT, doT, qa, da, ka, va, dq, dk, dv)

    def own(i, carry):
        base = pl.multiple_of(i * group, group)
        start = info[2 + i]

        @pl.when(start + group <= length)
        def _():
            bwd_diagonal(base, group, *refs)

        @pl.when((start < length) & (start + group > length))
        def _():
            bwd_chunk(base, base, group, group, 0, length - start, *refs)

        return carry

    lax.fori_loop(0, 2, own, 0)
    early = info[2]

    @pl.when(early + group <= length)
    def _():
        bwd_chunk(group, 0, group, group, None, None, *refs)

    @pl.when((early < length) & (early + group > length))
    def _():
        bwd_chunk(group, 0, group, group, None, length - early, *refs)

    for h in range(2):
        rows = slice(HEAD_DIM * h, HEAD_DIM * (h + 1))
        d_query = dq[rows, :] * 0.125
        dqkv[0, rows, :] = turn_back(d_query, cosine[...], sine[...]).astype(bf16)
        dqkv[1, rows, :] = turn_back(dk[rows, :] * LN2, cosine[...], sine[...]).astype(bf16)
    dqkv[2] = dv[...].astype(bf16)


def rows_of(count, first=0):
    return pl.BlockSpec((PAIR, count), lambda i, info: (first + i, 0))


def stats_of(count, first=0):
    return pl.BlockSpec((1, 2, count), lambda i, info: (first + i, 0, 0))


def planes_of(planes, count, first=0):
    return pl.BlockSpec((planes, PAIR, count), lambda i, info: (0, first + i, 0))


def whole(shape):
    return pl.BlockSpec(shape, lambda i, info: (0,) * len(shape))


def attention_call(kernel, pairs, in_specs, out_specs, out_shape, scratch, flops, name, alias={}):
    return pl.pallas_call(
        kernel,
        grid_spec=pltpu.PrefetchScalarGridSpec(
            num_scalar_prefetch=1,
            grid=(pairs,),
            in_specs=in_specs,
            out_specs=out_specs,
            scratch_shapes=scratch,
        ),
        out_shape=out_shape,
        input_output_aliases=alias,
        compiler_params=pltpu.CompilerParams(vmem_limit_bytes=VMEM),
        cost_estimate=pl.CostEstimate(
            flops=int(flops), bytes_accessed=1 << 25, transcendentals=0
        ),
        name=name,
    )


def attend_local(info, qT, kT, vT, group):
    width, n_q = qT.shape
    pairs = width // PAIR
    call = attention_call(
        functools.partial(fwd_local_kernel, group),
        pairs,
        [rows_of(n_q)] * 3,
        [rows_of(n_q), stats_of(n_q), stats_of(n_q)],
        [
            jax.ShapeDtypeStruct((width, n_q), f32),
            jax.ShapeDtypeStruct((pairs, 2, n_q), f32),
            jax.ShapeDtypeStruct((pairs, 2, n_q), f32),
        ],
        [],
        4 * width * 2 * group * group * 4,
        "attend_local",
    )
    return call(info, qT, kT, vT)


def attend_remote(info, qT, kT, vT, state, group, parts, kind, last):
    width, n_q = qT.shape
    n_k = kT.shape[1]
    pairs = width // PAIR
    scratch = [pltpu.VMEM((PAIR, n_q), f32)] if last else []
    call = attention_call(
        functools.partial(fwd_remote_kernel, group, parts, kind, last),
        pairs,
        [rows_of(n_q), rows_of(n_k), rows_of(n_k), rows_of(n_q), stats_of(n_q), stats_of(n_q)],
        [rows_of(n_q), stats_of(n_q), stats_of(n_q)],
        [
            jax.ShapeDtypeStruct((width, n_q), bf16 if last else f32),
            jax.ShapeDtypeStruct((pairs, 2, n_q), f32),
            jax.ShapeDtypeStruct((pairs, 2, n_q), f32),
        ],
        scratch,
        4 * width * group * group * 4,
        "attend_remote",
    )
    return call(info, qT, kT, vT, *state)


def back_scratch(n_q, n_k):
    rows = HEAD_DIM + 16
    return [
        pltpu.VMEM((2, rows, n_q), bf16),
        pltpu.VMEM((2, rows, n_q), bf16),
        pltpu.VMEM((2, rows, n_k), bf16),
        pltpu.VMEM((2, rows, n_k), bf16),
    ]


def back_remote(info, operands, lse, turns, group, parts, first, count, before):
    qT, kT = operands[:2]
    width, n_q = qT.shape
    n_k = kT.shape[1]
    half = HEAD_DIM // 2
    n_in = 1 + len(operands) + 1 + len(turns)
    call = attention_call(
        functools.partial(bwd_remote_kernel, group, parts),
        count,
        [rows_of(n_q, first), rows_of(n_k, first), rows_of(n_k, first)]
        + [rows_of(n_q, first)] * 2
        + [stats_of(n_q, first)]
        + [whole((half, n_k))] * 2
        + [pl.BlockSpec(memory_space=pl.ANY)] * len(before),
        [rows_of(n_q, first), planes_of(2, n_k, first)],
        [
            jax.ShapeDtypeStruct((width, n_q), f32),
            jax.ShapeDtypeStruct((2, width, n_k), bf16),
        ],
        back_scratch(n_q, n_k) + [pltpu.VMEM((PAIR, n_k), f32)] * 2,
        10 * count * PAIR * 2 * group * group * 4,
        "back_remote",
        {n_in + i: i for i in range(len(before))},
    )
    return call(info, *operands, lse, *turns, *before)


def back_local(info, operands, lse, turns, dq, group, first, count, before):
    qT = operands[0]
    width, n_q = qT.shape
    half = HEAD_DIM // 2
    n_in = 1 + len(operands) + 1 + len(turns) + 1
    call = attention_call(
        functools.partial(bwd_local_kernel, group),
        count,
        [rows_of(n_q, first)] * 5
        + [stats_of(n_q, first)]
        + [whole((half, n_q))] * 2
        + [rows_of(n_q, first)]
        + [pl.BlockSpec(memory_space=pl.ANY)] * len(before),
        planes_of(3, n_q, first),
        jax.ShapeDtypeStruct((3, width, n_q), bf16),
        back_scratch(n_q, n_q) + [pltpu.VMEM((PAIR, n_q), f32)] * 3,
        10 * count * PAIR * 2 * group * group * 4,
        "back_local",
        {n_in + i: i for i in range(len(before))},
    )
    return call(info, *operands, lse, *turns, dq, *before)


def normalize(values):
    centre = values - jnp.mean(values, axis=-1, keepdims=True)
    spread = jnp.mean(centre * centre, axis=-1, keepdims=True)
    rate = lax.rsqrt(spread + EPS)
    return centre * rate, rate


def norm_back(grad, unit, rate, gain):
    scaled = grad * gain
    first = jnp.mean(scaled, axis=-1, keepdims=True)
    second = jnp.mean(scaled * unit, axis=-1, keepdims=True)
    return rate * (scaled - first - unit * second)


GELU_A = 0.7978845608028654
GELU_B = 0.044715


def column_sum(values):
    return jnp.sum(values, axis=0, keepdims=True)


def block_kernel(
    span,
    oT,
    tokens,
    cotangent,
    w_out,
    w_up,
    w_down,
    b_out,
    b_up,
    b_down,
    gain_two,
    shift_two,
    gain_three,
    shift_three,
    gain_four,
    shift_four,
    result,
    d_middle_out,
    hidden_out,
    d_outer_out,
    normed_out,
    d_inner_out,
    d_branch_out,
    doT,
    small,
    small_up,
    slope,
):
    step = pl.program_id(0)

    @pl.when(step == 0)
    def _():
        small[...] = jnp.zeros(small.shape, f32)
        small_up[...] = jnp.zeros(small_up.shape, f32)

    wide = w_up.shape[1]
    branch = dot(oT[...], w_out[...], 0, 0) + b_out[...]
    unit_two, rate_two = normalize(branch)
    middle = tokens[...].astype(f32) + (unit_two * gain_two[...] + shift_two[...])
    unit_three, rate_three = normalize(middle)
    normed = (unit_three * gain_three[...] + shift_three[...]).astype(bf16)
    normed_out[...] = normed
    outer = None
    for c in range(wide // span):
        columns = slice(c * span, (c + 1) * span)
        inner = dot(normed, w_up[:, columns], 1, 0) + b_up[:, columns]
        square = inner * inner
        bend = jnp.tanh(inner * (GELU_A + (GELU_A * GELU_B) * square))
        half = 0.5 + 0.5 * bend
        hidden = (inner * half).astype(bf16)
        hidden_out[:, columns] = hidden
        slope[:, columns] = half + inner * (1.0 - bend * bend) * (
            0.5 * GELU_A + (1.5 * GELU_A * GELU_B) * square
        )
        term = dot(hidden, w_down[columns, :], 1, 0)
        outer = term if outer is None else outer + term
    unit_four, rate_four = normalize(outer + b_down[...])
    result[...] = (middle + (unit_four * gain_four[...] + shift_four[...])).astype(bf16)

    grad = cotangent[...].astype(f32)
    d_outer = norm_back(grad, unit_four, rate_four, gain_four[...]).astype(bf16)
    d_outer_out[...] = d_outer
    small[0:1, :] += column_sum(grad * unit_four)
    small[1:2, :] += column_sum(grad)
    small[2:3, :] += column_sum(d_outer.astype(f32))
    d_normed = None
    for c in range(wide // span):
        columns = slice(c * span, (c + 1) * span)
        d_hidden = dot(d_outer, w_down[columns, :], 1, 1)
        d_inner = (d_hidden * slope[:, columns]).astype(bf16)
        d_inner_out[:, columns] = d_inner
        small_up[:, columns] += column_sum(d_inner.astype(f32))
        term = dot(d_inner, w_up[:, columns], 1, 1)
        d_normed = term if d_normed is None else d_normed + term
    small[3:4, :] += column_sum(d_normed * unit_three)
    small[4:5, :] += column_sum(d_normed)
    d_middle = grad + norm_back(d_normed, unit_three, rate_three, gain_three[...])
    d_middle_out[...] = d_middle
    small[5:6, :] += column_sum(d_middle * unit_two)
    small[6:7, :] += column_sum(d_middle)
    d_branch = norm_back(d_middle, unit_two, rate_two, gain_two[...]).astype(bf16)
    d_branch_out[...] = d_branch
    small[7:8, :] += column_sum(d_branch.astype(f32))
    doT[...] = dot(w_out[...], d_branch, 1, 1).astype(bf16)


def block_call(oT, tokens, cotangent, weights, vectors):
    width, rows = oT.shape
    wide = weights[1].shape[1]
    step = min(256, rows)
    span = min(SPAN, wide)

    def lines(count):
        return pl.BlockSpec((step, count), lambda i: (i, 0))

    def fixed(shape):
        return pl.BlockSpec(shape, lambda i: (0, 0), pipeline_mode=pl.Buffered(1))

    def total(shape):
        return pl.BlockSpec(shape, lambda i: (0, 0))

    features = pl.BlockSpec((width, step), lambda i: (0, i))
    sizes = [width, width, wide, width, width, wide, width]
    kinds = [bf16, f32, bf16, bf16, bf16, bf16, bf16]
    return pl.pallas_call(
        functools.partial(block_kernel, span),
        grid=(rows // step,),
        in_specs=[features, lines(width), lines(width)]
        + [fixed(item.shape) for item in weights]
        + [fixed(item.shape) for item in vectors],
        out_specs=[lines(size) for size in sizes]
        + [features, total((8, width)), total((1, wide))],
        out_shape=[jax.ShapeDtypeStruct((rows, size), kind) for size, kind in zip(sizes, kinds)]
        + [
            jax.ShapeDtypeStruct((width, rows), bf16),
            jax.ShapeDtypeStruct((8, width), f32),
            jax.ShapeDtypeStruct((1, wide), f32),
        ],
        scratch_shapes=[pltpu.VMEM((step, wide), f32)],
        compiler_params=pltpu.CompilerParams(vmem_limit_bytes=VMEM),
        cost_estimate=pl.CostEstimate(
            flops=2 * 2 * rows * (width * width + 2 * width * wide),
            bytes_accessed=1 << 26,
            transcendentals=rows * wide,
        ),
        name="block",
    )(oT, tokens, cotangent, *weights, *vectors)


def bit_of(axis, position):
    return (lax.axis_index(axis) >> position) & 1


def swap(values, axis, position):
    size = lax.axis_size(axis)
    return lax.ppermute(values, axis, [(i, i ^ (1 << position)) for i in range(size)])


class Halving:
    def __init__(self, array, bits, order):
        self.bits = list(bits)
        self.order = list(order)
        rows = array.shape[0] >> len(bits)
        self.array = array.reshape((2,) * len(bits) + (rows, array.shape[1]))
        self.kept = self.received = None

    def send(self):
        bit = self.order.pop(0)
        at = self.bits.index(bit)
        mine = bit_of(*bit)
        away = lax.dynamic_index_in_dim(self.array, 1 - mine, at, False)
        self.kept = (self.array, mine, at)
        self.received = swap(away, *bit)
        self.bits.pop(at)

    def add(self):
        array, mine, at = self.kept
        kept = lax.dynamic_index_in_dim(array, mine, at, False).astype(f32)
        total = kept + self.received.astype(f32)
        self.array = total.astype(bf16) if self.bits else total

    def result(self):
        return self.array


class Adding:
    def __init__(self, array, order):
        self.array, self.order = array, list(order)

    def send(self):
        self.received = swap(self.array, *self.order.pop(0))

    def add(self):
        self.array = self.array + self.received


def tie(lead, sums):
    held, arrays = lax.optimization_barrier((lead, [item.array for item in sums]))
    for item, array in zip(sums, arrays):
        item.array = array
    return held


def turn_forward(values, cosine, sine):
    features, tokens = values.shape
    half = HEAD_DIM // 2
    pairs = values.reshape(features // HEAD_DIM, 2, half, tokens)
    first, second = pairs[:, 0], pairs[:, 1]
    turned = jnp.stack(
        [first * cosine - second * sine, second * cosine + first * sine], axis=1
    )
    return turned.reshape(features, tokens)


def angles(positions):
    half = HEAD_DIM // 2
    freqs = jnp.power(10000.0, -jnp.arange(half, dtype=f32) / half)
    theta = freqs[:, None] * positions.astype(f32)[None, :]
    return jnp.cos(theta), jnp.sin(theta)


def axis_bits(axis):
    return [(axis, position) for position in range(lax.axis_size(axis).bit_length() - 1)]


def body(
    inputs,
    cotangent,
    lengths,
    w_qkv,
    b_qkv,
    w_out,
    b_out,
    w_up,
    b_up,
    w_down,
    b_down,
    gain_one,
    shift_one,
    gain_two,
    shift_two,
    gain_three,
    shift_three,
    gain_four,
    shift_four,
):
    group = inputs.shape[3]
    width = inputs.shape[4]
    parts = lax.axis_size("narrow")
    place = lax.axis_index("narrow")
    others = parts - 1
    rows = 2 * group
    offsets = jnp.arange(group, dtype=jnp.int32)

    own_blocks = inputs.reshape(2, group, width)
    far_early, far_late = [], []
    for shift in range(1, parts):
        pairs = [((n + shift) % parts, n) for n in range(parts)]
        far_early.append(lax.ppermute(own_blocks[0], "narrow", pairs))
    for shift in range(1, parts):
        pairs = [((n + shift) % parts, n) for n in range(parts)]
        later = [(source, n) for source, n in pairs if source > n]
        far_late.append(lax.ppermute(own_blocks[1], "narrow", later))
    other = (place + 1 + jnp.arange(others, dtype=jnp.int32)) % parts

    early_at = place * group
    late_at = (2 * parts - 1 - place) * group
    info = jnp.stack([place, lengths[0], early_at, late_at]).astype(jnp.int32)
    own_pos = jnp.concatenate([early_at + offsets, late_at + offsets])
    far_early_pos = (other[:, None] * group + offsets[None]).reshape(-1)
    far_late_pos = ((2 * parts - 1 - other)[:, None] * group + offsets[None]).reshape(-1)
    cosine, sine = angles(own_pos)
    cosine_fe, sine_fe = angles(far_early_pos)
    cosine_fl, sine_fl = angles(far_late_pos)

    tokens = own_blocks.astype(f32).reshape(rows, width)
    normed_low = layer_norm(tokens, gain_one, shift_one).astype(bf16)
    mixedT = dot(w_qkv, normed_low, 0, 1) + b_qkv[:, None]
    qT = (turn_forward(mixedT[:width], cosine, sine) * (0.125 * LOG2E)).astype(bf16)
    kT = turn_forward(mixedT[width : 2 * width], cosine, sine).astype(bf16)
    vT = mixedT[2 * width :].astype(bf16)
    state = attend_local(info, qT, kT, vT, group)

    def far_keys(blocks, cos, sin):
        far = jnp.concatenate(blocks, axis=0).astype(f32)
        far_normed = layer_norm(far, gain_one, shift_one).astype(bf16)
        far_mixed = dot(w_qkv[:, width:], far_normed, 0, 1) + b_qkv[width:, None]
        keys = turn_forward(far_mixed[:width], cos, sin).astype(bf16)
        return far_normed, keys, far_mixed[width:].astype(bf16)

    normed_fe, kT_fe, vT_fe = far_keys(far_early, cosine_fe, sine_fe)
    state = attend_remote(info, qT, kT_fe, vT_fe, state, group, parts, 0, False)
    normed_fl, kT_fl, vT_fl = far_keys(far_late, cosine_fl, sine_fl)
    oT, lse, _ = attend_remote(info, qT, kT_fl, vT_fl, state, group, parts, 1, True)

    row = lambda vector: vector[None, :]
    blocks = block_call(
        oT,
        own_blocks.reshape(rows, width),
        cotangent.reshape(rows, width),
        [w_out, w_up, w_down],
        [row(item) for item in (b_out, b_up, b_down)]
        + [row(item) for item in (gain_two, shift_two, gain_three, shift_three)]
        + [row(item) for item in (gain_four, shift_four)],
    )
    result, d_middle, hidden, d_outer, normed_two, d_inner, d_branch, doT, small, small_up = blocks

    wide_bits = axis_bits("wide")
    narrow_bits = axis_bits("narrow")
    bits = wide_bits[::-1] + narrow_bits[::-1]
    first_order = wide_bits[:2] + narrow_bits + wide_bits[2:]
    second_order = wide_bits[:1] + narrow_bits + wide_bits[1:]
    steps = len(bits)

    sum_down = Halving(dot(d_outer, hidden, 0, 0).astype(bf16), bits, second_order)
    sum_down.send()
    sum_up = Halving(dot(d_inner, normed_two, 0, 0).astype(bf16), bits, first_order)
    sum_up.send()
    sum_out = Halving(dot(d_branch, oT, 0, 1).astype(bf16), bits, first_order)
    sum_out.send()
    early = Adding(jnp.concatenate([small.reshape(-1), small_up.reshape(-1)]), first_order)
    early.send()
    sums = [sum_down, sum_up, sum_out, early]

    def advance(lead):
        for item in sums:
            item.add()
        lead = tie(lead, sums)
        if sum_down.order:
            for item in sums:
                item.send()
        return lead

    kT_far = jnp.concatenate([kT_fe, kT_fl], axis=1)
    vT_far = jnp.concatenate([vT_fe, vT_fl], axis=1)
    turns_far = [
        jnp.concatenate([cosine_fe, cosine_fl], axis=1),
        jnp.concatenate([sine_fe, sine_fl], axis=1),
    ]
    heads = width // PAIR
    portions = 2 if heads % 2 == 0 else 1
    count = heads // portions
    far = []
    for portion in range(portions):
        doT = advance(doT)
        operands = [qT, kT_far, vT_far, doT, oT]
        far = back_remote(
            info, operands, lse, turns_far, group, parts, portion * count, count, far
        )
    dq_far, dkv_far = far
    dkv_far = dkv_far.reshape(2 * width, -1)
    w_qkvT = w_qkv.T
    d_normed_far = dot(dkv_far, w_qkvT[width:], 0, 0).astype(bf16)
    returned_early, returned_late = [], []
    for j in range(others):
        shift = j + 1
        pairs = [(n, (n + shift) % parts) for n in range(parts)]
        piece = d_normed_far[j * group : (j + 1) * group]
        returned_early.append(lax.ppermute(piece, "narrow", pairs))
    for j in range(others):
        shift = j + 1
        pairs = [(n, (n + shift) % parts) for n in range(parts)]
        later = [(n, owner) for n, owner in pairs if owner > n]
        piece = d_normed_far[(others + j) * group : (others + j + 1) * group]
        returned_late.append(lax.ppermute(piece, "narrow", later))
    dqkv = []
    for portion in range(portions):
        doT = advance(doT)
        operands = [qT, kT, vT, doT, oT]
        dqkv = [
            back_local(
                info, operands, lse, [cosine, sine], dq_far, group, portion * count, count, dqkv
            )
        ]
    dqkv = dqkv[0].reshape(3 * width, rows)
    while sum_down.order:
        dqkv = advance(dqkv)
    for item in sums:
        item.add()

    normed_far = jnp.concatenate([normed_fe, normed_fl], axis=0)
    grad_q = dot(dqkv[:width], normed_low, 1, 0)
    grad_kv = dot(dqkv[width:], normed_low, 1, 0) + dot(dkv_far, normed_far, 1, 0)
    grad_w_qkv = jnp.concatenate([grad_q.astype(bf16), grad_kv.astype(bf16)], axis=0)
    share = grad_w_qkv.shape[0] >> steps
    cut = share // 2
    pieces = grad_w_qkv.reshape(1 << steps, share, width)
    sum_first = Halving(pieces[:, :cut].reshape(-1, width), bits, first_order)
    sum_second = Halving(pieces[:, cut:].reshape(-1, width), bits, second_order)
    sum_first.send()
    sum_second.send()
    grad_b_qkv = jnp.sum(dqkv.astype(f32), axis=1) + jnp.concatenate(
        [jnp.zeros((width,), f32), jnp.sum(dkv_far.astype(f32), axis=1)]
    )
    weighted = w_qkvT.astype(f32)
    part_shift = jnp.sum(weighted * grad_b_qkv[:, None], axis=0)
    part_gain = jnp.sum(weighted * grad_w_qkv.astype(f32), axis=0)
    part_gain = (part_gain - shift_one * part_shift) / gain_one
    late = Adding(jnp.concatenate([grad_b_qkv, part_gain, part_shift]), first_order)
    late.send()
    sums = [sum_first, sum_second, late]

    dqkv = tie(dqkv, [])
    d_normed = dot(dqkv, w_qkvT, 0, 0)
    for item in sums:
        item.add()
    d_normed = tie(d_normed, sums)
    for item in sums:
        item.send()
    back_early = functools.reduce(jnp.add, [item.astype(f32) for item in returned_early])
    back_late = functools.reduce(jnp.add, [item.astype(f32) for item in returned_late])
    d_normed = d_normed + jnp.concatenate([back_early, back_late], axis=0)
    unit_one, rate_one = normalize(tokens)
    d_tokens = d_middle + norm_back(d_normed, unit_one, rate_one, gain_one)
    d_tokens = d_tokens.astype(bf16)
    while sum_first.order:
        for item in sums:
            item.add()
        d_tokens = tie(d_tokens, sums)
        for item in sums:
            item.send()
    for item in sums:
        item.add()

    qkv_rows = jnp.concatenate([sum_first.result(), sum_second.result()], axis=0)
    down_rows = sum_down.result().reshape(-1, w_down.shape[0])
    wide = w_up.shape[1]
    small = early.array[: 8 * width].reshape(8, width)
    small_up = early.array[8 * width :]
    late_small = late.array
    shape = inputs.shape
    return (
        result.reshape(shape),
        d_tokens.reshape(shape),
        qkv_rows.T,
        sum_out.result().T,
        sum_up.result().T,
        down_rows.T,
        late_small[: 3 * width],
        small[7],
        small_up,
        small[2],
        late_small[3 * width : 4 * width],
        late_small[4 * width :],
        small[5],
        small[6],
        small[3],
        small[4],
        small[0],
        small[1],
    )


def solution(mesh):
    tokens = P("wide", None, "narrow", None, None)
    columns = P(None, ("wide", "narrow"))
    in_specs = (tokens, tokens, P("wide")) + (P(),) * 16
    out_specs = (tokens, tokens) + (columns,) * 4 + (P(),) * 12
    return jax.shard_map(body, mesh=mesh, in_specs=in_specs, out_specs=out_specs, check_vma=False)
```

time: 3520 us -> 946 us (0.27)
  matrix products: 1820 us -> 145 us
  waiting for transfers between devices: 1030 us -> 24.8 us
  Pallas kernels: 0 us -> 465 us
  other arithmetic: 354 us -> 117 us
  local copies, waits for them, and re-layouts: 253 us -> 93.4 us
  starting transfers between devices: 0.37 us -> 85.4 us
    dot_general x28 -> x11, matrix products: 1820 us -> 145 us  [dot(): lax.dot_general(left, right, (((left_dim,), (right_dim,)), ((), ())), pre...]
    reduce_scatter x4 -> x0, waiting for transfers between devices: 886 us -> none  [the longest x1 361 us: body(): lax.psum_scatter(grad_w_up, ('wide', 'narrow'), scatter_dimension=1, tile...]
    pallas_call x0 -> x8, Pallas kernels: none -> 465 us  [the longest x2 117 us: back_local(): return call(info, *operands, lse, *turns, dq, *before)]
    reduce_sum x10 -> x4, other arithmetic: 210 us -> 23 us  [the longest x1 6.3 us: body(): part_gain = jnp.sum(weighted * grad_w_qkv.astype(f32), axis=0)]
    all_gather x4 -> x0, waiting for transfers between devices: 106 us -> none  [the longest x1 84.3 us: body(): lax.all_gather(keys_low, 'narrow', axis=2, tiled=True)]
    ppermute x0 -> x39, starting transfers between devices: none -> 85.4 us  [the longest x35 76 us: swap(): lax.ppermute(values, axis, [(i, i ^ 1 << position) for i in range(size)])]
    another operation x8 -> x0, local copies, waits for them, and re-layouts: 62.6 us -> none
    unnamed x153 -> x134, local copies, waits for them, and re-layouts: 75.5 us -> 26.1 us
  transfers between devices with their start and end apart: 9 -> 39, of which waited for: 6 -> 9; matrix products, arithmetic and copies ran while one was open for 67% -> 29% of each run, Pallas kernels for 0% -> 31%
where the time goes in v1:
time: 946 us; the launch traced here: 934 us
  Pallas kernels  465 us (49%)
  matrix products  145 us (15%)
  other arithmetic  117 us (12%)
  local copies, waits for them, and re-layouts  93.4 us (10%)
  starting transfers between devices  85.4 us (9%)
  waiting for transfers between devices  24.8 us (3%)
    dot_general x11, matrix products, dot(): lax.dot_general(left, right, (((left_dim,), (right_dim,)), ((), ())), pre...  145 us
    pallas_call x2, Pallas kernels, back_local(): return call(info, *operands, lse, *turns, dq, *before)  117 us
    pallas_call x1, Pallas kernels, block_call(): pl.pallas_call(functools.partial(block_kernel, span), grid=(rows // step,...  116 us
    pallas_call x2, Pallas kernels, back_remote(): return call(info, *operands, lse, *turns, *before)  97.2 us
    ppermute x35, starting transfers between devices, swap(): lax.ppermute(values, axis, [(i, i ^ 1 << position) for i in range(size)])  76 us
    pallas_call x1, Pallas kernels, attend_local(): return call(info, qT, kT, vT)  72.3 us
    pallas_call x2, Pallas kernels, attend_remote(): return call(info, qT, kT, vT, *state)  63.3 us
    convert_element_type x20, other arithmetic, add(): self.array = total.astype(bf16) if self.bits else total  31.8 us
  transfers between devices with their start and end apart: 39, of which 9 were waited for; matrix products, arithmetic and copies ran while one was open for 29% of the time, Pallas kernels for 31%

profile of v1, /device:TPU:0, one launch (start us, length us, event | category | flops | bytes accessed | tf_op | source)
XLA Modules:
  0.0 934.0 jit_solution(9941796266419009748)
XLA Ops:
  12.5 22.1 %add_bitcast_fusion = f32[3072,2048]{1,0:T(8,128)} fusion(bf16[1024,3072]{1,0:T(8,128)(2,1)} %param.22, f32[3072]{0:T(1024)S(1)} %copy-done.51, bf16[2048,1024]{1,0:T(8,128)(2,1)} %bitcast.235, f32[1024]{0:T(1024)S(1)} %copy-done.46, f32[1024]{0:T(1024)S(1)} %copy-done.36, f32[2048]{0:T(1024)S(1)} %get-tuple-element.224, f32[2048]{0:T(1024)S(1)} %get-tuple-element.225), kind=kOutput, calls=%fused_computation.1 | convolution fusion | flops 12903776256 | bytes 35688448 | tf_op jit(solution)/shard_map/dot_general | solution.py:30
  34.6 10.8 %fusion.69 = (f32[1024,2048]{1,0:T(8,128)}, f32[1024,2048]{1,0:T(8,128)}) fusion(f32[3072,2048]{1,0:T(8,128)} %add_bitcast_fusion), kind=kLoop, calls=%fused_computation.200 | loop fusion | bytes 33554432 | tf_op jit(solution)/shard_map/slice | solution.py:796
  45.4 6.0 slice.251.vT
  53.2 7.6 subtract_convert_fusion
  66.5 72.3 %attend_local.1 = (f32[1024,2048]{1,0:T(8,128)}, f32[8,2,2048]{2,1,0:T(2,128)}, f32[8,2,2048]{2,1,0:T(2,128)}) custom-call(s32[4]{0:T(128)} %pad_add_fusion.1.info, bf16[1024,2048]{1,0:T(8,128)(2,1)} %bitcast.266, bf16[1024,2048]{1,0:T(8,128)(2,1)} %bitcast.276, bf16[1024,2048]{1,0:T(8,128)(2,1)} %slice.251.vT), custom_call_target="tpu_custom_call" | custom-call | flops 34359738368 | bytes 33554432 | tf_op jit(solution)/shard_map/attend_local/pallas_call | solution.py:429
  174.7 31.8 %attend_remote.2 = (f32[1024,2048]{1,0:T(8,128)}, f32[8,2,2048]{2,1,0:T(2,128)}, f32[8,2,2048]{2,1,0:T(2,128)}) custom-call(s32[4]{0:T(128)} %pad_add_fusion.1.info, bf16[1024,2048]{1,0:T(8,128)(2,1)} %bitcast.267, bf16[1024,1024]{1,0:T(8,128)(2,1)} %bitcast.260, bf16[1024,1024]{1,0:T(8,128)(2,1)} %slice.252.vT, f32[1024,2048]{1,0:T(8,128)} %get-tuple-element.76.acc_in, ...), custom_call_target="tpu_custom_call" | custom-call | flops 17179869184 | bytes 33554432 | tf_op jit(solution)/shard_map/attend_remote/pallas_call | solution.py:451
  206.5 31.5 %attend_remote.3 = (bf16[1024,2048]{1,0:T(8,128)(2,1)}, f32[8,2,2048]{2,1,0:T(2,128)}, f32[8,2,2048]{2,1,0:T(2,128)}) custom-call(s32[4]{0:T(128)} %pad_add_fusion.1.info, bf16[1024,2048]{1,0:T(8,128)(2,1)} %bitcast.268, bf16[1024,1024]{1,0:T(8,128)(2,1)} %bitcast.262, bf16[1024,1024]{1,0:T(8,128)(2,1)} %slice.253.vT, ...), custom_call_target="tpu_custom_call" | custom-call | flops 17179869184 | bytes 33554432 | tf_op jit(solution)/shard_map/attend_remote/pallas_call | solution.py:451
  238.0 115.9 %block.1 = (bf16[2048,1024]{1,0:T(8,128)(2,1)}, f32[2048,1024]{1,0:T(8,128)}, bf16[2048,4096]{1,0:T(8,128)(2,1)}, bf16[2048,1024]{1,0:T(8,128)(2,1)}, bf16[2048,...) custom-call(bf16[1024,2048]{1,0:T(8,128)(2,1)} %get-tuple-element.82, ...), custom_call_target="tpu_custom_call" | custom-call | flops 77309411328 | bytes 67108864 | tf_op jit(solution)/shard_map/block/pallas_call | solution.py:641
  353.9 21.9 %convolution_convert_fusion = bf16[4096,1024]{1,0:T(8,128)(2,1)S(1)} fusion(bf16[2048,4096]{1,0:T(8,128)(2,1)} %get-tuple-element.88, bf16[2048,1024]{1,0:T(8,128)(2,1)} %get-tuple-element.89), kind=kOutput, calls=%fused_computation.30 | convolution fusion | flops 17184063488 | bytes 29360128 | tf_op jit(solution)/shard_map/dot_general | solution.py:30
  380.4 6.2 copy.58
  386.6 21.9 %convolution_convert_fusion.1 = bf16[1024,4096]{1,0:T(8,128)(2,1)S(1)} fusion(bf16[2048,1024]{1,0:T(8,128)(2,1)} %get-tuple-element.86, bf16[2048,4096]{1,0:T(8,128)(2,1)} %get-tuple-element.87), kind=kOutput, calls=%fused_computation.31 | convolution fusion | flops 17184063488 | bytes 29360128 | tf_op jit(solution)/shard_map/dot_general | solution.py:30
  414.3 8.8 copy.63
  423.9 5.2 fusion.7
  442.1 6.2 copy.70
  467.6 11.0 %collective-permute-start.6 = (bf16[2,2,2,32,4096]{4,3,0,1,2:T(8,128)(2,1)}, bf16[2,2,2,32,4096]{4,3,0,1,2:T(8,128)(2,1)}, u32[]{:S(2)}, u32[]{:S(2)}) collective-permute-start(bf16[2,2,2,32,4096]{4,3,0,1,2:T(8,128)(2,1)} %dynamic-slice_bitcast_fusion.1), channel_id=1, source_target_pairs={{0,1},{1,0},{2,3},{3,2},{4,5},{5,4},{6,7},{7,6},{8,9},{9,8},{10,11... | collective-permute-start | bytes 6291464 | tf_op jit(solution)/shard_map/ppermute | solution.py:672
  478.6 48.5 %back_remote.2 = (f32[1024,2048]{1,0:T(8,128)}, bf16[2,1024,2048]{2,1,0:T(8,128)(2,1)}) custom-call(s32[4]{0:T(128)} %pad_add_fusion.1.info, bf16[1024,2048]{1,0:T(8,128)(2,1)} %bitcast.269, bf16[1024,2048]{1,0:T(8,128)(2,1)} %pad_maximum_fusion.2.kT, bf16[1024,2048]{1,0:T(8,128)(2,1)} %pad_maximum_fusion.3.vT, bf16[1024,2048]{1,0:T(8,128)(2,1)} %get-tuple-element.108.doT, ...), custom_call_target="tpu_custom_call" | custom-call | flops 42949672960 | bytes 33554432 | tf_op jit(solution)/shard_map/back_remote/pallas_call | solution.py:488
  534.5 5.5 collective-permute-start.13
  544.1 48.7 %back_remote.3 = (f32[1024,2048]{1,0:T(8,128)}, bf16[2,1024,2048]{2,1,0:T(8,128)(2,1)}) custom-call(s32[4]{0:T(128)} %pad_add_fusion.1.info, bf16[1024,2048]{1,0:T(8,128)(2,1)} %bitcast.270, bf16[1024,2048]{1,0:T(8,128)(2,1)} %pad_maximum_fusion.2.kT, bf16[1024,2048]{1,0:T(8,128)(2,1)} %pad_maximum_fusion.3.vT, ...), custom_call_target="tpu_custom_call", output_to_operand_aliasing={{0}: (9, {}), {1}: (10, {})} | custom-call | flops 42949672960 | bytes 33554432 | tf_op jit(solution)/shard_map/back_remote/pallas_call | solution.py:488
  598.5 11.2 %fusion.38 = bf16[2048,1024]{1,0:T(8,128)(2,1)S(1)} fusion(bf16[2048,2048]{1,0:T(8,128)(2,1)S(1)} %bitcast.253, bf16[3072,1024]{1,0:T(8,128)(2,1)} %bitcast.242), kind=kOutput, calls=%fused_computation.76 | convolution fusion | flops 8592031744 | bytes 16777216 | tf_op jit(solution)/shard_map/dot_general | solution.py:30
  622.3 58.3 %back_local.2.rest_0_ = bf16[3,1024,2048]{2,1,0:T(8,128)(2,1)} custom-call(s32[4]{0:T(128)} %pad_add_fusion.1.info, bf16[1024,2048]{1,0:T(8,128)(2,1)} %bitcast.271, bf16[1024,2048]{1,0:T(8,128)(2,1)} %bitcast.277, bf16[1024,2048]{1,0:T(8,128)(2,1)} %slice.251.vT, bf16[1024,2048]{1,0:T(8,128)(2,1)} %get-tuple-element.108.doT, ...), custom_call_target="tpu_custom_call" | custom-call | flops 42949672960 | bytes 33554432 | tf_op jit(solution)/shard_map/back_local/pallas_call | solution.py:511
  689.3 58.5 %back_local.3 = bf16[3,1024,2048]{2,1,0:T(8,128)(2,1)} custom-call(s32[4]{0:T(128)} %pad_add_fusion.1.info, bf16[1024,2048]{1,0:T(8,128)(2,1)} %bitcast.272, bf16[1024,2048]{1,0:T(8,128)(2,1)} %bitcast.278, bf16[1024,2048]{1,0:T(8,128)(2,1)} %slice.251.vT, bf16[1024,2048]{1,0:T(8,128)(2,1)} %get-tuple-element.108.doT, ...), custom_call_target="tpu_custom_call", output_to_operand_aliasing={{}: (10, {})} | custom-call | flops 42949672960 | bytes 33554432 | tf_op jit(solution)/shard_map/back_local/pallas_call | solution.py:511
  747.8 6.3 convert_reduce_fusion
  754.1 8.3 slice.200
  762.4 9.4 %fusion.48 = bf16[1024,1024]{1,0:T(8,128)(2,1)} fusion(bf16[2048,1024]{1,0:T(8,128)(2,1)} %bitcast.274, bf16[3,1024,2048]{2,1,0:T(8,128)(2,1)} %back_local.3), kind=kOutput, calls=%fused_computation.99 | convolution fusion | flops 4296015872 | bytes 10485760 | tf_op jit(solution)/shard_map/dot_general | solution.py:30
  771.8 11.0 %fusion.75 = f32[2048,1024]{1,0:T(8,128)} fusion(bf16[2048,2048]{1,0:T(8,128)(2,1)S(1)} %bitcast.259, bf16[2048,1024]{1,0:T(8,128)(2,1)S(1)} %bitcast.275), kind=kOutput, calls=%fused_computation.206 | convolution fusion | flops 8589934592 | bytes 20971520 | tf_op jit(solution)/shard_map/dot_general | solution.py:30
  782.9 12.5 %add_convert_fusion.1 = bf16[2048,1024]{1,0:T(8,128)(2,1)} fusion(f32[2048,1024]{1,0:T(8,128)} %fusion.75, bf16[2048,2048]{1,0:T(8,128)(2,1)S(1)} %bitcast.256, bf16[1024,1024]{1,0:T(8,128)(2,1)S(1)} %copy-done.24, bf16[1024,1024]{1,0:T(8,128)(2,1)S(1)} %copy-done.22), kind=kOutput, calls=%fused_computation.25 | convolution fusion | flops 8602517504 | bytes 25165824 | tf_op jit(solution)/shard_map/dot_general | solution.py:30
  800.1 6.3 fusion
  813.6 20.7 %fusion.74 = f32[2048,1024]{1,0:T(8,128)S(1)} fusion(bf16[3072,2048]{1,0:T(8,128)(2,1)S(1)} %bitcast.239, bf16[1024,3072]{1,0:T(8,128)(2,1)} %param.22), kind=kOutput, calls=%fused_computation.205 | convolution fusion | flops 12884901888 | bytes 27262976 | tf_op jit(solution)/shard_map/dot_general | solution.py:30
  835.1 11.3 %collective-permute-start.38 = (f32[12288]{0:T(1024)S(1)}, f32[12288]{0:T(1024)S(1)}, u32[]{:S(2)}, u32[]{:S(2)}) collective-permute-start(f32[12288]{0:T(1024)S(1)} %add.435), channel_id=1, source_target_pairs={{0,16},{2,18},{4,20},{6,22},{8,24},{10,26},{12,28},{14,30},{16,0},... | collective-permute-start | bytes 147464 | tf_op jit(solution)/shard_map/ppermute | solution.py:672
  863.8 19.3 %collective-permute-start.25 = (f32[5120]{0:T(1024)S(1)}, f32[5120]{0:T(1024)S(1)}, u32[]{:S(2)}, u32[]{:S(2)}) collective-permute-start(f32[5120]{0:T(1024)S(1)} %fusion.66), channel_id=1, source_target_pairs={{0,4},{2,6},{4,0},{6,2},{8,12},{10,14},{12,8},{14,10},{16,20},{18,... | collective-permute-start | bytes 61448 | tf_op jit(solution)/shard_map/ppermute | solution.py:672
  883.5 5.8 fusion.68
  889.3 7.4 add_convert_fusion
  (330 shorter events, 202.5 us)
Async XLA Ops:
  5.5 134.4 %collective-permute-start.1 = (bf16[1024,1024]{1,0:T(8,128)(2,1)}, bf16[1024,1024]{1,0:T(8,128)(2,1)}, u32[]{:S(2)}, u32[]{:S(2)}) collective-permute-start(bf16[1024,1024]{1,0:T(8,128)(2,1)} %get-tuple-element.192), channel_id=1, source_target_pairs={{1,0},{0,1},{3,2},{2,3},{5,4},{4,5},{7,6},{6,7},{9,8},{8,9},{11,10... | collective-permute-start | bytes 6291464 | tf_op jit(solution)/shard_map/ppermute | solution.py:775
  8.4 135.8 %collective-permute-start = (bf16[1024,1024]{1,0:T(8,128)(2,1)}, bf16[1024,1024]{1,0:T(8,128)(2,1)}, u32[]{:S(2)}, u32[]{:S(2)}) collective-permute-start(bf16[1024,1024]{1,0:T(8,128)(2,1)} %get-tuple-element.193), channel_id=1, source_target_pairs={{1,0},{3,2},{5,4},{7,6},{9,8},{11,10},{13,12},{15,14},{17,16},{19,... | collective-permute-start | bytes 6291464 | tf_op jit(solution)/shard_map/ppermute | solution.py:779
  386.6 64.4 %collective-permute-start.3 = (bf16[2,2,2,2,128,1024]{4,5,0,1,3,2:T(8,128)(2,1)}, bf16[2,2,2,2,128,1024]{4,5,0,1,3,2:T(8,128)(2,1)}, u32[]{:S(2)}, u32[]{:S(2)}) collective-permute-start(bf16[2,2,2,2,128,1024]{4,5,0,1,3,2:T(8,128)(2,1)} %bitcast.279), channel_id=1, source_target_pairs={{0,2},{2,0},{4,6},{6,4},{8,10},{10,8},{12,14},{14,12},{16,18},{18,... | collective-permute-start | bytes 12582920 | tf_op jit(solution)/shard_map/ppermute | solution.py:672
  413.7 42.0 %collective-permute-start.2 = (bf16[2,2,2,2,32,4096]{5,4,0,1,2,3:T(8,128)(2,1)}, bf16[2,2,2,2,32,4096]{5,4,0,1,2,3:T(8,128)(2,1)}, u32[]{:S(2)}, u32[]{:S(2)}) collective-permute-start(bf16[2,2,2,2,32,4096]{5,4,0,1,2,3:T(8,128)(2,1)} %bitcast.230), channel_id=1, source_target_pairs={{0,2},{2,0},{4,6},{6,4},{8,10},{10,8},{12,14},{14,12},{16,18},{18,... | collective-permute-start | bytes 12582920 | tf_op jit(solution)/shard_map/ppermute | solution.py:672
  429.2 19.1 %collective-permute-start.5 = (f32[12288]{0:T(1024)S(1)}, f32[12288]{0:T(1024)S(1)}, u32[]{:S(2)}, u32[]{:S(2)}) collective-permute-start(f32[12288]{0:T(1024)S(1)} %pad_maximum_fusion.8), channel_id=1, source_target_pairs={{0,2},{2,0},{4,6},{6,4},{8,10},{10,8},{12,14},{14,12},{16,18},{18,... | collective-permute-start | bytes 147464 | tf_op jit(solution)/shard_map/ppermute | solution.py:672
  435.3 13.1 %collective-permute-start.4 = (bf16[2,2,2,2,32,1024]{5,4,0,1,3,2:T(8,128)(2,1)S(1)}, bf16[2,2,2,2,32,1024]{5,4,0,1,3,2:T(8,128)(2,1)S(1)}, u32[]{:S(2)}, u32[]{:S(2)}) collective-permute-start(bf16[2,2,2,2,32,1024]{5,4,0,1,3,2:T(8,128)(2,1)S(1)} %bitcast.281), channel_id=1, source_target_pairs={{0,2},{2,0},{4,6},{6,4},{8,10},{10,8},{12,14},{14,12},{16,18},{18,... | collective-permute-start | bytes 3145736 | tf_op jit(solution)/shard_map/ppermute | solution.py:672
  461.0 66.1 %collective-permute-start.9 = (f32[12288]{0:T(1024)S(1)}, f32[12288]{0:T(1024)S(1)}, u32[]{:S(2)}, u32[]{:S(2)}) collective-permute-start(f32[12288]{0:T(1024)S(1)} %fusion.67), channel_id=1, source_target_pairs={{0,4},{2,6},{4,0},{6,2},{8,12},{10,14},{12,8},{14,10},{16,20},{18,... | collective-permute-start | bytes 147464 | tf_op jit(solution)/shard_map/ppermute | solution.py:672
  462.6 64.5 %collective-permute-start.8 = (bf16[2,2,2,32,1024]{4,3,0,1,2:T(8,128)(2,1)S(1)}, bf16[2,2,2,32,1024]{4,3,0,1,2:T(8,128)(2,1)}, u32[]{:S(2)}, u32[]{:S(2)}) collective-permute-start(bf16[2,2,2,32,1024]{4,3,0,1,2:T(8,128)(2,1)S(1)} %dynamic-slice_bitcast_fusion.9), channel_id=1, source_target_pairs={{0,4},{2,6},{4,0},{6,2},{8,12},{10,14},{12,8},{14,10},{16,20},{18,... | collective-permute-start | bytes 1572872 | tf_op jit(solution)/shard_map/ppermute | solution.py:672
  464.6 63.9 %collective-permute-start.7 = (bf16[2,2,2,128,1024]{3,4,0,1,2:T(8,128)(2,1)}, bf16[2,2,2,128,1024]{3,4,0,1,2:T(8,128)(2,1)}, u32[]{:S(2)}, u32[]{:S(2)}) collective-permute-start(bf16[2,2,2,128,1024]{3,4,0,1,2:T(8,128)(2,1)} %dynamic-slice_bitcast_fusion), channel_id=1, source_target_pairs={{0,4},{2,6},{4,0},{6,2},{8,12},{10,14},{12,8},{14,10},{16,20},{18,... | collective-permute-start | bytes 6291464 | tf_op jit(solution)/shard_map/ppermute | solution.py:672
  467.6 63.7 %collective-permute-start.6 = (bf16[2,2,2,32,4096]{4,3,0,1,2:T(8,128)(2,1)}, bf16[2,2,2,32,4096]{4,3,0,1,2:T(8,128)(2,1)}, u32[]{:S(2)}, u32[]{:S(2)}) collective-permute-start(bf16[2,2,2,32,4096]{4,3,0,1,2:T(8,128)(2,1)} %dynamic-slice_bitcast_fusion.1), channel_id=1, source_target_pairs={{0,1},{1,0},{2,3},{3,2},{4,5},{5,4},{6,7},{7,6},{8,9},{9,8},{10,11... | collective-permute-start | bytes 6291464 | tf_op jit(solution)/shard_map/ppermute | solution.py:672
  534.5 77.9 %collective-permute-start.13 = (f32[12288]{0:T(1024)S(1)}, f32[12288]{0:T(1024)S(1)}, u32[]{:S(2)}, u32[]{:S(2)}) collective-permute-start(f32[12288]{0:T(1024)S(1)} %add.425), channel_id=1, source_target_pairs={{0,1},{1,0},{2,3},{3,2},{4,5},{5,4},{6,7},{7,6},{8,9},{9,8},{10,11... | collective-permute-start | bytes 147464 | tf_op jit(solution)/shard_map/ppermute | solution.py:672
  540.0 72.5 %collective-permute-start.12 = (bf16[2,2,32,1024]{3,2,0,1:T(8,128)(2,1)S(1)}, bf16[2,2,32,1024]{3,2,0,1:T(8,128)(2,1)}, u32[]{:S(2)}, u32[]{:S(2)}) collective-permute-start(bf16[2,2,32,1024]{3,2,0,1:T(8,128)(2,1)S(1)} %dynamic-slice_bitcast_fusion.14), channel_id=1, source_target_pairs={{0,1},{1,0},{2,3},{3,2},{4,5},{5,4},{6,7},{7,6},{8,9},{9,8},{10,11... | collective-permute-start | bytes 786440 | tf_op jit(solution)/shard_map/ppermute | solution.py:672
  540.1 73.4 %collective-permute-start.11 = (bf16[2,2,128,1024]{2,3,0,1:T(8,128)(2,1)S(1)}, bf16[2,2,128,1024]{2,3,0,1:T(8,128)(2,1)}, u32[]{:S(2)}, u32[]{:S(2)}) collective-permute-start(bf16[2,2,128,1024]{2,3,0,1:T(8,128)(2,1)S(1)} %dynamic-slice_bitcast_fusion.3), channel_id=1, source_target_pairs={{0,1},{1,0},{2,3},{3,2},{4,5},{5,4},{6,7},{7,6},{8,9},{9,8},{10,11... | collective-permute-start | bytes 3145736 | tf_op jit(solution)/shard_map/ppermute | solution.py:672
  543.3 71.8 %collective-permute-start.10 = (bf16[2,2,32,4096]{3,2,0,1:T(8,128)(2,1)}, bf16[2,2,32,4096]{3,2,0,1:T(8,128)(2,1)}, u32[]{:S(2)}, u32[]{:S(2)}) collective-permute-start(bf16[2,2,32,4096]{3,2,0,1:T(8,128)(2,1)} %dynamic-slice_bitcast_fusion.4), channel_id=1, source_target_pairs={{0,4},{2,6},{4,0},{6,2},{8,12},{10,14},{12,8},{14,10},{16,20},{18,... | collective-permute-start | bytes 3145736 | tf_op jit(solution)/shard_map/ppermute | solution.py:672
  612.4 270.9 %collective-permute-start.21 = (bf16[1024,1024]{1,0:T(8,128)(2,1)}, bf16[1024,1024]{1,0:T(8,128)(2,1)}, u32[]{:S(2)}, u32[]{:S(2)}) collective-permute-start(bf16[1024,1024]{1,0:T(8,128)(2,1)} %get-tuple-element.190), channel_id=1, source_target_pairs={{0,1},{1,0},{2,3},{3,2},{4,5},{5,4},{6,7},{7,6},{8,9},{9,8},{10,11... | collective-permute-start | bytes 6291464 | tf_op jit(solution)/shard_map/ppermute | solution.py:875
  616.6 64.0 %collective-permute-start.17 = (f32[12288]{0:T(1024)S(1)}, f32[12288]{0:T(1024)S(1)}, u32[]{:S(2)}, u32[]{:S(2)}) collective-permute-start(f32[12288]{0:T(1024)S(1)} %add.429), channel_id=1, source_target_pairs={{0,8},{2,10},{4,12},{6,14},{8,0},{10,2},{12,4},{14,6},{16,24},{18,... | collective-permute-start | bytes 147464 | tf_op jit(solution)/shard_map/ppermute | solution.py:672
  618.9 66.8 %collective-permute-start.16 = (bf16[2,32,1024]{2,1,0:T(8,128)(2,1)}, bf16[2,32,1024]{2,1,0:T(8,128)(2,1)}, u32[]{:S(2)}, u32[]{:S(2)}) collective-permute-start(bf16[2,32,1024]{2,1,0:T(8,128)(2,1)} %dynamic-slice_bitcast_fusion.17), channel_id=1, source_target_pairs={{0,8},{2,10},{4,12},{6,14},{8,0},{10,2},{12,4},{14,6},{16,24},{18,... | collective-permute-start | bytes 393224 | tf_op jit(solution)/shard_map/ppermute | solution.py:672
  619.4 67.3 %collective-permute-start.15 = (bf16[2,128,1024]{1,2,0:T(8,128)(2,1)S(1)}, bf16[2,128,1024]{1,2,0:T(8,128)(2,1)}, u32[]{:S(2)}, u32[]{:S(2)}) collective-permute-start(bf16[2,128,1024]{1,2,0:T(8,128)(2,1)S(1)} %dynamic-slice_bitcast_fusion.7), channel_id=1, source_target_pairs={{0,8},{2,10},{4,12},{6,14},{8,0},{10,2},{12,4},{14,6},{16,24},{18,... | collective-permute-start | bytes 1572872 | tf_op jit(solution)/shard_map/ppermute | solution.py:672
  621.9 66.0 %collective-permute-start.14 = (bf16[2,32,4096]{2,1,0:T(8,128)(2,1)}, bf16[2,32,4096]{2,1,0:T(8,128)(2,1)}, u32[]{:S(2)}, u32[]{:S(2)}) collective-permute-start(bf16[2,32,4096]{2,1,0:T(8,128)(2,1)} %dynamic-slice_bitcast_fusion.8), channel_id=1, source_target_pairs={{0,8},{2,10},{4,12},{6,14},{8,0},{10,2},{12,4},{14,6},{16,24},{18,... | collective-permute-start | bytes 1572872 | tf_op jit(solution)/shard_map/ppermute | solution.py:672
  680.6 202.7 %collective-permute-start.22 = (bf16[1024,1024]{1,0:T(8,128)(2,1)}, bf16[1024,1024]{1,0:T(8,128)(2,1)}, u32[]{:S(2)}, u32[]{:S(2)}) collective-permute-start(bf16[1024,1024]{1,0:T(8,128)(2,1)} %get-tuple-element.191), channel_id=1, source_target_pairs={{0,1},{2,3},{4,5},{6,7},{8,9},{10,11},{12,13},{14,15},{16,17},{18,... | collective-permute-start | bytes 6291464 | tf_op jit(solution)/shard_map/ppermute | solution.py:881
  806.4 28.7 %collective-permute-start.20 = (f32[5120]{0:T(1024)S(1)}, f32[5120]{0:T(1024)S(1)}, u32[]{:S(2)}, u32[]{:S(2)}) collective-permute-start(f32[5120]{0:T(1024)S(1)} %pad_maximum_fusion.9), channel_id=1, source_target_pairs={{0,2},{2,0},{4,6},{6,4},{8,10},{10,8},{12,14},{14,12},{16,18},{18,... | collective-permute-start | bytes 61448 | tf_op jit(solution)/shard_map/ppermute | solution.py:672
  809.5 52.0 %collective-permute-start.19 = (bf16[2,2,2,2,48,1024]{5,4,0,1,2,3:T(8,128)(2,1)}, bf16[2,2,2,2,48,1024]{5,4,0,1,2,3:T(8,128)(2,1)}, u32[]{:S(2)}, u32[]{:S(2)}) collective-permute-start(bf16[2,2,2,2,48,1024]{5,4,0,1,2,3:T(8,128)(2,1)} %bitcast.231), channel_id=1, source_target_pairs={{0,2},{2,0},{4,6},{6,4},{8,10},{10,8},{12,14},{14,12},{16,18},{18,... | collective-permute-start | bytes 4718600 | tf_op jit(solution)/shard_map/ppermute | solution.py:672
  811.6 45.7 %collective-permute-start.18 = (bf16[2,2,2,2,48,1024]{5,4,3,2,1,0:T(8,128)(2,1)}, bf16[2,2,2,2,48,1024]{5,4,3,2,1,0:T(8,128)(2,1)}, u32[]{:S(2)}, u32[]{:S(2)}) collective-permute-start(bf16[2,2,2,2,48,1024]{5,4,3,2,1,0:T(8,128)(2,1)} %dynamic-slice_bitcast_fusion.2), channel_id=1, source_target_pairs={{0,2},{2,0},{4,6},{6,4},{8,10},{10,8},{12,14},{14,12},{16,18},{18,... | collective-permute-start | bytes 4718600 | tf_op jit(solution)/shard_map/ppermute | solution.py:672
  835.1 14.5 %collective-permute-start.38 = (f32[12288]{0:T(1024)S(1)}, f32[12288]{0:T(1024)S(1)}, u32[]{:S(2)}, u32[]{:S(2)}) collective-permute-start(f32[12288]{0:T(1024)S(1)} %add.435), channel_id=1, source_target_pairs={{0,16},{2,18},{4,20},{6,22},{8,24},{10,26},{12,28},{14,30},{16,0},... | collective-permute-start | bytes 147464 | tf_op jit(solution)/shard_map/ppermute | solution.py:672
  855.7 48.2 %collective-permute-start.36 = (bf16[32,4096]{1,0:T(8,128)(2,1)}, bf16[32,4096]{1,0:T(8,128)(2,1)}, u32[]{:S(2)}, u32[]{:S(2)}) collective-permute-start(bf16[32,4096]{1,0:T(8,128)(2,1)} %dynamic-slice_bitcast_fusion.12), channel_id=1, source_target_pairs={{0,16},{2,18},{4,20},{6,22},{8,24},{10,26},{12,28},{14,30},{16,0},... | collective-permute-start | bytes 786440 | tf_op jit(solution)/shard_map/ppermute | solution.py:672
  857.3 55.6 %collective-permute-start.35 = (bf16[128,1024]{0,1:T(8,128)(2,1)S(1)}, bf16[128,1024]{0,1:T(8,128)(2,1)}, u32[]{:S(2)}, u32[]{:S(2)}) collective-permute-start(bf16[128,1024]{0,1:T(8,128)(2,1)S(1)} %dynamic-slice_bitcast_fusion.13), channel_id=1, source_target_pairs={{0,16},{2,18},{4,20},{6,22},{8,24},{10,26},{12,28},{14,30},{16,0},... | collective-permute-start | bytes 786440 | tf_op jit(solution)/shard_map/ppermute | solution.py:672
  863.8 32.9 %collective-permute-start.25 = (f32[5120]{0:T(1024)S(1)}, f32[5120]{0:T(1024)S(1)}, u32[]{:S(2)}, u32[]{:S(2)}) collective-permute-start(f32[5120]{0:T(1024)S(1)} %fusion.66), channel_id=1, source_target_pairs={{0,4},{2,6},{4,0},{6,2},{8,12},{10,14},{12,8},{14,10},{16,20},{18,... | collective-permute-start | bytes 61448 | tf_op jit(solution)/shard_map/ppermute | solution.py:672
  883.3 17.4 %collective-permute-start.24 = (bf16[2,2,2,48,1024]{4,3,0,1,2:T(8,128)(2,1)S(1)}, bf16[2,2,2,48,1024]{4,3,0,1,2:T(8,128)(2,1)S(1)}, u32[]{:S(2)}, u32[]{:S(2)}) collective-permute-start(bf16[2,2,2,48,1024]{4,3,0,1,2:T(8,128)(2,1)S(1)} %dynamic-slice_bitcast_fusion.5), channel_id=1, source_target_pairs={{0,1},{1,0},{2,3},{3,2},{4,5},{5,4},{6,7},{7,6},{8,9},{9,8},{10,11... | collective-permute-start | bytes 2359304 | tf_op jit(solution)/shard_map/ppermute | solution.py:672
  883.3 17.7 %collective-permute-start.23 = (bf16[2,2,2,48,1024]{4,3,2,1,0:T(8,128)(2,1)S(1)}, bf16[2,2,2,48,1024]{4,3,2,1,0:T(8,128)(2,1)S(1)}, u32[]{:S(2)}, u32[]{:S(2)}) collective-permute-start(bf16[2,2,2,48,1024]{4,3,2,1,0:T(8,128)(2,1)S(1)} %dynamic-slice_bitcast_fusion.6), channel_id=1, source_target_pairs={{0,4},{2,6},{4,0},{6,2},{8,12},{10,14},{12,8},{14,10},{16,20},{18,... | collective-permute-start | bytes 2359304 | tf_op jit(solution)/shard_map/ppermute | solution.py:672
  902.8 7.8 collective-permute-start.27
  903.2 7.8 collective-permute-start.26
  924.9 7.8 collective-permute-start.33
  (73 other events, 691.4 us)

commit v2 on v1

--- a/solution.py
+++ b/solution.py
@@ -18,12 +18,6 @@
 
 f32 = jnp.float32
 bf16 = jnp.bfloat16
-
-
-def layer_norm(values, gain, shift):
-    centre = values - jnp.mean(values, axis=-1, keepdims=True)
-    spread = jnp.mean(centre * centre, axis=-1, keepdims=True)
-    return centre * lax.rsqrt(spread + EPS) * gain + shift
 
 
 def dot(left, right, left_dim, right_dim):
@@ -233,8 +227,8 @@
     return [high, middle, low]
 
 
-def bwd_prepare(qT, kT, vT, doT, oT, lse, qa, da, ka, va):
-    n_q, n_k = qT.shape[1], kT.shape[1]
+def bwd_prepare(qT, keys, doT, oT, lse, qa, da, ka, va):
+    n_q, n_k = qT.shape[1], ka.shape[2]
     extra = qa.shape[1] - HEAD_DIM
     pad = jnp.zeros((extra - 3, n_q), f32)
     row_at = lax.broadcasted_iota(jnp.int32, (extra, n_k), 0)
@@ -249,13 +243,17 @@
         da[h, :HEAD_DIM, :] = doT[rows, :]
         parts = split_three(-delta) + [pad]
         da[h, HEAD_DIM:, :] = jnp.concatenate(parts, axis=0).astype(bf16)
-        ka[h, :HEAD_DIM, :] = kT[rows, :]
+        at = 0
+        for kT, vT in keys:
+            part = slice(at, at + kT.shape[1])
+            ka[h, :HEAD_DIM, part] = kT[rows, :]
+            va[h, :HEAD_DIM, part] = vT[rows, :]
+            at += kT.shape[1]
         ka[h, HEAD_DIM:, :] = tail
-        va[h, :HEAD_DIM, :] = vT[rows, :]
         va[h, HEAD_DIM:, :] = tail
 
 
-def bwd_chunk(q0, k0, q_n, k_n, offset, limit, qT, kT, doT, qa, da, ka, va, dq, dk, dv):
+def bwd_chunk(q0, k0, q_n, k_n, offset, limit, qT, doT, qa, da, ka, va, dq, dk, dv):
     queries, keys = pl.ds(q0, q_n), pl.ds(k0, k_n)
     for h in range(2):
         rows = slice(HEAD_DIM * h, HEAD_DIM * (h + 1))
@@ -271,10 +269,10 @@
         d_scores = (probs * d_probs).astype(bf16)
         dv[rows, keys] += dot(doT[rows, queries], probs.astype(bf16), 1, 0)
         dk[rows, keys] += dot(qT[rows, queries], d_scores, 1, 0)
-        dq[rows, queries] += dot(kT[rows, keys], d_scores, 1, 1)
-
-
-def bwd_diagonal(base, group, qT, kT, doT, qa, da, ka, va, dq, dk, dv):
+        dq[rows, queries] += dot(ka[h, :HEAD_DIM, keys], d_scores, 1, 1)
+
+
+def bwd_diagonal(base, group, qT, doT, qa, da, ka, va, dq, dk, dv):
     strip = min(256, group)
     count = group // strip
     for h in range(2):
@@ -293,7 +291,7 @@
             key = pad_right(dot(qT[rows, queries], d_scores, 1, 0), group - wide)
             d_values = value if d_values is None else d_values + value
             d_keys = key if d_keys is None else d_keys + key
-            d_queries.append(dot(kT[rows, keys], d_scores, 1, 1))
+            d_queries.append(dot(ka[h, :HEAD_DIM, keys], d_scores, 1, 1))
         here = pl.ds(base, group)
         dq[rows, here] += jnp.concatenate(d_queries, axis=1) if count > 1 else d_queries[0]
         dk[rows, here] += d_keys
@@ -308,14 +306,17 @@
     )
 
 
-def bwd_remote_kernel(group, parts, info, qT, kT, vT, doT, oT, lse, cosine, sine, *rest):
+def bwd_remote_kernel(
+    group, parts, info, qT, doT, oT, lse, cosine, sine, k_early, v_early, k_late, v_late, *rest
+):
     dq, dkv, *scratch = rest[-8:]
     qa, da, ka, va, dk, dv = scratch
-    bwd_prepare(qT, kT, vT, doT, oT, lse, qa, da, ka, va)
+    keys = [(k_early, v_early), (k_late, v_late)]
+    bwd_prepare(qT, keys, doT, oT, lse, qa, da, ka, va)
     dq[...] = jnp.zeros(dq.shape, f32)
     dk[...] = jnp.zeros(dk.shape, f32)
     dv[...] = jnp.zeros(dv.shape, f32)
-    refs = (qT, kT, doT, qa, da, ka, va, dq, dk, dv)
+    refs = (qT, doT, qa, da, ka, va, dq, dk, dv)
 
     def full(q0, k0):
         bwd_chunk(q0, k0, group, group, None, None, *refs)
@@ -326,19 +327,20 @@
     remote_steps(group, parts, 2, info, full, partial)
     for h in range(2):
         rows = slice(HEAD_DIM * h, HEAD_DIM * (h + 1))
-        dkv[0, rows, :] = turn_back(dk[rows, :] * LN2, cosine[...], sine[...]).astype(bf16)
-    dkv[1] = dv[...].astype(bf16)
-
-
-def bwd_local_kernel(group, info, qT, kT, vT, doT, oT, lse, cosine, sine, dq_in, *rest):
+        dkv[1, rows, :] = turn_back(dk[rows, :] * LN2, cosine[...], sine[...]).astype(bf16)
+    dkv[0] = jnp.zeros(dv.shape, bf16)
+    dkv[2] = dv[...].astype(bf16)
+
+
+def bwd_local_kernel(group, info, qT, doT, oT, lse, cosine, sine, kT, vT, dq_in, *rest):
     dqkv, *scratch = rest[-8:]
     qa, da, ka, va, dq, dk, dv = scratch
     length = info[1]
-    bwd_prepare(qT, kT, vT, doT, oT, lse, qa, da, ka, va)
+    bwd_prepare(qT, [(kT, vT)], doT, oT, lse, qa, da, ka, va)
     dq[...] = dq_in[...]
     dk[...] = jnp.zeros(dk.shape, f32)
     dv[...] = jnp.zeros(dv.shape, f32)
-    refs = (qT, kT, doT, qa, da, ka, va, dq, dk, dv)
+    refs = (qT, doT, qa, da, ka, va, dq, dk, dv)
 
     def own(i, carry):
         base = pl.multiple_of(i * group, group)
@@ -461,45 +463,43 @@
     ]
 
 
-def back_remote(info, operands, lse, turns, group, parts, first, count, before):
-    qT, kT = operands[:2]
-    width, n_q = qT.shape
-    n_k = kT.shape[1]
+def back_remote(info, operands, turns, keys, group, parts, first, count, before):
+    width, n_q = operands[0].shape
+    n_k = keys[0].shape[1] + keys[2].shape[1]
     half = HEAD_DIM // 2
-    n_in = 1 + len(operands) + 1 + len(turns)
+    n_in = 1 + len(operands) + len(turns) + len(keys)
     call = attention_call(
         functools.partial(bwd_remote_kernel, group, parts),
         count,
-        [rows_of(n_q, first), rows_of(n_k, first), rows_of(n_k, first)]
-        + [rows_of(n_q, first)] * 2
+        [rows_of(n_q, first)] * 3
         + [stats_of(n_q, first)]
         + [whole((half, n_k))] * 2
+        + [rows_of(item.shape[1], first) for item in keys]
         + [pl.BlockSpec(memory_space=pl.ANY)] * len(before),
-        [rows_of(n_q, first), planes_of(2, n_k, first)],
+        [rows_of(n_q, first), planes_of(3, n_k, first)],
         [
             jax.ShapeDtypeStruct((width, n_q), f32),
-            jax.ShapeDtypeStruct((2, width, n_k), bf16),
+            jax.ShapeDtypeStruct((3, width, n_k), bf16),
         ],
         back_scratch(n_q, n_k) + [pltpu.VMEM((PAIR, n_k), f32)] * 2,
         10 * count * PAIR * 2 * group * group * 4,
         "back_remote",
         {n_in + i: i for i in range(len(before))},
     )
-    return call(info, *operands, lse, *turns, *before)
-
-
-def back_local(info, operands, lse, turns, dq, group, first, count, before):
-    qT = operands[0]
-    width, n_q = qT.shape
+    return call(info, *operands, *turns, *keys, *before)
+
+
+def back_local(info, operands, turns, keys, dq, group, first, count, before):
+    width, n_q = operands[0].shape
     half = HEAD_DIM // 2
-    n_in = 1 + len(operands) + 1 + len(turns) + 1
+    n_in = 1 + len(operands) + len(turns) + len(keys) + 1
     call = attention_call(
         functools.partial(bwd_local_kernel, group),
         count,
-        [rows_of(n_q, first)] * 5
+        [rows_of(n_q, first)] * 3
         + [stats_of(n_q, first)]
         + [whole((half, n_q))] * 2
-        + [rows_of(n_q, first)]
+        + [rows_of(n_q, first)] * 3
         + [pl.BlockSpec(memory_space=pl.ANY)] * len(before),
         planes_of(3, n_q, first),
         jax.ShapeDtypeStruct((3, width, n_q), bf16),
@@ -508,7 +508,7 @@
         "back_local",
         {n_in + i: i for i in range(len(before))},
     )
-    return call(info, *operands, lse, *turns, dq, *before)
+    return call(info, *operands, *turns, *keys, dq, *before)
 
 
 def normalize(values):
@@ -663,6 +663,236 @@
     )(oT, tokens, cotangent, *weights, *vectors)
 
 
+def turn(values, cosine, sine):
+    half = HEAD_DIM // 2
+    first, second = values[:half], values[half:]
+    return jnp.concatenate(
+        [first * cosine - second * sine, second * cosine + first * sine], axis=0
+    )
+
+
+def project_kernel(sections, tokens, w, b, gain, shift, cosine, sine, normed_out, *outs):
+    unit, rate = normalize(tokens[...].astype(f32))
+    normed = (unit * gain[...] + shift[...]).astype(bf16)
+    normed_out[...] = normed
+    width = tokens.shape[1]
+    chunk = min(256, width)
+    for section, out in zip(sections, outs):
+        for c in range(width // chunk):
+            at = section * width + c * chunk
+            mixed = dot(w[:, at : at + chunk], normed, 0, 1) + b[at : at + chunk, :]
+            for h in range(chunk // HEAD_DIM):
+                rows = slice(h * HEAD_DIM, (h + 1) * HEAD_DIM)
+                place = slice(c * chunk + h * HEAD_DIM, c * chunk + (h + 1) * HEAD_DIM)
+                value = mixed[rows]
+                if section < 2:
+                    value = turn(value, cosine[...], sine[...])
+                if section == 0:
+                    value = value * (0.125 * LOG2E)
+                out[place, :] = value.astype(bf16)
+
+
+def project(tokens, w, b, gain, shift, cosine, sine, sections, start=0):
+    rows, width = tokens.shape
+    step = min(512, rows)
+    half = HEAD_DIM // 2
+    first = start // step
+
+    def fixed(shape):
+        return pl.BlockSpec(shape, lambda i: (0, 0), pipeline_mode=pl.Buffered(1))
+
+    lines = pl.BlockSpec((step, width), lambda i: (i, 0))
+    features = pl.BlockSpec((width, step), lambda i: (0, i))
+    turns = pl.BlockSpec((half, step), lambda i: (0, first + i))
+    return pl.pallas_call(
+        functools.partial(project_kernel, sections),
+        grid=(rows // step,),
+        in_specs=[lines, fixed(w.shape), fixed(b.shape), fixed(gain.shape), fixed(shift.shape)]
+        + [turns] * 2,
+        out_specs=[lines] + [features] * len(sections),
+        out_shape=[jax.ShapeDtypeStruct((rows, width), bf16)]
+        + [jax.ShapeDtypeStruct((width, rows), bf16)] * len(sections),
+        compiler_params=pltpu.CompilerParams(vmem_limit_bytes=VMEM),
+        cost_estimate=pl.CostEstimate(
+            flops=2 * rows * width * width * len(sections),
+            bytes_accessed=1 << 24,
+            transcendentals=0,
+        ),
+        name="project",
+    )(tokens, w, b, gain, shift, cosine, sine)
+
+
+def unproject_kernel(planes, finish, *refs):
+    d_mixed, w, out = refs[: len(planes)], refs[len(planes)], refs[-1]
+    width = w.shape[0]
+    total = None
+    for plane, ref in zip(planes, d_mixed):
+        term = dot(ref[0], w[:, plane * width : (plane + 1) * width], 0, 1)
+        total = term if total is None else total + term
+    if not finish:
+        out[...] = total.astype(bf16)
+        return
+    returned, tokens, d_middle, gain = refs[len(planes) + 1 : len(planes) + 5]
+    total = total + returned[...].astype(f32)
+    unit, rate = normalize(tokens[...].astype(f32))
+    out[...] = (d_middle[...] + norm_back(total, unit, rate, gain[...])).astype(bf16)
+
+
+def unproject(d_mixed, w, planes, start, count, finish=(), before=()):
+    _, width, total = d_mixed.shape
+    step = min(256, count)
+    first = start // step
+
+    def fixed(shape):
+        return pl.BlockSpec(shape, lambda i: (0, 0), pipeline_mode=pl.Buffered(1))
+
+    def plane_of(plane):
+        return pl.BlockSpec((1, width, step), lambda i: (plane, 0, first + i))
+
+    lines = pl.BlockSpec((step, width), lambda i: (i, 0))
+    later = pl.BlockSpec((step, width), lambda i: (first + i, 0))
+    specs = [lines, later, later, fixed(finish[-1].shape)] if finish else []
+    n_in = len(planes) + 1 + len(finish)
+    return pl.pallas_call(
+        functools.partial(unproject_kernel, planes, bool(finish)),
+        grid=(count // step,),
+        in_specs=[plane_of(plane) for plane in planes]
+        + [fixed(w.shape)]
+        + specs
+        + [pl.BlockSpec(memory_space=pl.ANY)] * len(before),
+        out_specs=later if finish else lines,
+        out_shape=jax.ShapeDtypeStruct((total if finish else count, width), bf16),
+        input_output_aliases={n_in + i: i for i in range(len(before))},
+        compiler_params=pltpu.CompilerParams(vmem_limit_bytes=VMEM),
+        cost_estimate=pl.CostEstimate(
+            flops=2 * count * width * width * len(planes),
+            bytes_accessed=1 << 24,
+            transcendentals=0,
+        ),
+        name="unproject",
+    )(*[d_mixed] * len(planes), w, *finish, *before)
+
+
+def divide(total, share, core, kept, given):
+    own, other = [], []
+    for i in range(0, total.shape[0], 2 * share):
+        zero, one = total[i : i + share], total[i + share : i + 2 * share]
+        own.append(jnp.where(core == 0, zero, one))
+        other.append(jnp.where(core == 0, one, zero))
+    kept[...] = jnp.concatenate(own, axis=0).astype(bf16)
+    given[...] = jnp.concatenate(other, axis=0).astype(bf16)
+
+
+def outer_kernel(share, right_dim, core, left, right, kept, given):
+    divide(dot(left[...], right[...], 0, right_dim), share, core[0], kept, given)
+
+
+def outer_halves(core, left, right, right_dim, parts):
+    rows, height = left.shape
+    width = right.shape[1 - right_dim]
+    share = height // parts
+    high = max(2 * share, min(512, height))
+    wide = min(1024, width)
+    if right_dim == 0:
+        right_spec = pl.BlockSpec((rows, wide), lambda j, i, core: (0, j))
+    else:
+        right_spec = pl.BlockSpec((wide, rows), lambda j, i, core: (j, 0))
+    out_spec = pl.BlockSpec((high // 2, wide), lambda j, i, core: (i, j))
+    out = jax.ShapeDtypeStruct((height // 2, width), bf16)
+    return pl.pallas_call(
+        functools.partial(outer_kernel, share, right_dim),
+        grid_spec=pltpu.PrefetchScalarGridSpec(
+            num_scalar_prefetch=1,
+            grid=(width // wide, height // high),
+            in_specs=[pl.BlockSpec((rows, high), lambda j, i, core: (0, i)), right_spec],
+            out_specs=[out_spec] * 2,
+        ),
+        out_shape=[out] * 2,
+        compiler_params=pltpu.CompilerParams(vmem_limit_bytes=VMEM),
+        cost_estimate=pl.CostEstimate(
+            flops=2 * rows * height * width, bytes_accessed=1 << 25, transcendentals=0
+        ),
+        name="outer",
+    )(core, left, right)
+
+
+def mixed_kernel(
+    share, first_far, core, d_own, d_far, normed, far_early, far_late, w, kept, given, bias, sums
+):
+    step = pl.program_id(0)
+    total = dot(d_own[...], normed[...], 1, 0)
+    bias[...] = jnp.sum(d_own[...].astype(f32), axis=1, keepdims=True)
+
+    @pl.when(step == 0)
+    def _():
+        sums[...] = jnp.zeros(sums.shape, f32)
+
+    def finish(value):
+        divide(value, share, core[0], kept, given)
+        weights = w[...].astype(f32).T
+        sums[0:1, :] += column_sum(weights * value)
+        sums[1:2, :] += column_sum(weights * bias[...])
+
+    @pl.when(step < first_far)
+    def _():
+        finish(total)
+
+    @pl.when(step >= first_far)
+    def _():
+        split = far_early.shape[0]
+        bias[...] += jnp.sum(d_far[...].astype(f32), axis=1, keepdims=True)
+        finish(
+            total
+            + dot(d_far[:, :split], far_early[...], 1, 0)
+            + dot(d_far[:, split:], far_late[...], 1, 0)
+        )
+
+
+def mixed_halves(core, d_own, d_far, normed, far_early, far_late, w, parts):
+    height, rows = d_own.shape
+    far = d_far.shape[1]
+    width = normed.shape[1]
+    share = height // parts
+    high = 2 * share * max(1, 384 // (2 * share))
+    first_far = width // high
+
+    def fixed(shape):
+        return pl.BlockSpec(shape, lambda i, core: (0, 0), pipeline_mode=pl.Buffered(1))
+
+    out_spec = pl.BlockSpec((high // 2, width), lambda i, core: (i, 0))
+    out = jax.ShapeDtypeStruct((height // 2, width), bf16)
+    return pl.pallas_call(
+        functools.partial(mixed_kernel, share, first_far),
+        grid_spec=pltpu.PrefetchScalarGridSpec(
+            num_scalar_prefetch=1,
+            grid=(height // high,),
+            in_specs=[
+                pl.BlockSpec((high, rows), lambda i, core: (i, 0)),
+                pl.BlockSpec((high, far), lambda i, core: (jnp.maximum(i, first_far), 0)),
+                fixed(normed.shape),
+                fixed(far_early.shape),
+                fixed(far_late.shape),
+                pl.BlockSpec((width, high), lambda i, core: (0, i)),
+            ],
+            out_specs=[out_spec] * 2
+            + [
+                pl.BlockSpec((high, 1), lambda i, core: (i, 0)),
+                pl.BlockSpec((2, width), lambda i, core: (0, 0)),
+            ],
+        ),
+        out_shape=[out] * 2
+        + [
+            jax.ShapeDtypeStruct((height, 1), f32),
+            jax.ShapeDtypeStruct((2, width), f32),
+        ],
+        compiler_params=pltpu.CompilerParams(vmem_limit_bytes=VMEM),
+        cost_estimate=pl.CostEstimate(
+            flops=2 * (rows + far) * height * width, bytes_accessed=1 << 25, transcendentals=0
+        ),
+        name="mixed",
+    )(core, d_own, d_far, normed, far_early, far_late, w)
+
+
 def bit_of(axis, position):
     return (lax.axis_index(axis) >> position) & 1
 
@@ -678,54 +908,62 @@
         self.order = list(order)
         rows = array.shape[0] >> len(bits)
         self.array = array.reshape((2,) * len(bits) + (rows, array.shape[1]))
-        self.kept = self.received = None
+
+    def split(self):
+        self.bit = self.order.pop(0)
+        at = self.bits.index(self.bit)
+        self.mine = bit_of(*self.bit)
+        self.away = lax.dynamic_index_in_dim(self.array, 1 - self.mine, at, False)
+        self.at = at
+        self.bits.pop(at)
 
     def send(self):
-        bit = self.order.pop(0)
-        at = self.bits.index(bit)
-        mine = bit_of(*bit)
-        away = lax.dynamic_index_in_dim(self.array, 1 - mine, at, False)
-        self.kept = (self.array, mine, at)
-        self.received = swap(away, *bit)
-        self.bits.pop(at)
+        self.received = swap(self.away, *self.bit)
 
     def add(self):
-        array, mine, at = self.kept
-        kept = lax.dynamic_index_in_dim(array, mine, at, False).astype(f32)
+        kept = lax.dynamic_index_in_dim(self.array, self.mine, self.at, False).astype(f32)
         total = kept + self.received.astype(f32)
         self.array = total.astype(bf16) if self.bits else total
 
-    def result(self):
-        return self.array
+
+class Crossing(Halving):
+    def __init__(self, halves, bits, order):
+        kept, given = halves
+        super().__init__(kept, bits, order)
+        self.received = swap(given, "wide", 0).reshape(self.array.shape)
+
+    def add(self):
+        if hasattr(self, "bit"):
+            super().add()
+        else:
+            total = self.array.astype(f32) + self.received.astype(f32)
+            self.array = total.astype(bf16)
 
 
 class Adding:
     def __init__(self, array, order):
         self.array, self.order = array, list(order)
 
+    def split(self):
+        self.bit = self.order.pop(0)
+        self.away = self.array
+
     def send(self):
-        self.received = swap(self.array, *self.order.pop(0))
+        self.received = swap(self.away, *self.bit)
 
     def add(self):
         self.array = self.array + self.received
 
 
-def tie(lead, sums):
-    held, arrays = lax.optimization_barrier((lead, [item.array for item in sums]))
-    for item, array in zip(sums, arrays):
-        item.array = array
-    return held
-
-
-def turn_forward(values, cosine, sine):
-    features, tokens = values.shape
-    half = HEAD_DIM // 2
-    pairs = values.reshape(features // HEAD_DIM, 2, half, tokens)
-    first, second = pairs[:, 0], pairs[:, 1]
-    turned = jnp.stack(
-        [first * cosine - second * sine, second * cosine + first * sine], axis=1
-    )
-    return turned.reshape(features, tokens)
+def launch(lead, sums, *others):
+    for item in sums:
+        item.split()
+    held = (lead, others, [(item.array, item.away) for item in sums])
+    lead, others, arrays = lax.optimization_barrier(held)
+    for item, (array, away) in zip(sums, arrays):
+        item.array, item.away = array, away
+        item.send()
+    return (lead, *others)
 
 
 def angles(positions):
@@ -766,6 +1004,7 @@
     place = lax.axis_index("narrow")
     others = parts - 1
     rows = 2 * group
+    far_rows = others * group
     offsets = jnp.arange(group, dtype=jnp.int32)
 
     own_blocks = inputs.reshape(2, group, width)
@@ -782,37 +1021,33 @@
     early_at = place * group
     late_at = (2 * parts - 1 - place) * group
     info = jnp.stack([place, lengths[0], early_at, late_at]).astype(jnp.int32)
-    own_pos = jnp.concatenate([early_at + offsets, late_at + offsets])
-    far_early_pos = (other[:, None] * group + offsets[None]).reshape(-1)
-    far_late_pos = ((2 * parts - 1 - other)[:, None] * group + offsets[None]).reshape(-1)
-    cosine, sine = angles(own_pos)
-    cosine_fe, sine_fe = angles(far_early_pos)
-    cosine_fl, sine_fl = angles(far_late_pos)
-
-    tokens = own_blocks.astype(f32).reshape(rows, width)
-    normed_low = layer_norm(tokens, gain_one, shift_one).astype(bf16)
-    mixedT = dot(w_qkv, normed_low, 0, 1) + b_qkv[:, None]
-    qT = (turn_forward(mixedT[:width], cosine, sine) * (0.125 * LOG2E)).astype(bf16)
-    kT = turn_forward(mixedT[width : 2 * width], cosine, sine).astype(bf16)
-    vT = mixedT[2 * width :].astype(bf16)
+    core = bit_of("wide", 0).astype(jnp.int32)[None]
+    starts = jnp.stack([early_at, late_at])
+    turns = angles((starts[:, None] + offsets[None]).reshape(-1))
+    starts = jnp.concatenate([other, 2 * parts - 1 - other]) * group
+    turns_far = angles((starts[:, None] + offsets[None]).reshape(-1))
+
+    def row(vector):
+        return vector[None, :]
+
+    norm_one = [row(gain_one), row(shift_one)]
+    b_column = b_qkv[:, None]
+    tokens = own_blocks.reshape(rows, width)
+    normed, qT, kT, vT = project(tokens, w_qkv, b_column, *norm_one, *turns, (0, 1, 2))
     state = attend_local(info, qT, kT, vT, group)
 
-    def far_keys(blocks, cos, sin):
-        far = jnp.concatenate(blocks, axis=0).astype(f32)
-        far_normed = layer_norm(far, gain_one, shift_one).astype(bf16)
-        far_mixed = dot(w_qkv[:, width:], far_normed, 0, 1) + b_qkv[width:, None]
-        keys = turn_forward(far_mixed[:width], cos, sin).astype(bf16)
-        return far_normed, keys, far_mixed[width:].astype(bf16)
-
-    normed_fe, kT_fe, vT_fe = far_keys(far_early, cosine_fe, sine_fe)
+    def far_keys(blocks, start):
+        far = jnp.concatenate(blocks, axis=0) if others > 1 else blocks[0]
+        return project(far, w_qkv, b_column, *norm_one, *turns_far, (1, 2), start)
+
+    normed_fe, kT_fe, vT_fe = far_keys(far_early, 0)
     state = attend_remote(info, qT, kT_fe, vT_fe, state, group, parts, 0, False)
-    normed_fl, kT_fl, vT_fl = far_keys(far_late, cosine_fl, sine_fl)
+    normed_fl, kT_fl, vT_fl = far_keys(far_late, far_rows)
     oT, lse, _ = attend_remote(info, qT, kT_fl, vT_fl, state, group, parts, 1, True)
 
-    row = lambda vector: vector[None, :]
     blocks = block_call(
         oT,
-        own_blocks.reshape(rows, width),
+        tokens,
         cotangent.reshape(rows, width),
         [w_out, w_up, w_down],
         [row(item) for item in (b_out, b_up, b_down)]
@@ -823,134 +1058,148 @@
 
     wide_bits = axis_bits("wide")
     narrow_bits = axis_bits("narrow")
-    bits = wide_bits[::-1] + narrow_bits[::-1]
-    first_order = wide_bits[:2] + narrow_bits + wide_bits[2:]
-    second_order = wide_bits[:1] + narrow_bits + wide_bits[1:]
-    steps = len(bits)
-
-    sum_down = Halving(dot(d_outer, hidden, 0, 0).astype(bf16), bits, second_order)
-    sum_down.send()
-    sum_up = Halving(dot(d_inner, normed_two, 0, 0).astype(bf16), bits, first_order)
-    sum_up.send()
-    sum_out = Halving(dot(d_branch, oT, 0, 1).astype(bf16), bits, first_order)
-    sum_out.send()
-    early = Adding(jnp.concatenate([small.reshape(-1), small_up.reshape(-1)]), first_order)
+    devices = 1 << (len(wide_bits) + len(narrow_bits))
+    cores = lax.axis_size("wide")
+    bits = wide_bits[:0:-1] + narrow_bits[::-1]
+    first_order = wide_bits[1:2] + narrow_bits + wide_bits[2:]
+    second_order = narrow_bits + wide_bits[1:]
+
+    sum_down = Crossing(outer_halves(core, d_outer, hidden, 0, cores), bits, second_order)
+    sum_up = Crossing(outer_halves(core, d_inner, normed_two, 0, cores), bits, first_order)
+    sum_out = Crossing(outer_halves(core, d_branch, oT, 1, cores), bits, first_order)
+    early = Adding(jnp.concatenate([small.reshape(-1), small_up.reshape(-1)]), wide_bits[:1] + first_order)
+    early.split()
     early.send()
     sums = [sum_down, sum_up, sum_out, early]
 
-    def advance(lead):
+    def advance(lead, *others):
         for item in sums:
             item.add()
-        lead = tie(lead, sums)
-        if sum_down.order:
-            for item in sums:
-                item.send()
-        return lead
-
-    kT_far = jnp.concatenate([kT_fe, kT_fl], axis=1)
-    vT_far = jnp.concatenate([vT_fe, vT_fl], axis=1)
-    turns_far = [
-        jnp.concatenate([cosine_fe, cosine_fl], axis=1),
-        jnp.concatenate([sine_fe, sine_fl], axis=1),
-    ]
+        return launch(lead, sums, *others)
+
     heads = width // PAIR
     portions = 2 if heads % 2 == 0 else 1
     count = heads // portions
+    keys_far = [kT_fe, vT_fe, kT_fl, vT_fl]
     far = []
     for portion in range(portions):
-        doT = advance(doT)
-        operands = [qT, kT_far, vT_far, doT, oT]
+        (doT,) = advance(doT)
         far = back_remote(
-            info, operands, lse, turns_far, group, parts, portion * count, count, far
+            info,
+            [qT, doT, oT, lse],
+            turns_far,
+            keys_far,
+            group,
+            parts,
+            portion * count,
+            count,
+            far,
         )
-    dq_far, dkv_far = far
-    dkv_far = dkv_far.reshape(2 * width, -1)
-    w_qkvT = w_qkv.T
-    d_normed_far = dot(dkv_far, w_qkvT[width:], 0, 0).astype(bf16)
-    returned_early, returned_late = [], []
-    for j in range(others):
-        shift = j + 1
-        pairs = [(n, (n + shift) % parts) for n in range(parts)]
-        piece = d_normed_far[j * group : (j + 1) * group]
-        returned_early.append(lax.ppermute(piece, "narrow", pairs))
-    for j in range(others):
-        shift = j + 1
-        pairs = [(n, (n + shift) % parts) for n in range(parts)]
-        later = [(n, owner) for n, owner in pairs if owner > n]
-        piece = d_normed_far[(others + j) * group : (others + j + 1) * group]
-        returned_late.append(lax.ppermute(piece, "narrow", later))
-    dqkv = []
+    dq_far, d_far = far
+    d_early = unproject(d_far, w_qkv, (1, 2), 0, far_rows)
+    d_late = unproject(d_far, w_qkv, (1, 2), far_rows, far_rows)
+
+    def give_back(d_early, d_late):
+        early_blocks, late_blocks = [], []
+        for j in range(others):
+            pairs = [(n, (n + j + 1) % parts) for n in range(parts)]
+            piece = d_early[j * group : (j + 1) * group]
+            early_blocks.append(lax.ppermute(piece, "narrow", pairs))
+        for j in range(others):
+            pairs = [(n, (n + j + 1) % parts) for n in range(parts)]
+            later = [(n, owner) for n, owner in pairs if owner > n]
+            piece = d_late[j * group : (j + 1) * group]
+            late_blocks.append(lax.ppermute(piece, "narrow", later))
+        return early_blocks, late_blocks
+
+    d_mixed = []
     for portion in range(portions):
-        doT = advance(doT)
-        operands = [qT, kT, vT, doT, oT]
-        dqkv = [
+        doT, d_early, d_late = advance(doT, d_early, d_late)
+        if not portion:
+            returned_early, returned_late = give_back(d_early, d_late)
+        d_mixed = [
             back_local(
-                info, operands, lse, [cosine, sine], dq_far, group, portion * count, count, dqkv
+                info,
+                [qT, doT, oT, lse],
+                turns,
+                [kT, vT],
+                dq_far,
+                group,
+                portion * count,
+                count,
+                d_mixed,
             )
         ]
-    dqkv = dqkv[0].reshape(3 * width, rows)
+    d_mixed = d_mixed[0]
     while sum_down.order:
-        dqkv = advance(dqkv)
+        (d_mixed,) = advance(d_mixed)
     for item in sums:
         item.add()
 
-    normed_far = jnp.concatenate([normed_fe, normed_fl], axis=0)
-    grad_q = dot(dqkv[:width], normed_low, 1, 0)
-    grad_kv = dot(dqkv[width:], normed_low, 1, 0) + dot(dkv_far, normed_far, 1, 0)
-    grad_w_qkv = jnp.concatenate([grad_q.astype(bf16), grad_kv.astype(bf16)], axis=0)
-    share = grad_w_qkv.shape[0] >> steps
-    cut = share // 2
-    pieces = grad_w_qkv.reshape(1 << steps, share, width)
-    sum_first = Halving(pieces[:, :cut].reshape(-1, width), bits, first_order)
-    sum_second = Halving(pieces[:, cut:].reshape(-1, width), bits, second_order)
-    sum_first.send()
-    sum_second.send()
-    grad_b_qkv = jnp.sum(dqkv.astype(f32), axis=1) + jnp.concatenate(
-        [jnp.zeros((width,), f32), jnp.sum(dkv_far.astype(f32), axis=1)]
+    kept, given, bias, weighted = mixed_halves(
+        core,
+        d_mixed.reshape(3 * width, rows),
+        d_far.reshape(3 * width, -1),
+        normed,
+        normed_fe,
+        normed_fl,
+        w_qkv,
+        cores,
     )
-    weighted = w_qkvT.astype(f32)
-    part_shift = jnp.sum(weighted * grad_b_qkv[:, None], axis=0)
-    part_gain = jnp.sum(weighted * grad_w_qkv.astype(f32), axis=0)
-    part_gain = (part_gain - shift_one * part_shift) / gain_one
-    late = Adding(jnp.concatenate([grad_b_qkv, part_gain, part_shift]), first_order)
+    crossing = Crossing((kept, given), bits, [])
+    part_shift = weighted[1]
+    part_gain = (weighted[0] - shift_one * part_shift) / gain_one
+    late = Adding(
+        jnp.concatenate([bias.reshape(-1), part_gain, part_shift]), wide_bits[:1] + first_order
+    )
+    late.split()
     late.send()
-    sums = [sum_first, sum_second, late]
-
-    dqkv = tie(dqkv, [])
-    d_normed = dot(dqkv, w_qkvT, 0, 0)
+    crossing.add()
+    late.add()
+    share = 3 * width // devices
+    third_order = wide_bits[2:3] + wide_bits[1:2] + narrow_bits + wide_bits[3:]
+    orders = [first_order, narrow_bits + wide_bits[2:3] + wide_bits[1:2] + wide_bits[3:], third_order]
+    runs = crossing.array.reshape(-1, share, width)
+    cut = share // 3
+    pieces = [
+        Halving(runs[:, i * cut : (i + 1) * cut].reshape(-1, width), bits, order)
+        for i, order in enumerate(orders)
+    ]
+    sums = pieces + [late]
+    (d_mixed,) = launch(d_mixed, sums)
+    back_early = functools.reduce(jnp.add, [item.astype(f32) for item in returned_early])
+    back_late = functools.reduce(jnp.add, [item.astype(f32) for item in returned_late])
+    if others == 1:
+        back_early, back_late = returned_early[0], returned_late[0]
+    d_tokens = []
+    for i, returned in enumerate((back_early, back_late)):
+        finish = (returned, tokens, d_middle, row(gain_one))
+        d_tokens = [
+            unproject(d_mixed, w_qkv, (0, 1, 2), i * group, group, finish, d_tokens)
+        ]
+        for item in sums:
+            item.add()
+        if late.order:
+            d_mixed, d_tokens[0] = launch(d_mixed, sums, d_tokens[0])
+    while late.order:
+        for item in sums:
+            item.add()
+        (d_tokens[0],) = launch(d_tokens[0], sums)
     for item in sums:
         item.add()
-    d_normed = tie(d_normed, sums)
-    for item in sums:
-        item.send()
-    back_early = functools.reduce(jnp.add, [item.astype(f32) for item in returned_early])
-    back_late = functools.reduce(jnp.add, [item.astype(f32) for item in returned_late])
-    d_normed = d_normed + jnp.concatenate([back_early, back_late], axis=0)
-    unit_one, rate_one = normalize(tokens)
-    d_tokens = d_middle + norm_back(d_normed, unit_one, rate_one, gain_one)
-    d_tokens = d_tokens.astype(bf16)
-    while sum_first.order:
-        for item in sums:
-            item.add()
-        d_tokens = tie(d_tokens, sums)
-        for item in sums:
-            item.send()
-    for item in sums:
-        item.add()
-
-    qkv_rows = jnp.concatenate([sum_first.result(), sum_second.result()], axis=0)
-    down_rows = sum_down.result().reshape(-1, w_down.shape[0])
-    wide = w_up.shape[1]
+
+    qkv_rows = jnp.concatenate([item.array for item in pieces], axis=0)
+    down_rows = sum_down.array
     small = early.array[: 8 * width].reshape(8, width)
     small_up = early.array[8 * width :]
     late_small = late.array
     shape = inputs.shape
     return (
         result.reshape(shape),
-        d_tokens.reshape(shape),
+        d_tokens[0].reshape(shape),
         qkv_rows.T,
-        sum_out.result().T,
-        sum_up.result().T,
+        sum_out.array.T,
+        sum_up.array.T,
         down_rows.T,
         late_small[: 3 * width],
         small[7],

time: 946 us -> 894 us (0.945)
  matrix products: 145 us -> 0 us
  starting transfers between devices: 85.4 us -> 204 us
  Pallas kernels: 465 us -> 535 us
  other arithmetic: 117 us -> 47.1 us
  local copies, waits for them, and re-layouts: 93.4 us -> 39.6 us
  waiting for transfers between devices: 24.8 us -> 54.9 us
    dot_general x11 -> x0, matrix products: 145 us -> none  [dot(): lax.dot_general(left, right, (((left_dim,), (right_dim,)), ((), ())), pre...]
    ppermute x35 -> x38, starting transfers between devices: 76 us -> 195 us  [swap(): lax.ppermute(values, axis, [(i, i ^ 1 << position) for i in range(size)])]
    pallas_call x4 -> x15, Pallas kernels: 214 us -> 327 us  [the longest x2 87.9 us: back_local(): return call(info, *operands, *turns, *keys, dq, *before)]
    reduce_sum x10 -> x0, other arithmetic: 33.8 us -> none  [the longest x1 6.3 us: body(): part_gain = jnp.sum(weighted * grad_w_qkv.astype(f32), axis=0)]
    slice x11 -> x2, local copies, waits for them, and re-layouts: 34.2 us -> 1.13 us  [the longest x1 0.79 us: body(): part_gain = (weighted[0] - shift_one * part_shift) / gain_one]
    ppermute x35 -> x38, waiting for transfers between devices: 24.8 us -> 54.9 us  [swap(): lax.ppermute(values, axis, [(i, i ^ 1 << position) for i in range(size)])]
    pallas_call x1, Pallas kernels: 72.3 us -> 46.8 us  [attend_local(): return call(info, qT, kT, vT)]
    pallas_call x2, Pallas kernels: 63.3 us -> 45.1 us  [attend_remote(): return call(info, qT, kT, vT, *state)]
  transfers between devices with their start and end apart: 39 -> 42, of which waited for: 9 -> 14; matrix products, arithmetic and copies ran while one was open for 29% -> 7% of each run, Pallas kernels for 31% -> 34%
where the time goes in v2:
time: 894 us; the launch traced here: 883 us
  Pallas kernels  535 us (60%)
  starting transfers between devices  204 us (23%)
  waiting for transfers between devices  54.9 us (6%)
  other arithmetic  47.1 us (5%)
  local copies, waits for them, and re-layouts  39.6 us (4%)
    ppermute x38, starting transfers between devices, swap(): lax.ppermute(values, axis, [(i, i ^ 1 << position) for i in range(size)])  195 us
    pallas_call x1, Pallas kernels, block_call(): pl.pallas_call(functools.partial(block_kernel, span), grid=(rows // step,...  116 us
    pallas_call x2, Pallas kernels, back_local(): return call(info, *operands, *turns, *keys, dq, *before)  87.9 us
    pallas_call x2, Pallas kernels, back_remote(): return call(info, *operands, *turns, *keys, *before)  56.9 us
    pallas_call x3, Pallas kernels, outer_halves(): pl.pallas_call(functools.partial(outer_kernel, share, right_dim), grid_sp...  56.8 us
    ppermute x38, waiting for transfers between devices, swap(): lax.ppermute(values, axis, [(i, i ^ 1 << position) for i in range(size)])  54.9 us
    pallas_call x4, Pallas kernels, unproject(): pl.pallas_call(functools.partial(unproject_kernel, planes, bool(finish)),...  47.1 us
    pallas_call x1, Pallas kernels, attend_local(): return call(info, qT, kT, vT)  46.8 us
  transfers between devices with their start and end apart: 42, of which 14 were waited for; matrix products, arithmetic and copies ran while one was open for 7% of the time, Pallas kernels for 34%

profile of v2, /device:TPU:0, one launch (start us, length us, event | category | flops | bytes accessed | tf_op | source)
XLA Modules:
  0.0 883.1 jit_solution(5288881082188332723)
XLA Ops:
  0.7 4.7 slice_bitcast_fusion
  15.6 21.7 %project.3 = (bf16[2048,1024]{1,0:T(8,128)(2,1)}, bf16[1024,2048]{1,0:T(8,128)(2,1)}, bf16[1024,2048]{1,0:T(8,128)(2,1)}, bf16[1024,2048]{1,0:T(8,128)(2,1)}) custom-call(bf16[2048,1024]{1,0:T(8,128)(2,1)} %bitcast.184, bf16[1024,3072]{1,0:T(8,128)(2,1)} %refs_3_.3, f32[3072,1]{1,0:T(8,128)} %copy.49.b, f32[1,1024]{1,0:T(1,128)} %bitcast.209, ...), custom_call_target="tpu_custom_call" | custom-call | flops 12884901888 | bytes 16777216 | tf_op jit(solution)/shard_map/project/pallas_call | solution.py:707
  37.3 46.8 %attend_local.1 = (f32[1024,2048]{1,0:T(8,128)}, f32[8,2,2048]{2,1,0:T(2,128)}, f32[8,2,2048]{2,1,0:T(2,128)}) custom-call(s32[4]{0:T(128)} %pad_add_fusion.info, bf16[1024,2048]{1,0:T(8,128)(2,1)} %get-tuple-element.135.qT, bf16[1024,2048]{1,0:T(8,128)(2,1)} %get-tuple-element.140.kT, bf16[1024,2048]{1,0:T(8,128)(2,1)} %get-tuple-element.141.vT), custom_call_target="tpu_custom_call" | custom-call | flops 34359738368 | bytes 33554432 | tf_op jit(solution)/shard_map/attend_local/pallas_call | solution.py:431
  84.1 11.1 %project.5 = (bf16[1024,1024]{1,0:T(8,128)(2,1)}, bf16[1024,1024]{1,0:T(8,128)(2,1)}, bf16[1024,1024]{1,0:T(8,128)(2,1)}) custom-call(bf16[1024,1024]{1,0:T(8,128)(2,1)} %collective-permute-done.1.tokens, bf16[1024,3072]{1,0:T(8,128)(2,1)} %refs_3_.3, f32[3072,1]{1,0:T(8,128)} %copy.49.b, f32[1,1024]{1,0:T(1,128)} %bitcast.210, f32[1,1024]{1,0:T(1,128)} %bitcast.220, ...), custom_call_target="tpu_custom_call" | custom-call | flops 4294967296 | bytes 16777216 | tf_op jit(solution)/shard_map/project/pallas_call | solution.py:707
  95.3 34.8 %attend_remote.2 = (f32[1024,2048]{1,0:T(8,128)}, f32[8,2,2048]{2,1,0:T(2,128)}, f32[8,2,2048]{2,1,0:T(2,128)}) custom-call(s32[4]{0:T(128)} %pad_add_fusion.info, bf16[1024,2048]{1,0:T(8,128)(2,1)} %get-tuple-element.135.qT, bf16[1024,1024]{1,0:T(8,128)(2,1)} %get-tuple-element.138.kT.k_early, bf16[1024,1024]{1,0:T(8,128)(2,1)} %get-tuple-element.139.vT.v_early, ...), custom_call_target="tpu_custom_call" | custom-call | flops 17179869184 | bytes 33554432 | tf_op jit(solution)/shard_map/attend_remote/pallas_call | solution.py:453
  130.0 11.1 %project.4 = (bf16[1024,1024]{1,0:T(8,128)(2,1)}, bf16[1024,1024]{1,0:T(8,128)(2,1)}, bf16[1024,1024]{1,0:T(8,128)(2,1)}) custom-call(bf16[1024,1024]{1,0:T(8,128)(2,1)} %collective-permute-done.tokens, bf16[1024,3072]{1,0:T(8,128)(2,1)} %refs_3_.3, f32[3072,1]{1,0:T(8,128)} %copy.49.b, f32[1,1024]{1,0:T(1,128)} %bitcast.211, f32[1,1024]{1,0:T(1,128)} %bitcast.221, ...), custom_call_target="tpu_custom_call" | custom-call | flops 4294967296 | bytes 16777216 | tf_op jit(solution)/shard_map/project/pallas_call | solution.py:707
  141.2 10.3 %attend_remote.3 = (bf16[1024,2048]{1,0:T(8,128)(2,1)}, f32[8,2,2048]{2,1,0:T(2,128)}, f32[8,2,2048]{2,1,0:T(2,128)}) custom-call(s32[4]{0:T(128)} %pad_add_fusion.info, bf16[1024,2048]{1,0:T(8,128)(2,1)} %get-tuple-element.135.qT, bf16[1024,1024]{1,0:T(8,128)(2,1)} %get-tuple-element.136.kT.k_late, bf16[1024,1024]{1,0:T(8,128)(2,1)} %get-tuple-element.137.vT.v_late, ...), custom_call_target="tpu_custom_call" | custom-call | flops 17179869184 | bytes 33554432 | tf_op jit(solution)/shard_map/attend_remote/pallas_call | solution.py:453
  151.5 116.2 %block.1 = (bf16[2048,1024]{1,0:T(8,128)(2,1)}, f32[2048,1024]{1,0:T(8,128)}, bf16[2048,4096]{1,0:T(8,128)(2,1)}, bf16[2048,1024]{1,0:T(8,128)(2,1)}, bf16[2048,...) custom-call(bf16[1024,2048]{1,0:T(8,128)(2,1)} %get-tuple-element.14, ...), custom_call_target="tpu_custom_call" | custom-call | flops 77309411328 | bytes 67108864 | tf_op jit(solution)/shard_map/block/pallas_call | solution.py:641
  267.7 22.9 %outer.4 = (bf16[2048,1024]{1,0:T(8,128)(2,1)}, bf16[2048,1024]{1,0:T(8,128)(2,1)}) custom-call(s32[1]{0:T(128)} %bitcast.22.core, bf16[2048,4096]{1,0:T(8,128)(2,1)} %get-tuple-element.155.left, bf16[2048,1024]{1,0:T(8,128)(2,1)} %get-tuple-element.156.right), custom_call_target="tpu_custom_call" | custom-call | flops 17179869184 | bytes 33554432 | tf_op jit(solution)/shard_map/outer/pallas_call | solution.py:802
  290.6 32.8 %collective-permute-start.3 = (bf16[2048,1024]{1,0:T(8,128)(2,1)}, bf16[2048,1024]{1,0:T(8,128)(2,1)}, u32[]{:S(2)}, u32[]{:S(2)}) collective-permute-start(bf16[2048,1024]{1,0:T(8,128)(2,1)} %get-tuple-element.158), channel_id=1, source_target_pairs={{0,2},{2,0},{4,6},{6,4},{8,10},{10,8},{12,14},{14,12},{16,18},{18,... | collective-permute-start | bytes 12582920 | tf_op jit(solution)/shard_map/ppermute | solution.py:902
  323.4 25.3 %outer.3 = (bf16[512,4096]{1,0:T(8,128)(2,1)}, bf16[512,4096]{1,0:T(8,128)(2,1)}) custom-call(s32[1]{0:T(128)} %bitcast.22.core, bf16[2048,1024]{1,0:T(8,128)(2,1)} %get-tuple-element.151.left, bf16[2048,4096]{1,0:T(8,128)(2,1)} %get-tuple-element.152.right), custom_call_target="tpu_custom_call" | custom-call | flops 17179869184 | bytes 33554432 | tf_op jit(solution)/shard_map/outer/pallas_call | solution.py:802
  348.7 8.6 outer.5
  371.9 5.0 add_convert_fusion.1
  383.9 14.5 %collective-permute-start.6 = (bf16[2,2,2,32,4096]{4,3,0,1,2:T(8,128)(2,1)}, bf16[2,2,2,32,4096]{4,3,0,1,2:T(8,128)(2,1)}, u32[]{:S(2)}, u32[]{:S(2)}) collective-permute-start(bf16[2,2,2,32,4096]{4,3,0,1,2:T(8,128)(2,1)} %copy_bitcast_fusion), channel_id=1, source_target_pairs={{0,1},{1,0},{2,3},{3,2},{4,5},{5,4},{6,7},{7,6},{8,9},{9,8},{10,11... | collective-permute-start | bytes 6291464 | tf_op jit(solution)/shard_map/ppermute | solution.py:902
  398.4 28.4 %back_remote.2 = (f32[1024,2048]{1,0:T(8,128)}, bf16[3,1024,2048]{2,1,0:T(8,128)(2,1)}) custom-call(s32[4]{0:T(128)} %pad_add_fusion.info, bf16[1024,2048]{1,0:T(8,128)(2,1)} %get-tuple-element.135.qT, bf16[1024,2048]{1,0:T(8,128)(2,1)} %get-tuple-element.197.doT, bf16[1024,2048]{1,0:T(8,128)(2,1)} %get-tuple-element.148.oT.right, ...), custom_call_target="tpu_custom_call" | custom-call | flops 42949672960 | bytes 33554432 | tf_op jit(solution)/shard_map/back_remote/pallas_call | solution.py:489
  426.7 6.3 copy.56
  434.3 6.5 collective-permute-done.7
  448.3 14.8 %collective-permute-start.13 = (f32[12288]{0:T(1024)S(1)}, f32[12288]{0:T(1024)S(1)}, u32[]{:S(2)}, u32[]{:S(2)}) collective-permute-start(f32[12288]{0:T(1024)S(1)} %add.272), channel_id=1, source_target_pairs={{0,1},{1,0},{2,3},{3,2},{4,5},{5,4},{6,7},{7,6},{8,9},{9,8},{10,11... | collective-permute-start | bytes 147464 | tf_op jit(solution)/shard_map/ppermute | solution.py:902
  466.0 28.5 %back_remote.3 = (f32[1024,2048]{1,0:T(8,128)}, bf16[3,1024,2048]{2,1,0:T(8,128)(2,1)}) custom-call(s32[4]{0:T(128)} %pad_add_fusion.info, bf16[1024,2048]{1,0:T(8,128)(2,1)} %get-tuple-element.135.qT, bf16[1024,2048]{1,0:T(8,128)(2,1)} %get-tuple-element.197.doT, ...), custom_call_target="tpu_custom_call", output_to_operand_aliasing={{0}: (11, {}), {1}: (12, {})} | custom-call | flops 42949672960 | bytes 33554432 | tf_op jit(solution)/shard_map/back_remote/pallas_call | solution.py:489
  494.6 9.3 %unproject.4 = bf16[1024,1024]{1,0:T(8,128)(2,1)} custom-call(bf16[3,1024,2048]{2,1,0:T(8,128)(2,1)} %get-tuple-element.177.refs_0_.refs_1_, bf16[3,1024,2048]{2,1,0:T(8,128)(2,1)} %get-tuple-element.177.refs_0_.refs_1_, bf16[1024,3072]{1,0:T(8,128)(2,1)} %refs_3_.3), custom_call_target="tpu_custom_call" | custom-call | flops 4294967296 | bytes 16777216 | tf_op jit(solution)/shard_map/unproject/pallas_call | solution.py:756
  503.8 9.3 %unproject.5 = bf16[1024,1024]{1,0:T(8,128)(2,1)} custom-call(bf16[3,1024,2048]{2,1,0:T(8,128)(2,1)} %get-tuple-element.177.refs_0_.refs_1_, bf16[3,1024,2048]{2,1,0:T(8,128)(2,1)} %get-tuple-element.177.refs_0_.refs_1_, bf16[1024,3072]{1,0:T(8,128)(2,1)} %refs_3_.3), custom_call_target="tpu_custom_call" | custom-call | flops 4294967296 | bytes 16777216 | tf_op jit(solution)/shard_map/unproject/pallas_call | solution.py:756
  521.0 24.5 %collective-permute-start.17 = (f32[12288]{0:T(1024)S(1)}, f32[12288]{0:T(1024)S(1)}, u32[]{:S(2)}, u32[]{:S(2)}) collective-permute-start(f32[12288]{0:T(1024)S(1)} %add.277), channel_id=1, source_target_pairs={{0,8},{2,10},{4,12},{6,14},{8,0},{10,2},{12,4},{14,6},{16,24},{18,... | collective-permute-start | bytes 147464 | tf_op jit(solution)/shard_map/ppermute | solution.py:902
  547.5 43.8 %back_local.2.rest_0_ = bf16[3,1024,2048]{2,1,0:T(8,128)(2,1)} custom-call(s32[4]{0:T(128)} %pad_add_fusion.info, bf16[1024,2048]{1,0:T(8,128)(2,1)} %get-tuple-element.135.qT, bf16[1024,2048]{1,0:T(8,128)(2,1)} %get-tuple-element.197.doT, bf16[1024,2048]{1,0:T(8,128)(2,1)} %get-tuple-element.148.oT.right, f32[8,2,2048]{2,1,0:T(2,128)} %get-tuple-element.174.lse, ...), custom_call_target="tpu_custom_call" | custom-call | flops 42949672960 | bytes 33554432 | tf_op jit(solution)/shard_map/back_local/pallas_call | solution.py:511
  597.7 44.1 %back_local.3.refs_0_.refs_1_.refs_2_ = bf16[3,1024,2048]{2,1,0:T(8,128)(2,1)} custom-call(s32[4]{0:T(128)} %pad_add_fusion.info, bf16[1024,2048]{1,0:T(8,128)(2,1)} %get-tuple-element.135.qT, bf16[1024,2048]{1,0:T(8,128)(2,1)} %get-tuple-element.197.doT, bf16[1024,2048]{1,0:T(8,128)(2,1)} %get-tuple-element.148.oT.right, ...), custom_call_target="tpu_custom_call", output_to_operand_aliasing={{}: (10, {})} | custom-call | flops 42949672960 | bytes 33554432 | tf_op jit(solution)/shard_map/back_local/pallas_call | solution.py:511
  641.8 34.5 %mixed.1 = (bf16[1536,1024]{1,0:T(8,128)(2,1)}, bf16[1536,1024]{1,0:T(8,128)(2,1)}, f32[3072,1]{1,0:T(8,128)}, f32[2,1024]{1,0:T(2,128)}) custom-call(s32[1]{0:T(128)} %bitcast.22.core, bf16[3072,2048]{1,0:T(8,128)(2,1)} %bitcast.182, bf16[3072,2048]{1,0:T(8,128)(2,1)} %bitcast.183, bf16[2048,1024]{1,0:T(8,128)(2,1)} %get-tuple-element.199.normed, ...), custom_call_target="tpu_custom_call" | custom-call | flops 25769803776 | bytes 33554432 | tf_op jit(solution)/shard_map/mixed/pallas_call | solution.py:864
  676.4 26.3 %collective-permute-start.18 = (bf16[1536,1024]{1,0:T(8,128)(2,1)}, bf16[1536,1024]{1,0:T(8,128)(2,1)S(1)}, u32[]{:S(2)}, u32[]{:S(2)}) collective-permute-start(bf16[1536,1024]{1,0:T(8,128)(2,1)} %get-tuple-element.203), channel_id=1, source_target_pairs={{0,2},{2,0},{4,6},{6,4},{8,10},{10,8},{12,14},{14,12},{16,18},{18,... | collective-permute-start | bytes 9437192 | tf_op jit(solution)/shard_map/ppermute | solution.py:902
  735.7 20.4 %collective-permute-start.23 = (bf16[2,2,2,32,1024]{4,3,0,2,1:T(8,128)(2,1)}, bf16[2,2,2,32,1024]{4,3,0,2,1:T(8,128)(2,1)S(1)}, u32[]{:S(2)}, u32[]{:S(2)}) collective-permute-start(bf16[2,2,2,32,1024]{4,3,0,2,1:T(8,128)(2,1)} %copy_bitcast_fusion.1), channel_id=1, source_target_pairs={{0,8},{2,10},{4,12},{6,14},{8,0},{10,2},{12,4},{14,6},{16,24},{18,... | collective-permute-start | bytes 1572872 | tf_op jit(solution)/shard_map/ppermute | solution.py:902
  756.1 14.3 %unproject.6.refs_8_ = bf16[2048,1024]{1,0:T(8,128)(2,1)} custom-call(bf16[3,1024,2048]{2,1,0:T(8,128)(2,1)} %back_local.3.refs_0_.refs_1_.refs_2_, bf16[3,1024,2048]{2,1,0:T(8,128)(2,1)} %back_local.3.refs_0_.refs_1_.refs_2_, bf16[3,1024,2048]{2,1,0:T(8,128)(2,1)} %back_local.3.refs_0_.refs_1_.refs_2_, bf16[1024,3072]{1,0:T(8,128)(2,1)} %refs_3_.3, ...), custom_call_target="tpu_custom_call" | custom-call | flops 6442450944 | bytes 16777216 | tf_op jit(solution)/shard_map/unproject/pallas_call | solution.py:756
  780.4 28.8 %collective-permute-done.22 = bf16[2,2,2,32,1024]{4,3,0,2,1:T(8,128)(2,1)} collective-permute-done((bf16[2,2,2,32,1024]{4,3,0,2,1:T(8,128)(2,1)}, bf16[2,2,2,32,1024]{4,3,0,2,1:T(8,128)(2,1)}, u32[]{:S(2)}, u32[]{:S(2)}) %collective-permute-start.22) | collective-permute-done | bytes 524320 | tf_op jit(solution)/shard_map/ppermute | solution.py:902
  815.4 23.3 %collective-permute-start.27 = (bf16[2,2,32,1024]{3,2,0,1:T(8,128)(2,1)}, bf16[2,2,32,1024]{3,2,0,1:T(8,128)(2,1)}, u32[]{:S(2)}, u32[]{:S(2)}) collective-permute-start(bf16[2,2,32,1024]{3,2,0,1:T(8,128)(2,1)} %dynamic-slice_bitcast_fusion.6), channel_id=1, source_target_pairs={{0,8},{2,10},{4,12},{6,14},{8,0},{10,2},{12,4},{14,6},{16,24},{18,... | collective-permute-start | bytes 786440 | tf_op jit(solution)/shard_map/ppermute | solution.py:902
  838.7 14.3 %unproject.7 = bf16[2048,1024]{1,0:T(8,128)(2,1)} custom-call(bf16[3,1024,2048]{2,1,0:T(8,128)(2,1)} %back_local.3.refs_0_.refs_1_.refs_2_, bf16[3,1024,2048]{2,1,0:T(8,128)(2,1)} %back_local.3.refs_0_.refs_1_.refs_2_, bf16[3,1024,2048]{2,1,0:T(8,128)(2,1)} %back_local.3.refs_0_.refs_1_.refs_2_, ...), custom_call_target="tpu_custom_call", output_to_operand_aliasing={{}: (8, {})} | custom-call | flops 6442450944 | bytes 16777216 | tf_op jit(solution)/shard_map/unproject/pallas_call | solution.py:756
  855.2 5.0 collective-permute-done.26
  (207 shorter events, 132.9 us)
Async XLA Ops:
  5.4 78.7 %collective-permute-start.1 = (bf16[1024,1024]{1,0:T(8,128)(2,1)}, bf16[1024,1024]{1,0:T(8,128)(2,1)}, u32[]{:S(2)}, u32[]{:S(2)}) collective-permute-start(bf16[1024,1024]{1,0:T(8,128)(2,1)} %get-tuple-element.288), channel_id=1, source_target_pairs={{1,0},{0,1},{3,2},{2,3},{5,4},{4,5},{7,6},{6,7},{9,8},{8,9},{11,10... | collective-permute-start | bytes 6291464 | tf_op jit(solution)/shard_map/ppermute | solution.py:1014
  8.4 121.7 %collective-permute-start = (bf16[1024,1024]{1,0:T(8,128)(2,1)}, bf16[1024,1024]{1,0:T(8,128)(2,1)}, u32[]{:S(2)}, u32[]{:S(2)}) collective-permute-start(bf16[1024,1024]{1,0:T(8,128)(2,1)} %get-tuple-element.289), channel_id=1, source_target_pairs={{1,0},{3,2},{5,4},{7,6},{9,8},{11,10},{13,12},{15,14},{17,16},{19,... | collective-permute-start | bytes 6291464 | tf_op jit(solution)/shard_map/ppermute | solution.py:1018
  290.6 72.2 %collective-permute-start.3 = (bf16[2048,1024]{1,0:T(8,128)(2,1)}, bf16[2048,1024]{1,0:T(8,128)(2,1)}, u32[]{:S(2)}, u32[]{:S(2)}) collective-permute-start(bf16[2048,1024]{1,0:T(8,128)(2,1)} %get-tuple-element.158), channel_id=1, source_target_pairs={{0,2},{2,0},{4,6},{6,4},{8,10},{10,8},{12,14},{14,12},{16,18},{18,... | collective-permute-start | bytes 12582920 | tf_op jit(solution)/shard_map/ppermute | solution.py:902
  348.7 23.2 %collective-permute-start.2 = (bf16[512,4096]{1,0:T(8,128)(2,1)}, bf16[512,4096]{1,0:T(8,128)(2,1)}, u32[]{:S(2)}, u32[]{:S(2)}) collective-permute-start(bf16[512,4096]{1,0:T(8,128)(2,1)} %get-tuple-element.154), channel_id=1, source_target_pairs={{0,2},{2,0},{4,6},{6,4},{8,10},{10,8},{12,14},{14,12},{16,18},{18,... | collective-permute-start | bytes 12582920 | tf_op jit(solution)/shard_map/ppermute | solution.py:902
  380.3 52.7 %collective-permute-start.9 = (f32[12288]{0:T(1024)S(1)}, f32[12288]{0:T(1024)S(1)}, u32[]{:S(2)}, u32[]{:S(2)}) collective-permute-start(f32[12288]{0:T(1024)S(1)} %fusion.22), channel_id=1, source_target_pairs={{0,4},{2,6},{4,0},{6,2},{8,12},{10,14},{12,8},{14,10},{16,20},{18,... | collective-permute-start | bytes 147464 | tf_op jit(solution)/shard_map/ppermute | solution.py:902
  381.8 51.2 %collective-permute-start.8 = (bf16[2,2,2,32,1024]{4,3,0,1,2:T(8,128)(2,1)S(1)}, bf16[2,2,2,32,1024]{4,3,0,1,2:T(8,128)(2,1)}, u32[]{:S(2)}, u32[]{:S(2)}) collective-permute-start(bf16[2,2,2,32,1024]{4,3,0,1,2:T(8,128)(2,1)S(1)} %copy-done.18), channel_id=1, source_target_pairs={{0,4},{2,6},{4,0},{6,2},{8,12},{10,14},{12,8},{14,10},{16,20},{18,... | collective-permute-start | bytes 1572872 | tf_op jit(solution)/shard_map/ppermute | solution.py:902
  382.4 58.4 %collective-permute-start.7 = (bf16[2,2,2,128,1024]{3,4,0,1,2:T(8,128)(2,1)}, bf16[2,2,2,128,1024]{3,4,0,1,2:T(8,128)(2,1)}, u32[]{:S(2)}, u32[]{:S(2)}) collective-permute-start(bf16[2,2,2,128,1024]{3,4,0,1,2:T(8,128)(2,1)} %bitcast.26), channel_id=1, source_target_pairs={{0,4},{2,6},{4,0},{6,2},{8,12},{10,14},{12,8},{14,10},{16,20},{18,... | collective-permute-start | bytes 6291464 | tf_op jit(solution)/shard_map/ppermute | solution.py:902
  383.9 59.9 %collective-permute-start.6 = (bf16[2,2,2,32,4096]{4,3,0,1,2:T(8,128)(2,1)}, bf16[2,2,2,32,4096]{4,3,0,1,2:T(8,128)(2,1)}, u32[]{:S(2)}, u32[]{:S(2)}) collective-permute-start(bf16[2,2,2,32,4096]{4,3,0,1,2:T(8,128)(2,1)} %copy_bitcast_fusion), channel_id=1, source_target_pairs={{0,1},{1,0},{2,3},{3,2},{4,5},{5,4},{6,7},{7,6},{8,9},{9,8},{10,11... | collective-permute-start | bytes 6291464 | tf_op jit(solution)/shard_map/ppermute | solution.py:902
  448.3 64.8 %collective-permute-start.13 = (f32[12288]{0:T(1024)S(1)}, f32[12288]{0:T(1024)S(1)}, u32[]{:S(2)}, u32[]{:S(2)}) collective-permute-start(f32[12288]{0:T(1024)S(1)} %add.272), channel_id=1, source_target_pairs={{0,1},{1,0},{2,3},{3,2},{4,5},{5,4},{6,7},{7,6},{8,9},{9,8},{10,11... | collective-permute-start | bytes 147464 | tf_op jit(solution)/shard_map/ppermute | solution.py:902
  463.1 50.0 %collective-permute-start.12 = (bf16[2,2,32,1024]{3,2,0,1:T(8,128)(2,1)S(1)}, bf16[2,2,32,1024]{3,2,0,1:T(8,128)(2,1)}, u32[]{:S(2)}, u32[]{:S(2)}) collective-permute-start(bf16[2,2,32,1024]{3,2,0,1:T(8,128)(2,1)S(1)} %dynamic-slice_bitcast_fusion.10), channel_id=1, source_target_pairs={{0,1},{1,0},{2,3},{3,2},{4,5},{5,4},{6,7},{7,6},{8,9},{9,8},{10,11... | collective-permute-start | bytes 786440 | tf_op jit(solution)/shard_map/ppermute | solution.py:902
  463.1 51.9 %collective-permute-start.11 = (bf16[2,2,128,1024]{2,3,0,1:T(8,128)(2,1)S(1)}, bf16[2,2,128,1024]{2,3,0,1:T(8,128)(2,1)}, u32[]{:S(2)}, u32[]{:S(2)}) collective-permute-start(bf16[2,2,128,1024]{2,3,0,1:T(8,128)(2,1)S(1)} %dynamic-slice_bitcast_fusion), channel_id=1, source_target_pairs={{0,1},{1,0},{2,3},{3,2},{4,5},{5,4},{6,7},{7,6},{8,9},{9,8},{10,11... | collective-permute-start | bytes 3145736 | tf_op jit(solution)/shard_map/ppermute | solution.py:902
  465.1 52.5 %collective-permute-start.10 = (bf16[2,2,32,4096]{3,2,0,1:T(8,128)(2,1)}, bf16[2,2,32,4096]{3,2,0,1:T(8,128)(2,1)}, u32[]{:S(2)}, u32[]{:S(2)}) collective-permute-start(bf16[2,2,32,4096]{3,2,0,1:T(8,128)(2,1)} %dynamic-slice_bitcast_fusion.1), channel_id=1, source_target_pairs={{0,4},{2,6},{4,0},{6,2},{8,12},{10,14},{12,8},{14,10},{16,20},{18,... | collective-permute-start | bytes 3145736 | tf_op jit(solution)/shard_map/ppermute | solution.py:902
  521.0 70.3 %collective-permute-start.17 = (f32[12288]{0:T(1024)S(1)}, f32[12288]{0:T(1024)S(1)}, u32[]{:S(2)}, u32[]{:S(2)}) collective-permute-start(f32[12288]{0:T(1024)S(1)} %add.277), channel_id=1, source_target_pairs={{0,8},{2,10},{4,12},{6,14},{8,0},{10,2},{12,4},{14,6},{16,24},{18,... | collective-permute-start | bytes 147464 | tf_op jit(solution)/shard_map/ppermute | solution.py:902
  545.4 45.9 %collective-permute-start.16 = (bf16[2,32,1024]{2,1,0:T(8,128)(2,1)}, bf16[2,32,1024]{2,1,0:T(8,128)(2,1)}, u32[]{:S(2)}, u32[]{:S(2)}) collective-permute-start(bf16[2,32,1024]{2,1,0:T(8,128)(2,1)} %dynamic-slice_bitcast_fusion.14), channel_id=1, source_target_pairs={{0,8},{2,10},{4,12},{6,14},{8,0},{10,2},{12,4},{14,6},{16,24},{18,... | collective-permute-start | bytes 393224 | tf_op jit(solution)/shard_map/ppermute | solution.py:902
  545.5 46.8 %collective-permute-start.15 = (bf16[2,128,1024]{1,2,0:T(8,128)(2,1)}, bf16[2,128,1024]{1,2,0:T(8,128)(2,1)}, u32[]{:S(2)}, u32[]{:S(2)}) collective-permute-start(bf16[2,128,1024]{1,2,0:T(8,128)(2,1)} %dynamic-slice_bitcast_fusion.3), channel_id=1, source_target_pairs={{0,8},{2,10},{4,12},{6,14},{8,0},{10,2},{12,4},{14,6},{16,24},{18,... | collective-permute-start | bytes 1572872 | tf_op jit(solution)/shard_map/ppermute | solution.py:902
  547.5 47.5 %collective-permute-start.14 = (bf16[2,32,4096]{2,1,0:T(8,128)(2,1)}, bf16[2,32,4096]{2,1,0:T(8,128)(2,1)S(1)}, u32[]{:S(2)}, u32[]{:S(2)}) collective-permute-start(bf16[2,32,4096]{2,1,0:T(8,128)(2,1)} %dynamic-slice_bitcast_fusion.4), channel_id=1, source_target_pairs={{0,8},{2,10},{4,12},{6,14},{8,0},{10,2},{12,4},{14,6},{16,24},{18,... | collective-permute-start | bytes 1572872 | tf_op jit(solution)/shard_map/ppermute | solution.py:902
  676.4 48.0 %collective-permute-start.18 = (bf16[1536,1024]{1,0:T(8,128)(2,1)}, bf16[1536,1024]{1,0:T(8,128)(2,1)S(1)}, u32[]{:S(2)}, u32[]{:S(2)}) collective-permute-start(bf16[1536,1024]{1,0:T(8,128)(2,1)} %get-tuple-element.203), channel_id=1, source_target_pairs={{0,2},{2,0},{4,6},{6,4},{8,10},{10,8},{12,14},{14,12},{16,18},{18,... | collective-permute-start | bytes 9437192 | tf_op jit(solution)/shard_map/ppermute | solution.py:902
  705.4 8.0 collective-permute-start.19
  705.5 50.6 %collective-permute-start.20 = (bf16[1024,1024]{1,0:T(8,128)(2,1)}, bf16[1024,1024]{1,0:T(8,128)(2,1)}, u32[]{:S(2)}, u32[]{:S(2)}) collective-permute-start(bf16[1024,1024]{1,0:T(8,128)(2,1)} %unproject.4), channel_id=1, source_target_pairs={{0,1},{1,0},{2,3},{3,2},{4,5},{5,4},{6,7},{7,6},{8,9},{9,8},{10,11... | collective-permute-start | bytes 6291464 | tf_op jit(solution)/shard_map/ppermute | solution.py:1107
  707.1 108.3 %collective-permute-start.25 = (bf16[1024,1024]{1,0:T(8,128)(2,1)}, bf16[1024,1024]{1,0:T(8,128)(2,1)}, u32[]{:S(2)}, u32[]{:S(2)}) collective-permute-start(bf16[1024,1024]{1,0:T(8,128)(2,1)} %unproject.5), channel_id=1, source_target_pairs={{0,1},{2,3},{4,5},{6,7},{8,9},{10,11},{12,13},{14,15},{16,17},{18,... | collective-permute-start | bytes 6291464 | tf_op jit(solution)/shard_map/ppermute | solution.py:1112
  713.4 148.6 %collective-permute-start.39 = (bf16[32,4096]{1,0:T(8,128)(2,1)}, bf16[32,4096]{1,0:T(8,128)(2,1)}, u32[]{:S(2)}, u32[]{:S(2)}) collective-permute-start(bf16[32,4096]{1,0:T(8,128)(2,1)} %dynamic-slice_bitcast_fusion.9), channel_id=1, source_target_pairs={{0,16},{2,18},{4,20},{6,22},{8,24},{10,26},{12,28},{14,30},{16,0},... | collective-permute-start | bytes 786440 | tf_op jit(solution)/shard_map/ppermute | solution.py:902
  715.8 7.9 collective-permute-start.37
  731.0 39.4 %collective-permute-start.24 = (f32[5120]{0:T(1024)}, f32[5120]{0:T(1024)S(1)}, u32[]{:S(2)}, u32[]{:S(2)}) collective-permute-start(f32[5120]{0:T(1024)} %fusion.21), channel_id=1, source_target_pairs={{0,4},{2,6},{4,0},{6,2},{8,12},{10,14},{12,8},{14,10},{16,20},{18,... | collective-permute-start | bytes 61448 | tf_op jit(solution)/shard_map/ppermute | solution.py:902
  735.7 37.9 %collective-permute-start.23 = (bf16[2,2,2,32,1024]{4,3,0,2,1:T(8,128)(2,1)}, bf16[2,2,2,32,1024]{4,3,0,2,1:T(8,128)(2,1)S(1)}, u32[]{:S(2)}, u32[]{:S(2)}) collective-permute-start(bf16[2,2,2,32,1024]{4,3,0,2,1:T(8,128)(2,1)} %copy_bitcast_fusion.1), channel_id=1, source_target_pairs={{0,8},{2,10},{4,12},{6,14},{8,0},{10,2},{12,4},{14,6},{16,24},{18,... | collective-permute-start | bytes 1572872 | tf_op jit(solution)/shard_map/ppermute | solution.py:902
  756.1 53.0 %collective-permute-start.22 = (bf16[2,2,2,32,1024]{4,3,0,2,1:T(8,128)(2,1)}, bf16[2,2,2,32,1024]{4,3,0,2,1:T(8,128)(2,1)}, u32[]{:S(2)}, u32[]{:S(2)}) collective-permute-start(bf16[2,2,2,32,1024]{4,3,0,2,1:T(8,128)(2,1)} %copy_bitcast_fusion.2), channel_id=1, source_target_pairs={{0,1},{1,0},{2,3},{3,2},{4,5},{5,4},{6,7},{7,6},{8,9},{9,8},{10,11... | collective-permute-start | bytes 1572872 | tf_op jit(solution)/shard_map/ppermute | solution.py:902
  770.4 101.8 %collective-permute-start.38 = (bf16[128,1024]{0,1:T(8,128)(2,1)S(1)}, bf16[128,1024]{0,1:T(8,128)(2,1)}, u32[]{:S(2)}, u32[]{:S(2)}) collective-permute-start(bf16[128,1024]{0,1:T(8,128)(2,1)S(1)} %copy-done.19), channel_id=1, source_target_pairs={{0,16},{2,18},{4,20},{6,22},{8,24},{10,26},{12,28},{14,30},{16,0},... | collective-permute-start | bytes 786440 | tf_op jit(solution)/shard_map/ppermute | solution.py:902
  774.4 37.0 %collective-permute-start.21 = (bf16[2,2,2,32,1024]{4,3,2,1,0:T(8,128)(2,1)}, bf16[2,2,2,32,1024]{4,3,2,1,0:T(8,128)(2,1)S(1)}, u32[]{:S(2)}, u32[]{:S(2)}) collective-permute-start(bf16[2,2,2,32,1024]{4,3,2,1,0:T(8,128)(2,1)} %dynamic-slice_bitcast_fusion.2), channel_id=1, source_target_pairs={{0,4},{2,6},{4,0},{6,2},{8,12},{10,14},{12,8},{14,10},{16,20},{18,... | collective-permute-start | bytes 1572872 | tf_op jit(solution)/shard_map/ppermute | solution.py:902
  812.4 40.5 %collective-permute-start.29 = (f32[5120]{0:T(1024)S(1)}, f32[5120]{0:T(1024)S(1)}, u32[]{:S(2)}, u32[]{:S(2)}) collective-permute-start(f32[5120]{0:T(1024)S(1)} %add.289), channel_id=1, source_target_pairs={{0,1},{1,0},{2,3},{3,2},{4,5},{5,4},{6,7},{7,6},{8,9},{9,8},{10,11... | collective-permute-start | bytes 61448 | tf_op jit(solution)/shard_map/ppermute | solution.py:902
  814.9 38.2 %collective-permute-start.28 = (bf16[2,2,32,1024]{3,2,0,1:T(8,128)(2,1)}, bf16[2,2,32,1024]{3,2,0,1:T(8,128)(2,1)}, u32[]{:S(2)}, u32[]{:S(2)}) collective-permute-start(bf16[2,2,32,1024]{3,2,0,1:T(8,128)(2,1)} %dynamic-slice_bitcast_fusion.5), channel_id=1, source_target_pairs={{0,4},{2,6},{4,0},{6,2},{8,12},{10,14},{12,8},{14,10},{16,20},{18,... | collective-permute-start | bytes 786440 | tf_op jit(solution)/shard_map/ppermute | solution.py:902
  815.4 38.7 %collective-permute-start.27 = (bf16[2,2,32,1024]{3,2,0,1:T(8,128)(2,1)}, bf16[2,2,32,1024]{3,2,0,1:T(8,128)(2,1)}, u32[]{:S(2)}, u32[]{:S(2)}) collective-permute-start(bf16[2,2,32,1024]{3,2,0,1:T(8,128)(2,1)} %dynamic-slice_bitcast_fusion.6), channel_id=1, source_target_pairs={{0,8},{2,10},{4,12},{6,14},{8,0},{10,2},{12,4},{14,6},{16,24},{18,... | collective-permute-start | bytes 786440 | tf_op jit(solution)/shard_map/ppermute | solution.py:902
  869.3 7.7 collective-permute-start.40
  874.1 7.3 collective-permute-start.35
  (35 other events, 367.9 us)

commit v3 on v2

--- a/solution.py
+++ b/solution.py
@@ -26,7 +26,7 @@
     )
 
 
-def fwd_chunk(q0, k0, q_n, k_n, offset, limit, qT, kT, vT, m_ref, l_ref, acc):
+def fwd_chunk(q0, k0, q_n, k_n, limit, qT, kT, vT, m_ref, l_ref, acc):
     queries = pl.ds(q0, q_n)
     strip = min(256, k_n)
     for h in range(2):
@@ -37,13 +37,9 @@
         for j in range(k_n // strip):
             keys = pl.ds(k0 + j * strip, strip)
             scores = dot(kT[rows, keys], qT[rows, queries], 0, 0)
-            if offset is not None or limit is not None:
-                key_at = j * strip + lax.broadcasted_iota(jnp.int32, (strip, q_n), 0)
-                query_at = lax.broadcasted_iota(jnp.int32, (1, q_n), 1)
-                last = jnp.zeros((1, q_n), jnp.int32) + (limit - 1)
-                if offset is not None:
-                    last = jnp.minimum(query_at + offset, last)
-                scores = jnp.where(key_at <= last, scores, NEG)
+            if limit is not None:
+                key_at = lax.broadcasted_iota(jnp.int32, (strip, q_n), 0)
+                scores = jnp.where(key_at < limit - j * strip, scores, NEG)
             strips.append(scores)
             new = jnp.maximum(new, jnp.max(scores, axis=0, keepdims=True))
         factor = jnp.exp2(old - new)
@@ -71,7 +67,7 @@
     return jnp.concatenate([values, jnp.zeros((values.shape[0], count), f32)], axis=1)
 
 
-def fwd_diagonal(base, group, qT, kT, vT, m_ref, l_ref, acc):
+def fwd_diagonal(base, group, limit, qT, kT, vT, m_ref, l_ref, acc):
     strip = min(256, group)
     count = group // strip
     for h in range(2):
@@ -83,7 +79,10 @@
             scores = dot(kT[rows, keys], qT[rows, queries], 0, 0)
             key_at = lax.broadcasted_iota(jnp.int32, scores.shape, 0)
             query_at = lax.broadcasted_iota(jnp.int32, scores.shape, 1)
-            strips.append(jnp.where(key_at <= query_at, scores, NEG))
+            scores = jnp.where(key_at <= query_at, scores, NEG)
+            if limit is not None:
+                scores = jnp.where(key_at < limit - j * strip, scores, NEG)
+            strips.append(scores)
         peaks = []
         for g in range(count):
             peak = None
@@ -120,11 +119,11 @@
 
         @pl.when(start + group <= length)
         def _():
-            fwd_diagonal(base, group, *refs)
+            fwd_diagonal(base, group, None, *refs)
 
         @pl.when((start < length) & (start + group > length))
         def _():
-            fwd_chunk(base, base, group, group, 0, length - start, *refs)
+            fwd_diagonal(base, group, length - start, *refs)
 
         return carry
 
@@ -133,20 +132,26 @@
 
     @pl.when(early + group <= length)
     def _():
-        fwd_chunk(group, 0, group, group, None, None, *refs)
+        fwd_chunk(group, 0, group, group, None, *refs)
 
     @pl.when((early < length) & (early + group > length))
     def _():
-        fwd_chunk(group, 0, group, group, None, length - early, *refs)
-
-
-def remote_steps(group, parts, kind, info, full, partial):
+        fwd_chunk(group, 0, group, group, length - early, *refs)
+
+
+def remote_steps(group, parts, info, full, partial):
     place, length = info[0], info[1]
 
-    def visit(q_block, k_slot, k_block, wanted):
-        q0 = pl.multiple_of(q_block * group, group)
-        k0 = pl.multiple_of(k_slot * group, group)
-        start = k_block * group
+    def visit(i, carry):
+        j, turn_at = i // 3, lax.rem(i, 3)
+        other = lax.rem(place + 1 + j, parts)
+        late_key = turn_at == 2
+        block = jnp.where(late_key, 2 * parts - 1 - other, other)
+        before = (other < place).astype(jnp.int32)
+        wanted = jnp.where(turn_at == 0, before, jnp.where(late_key, 1 - before, 1)) == 1
+        q0 = pl.multiple_of(jnp.where(turn_at == 0, 0, group), group)
+        k0 = pl.multiple_of((2 * j + jnp.where(late_key, 1, 0)) * group, group)
+        start = block * group
 
         @pl.when(wanted & (start + group <= length))
         def _():
@@ -156,67 +161,31 @@
         def _():
             partial(q0, k0, length - start)
 
-    others = parts - 1
-
-    def early(i, carry):
-        j = i // 2
-        other = lax.rem(place + 1 + j, parts)
-        late_query = lax.rem(i, 2)
-        visit(late_query, j, other, (late_query == 1) | (other < place))
         return carry
 
-    def late(j, carry):
-        other = lax.rem(place + 1 + j, parts)
-        slot = j + (others if kind == 2 else 0)
-        visit(1, slot, 2 * parts - 1 - other, other > place)
-        return carry
-
-    if kind == 2:
-
-        def both(i, carry):
-            is_early = i < 2 * others
-            j = jnp.where(is_early, i // 2, i - 2 * others)
-            other = lax.rem(place + 1 + j, parts)
-            late_query = jnp.where(is_early, lax.rem(i, 2), 1)
-            slot = jnp.where(is_early, j, j + others)
-            block = jnp.where(is_early, other, 2 * parts - 1 - other)
-            wanted = jnp.where(
-                is_early,
-                ((late_query == 1) | (other < place)).astype(jnp.int32),
-                (other > place).astype(jnp.int32),
-            )
-            visit(late_query, slot, block, wanted == 1)
-            return carry
-
-        lax.fori_loop(0, 3 * others, both, 0)
-    elif kind == 0:
-        lax.fori_loop(0, 2 * others, early, 0)
-    else:
-        lax.fori_loop(0, others, late, 0)
+    lax.fori_loop(0, 3 * (parts - 1), visit, 0)
 
 
 def fwd_remote_kernel(
-    group, parts, kind, last, info, qT, kT, vT, acc_in, m_in, l_in, out, m_out, l_out, *scratch
+    group, parts, info, qT, kT, vT, acc_in, m_in, l_in, out, lse, acc, m_ref, l_ref
 ):
-    acc = scratch[0] if last else out
     acc[...] = acc_in[...]
-    m_out[...] = m_in[...]
-    l_out[...] = l_in[...]
-    refs = (qT, kT, vT, m_out.at[0], l_out.at[0], acc)
+    m_ref[...] = m_in[0]
+    l_ref[...] = l_in[0]
+    refs = (qT, kT, vT, m_ref, l_ref, acc)
 
     def full(q0, k0):
-        fwd_chunk(q0, k0, group, group, None, None, *refs)
+        fwd_chunk(q0, k0, group, group, None, *refs)
 
     def partial(q0, k0, limit):
-        fwd_chunk(q0, k0, group, group, None, limit, *refs)
-
-    remote_steps(group, parts, kind, info, full, partial)
-    if last:
-        for h in range(2):
-            rows = slice(HEAD_DIM * h, HEAD_DIM * (h + 1))
-            total = l_out[0, h : h + 1, :]
-            out[rows, :] = (acc[rows, :] / total).astype(bf16)
-            m_out[0, h : h + 1, :] = m_out[0, h : h + 1, :] + jnp.log2(total)
+        fwd_chunk(q0, k0, group, group, limit, *refs)
+
+    remote_steps(group, parts, info, full, partial)
+    for h in range(2):
+        rows = slice(HEAD_DIM * h, HEAD_DIM * (h + 1))
+        total = l_ref[h : h + 1, :]
+        out[rows, :] = (acc[rows, :] / total).astype(bf16)
+        lse[0, h : h + 1, :] = m_ref[h : h + 1, :] + jnp.log2(total)
 
 
 def split_three(values):
@@ -227,7 +196,7 @@
     return [high, middle, low]
 
 
-def bwd_prepare(qT, keys, doT, oT, lse, qa, da, ka, va):
+def bwd_prepare(qT, kT, vT, doT, oT, lse, qa, da, ka, va):
     n_q, n_k = qT.shape[1], ka.shape[2]
     extra = qa.shape[1] - HEAD_DIM
     pad = jnp.zeros((extra - 3, n_q), f32)
@@ -243,28 +212,20 @@
         da[h, :HEAD_DIM, :] = doT[rows, :]
         parts = split_three(-delta) + [pad]
         da[h, HEAD_DIM:, :] = jnp.concatenate(parts, axis=0).astype(bf16)
-        at = 0
-        for kT, vT in keys:
-            part = slice(at, at + kT.shape[1])
-            ka[h, :HEAD_DIM, part] = kT[rows, :]
-            va[h, :HEAD_DIM, part] = vT[rows, :]
-            at += kT.shape[1]
+        ka[h, :HEAD_DIM, :] = kT[rows, :]
+        va[h, :HEAD_DIM, :] = vT[rows, :]
         ka[h, HEAD_DIM:, :] = tail
         va[h, HEAD_DIM:, :] = tail
 
 
-def bwd_chunk(q0, k0, q_n, k_n, offset, limit, qT, doT, qa, da, ka, va, dq, dk, dv):
+def bwd_chunk(q0, k0, q_n, k_n, limit, qT, doT, qa, da, ka, va, dq, dk, dv):
     queries, keys = pl.ds(q0, q_n), pl.ds(k0, k_n)
     for h in range(2):
         rows = slice(HEAD_DIM * h, HEAD_DIM * (h + 1))
         probs = jnp.exp2(dot(qa[h, :, queries], ka[h, :, keys], 0, 0))
-        if offset is not None or limit is not None:
+        if limit is not None:
             key_at = lax.broadcasted_iota(jnp.int32, (q_n, k_n), 1)
-            last = jnp.zeros((q_n, 1), jnp.int32) + (limit - 1)
-            if offset is not None:
-                query_at = lax.broadcasted_iota(jnp.int32, (q_n, 1), 0)
-                last = jnp.minimum(query_at + offset, last)
-            probs = jnp.where(key_at <= last, probs, 0.0)
+            probs = jnp.where(key_at < limit, probs, 0.0)
         d_probs = dot(da[h, :, queries], va[h, :, keys], 0, 0)
         d_scores = (probs * d_probs).astype(bf16)
         dv[rows, keys] += dot(doT[rows, queries], probs.astype(bf16), 1, 0)
@@ -272,7 +233,7 @@
         dq[rows, queries] += dot(ka[h, :HEAD_DIM, keys], d_scores, 1, 1)
 
 
-def bwd_diagonal(base, group, qT, doT, qa, da, ka, va, dq, dk, dv):
+def bwd_diagonal(base, group, limit, qT, doT, qa, da, ka, va, dq, dk, dv):
     strip = min(256, group)
     count = group // strip
     for h in range(2):
@@ -285,6 +246,8 @@
             query_at = lax.broadcasted_iota(jnp.int32, probs.shape, 0)
             key_at = lax.broadcasted_iota(jnp.int32, probs.shape, 1)
             probs = jnp.where(key_at <= query_at + j * strip, probs, 0.0)
+            if limit is not None:
+                probs = jnp.where(key_at < limit, probs, 0.0)
             d_probs = dot(da[h, :, queries], va[h, :, keys], 0, 0)
             d_scores = (probs * d_probs).astype(bf16)
             value = pad_right(dot(doT[rows, queries], probs.astype(bf16), 1, 0), group - wide)
@@ -306,25 +269,22 @@
     )
 
 
-def bwd_remote_kernel(
-    group, parts, info, qT, doT, oT, lse, cosine, sine, k_early, v_early, k_late, v_late, *rest
-):
+def bwd_remote_kernel(group, parts, info, qT, doT, oT, lse, cosine, sine, kT, vT, *rest):
     dq, dkv, *scratch = rest[-8:]
     qa, da, ka, va, dk, dv = scratch
-    keys = [(k_early, v_early), (k_late, v_late)]
-    bwd_prepare(qT, keys, doT, oT, lse, qa, da, ka, va)
+    bwd_prepare(qT, kT, vT, doT, oT, lse, qa, da, ka, va)
     dq[...] = jnp.zeros(dq.shape, f32)
     dk[...] = jnp.zeros(dk.shape, f32)
     dv[...] = jnp.zeros(dv.shape, f32)
     refs = (qT, doT, qa, da, ka, va, dq, dk, dv)
 
     def full(q0, k0):
-        bwd_chunk(q0, k0, group, group, None, None, *refs)
+        bwd_chunk(q0, k0, group, group, None, *refs)
 
     def partial(q0, k0, limit):
-        bwd_chunk(q0, k0, group, group, None, limit, *refs)
-
-    remote_steps(group, parts, 2, info, full, partial)
+        bwd_chunk(q0, k0, group, group, limit, *refs)
+
+    remote_steps(group, parts, info, full, partial)
     for h in range(2):
         rows = slice(HEAD_DIM * h, HEAD_DIM * (h + 1))
         dkv[1, rows, :] = turn_back(dk[rows, :] * LN2, cosine[...], sine[...]).astype(bf16)
@@ -336,7 +296,7 @@
     dqkv, *scratch = rest[-8:]
     qa, da, ka, va, dq, dk, dv = scratch
     length = info[1]
-    bwd_prepare(qT, [(kT, vT)], doT, oT, lse, qa, da, ka, va)
+    bwd_prepare(qT, kT, vT, doT, oT, lse, qa, da, ka, va)
     dq[...] = dq_in[...]
     dk[...] = jnp.zeros(dk.shape, f32)
     dv[...] = jnp.zeros(dv.shape, f32)
@@ -348,11 +308,11 @@
 
         @pl.when(start + group <= length)
         def _():
-            bwd_diagonal(base, group, *refs)
+            bwd_diagonal(base, group, None, *refs)
 
         @pl.when((start < length) & (start + group > length))
         def _():
-            bwd_chunk(base, base, group, group, 0, length - start, *refs)
+            bwd_diagonal(base, group, length - start, *refs)
 
         return carry
 
@@ -361,11 +321,11 @@
 
     @pl.when(early + group <= length)
     def _():
-        bwd_chunk(group, 0, group, group, None, None, *refs)
+        bwd_chunk(group, 0, group, group, None, *refs)
 
     @pl.when((early < length) & (early + group > length))
     def _():
-        bwd_chunk(group, 0, group, group, None, length - early, *refs)
+        bwd_chunk(group, 0, group, group, length - early, *refs)
 
     for h in range(2):
         rows = slice(HEAD_DIM * h, HEAD_DIM * (h + 1))
@@ -431,23 +391,21 @@
     return call(info, qT, kT, vT)
 
 
-def attend_remote(info, qT, kT, vT, state, group, parts, kind, last):
+def attend_remote(info, qT, kT, vT, state, group, parts):
     width, n_q = qT.shape
     n_k = kT.shape[1]
     pairs = width // PAIR
-    scratch = [pltpu.VMEM((PAIR, n_q), f32)] if last else []
     call = attention_call(
-        functools.partial(fwd_remote_kernel, group, parts, kind, last),
+        functools.partial(fwd_remote_kernel, group, parts),
         pairs,
         [rows_of(n_q), rows_of(n_k), rows_of(n_k), rows_of(n_q), stats_of(n_q), stats_of(n_q)],
-        [rows_of(n_q), stats_of(n_q), stats_of(n_q)],
+        [rows_of(n_q), stats_of(n_q)],
         [
-            jax.ShapeDtypeStruct((width, n_q), bf16 if last else f32),
-            jax.ShapeDtypeStruct((pairs, 2, n_q), f32),
+            jax.ShapeDtypeStruct((width, n_q), bf16),
             jax.ShapeDtypeStruct((pairs, 2, n_q), f32),
         ],
-        scratch,
-        4 * width * group * group * 4,
+        [pltpu.VMEM((PAIR, n_q), f32)] + [pltpu.VMEM((2, n_q), f32)] * 2,
+        4 * width * 2 * group * group * 4,
         "attend_remote",
     )
     return call(info, qT, kT, vT, *state)
@@ -465,7 +423,7 @@
 
 def back_remote(info, operands, turns, keys, group, parts, first, count, before):
     width, n_q = operands[0].shape
-    n_k = keys[0].shape[1] + keys[2].shape[1]
+    n_k = keys[0].shape[1]
     half = HEAD_DIM // 2
     n_in = 1 + len(operands) + len(turns) + len(keys)
     call = attention_call(
@@ -474,7 +432,7 @@
         [rows_of(n_q, first)] * 3
         + [stats_of(n_q, first)]
         + [whole((half, n_k))] * 2
-        + [rows_of(item.shape[1], first) for item in keys]
+        + [rows_of(n_k, first)] * 2
         + [pl.BlockSpec(memory_space=pl.ANY)] * len(before),
         [rows_of(n_q, first), planes_of(3, n_k, first)],
         [
@@ -692,18 +650,17 @@
                 out[place, :] = value.astype(bf16)
 
 
-def project(tokens, w, b, gain, shift, cosine, sine, sections, start=0):
+def project(tokens, w, b, gain, shift, cosine, sine, sections):
     rows, width = tokens.shape
     step = min(512, rows)
     half = HEAD_DIM // 2
-    first = start // step
 
     def fixed(shape):
         return pl.BlockSpec(shape, lambda i: (0, 0), pipeline_mode=pl.Buffered(1))
 
     lines = pl.BlockSpec((step, width), lambda i: (i, 0))
     features = pl.BlockSpec((width, step), lambda i: (0, i))
-    turns = pl.BlockSpec((half, step), lambda i: (0, first + i))
+    turns = pl.BlockSpec((half, step), lambda i: (0, i))
     return pl.pallas_call(
         functools.partial(project_kernel, sections),
         grid=(rows // step,),
@@ -751,7 +708,7 @@
 
     lines = pl.BlockSpec((step, width), lambda i: (i, 0))
     later = pl.BlockSpec((step, width), lambda i: (first + i, 0))
-    specs = [lines, later, later, fixed(finish[-1].shape)] if finish else []
+    specs = [later] * 3 + [fixed(finish[-1].shape)] if finish else []
     n_in = len(planes) + 1 + len(finish)
     return pl.pallas_call(
         functools.partial(unproject_kernel, planes, bool(finish)),
@@ -773,53 +730,83 @@
     )(*[d_mixed] * len(planes), w, *finish, *before)
 
 
-def divide(total, share, core, kept, given):
-    own, other = [], []
-    for i in range(0, total.shape[0], 2 * share):
-        zero, one = total[i : i + share], total[i + share : i + 2 * share]
-        own.append(jnp.where(core == 0, zero, one))
-        other.append(jnp.where(core == 0, one, zero))
-    kept[...] = jnp.concatenate(own, axis=0).astype(bf16)
-    given[...] = jnp.concatenate(other, axis=0).astype(bf16)
-
-
-def outer_kernel(share, right_dim, core, left, right, kept, given):
-    divide(dot(left[...], right[...], 0, right_dim), share, core[0], kept, given)
-
-
-def outer_halves(core, left, right, right_dim, parts):
+def divide(total, run, levels, near, marks, orders, outs):
+    chunks = [total[at : at + run] for at in range(0, total.shape[0], run)]
+    bits = [("narrow", i) for i in range(near)] + [("wide", i) for i in range(levels + 1)]
+    for place, (axis, position) in enumerate(bits):
+        mine = (marks[1 if axis == "narrow" else 0] >> position) & 1
+        chunks = [
+            jnp.where(mine == 1, chunks[k ^ (1 << place)], chunks[k]) for k in range(len(chunks))
+        ]
+    cut = run // len(orders)
+    for i, order in enumerate(orders):
+        for k, chunk in enumerate(chunks):
+            value = {bit: (k >> place) & 1 for place, bit in enumerate(bits)}
+            out = outs[2 * i + value["wide", 0]]
+            index = tuple(value.get(bit, 0) for bit in order)
+            out[index] = chunk[i * cut : (i + 1) * cut].astype(bf16)
+
+
+def divided(orders, levels, run, height, wide, width):
+    cut = run // len(orders)
+    specs, shapes = [], []
+    for order in orders:
+
+        def held(bit):
+            return bit[0] == "narrow" or bit[1] <= levels
+
+        def index(j, i, marks, order=order):
+            relative = i ^ (marks[0] >> (levels + 1))
+            at = [0 if held(bit) else (relative >> (bit[1] - 1 - levels)) & 1 for bit in order]
+            return (*at, 0, j)
+
+        block = tuple(2 if held(bit) else 1 for bit in order) + (cut, wide)
+        specs += [pl.BlockSpec(block, index)] * 2
+        shapes += [jax.ShapeDtypeStruct((2,) * len(order) + (cut, width), bf16)] * 2
+    return specs, shapes
+
+
+def outer_kernel(run, levels, near, orders, right_dim, marks, left, right, *outs):
+    divide(dot(left[...], right[...], 0, right_dim), run, levels, near, marks, orders, outs)
+
+
+def outer_halves(marks, left, right, right_dim, cores, parts, order):
     rows, height = left.shape
     width = right.shape[1 - right_dim]
-    share = height // parts
+    share = height // cores
     high = max(2 * share, min(512, height))
+    levels = (high // (2 * share)).bit_length() - 1
     wide = min(1024, width)
     if right_dim == 0:
-        right_spec = pl.BlockSpec((rows, wide), lambda j, i, core: (0, j))
+        right_spec = pl.BlockSpec((rows, wide), lambda j, i, marks: (0, j))
     else:
-        right_spec = pl.BlockSpec((wide, rows), lambda j, i, core: (j, 0))
-    out_spec = pl.BlockSpec((high // 2, wide), lambda j, i, core: (i, j))
-    out = jax.ShapeDtypeStruct((height // 2, width), bf16)
-    return pl.pallas_call(
-        functools.partial(outer_kernel, share, right_dim),
+        right_spec = pl.BlockSpec((wide, rows), lambda j, i, marks: (j, 0))
+    run = share // parts
+    near = parts.bit_length() - 1
+    specs, shapes = divided([order], levels, run, height, wide, width)
+    halves = pl.pallas_call(
+        functools.partial(outer_kernel, run, levels, near, [order], right_dim),
         grid_spec=pltpu.PrefetchScalarGridSpec(
             num_scalar_prefetch=1,
             grid=(width // wide, height // high),
-            in_specs=[pl.BlockSpec((rows, high), lambda j, i, core: (0, i)), right_spec],
-            out_specs=[out_spec] * 2,
+            in_specs=[pl.BlockSpec((rows, high), lambda j, i, marks: (0, i)), right_spec],
+            out_specs=specs,
         ),
-        out_shape=[out] * 2,
+        out_shape=shapes,
         compiler_params=pltpu.CompilerParams(vmem_limit_bytes=VMEM),
         cost_estimate=pl.CostEstimate(
             flops=2 * rows * height * width, bytes_accessed=1 << 25, transcendentals=0
         ),
         name="outer",
-    )(core, left, right)
+    )(marks, left, right)
+    return [item.reshape(height // 2, width) for item in halves]
 
 
 def mixed_kernel(
-    share, first_far, core, d_own, d_far, normed, far_early, far_late, w, kept, given, bias, sums
+    run, levels, near, orders, first_far, marks, d_own, d_far, normed, normed_far, w, *outs
 ):
-    step = pl.program_id(0)
+    *halves, bias, sums = outs
+    step = pl.program_id(1)
     total = dot(d_own[...], normed[...], 1, 0)
     bias[...] = jnp.sum(d_own[...].astype(f32), axis=1, keepdims=True)
 
@@ -828,7 +815,7 @@
         sums[...] = jnp.zeros(sums.shape, f32)
 
     def finish(value):
-        divide(value, share, core[0], kept, given)
+        divide(value, run, levels, near, marks, orders, halves)
         weights = w[...].astype(f32).T
         sums[0:1, :] += column_sum(weights * value)
         sums[1:2, :] += column_sum(weights * bias[...])
@@ -839,48 +826,45 @@
 
     @pl.when(step >= first_far)
     def _():
-        split = far_early.shape[0]
         bias[...] += jnp.sum(d_far[...].astype(f32), axis=1, keepdims=True)
-        finish(
-            total
-            + dot(d_far[:, :split], far_early[...], 1, 0)
-            + dot(d_far[:, split:], far_late[...], 1, 0)
-        )
-
-
-def mixed_halves(core, d_own, d_far, normed, far_early, far_late, w, parts):
+        finish(total + dot(d_far[...], normed_far[...], 1, 0))
+
+
+def mixed_halves(marks, d_own, d_far, normed, normed_far, w, cores, parts, orders):
     height, rows = d_own.shape
     far = d_far.shape[1]
     width = normed.shape[1]
-    share = height // parts
-    high = 2 * share * max(1, 384 // (2 * share))
+    share = height // cores
+    pairs = max(1, 384 // (2 * share))
+    levels = pairs.bit_length() - 1
+    high = 2 * share * pairs
     first_far = width // high
+    run = share // parts
+    near = parts.bit_length() - 1
 
     def fixed(shape):
-        return pl.BlockSpec(shape, lambda i, core: (0, 0), pipeline_mode=pl.Buffered(1))
-
-    out_spec = pl.BlockSpec((high // 2, width), lambda i, core: (i, 0))
-    out = jax.ShapeDtypeStruct((height // 2, width), bf16)
-    return pl.pallas_call(
-        functools.partial(mixed_kernel, share, first_far),
+        return pl.BlockSpec(shape, lambda j, i, marks: (0, 0), pipeline_mode=pl.Buffered(1))
+
+    specs, shapes = divided(orders, levels, run, height, width, width)
+    *halves, bias, sums = pl.pallas_call(
+        functools.partial(mixed_kernel, run, levels, near, orders, first_far),
         grid_spec=pltpu.PrefetchScalarGridSpec(
             num_scalar_prefetch=1,
-            grid=(height // high,),
+            grid=(1, height // high),
             in_specs=[
-                pl.BlockSpec((high, rows), lambda i, core: (i, 0)),
-                pl.BlockSpec((high, far), lambda i, core: (jnp.maximum(i, first_far), 0)),
+                pl.BlockSpec((high, rows), lambda j, i, marks: (i, 0)),
+                pl.BlockSpec((high, far), lambda j, i, marks: (jnp.maximum(i, first_far), 0)),
                 fixed(normed.shape),
-                fixed(far_early.shape),
-                fixed(far_late.shape),
-                pl.BlockSpec((width, high), lambda i, core: (0, i)),
+                fixed(normed_far.shape),
+                pl.BlockSpec((width, high), lambda j, i, marks: (0, i)),
             ],
-            out_specs=[out_spec] * 2
+            out_specs=specs
             + [
-                pl.BlockSpec((high, 1), lambda i, core: (i, 0)),
-                pl.BlockSpec((2, width), lambda i, core: (0, 0)),
+                pl.BlockSpec((high, 1), lambda j, i, marks: (i, 0)),
+                pl.BlockSpec((2, width), lambda j, i, marks: (0, 0)),
             ],
         ),
-        out_shape=[out] * 2
+        out_shape=shapes
         + [
             jax.ShapeDtypeStruct((height, 1), f32),
             jax.ShapeDtypeStruct((2, width), f32),
@@ -890,7 +874,9 @@
             flops=2 * (rows + far) * height * width, bytes_accessed=1 << 25, transcendentals=0
         ),
         name="mixed",
-    )(core, d_own, d_far, normed, far_early, far_late, w)
+    )(marks, d_own, d_far, normed, normed_far, w)
+    halves = [item.reshape(-1, width) for item in halves]
+    return [halves[i : i + 2] for i in range(0, len(halves), 2)], bias, sums
 
 
 def bit_of(axis, position):
@@ -903,67 +889,101 @@
 
 
 class Halving:
-    def __init__(self, array, bits, order):
-        self.bits = list(bits)
+    def __init__(self, halves, order):
         self.order = list(order)
-        rows = array.shape[0] >> len(bits)
-        self.array = array.reshape((2,) * len(bits) + (rows, array.shape[1]))
-
-    def split(self):
-        self.bit = self.order.pop(0)
-        at = self.bits.index(self.bit)
-        self.mine = bit_of(*self.bit)
-        self.away = lax.dynamic_index_in_dim(self.array, 1 - self.mine, at, False)
-        self.at = at
-        self.bits.pop(at)
-
-    def send(self):
-        self.received = swap(self.away, *self.bit)
-
-    def add(self):
-        kept = lax.dynamic_index_in_dim(self.array, self.mine, self.at, False).astype(f32)
-        total = kept + self.received.astype(f32)
-        self.array = total.astype(bf16) if self.bits else total
-
-
-class Crossing(Halving):
-    def __init__(self, halves, bits, order):
         kept, given = halves
-        super().__init__(kept, bits, order)
-        self.received = swap(given, "wide", 0).reshape(self.array.shape)
-
-    def add(self):
-        if hasattr(self, "bit"):
-            super().add()
-        else:
-            total = self.array.astype(f32) + self.received.astype(f32)
-            self.array = total.astype(bf16)
+        self.terms = [kept, swap(given, "wide", 0)]
+
+    def send(self, array, away):
+        self.terms = [array, swap(away, *self.order.pop(0))]
 
 
 class Adding:
     def __init__(self, array, order):
-        self.array, self.order = array, list(order)
-
-    def split(self):
-        self.bit = self.order.pop(0)
-        self.away = self.array
-
-    def send(self):
-        self.received = swap(self.away, *self.bit)
-
-    def add(self):
-        self.array = self.array + self.received
-
-
-def launch(lead, sums, *others):
-    for item in sums:
-        item.split()
-    held = (lead, others, [(item.array, item.away) for item in sums])
-    lead, others, arrays = lax.optimization_barrier(held)
-    for item, (array, away) in zip(sums, arrays):
-        item.array, item.away = array, away
-        item.send()
+        self.order = list(order)
+        self.terms = [array, swap(array, *self.order.pop(0))]
+
+    def send(self, total):
+        self.terms = [total, swap(total, *self.order.pop(0))]
+
+
+def halve_kernel(count, *refs):
+    ins, outs = refs[: 4 * count + 2], refs[4 * count + 2 :]
+    for i in range(count):
+        one, two = ins[4 * i : 4 * i + 2], ins[4 * i + 2 : 4 * i + 4]
+        for half in range(2):
+            total = one[half][0].astype(f32) + two[half][0].astype(f32)
+            outs[2 * i + half][...] = total.astype(bf16)
+    outs[-1][...] = ins[-2][...] + ins[-1][...]
+
+
+def halve(sums, small):
+    heights = [item.terms[0].shape[0] // 2 for item in sums]
+    grid = 4 if all(height % 64 == 0 for height in heights) else 1
+    operands, in_specs, out_specs, out_shape = [], [], [], []
+    for item, height in zip(sums, heights):
+        width = item.terms[0].shape[1]
+        block = (height // grid, width)
+        for term in item.terms:
+            for half in range(2):
+                operands.append(term.reshape(2, height, width))
+                in_specs.append(pl.BlockSpec((1, *block), lambda i, half=half: (half, i, 0)))
+        out_specs += [pl.BlockSpec(block, lambda i: (i, 0))] * 2
+        out_shape += [jax.ShapeDtypeStruct((height, width), bf16)] * 2
+    whole_small = pl.BlockSpec(small.terms[0].shape, lambda i: (0, 0))
+    return pl.pallas_call(
+        functools.partial(halve_kernel, len(sums)),
+        grid=(grid,),
+        in_specs=in_specs + [whole_small] * 2,
+        out_specs=out_specs + [whole_small],
+        out_shape=out_shape + [jax.ShapeDtypeStruct(small.terms[0].shape, f32)],
+        compiler_params=pltpu.CompilerParams(vmem_limit_bytes=VMEM),
+        name="halve",
+    )(*operands, *small.terms)
+
+
+def launch(lead, sums, small, *others):
+    lead, others, halves = lax.optimization_barrier((lead, others, halve(sums, small)))
+    for i, item in enumerate(sums):
+        item.send(halves[2 * i], halves[2 * i + 1])
+    small.send(halves[-1])
     return (lead, *others)
+
+
+def settle(lead, sums, small):
+    everything = sums + [small]
+    lead, terms = lax.optimization_barrier((lead, [item.terms for item in everything]))
+    for item, arrays in zip(everything, terms):
+        item.terms = list(arrays)
+    return lead
+
+
+def collect_kernel(groups, *refs):
+    at = 0
+    for out, count in zip(refs[-len(groups) :], groups):
+        parts = [
+            refs[at + 2 * i][...].astype(f32) + refs[at + 2 * i + 1][...].astype(f32)
+            for i in range(count)
+        ]
+        at += 2 * count
+        height = parts[0].shape[0]
+        for i, part in enumerate(parts):
+            out[i * height : (i + 1) * height, :] = part
+
+
+def collect(groups):
+    operands = [term for group in groups for item in group for term in item.terms]
+    return pl.pallas_call(
+        functools.partial(collect_kernel, [len(group) for group in groups]),
+        out_shape=[
+            jax.ShapeDtypeStruct(
+                (sum(item.terms[0].shape[0] for item in group), group[0].terms[0].shape[1]), f32
+            )
+            for group in groups
+        ],
+        compiler_params=pltpu.CompilerParams(vmem_limit_bytes=VMEM),
+        name="collect",
+    )(*operands)
 
 
 def angles(positions):
@@ -1002,48 +1022,44 @@
     width = inputs.shape[4]
     parts = lax.axis_size("narrow")
     place = lax.axis_index("narrow")
+    cores = lax.axis_size("wide")
     others = parts - 1
     rows = 2 * group
-    far_rows = others * group
     offsets = jnp.arange(group, dtype=jnp.int32)
 
-    own_blocks = inputs.reshape(2, group, width)
-    far_early, far_late = [], []
-    for shift in range(1, parts):
-        pairs = [((n + shift) % parts, n) for n in range(parts)]
-        far_early.append(lax.ppermute(own_blocks[0], "narrow", pairs))
-    for shift in range(1, parts):
-        pairs = [((n + shift) % parts, n) for n in range(parts)]
-        later = [(source, n) for source, n in pairs if source > n]
-        far_late.append(lax.ppermute(own_blocks[1], "narrow", later))
+    def row(vector):
+        return vector[None, :]
+
+    def positions(owners):
+        starts = jnp.stack([owners, 2 * parts - 1 - owners], axis=1).reshape(-1) * group
+        return (starts[:, None] + offsets[None]).reshape(-1)
+
+    def joined(items):
+        return jnp.concatenate(items, axis=0) if len(items) > 1 else items[0]
+
+    tokens = inputs.reshape(rows, width)
+    far_tokens = joined(
+        [
+            lax.ppermute(tokens, "narrow", [((n + shift) % parts, n) for n in range(parts)])
+            for shift in range(1, parts)
+        ]
+    )
     other = (place + 1 + jnp.arange(others, dtype=jnp.int32)) % parts
-
     early_at = place * group
     late_at = (2 * parts - 1 - place) * group
     info = jnp.stack([place, lengths[0], early_at, late_at]).astype(jnp.int32)
-    core = bit_of("wide", 0).astype(jnp.int32)[None]
-    starts = jnp.stack([early_at, late_at])
-    turns = angles((starts[:, None] + offsets[None]).reshape(-1))
-    starts = jnp.concatenate([other, 2 * parts - 1 - other]) * group
-    turns_far = angles((starts[:, None] + offsets[None]).reshape(-1))
-
-    def row(vector):
-        return vector[None, :]
+    marks = jnp.stack([lax.axis_index("wide"), place]).astype(jnp.int32)
+    turns = angles(positions(place[None]))
+    turns_far = angles(positions(other))
 
     norm_one = [row(gain_one), row(shift_one)]
     b_column = b_qkv[:, None]
-    tokens = own_blocks.reshape(rows, width)
     normed, qT, kT, vT = project(tokens, w_qkv, b_column, *norm_one, *turns, (0, 1, 2))
     state = attend_local(info, qT, kT, vT, group)
-
-    def far_keys(blocks, start):
-        far = jnp.concatenate(blocks, axis=0) if others > 1 else blocks[0]
-        return project(far, w_qkv, b_column, *norm_one, *turns_far, (1, 2), start)
-
-    normed_fe, kT_fe, vT_fe = far_keys(far_early, 0)
-    state = attend_remote(info, qT, kT_fe, vT_fe, state, group, parts, 0, False)
-    normed_fl, kT_fl, vT_fl = far_keys(far_late, far_rows)
-    oT, lse, _ = attend_remote(info, qT, kT_fl, vT_fl, state, group, parts, 1, True)
+    normed_far, kT_far, vT_far = project(
+        far_tokens, w_qkv, b_column, *norm_one, *turns_far, (1, 2)
+    )
+    oT, lse = attend_remote(info, qT, kT_far, vT_far, state, group, parts)
 
     blocks = block_call(
         oT,
@@ -1058,37 +1074,33 @@
 
     wide_bits = axis_bits("wide")
     narrow_bits = axis_bits("narrow")
-    devices = 1 << (len(wide_bits) + len(narrow_bits))
-    cores = lax.axis_size("wide")
-    bits = wide_bits[:0:-1] + narrow_bits[::-1]
     first_order = wide_bits[1:2] + narrow_bits + wide_bits[2:]
     second_order = narrow_bits + wide_bits[1:]
-
-    sum_down = Crossing(outer_halves(core, d_outer, hidden, 0, cores), bits, second_order)
-    sum_up = Crossing(outer_halves(core, d_inner, normed_two, 0, cores), bits, first_order)
-    sum_out = Crossing(outer_halves(core, d_branch, oT, 1, cores), bits, first_order)
-    early = Adding(jnp.concatenate([small.reshape(-1), small_up.reshape(-1)]), wide_bits[:1] + first_order)
-    early.split()
-    early.send()
-    sums = [sum_down, sum_up, sum_out, early]
-
-    def advance(lead, *others):
-        for item in sums:
-            item.add()
-        return launch(lead, sums, *others)
+    third_order = narrow_bits + wide_bits[2:3] + wide_bits[1:2] + wide_bits[3:]
+    fourth_order = wide_bits[2:3] + wide_bits[1:2] + narrow_bits + wide_bits[3:]
+    small_order = wide_bits[:1] + first_order
+
+    def outer(left, right, right_dim, order):
+        return Halving(outer_halves(marks, left, right, right_dim, cores, parts, order), order)
+
+    sum_up = outer(d_inner, normed_two, 0, first_order)
+    sum_down = outer(d_outer, hidden, 0, second_order)
+    sum_out = outer(d_branch, oT, 1, first_order)
+    flat = jnp.concatenate([small.reshape(-1), small_up.reshape(-1)])
+    early = Adding(flat.reshape(-1, PAIR), small_order)
+    sums = [sum_down, sum_up, sum_out]
 
     heads = width // PAIR
     portions = 2 if heads % 2 == 0 else 1
     count = heads // portions
-    keys_far = [kT_fe, vT_fe, kT_fl, vT_fl]
     far = []
     for portion in range(portions):
-        (doT,) = advance(doT)
+        (doT,) = launch(doT, sums, early)
         far = back_remote(
             info,
             [qT, doT, oT, lse],
             turns_far,
-            keys_far,
+            [kT_far, vT_far],
             group,
             parts,
             portion * count,
@@ -1096,27 +1108,19 @@
             far,
         )
     dq_far, d_far = far
-    d_early = unproject(d_far, w_qkv, (1, 2), 0, far_rows)
-    d_late = unproject(d_far, w_qkv, (1, 2), far_rows, far_rows)
-
-    def give_back(d_early, d_late):
-        early_blocks, late_blocks = [], []
-        for j in range(others):
-            pairs = [(n, (n + j + 1) % parts) for n in range(parts)]
-            piece = d_early[j * group : (j + 1) * group]
-            early_blocks.append(lax.ppermute(piece, "narrow", pairs))
-        for j in range(others):
-            pairs = [(n, (n + j + 1) % parts) for n in range(parts)]
-            later = [(n, owner) for n, owner in pairs if owner > n]
-            piece = d_late[j * group : (j + 1) * group]
-            late_blocks.append(lax.ppermute(piece, "narrow", later))
-        return early_blocks, late_blocks
-
+    d_back = unproject(d_far, w_qkv, (1, 2), 0, others * rows)
     d_mixed = []
     for portion in range(portions):
-        doT, d_early, d_late = advance(doT, d_early, d_late)
+        doT, d_back = launch(doT, sums, early, d_back)
         if not portion:
-            returned_early, returned_late = give_back(d_early, d_late)
+            returned = [
+                lax.ppermute(
+                    d_back[j * rows : (j + 1) * rows] if others > 1 else d_back,
+                    "narrow",
+                    [(n, (n + j + 1) % parts) for n in range(parts)],
+                )
+                for j in range(others)
+            ]
         d_mixed = [
             back_local(
                 info,
@@ -1131,76 +1135,56 @@
             )
         ]
     d_mixed = d_mixed[0]
-    while sum_down.order:
-        (d_mixed,) = advance(d_mixed)
-    for item in sums:
-        item.add()
-
-    kept, given, bias, weighted = mixed_halves(
-        core,
+    while early.order:
+        (d_mixed,) = launch(d_mixed, sums, early)
+    d_mixed = settle(d_mixed, sums, early)
+    d_mixed, returned = lax.optimization_barrier((d_mixed, returned))
+    if others > 1:
+        returned = [functools.reduce(jnp.add, [item.astype(f32) for item in returned])]
+
+    orders = [first_order, third_order, fourth_order]
+    pieces, bias, weighted = mixed_halves(
+        marks,
         d_mixed.reshape(3 * width, rows),
         d_far.reshape(3 * width, -1),
         normed,
-        normed_fe,
-        normed_fl,
+        normed_far,
         w_qkv,
         cores,
+        parts,
+        orders,
     )
-    crossing = Crossing((kept, given), bits, [])
+    pieces = [Halving(halves, order) for halves, order in zip(pieces, orders)]
     part_shift = weighted[1]
     part_gain = (weighted[0] - shift_one * part_shift) / gain_one
-    late = Adding(
-        jnp.concatenate([bias.reshape(-1), part_gain, part_shift]), wide_bits[:1] + first_order
-    )
-    late.split()
-    late.send()
-    crossing.add()
-    late.add()
-    share = 3 * width // devices
-    third_order = wide_bits[2:3] + wide_bits[1:2] + narrow_bits + wide_bits[3:]
-    orders = [first_order, narrow_bits + wide_bits[2:3] + wide_bits[1:2] + wide_bits[3:], third_order]
-    runs = crossing.array.reshape(-1, share, width)
-    cut = share // 3
-    pieces = [
-        Halving(runs[:, i * cut : (i + 1) * cut].reshape(-1, width), bits, order)
-        for i, order in enumerate(orders)
-    ]
-    sums = pieces + [late]
-    (d_mixed,) = launch(d_mixed, sums)
-    back_early = functools.reduce(jnp.add, [item.astype(f32) for item in returned_early])
-    back_late = functools.reduce(jnp.add, [item.astype(f32) for item in returned_late])
-    if others == 1:
-        back_early, back_late = returned_early[0], returned_late[0]
+    flat = jnp.concatenate([bias.reshape(-1), part_gain, part_shift])
+    late = Adding(flat.reshape(-1, PAIR), small_order)
+    sum_w_down, sum_w_up, sum_w_out = collect([[item] for item in sums])
+    (d_mixed,) = launch(d_mixed, pieces, late)
     d_tokens = []
-    for i, returned in enumerate((back_early, back_late)):
-        finish = (returned, tokens, d_middle, row(gain_one))
+    for i in range(2):
+        finish = (returned[0], tokens, d_middle, row(gain_one))
         d_tokens = [
             unproject(d_mixed, w_qkv, (0, 1, 2), i * group, group, finish, d_tokens)
         ]
-        for item in sums:
-            item.add()
         if late.order:
-            d_mixed, d_tokens[0] = launch(d_mixed, sums, d_tokens[0])
+            d_mixed, d_tokens[0] = launch(d_mixed, pieces, late, d_tokens[0])
     while late.order:
-        for item in sums:
-            item.add()
-        (d_tokens[0],) = launch(d_tokens[0], sums)
-    for item in sums:
-        item.add()
-
-    qkv_rows = jnp.concatenate([item.array for item in pieces], axis=0)
-    down_rows = sum_down.array
-    small = early.array[: 8 * width].reshape(8, width)
-    small_up = early.array[8 * width :]
-    late_small = late.array
+        (d_tokens[0],) = launch(d_tokens[0], pieces, late)
+
+    (sum_w_qkv,) = collect([pieces])
+    early_small = (early.terms[0] + early.terms[1]).reshape(-1)
+    small = early_small[: 8 * width].reshape(8, width)
+    small_up = early_small[8 * width :]
+    late_small = (late.terms[0] + late.terms[1]).reshape(-1)
     shape = inputs.shape
     return (
         result.reshape(shape),
         d_tokens[0].reshape(shape),
-        qkv_rows.T,
-        sum_out.array.T,
-        sum_up.array.T,
-        down_rows.T,
+        sum_w_qkv.T,
+        sum_w_out.T,
+        sum_w_up.T,
+        sum_w_down.T,
         late_small[: 3 * width],
         small[7],
         small_up,

time: 894 us -> 772 us (0.86)
  starting transfers between devices: 204 us -> 45 us
  Pallas kernels: 535 us -> 676 us
  other arithmetic: 47.1 us -> 6.86 us
  waiting for transfers between devices: 54.9 us -> 20.4 us
  local copies, waits for them, and re-layouts: 39.6 us -> 14.5 us
    ppermute x38 -> x40, starting transfers between devices: 195 us -> 40 us  [swap(): lax.ppermute(values, axis, [(i, i ^ 1 << position) for i in range(size)])]
    pallas_call x4 -> x14, Pallas kernels: 91.3 us -> 141 us  [the longest x3 61.6 us: outer_halves(): pl.pallas_call(functools.partial(outer_kernel, run, levels, near, [order]...]
    pallas_call x2, Pallas kernels: 56.9 us -> 97.1 us  [back_remote(): return call(info, *operands, *turns, *keys, *before)]
    convert_element_type x22 -> x0, other arithmetic: 35.2 us -> none  [the longest x18 20.8 us: add(): self.array = total.astype(bf16) if self.bits else total]
    ppermute x38 -> x40, waiting for transfers between devices: 54.9 us -> 20.4 us  [swap(): lax.ppermute(values, axis, [(i, i ^ 1 << position) for i in range(size)])]
    pallas_call x2, Pallas kernels: 87.9 us -> 117 us  [back_local(): return call(info, *operands, *turns, *keys, dq, *before)]
    pallas_call x1, Pallas kernels: 46.8 us -> 63.5 us  [attend_local(): return call(info, qT, kT, vT)]
    squeeze x24 -> x1, local copies, waits for them, and re-layouts: 17.2 us -> 0.62 us  [body(): small[1]]
  transfers between devices with their start and end apart: 42 -> 42, of which waited for: 14 -> 11; matrix products, arithmetic and copies ran while one was open for 7% -> 2% of each run, Pallas kernels for 34% -> 50%
where the time goes in v3:
time: 772 us; the launch traced here: 765 us
  Pallas kernels  676 us (88%)
  starting transfers between devices  45 us (6%)
  waiting for transfers between devices  20.4 us (3%)
  local copies, waits for them, and re-layouts  14.5 us (2%)
    pallas_call x2, Pallas kernels, back_local(): return call(info, *operands, *turns, *keys, dq, *before)  117 us
    pallas_call x1, Pallas kernels, block_call(): pl.pallas_call(functools.partial(block_kernel, span), grid=(rows // step,...  116 us
    pallas_call x2, Pallas kernels, back_remote(): return call(info, *operands, *turns, *keys, *before)  97.1 us
    pallas_call x1, Pallas kernels, attend_local(): return call(info, qT, kT, vT)  63.5 us
    pallas_call x3, Pallas kernels, outer_halves(): pl.pallas_call(functools.partial(outer_kernel, run, levels, near, [order]...  61.6 us
    pallas_call x1, Pallas kernels, attend_remote(): return call(info, qT, kT, vT, *state)  59.7 us
    pallas_call x3, Pallas kernels, unproject(): pl.pallas_call(functools.partial(unproject_kernel, planes, bool(finish)),...  42.8 us
    ppermute x40, starting transfers between devices, swap(): lax.ppermute(values, axis, [(i, i ^ 1 << position) for i in range(size)])  40 us
  transfers between devices with their start and end apart: 42, of which 11 were waited for; matrix products, arithmetic and copies ran while one was open for 2% of the time, Pallas kernels for 50%

profile of v3, /device:TPU:0, one launch (start us, length us, event | category | flops | bytes accessed | tf_op | source)
XLA Modules:
  0.0 765.1 jit_solution(3669407117301037456)
XLA Ops:
  0.7 3.0 collective-permute-start
  8.2 2.7 multiply_sine_fusion
  10.9 21.7 %project.2 = (bf16[2048,1024]{1,0:T(8,128)(2,1)}, bf16[1024,2048]{1,0:T(8,128)(2,1)}, bf16[1024,2048]{1,0:T(8,128)(2,1)}, bf16[1024,2048]{1,0:T(8,128)(2,1)}) custom-call(bf16[2048,1024]{1,0:T(8,128)(2,1)} %bitcast.139, bf16[1024,3072]{1,0:T(8,128)(2,1)} %refs_3_.3, f32[3072,1]{1,0:T(8,128)} %copy.44.b, f32[1,1024]{1,0:T(1,128)} %bitcast.229, ...), custom_call_target="tpu_custom_call" | custom-call | flops 12884901888 | bytes 16777216 | tf_op jit(solution)/shard_map/project/pallas_call | solution.py:664
  32.6 63.5 %attend_local.1 = (f32[1024,2048]{1,0:T(8,128)}, f32[8,2,2048]{2,1,0:T(2,128)}, f32[8,2,2048]{2,1,0:T(2,128)}) custom-call(s32[4]{0:T(128)} %pad_add_fusion.info, bf16[1024,2048]{1,0:T(8,128)(2,1)} %get-tuple-element.194.qT, bf16[1024,2048]{1,0:T(8,128)(2,1)} %get-tuple-element.197.kT, bf16[1024,2048]{1,0:T(8,128)(2,1)} %get-tuple-element.198.vT), custom_call_target="tpu_custom_call" | custom-call | flops 34359738368 | bytes 33554432 | tf_op jit(solution)/shard_map/attend_local/pallas_call | solution.py:391
  96.1 17.3 %project.3 = (bf16[2048,1024]{1,0:T(8,128)(2,1)}, bf16[1024,2048]{1,0:T(8,128)(2,1)}, bf16[1024,2048]{1,0:T(8,128)(2,1)}) custom-call(bf16[2048,1024]{1,0:T(8,128)(2,1)} %collective-permute-done.tokens, bf16[1024,3072]{1,0:T(8,128)(2,1)} %refs_3_.3, f32[3072,1]{1,0:T(8,128)} %copy.44.b, f32[1,1024]{1,0:T(1,128)} %bitcast.230, f32[1,1024]{1,0:T(1,128)} %bitcast.240, ...), custom_call_target="tpu_custom_call" | custom-call | flops 8589934592 | bytes 16777216 | tf_op jit(solution)/shard_map/project/pallas_call | solution.py:664
  113.4 59.7 %attend_remote.1 = (bf16[1024,2048]{1,0:T(8,128)(2,1)}, f32[8,2,2048]{2,1,0:T(2,128)}) custom-call(s32[4]{0:T(128)} %pad_add_fusion.info, bf16[1024,2048]{1,0:T(8,128)(2,1)} %get-tuple-element.194.qT, bf16[1024,2048]{1,0:T(8,128)(2,1)} %get-tuple-element.195.kT, bf16[1024,2048]{1,0:T(8,128)(2,1)} %get-tuple-element.196.vT, ...), custom_call_target="tpu_custom_call" | custom-call | flops 34359738368 | bytes 33554432 | tf_op jit(solution)/shard_map/attend_remote/pallas_call | solution.py:411
  173.1 116.2 %block.1 = (bf16[2048,1024]{1,0:T(8,128)(2,1)}, f32[2048,1024]{1,0:T(8,128)}, bf16[2048,4096]{1,0:T(8,128)(2,1)}, bf16[2048,1024]{1,0:T(8,128)(2,1)}, bf16[2048,...) custom-call(bf16[1024,2048]{1,0:T(8,128)(2,1)} %get-tuple-element.20, ...), custom_call_target="tpu_custom_call" | custom-call | flops 77309411328 | bytes 67108864 | tf_op jit(solution)/shard_map/block/pallas_call | solution.py:599
  289.3 27.1 %outer.3 = (bf16[2,2,2,2,32,4096]{5,4,3,2,1,0:T(8,128)(2,1)}, bf16[2,2,2,2,32,4096]{5,4,3,2,1,0:T(8,128)(2,1)}) custom-call(s32[2]{0:T(128)} %pad_add_fusion.1.marks, bf16[2048,1024]{1,0:T(8,128)(2,1)} %get-tuple-element.205.left, bf16[2048,4096]{1,0:T(8,128)(2,1)} %get-tuple-element.206.right), custom_call_target="tpu_custom_call" | custom-call | flops 17179869184 | bytes 33554432 | tf_op jit(solution)/shard_map/outer/pallas_call | solution.py:787
  316.4 24.5 %outer.4 = (bf16[2,2,2,2,128,1024]{5,4,3,2,1,0:T(8,128)(2,1)}, bf16[2,2,2,2,128,1024]{5,4,3,2,1,0:T(8,128)(2,1)}) custom-call(s32[2]{0:T(128)} %pad_add_fusion.1.marks, bf16[2048,4096]{1,0:T(8,128)(2,1)} %get-tuple-element.209.left, bf16[2048,1024]{1,0:T(8,128)(2,1)} %get-tuple-element.210.right), custom_call_target="tpu_custom_call" | custom-call | flops 17179869184 | bytes 33554432 | tf_op jit(solution)/shard_map/outer/pallas_call | solution.py:787
  341.5 9.9 %outer.5 = (bf16[2,2,2,2,32,1024]{5,4,3,2,1,0:T(8,128)(2,1)}, bf16[2,2,2,2,32,1024]{5,4,3,2,1,0:T(8,128)(2,1)}) custom-call(s32[2]{0:T(128)} %pad_add_fusion.1.marks, bf16[2048,1024]{1,0:T(8,128)(2,1)} %get-tuple-element.213.left, bf16[1024,2048]{1,0:T(8,128)(2,1)} %get-tuple-element.202.oT.right), custom_call_target="tpu_custom_call" | custom-call | flops 4294967296 | bytes 33554432 | tf_op jit(solution)/shard_map/outer/pallas_call | solution.py:787
  355.3 10.8 %halve.8 = (bf16[256,4096]{1,0:T(8,128)(2,1)}, bf16[256,4096]{1,0:T(8,128)(2,1)}, bf16[1024,1024]{1,0:T(8,128)(2,1)}, bf16[1024,1024]{1,0:T(8,128)(2,1)}, bf16[2...) custom-call(bf16[2,256,4096]{2,1,0:T(8,128)(2,1)} %bitcast.144, ...), custom_call_target="tpu_custom_call" | custom-call | tf_op jit(solution)/shard_map/halve/pallas_call | solution.py:934
  369.8 48.5 %back_remote.2 = (f32[1024,2048]{1,0:T(8,128)}, bf16[3,1024,2048]{2,1,0:T(8,128)(2,1)}) custom-call(s32[4]{0:T(128)} %pad_add_fusion.info, bf16[1024,2048]{1,0:T(8,128)(2,1)} %get-tuple-element.194.qT, bf16[1024,2048]{1,0:T(8,128)(2,1)} %get-tuple-element.275.doT, bf16[1024,2048]{1,0:T(8,128)(2,1)} %get-tuple-element.202.oT.right, ...), custom_call_target="tpu_custom_call" | custom-call | flops 42949672960 | bytes 33554432 | tf_op jit(solution)/shard_map/back_remote/pallas_call | solution.py:447
  418.4 8.1 %collective-permute-done.6 = bf16[1024,1024]{1,0:T(8,128)(2,1)} collective-permute-done((bf16[1024,1024]{1,0:T(8,128)(2,1)}, bf16[1024,1024]{1,0:T(8,128)(2,1)}, u32[]{:S(2)}, u32[]{:S(2)}) %collective-permute-start.6) | collective-permute-done | bytes 2097184 | tf_op jit(solution)/shard_map/ppermute | solution.py:888
  426.5 6.6 halve.9
  436.7 48.6 %back_remote.3 = (f32[1024,2048]{1,0:T(8,128)}, bf16[3,1024,2048]{2,1,0:T(8,128)(2,1)}) custom-call(s32[4]{0:T(128)} %pad_add_fusion.info, bf16[1024,2048]{1,0:T(8,128)(2,1)} %get-tuple-element.194.qT, bf16[1024,2048]{1,0:T(8,128)(2,1)} %get-tuple-element.275.doT, ...), custom_call_target="tpu_custom_call", output_to_operand_aliasing={{0}: (9, {}), {1}: (10, {})} | custom-call | flops 42949672960 | bytes 33554432 | tf_op jit(solution)/shard_map/back_remote/pallas_call | solution.py:447
  485.3 14.7 %unproject.3 = bf16[2048,1024]{1,0:T(8,128)(2,1)} custom-call(bf16[3,1024,2048]{2,1,0:T(8,128)(2,1)} %get-tuple-element.244.refs_0_.refs_1_, bf16[3,1024,2048]{2,1,0:T(8,128)(2,1)} %get-tuple-element.244.refs_0_.refs_1_, bf16[1024,3072]{1,0:T(8,128)(2,1)} %refs_3_.3), custom_call_target="tpu_custom_call" | custom-call | flops 8589934592 | bytes 16777216 | tf_op jit(solution)/shard_map/unproject/pallas_call | solution.py:713
  501.1 4.6 halve.10
  505.7 3.1 collective-permute-start.16
  512.8 58.6 %back_local.2.rest_0_ = bf16[3,1024,2048]{2,1,0:T(8,128)(2,1)} custom-call(s32[4]{0:T(128)} %pad_add_fusion.info, bf16[1024,2048]{1,0:T(8,128)(2,1)} %get-tuple-element.194.qT, bf16[1024,2048]{1,0:T(8,128)(2,1)} %get-tuple-element.275.doT, bf16[1024,2048]{1,0:T(8,128)(2,1)} %get-tuple-element.202.oT.right, f32[8,2,2048]{2,1,0:T(2,128)} %get-tuple-element.241.lse, ...), custom_call_target="tpu_custom_call" | custom-call | flops 42949672960 | bytes 33554432 | tf_op jit(solution)/shard_map/back_local/pallas_call | solution.py:469
  572.5 2.6 halve.11
  575.1 4.0 collective-permute-start.20
  579.2 2.8 collective-permute-start.17
  582.1 58.3 %back_local.3.refs_0_.refs_1_.refs_2_ = bf16[3,1024,2048]{2,1,0:T(8,128)(2,1)} custom-call(s32[4]{0:T(128)} %pad_add_fusion.info, bf16[1024,2048]{1,0:T(8,128)(2,1)} %get-tuple-element.194.qT, bf16[1024,2048]{1,0:T(8,128)(2,1)} %get-tuple-element.275.doT, bf16[1024,2048]{1,0:T(8,128)(2,1)} %get-tuple-element.202.oT.right, ...), custom_call_target="tpu_custom_call", output_to_operand_aliasing={{}: (10, {})} | custom-call | flops 42949672960 | bytes 33554432 | tf_op jit(solution)/shard_map/back_local/pallas_call | solution.py:469
  640.5 36.6 %mixed.1 = (bf16[2,2,2,2,32,1024]{5,4,3,2,1,0:T(8,128)(2,1)}, bf16[2,2,2,2,32,1024]{5,4,3,2,1,0:T(8,128)(2,1)}, bf16[2,2,2,2,32,1024]{5,4,3,2,1,0:T(8,128)(2,1)}...) custom-call(s32[2]{0:T(128)} %pad_add_fusion.1.marks, ...), custom_call_target="tpu_custom_call" | custom-call | flops 25769803776 | bytes 33554432 | tf_op jit(solution)/shard_map/mixed/pallas_call | solution.py:849
  683.9 5.0 halve.12
  694.8 14.1 %unproject.4.refs_8_ = bf16[2048,1024]{1,0:T(8,128)(2,1)} custom-call(bf16[3,1024,2048]{2,1,0:T(8,128)(2,1)} %back_local.3.refs_0_.refs_1_.refs_2_, bf16[3,1024,2048]{2,1,0:T(8,128)(2,1)} %back_local.3.refs_0_.refs_1_.refs_2_, bf16[3,1024,2048]{2,1,0:T(8,128)(2,1)} %back_local.3.refs_0_.refs_1_.refs_2_, bf16[1024,3072]{1,0:T(8,128)(2,1)} %refs_3_.3, ...), custom_call_target="tpu_custom_call" | custom-call | flops 6442450944 | bytes 16777216 | tf_op jit(solution)/shard_map/unproject/pallas_call | solution.py:713
  710.1 3.8 halve.13
  716.8 14.1 %unproject.5 = bf16[2048,1024]{1,0:T(8,128)(2,1)} custom-call(bf16[3,1024,2048]{2,1,0:T(8,128)(2,1)} %back_local.3.refs_0_.refs_1_.refs_2_, bf16[3,1024,2048]{2,1,0:T(8,128)(2,1)} %back_local.3.refs_0_.refs_1_.refs_2_, bf16[3,1024,2048]{2,1,0:T(8,128)(2,1)} %back_local.3.refs_0_.refs_1_.refs_2_, ...), custom_call_target="tpu_custom_call", output_to_operand_aliasing={{}: (8, {})} | custom-call | flops 6442450944 | bytes 16777216 | tf_op jit(solution)/shard_map/unproject/pallas_call | solution.py:713
  731.7 3.3 halve.14
  739.3 3.0 collective-permute-done.34
  746.3 2.9 collective-permute-start.41
  754.2 2.9 collective-permute-start.39
  (177 shorter events, 60.2 us)
Async XLA Ops:
  0.7 95.5 %collective-permute-start = (bf16[2048,1024]{1,0:T(8,128)(2,1)}, bf16[2048,1024]{1,0:T(8,128)(2,1)}, u32[]{:S(2)}, u32[]{:S(2)}) collective-permute-start(bf16[2048,1024]{1,0:T(8,128)(2,1)} %bitcast.138), channel_id=1, source_target_pairs={{1,0},{0,1},{3,2},{2,3},{5,4},{4,5},{7,6},{6,7},{9,8},{8,9},{11,10... | collective-permute-start | bytes 12582920 | tf_op jit(solution)/shard_map/ppermute | solution.py:1043
  316.4 37.9 %collective-permute-start.1 = (bf16[512,4096]{1,0:T(8,128)(2,1)}, bf16[512,4096]{1,0:T(8,128)(2,1)}, u32[]{:S(2)}, u32[]{:S(2)}) collective-permute-start(bf16[512,4096]{1,0:T(8,128)(2,1)} %bitcast.242), channel_id=1, source_target_pairs={{0,2},{2,0},{4,6},{6,4},{8,10},{10,8},{12,14},{14,12},{16,18},{18,... | collective-permute-start | bytes 12582920 | tf_op jit(solution)/shard_map/ppermute | solution.py:888
  341.0 13.4 %collective-permute-start.2 = (bf16[2048,1024]{1,0:T(8,128)(2,1)}, bf16[2048,1024]{1,0:T(8,128)(2,1)}, u32[]{:S(2)}, u32[]{:S(2)}) collective-permute-start(bf16[2048,1024]{1,0:T(8,128)(2,1)} %bitcast.243), channel_id=1, source_target_pairs={{0,2},{2,0},{4,6},{6,4},{8,10},{10,8},{12,14},{14,12},{16,18},{18,... | collective-permute-start | bytes 12582920 | tf_op jit(solution)/shard_map/ppermute | solution.py:888
  366.1 52.2 %collective-permute-start.8 = (f32[96,128]{1,0:T(8,128)}, f32[96,128]{1,0:T(8,128)S(1)}, u32[]{:S(2)}, u32[]{:S(2)}) collective-permute-start(f32[96,128]{1,0:T(8,128)} %get-tuple-element.232.refs_12_), channel_id=1, source_target_pairs={{0,4},{2,6},{4,0},{6,2},{8,12},{10,14},{12,8},{14,10},{16,20},{18,... | collective-permute-start | bytes 147464 | tf_op jit(solution)/shard_map/ppermute | solution.py:888
  366.8 51.5 %collective-permute-start.7 = (bf16[256,1024]{1,0:T(8,128)(2,1)}, bf16[256,1024]{1,0:T(8,128)(2,1)S(1)}, u32[]{:S(2)}, u32[]{:S(2)}) collective-permute-start(bf16[256,1024]{1,0:T(8,128)(2,1)} %get-tuple-element.231), channel_id=1, source_target_pairs={{0,4},{2,6},{4,0},{6,2},{8,12},{10,14},{12,8},{14,10},{16,20},{18,... | collective-permute-start | bytes 1572872 | tf_op jit(solution)/shard_map/ppermute | solution.py:888
  368.2 50.2 %collective-permute-start.5 = (bf16[256,4096]{1,0:T(8,128)(2,1)}, bf16[256,4096]{1,0:T(8,128)(2,1)}, u32[]{:S(2)}, u32[]{:S(2)}) collective-permute-start(bf16[256,4096]{1,0:T(8,128)(2,1)} %get-tuple-element.227), channel_id=1, source_target_pairs={{0,1},{1,0},{2,3},{3,2},{4,5},{5,4},{6,7},{7,6},{8,9},{9,8},{10,11... | collective-permute-start | bytes 6291464 | tf_op jit(solution)/shard_map/ppermute | solution.py:888
  368.4 58.2 %collective-permute-start.6 = (bf16[1024,1024]{1,0:T(8,128)(2,1)}, bf16[1024,1024]{1,0:T(8,128)(2,1)}, u32[]{:S(2)}, u32[]{:S(2)}) collective-permute-start(bf16[1024,1024]{1,0:T(8,128)(2,1)} %get-tuple-element.229), channel_id=1, source_target_pairs={{0,4},{2,6},{4,0},{6,2},{8,12},{10,14},{12,8},{14,10},{16,20},{18,... | collective-permute-start | bytes 6291464 | tf_op jit(solution)/shard_map/ppermute | solution.py:888
  433.1 66.9 %collective-permute-start.12 = (f32[96,128]{1,0:T(8,128)}, f32[96,128]{1,0:T(8,128)S(1)}, u32[]{:S(2)}, u32[]{:S(2)}) collective-permute-start(f32[96,128]{1,0:T(8,128)} %get-tuple-element.251.refs_12_), channel_id=1, source_target_pairs={{0,1},{1,0},{2,3},{3,2},{4,5},{5,4},{6,7},{7,6},{8,9},{9,8},{10,11... | collective-permute-start | bytes 147464 | tf_op jit(solution)/shard_map/ppermute | solution.py:888
  433.6 66.5 %collective-permute-start.11 = (bf16[128,1024]{1,0:T(8,128)(2,1)}, bf16[128,1024]{1,0:T(8,128)(2,1)S(1)}, u32[]{:S(2)}, u32[]{:S(2)}) collective-permute-start(bf16[128,1024]{1,0:T(8,128)(2,1)} %get-tuple-element.250), channel_id=1, source_target_pairs={{0,1},{1,0},{2,3},{3,2},{4,5},{5,4},{6,7},{7,6},{8,9},{9,8},{10,11... | collective-permute-start | bytes 786440 | tf_op jit(solution)/shard_map/ppermute | solution.py:888
  435.2 64.8 %collective-permute-start.9 = (bf16[128,4096]{1,0:T(8,128)(2,1)}, bf16[128,4096]{1,0:T(8,128)(2,1)S(1)}, u32[]{:S(2)}, u32[]{:S(2)}) collective-permute-start(bf16[128,4096]{1,0:T(8,128)(2,1)} %get-tuple-element.246), channel_id=1, source_target_pairs={{0,4},{2,6},{4,0},{6,2},{8,12},{10,14},{12,8},{14,10},{16,20},{18,... | collective-permute-start | bytes 3145736 | tf_op jit(solution)/shard_map/ppermute | solution.py:888
  436.1 64.0 %collective-permute-start.10 = (bf16[512,1024]{1,0:T(8,128)(2,1)}, bf16[512,1024]{1,0:T(8,128)(2,1)}, u32[]{:S(2)}, u32[]{:S(2)}) collective-permute-start(bf16[512,1024]{1,0:T(8,128)(2,1)} %get-tuple-element.248), channel_id=1, source_target_pairs={{0,1},{1,0},{2,3},{3,2},{4,5},{5,4},{6,7},{7,6},{8,9},{9,8},{10,11... | collective-permute-start | bytes 3145736 | tf_op jit(solution)/shard_map/ppermute | solution.py:888
  505.7 65.8 %collective-permute-start.16 = (f32[96,128]{1,0:T(8,128)}, f32[96,128]{1,0:T(8,128)S(1)}, u32[]{:S(2)}, u32[]{:S(2)}) collective-permute-start(f32[96,128]{1,0:T(8,128)} %get-tuple-element.267.refs_12_), channel_id=1, source_target_pairs={{0,8},{2,10},{4,12},{6,14},{8,0},{10,2},{12,4},{14,6},{16,24},{18,... | collective-permute-start | bytes 147464 | tf_op jit(solution)/shard_map/ppermute | solution.py:888
  508.8 62.7 %collective-permute-start.15 = (bf16[64,1024]{1,0:T(8,128)(2,1)}, bf16[64,1024]{1,0:T(8,128)(2,1)S(1)}, u32[]{:S(2)}, u32[]{:S(2)}) collective-permute-start(bf16[64,1024]{1,0:T(8,128)(2,1)} %get-tuple-element.266), channel_id=1, source_target_pairs={{0,8},{2,10},{4,12},{6,14},{8,0},{10,2},{12,4},{14,6},{16,24},{18,... | collective-permute-start | bytes 393224 | tf_op jit(solution)/shard_map/ppermute | solution.py:888
  508.9 62.6 %collective-permute-start.13 = (bf16[64,4096]{1,0:T(8,128)(2,1)}, bf16[64,4096]{1,0:T(8,128)(2,1)S(1)}, u32[]{:S(2)}, u32[]{:S(2)}) collective-permute-start(bf16[64,4096]{1,0:T(8,128)(2,1)} %get-tuple-element.262), channel_id=1, source_target_pairs={{0,8},{2,10},{4,12},{6,14},{8,0},{10,2},{12,4},{14,6},{16,24},{18,... | collective-permute-start | bytes 1572872 | tf_op jit(solution)/shard_map/ppermute | solution.py:888
  510.8 60.7 %collective-permute-start.14 = (bf16[256,1024]{1,0:T(8,128)(2,1)}, bf16[256,1024]{1,0:T(8,128)(2,1)S(1)}, u32[]{:S(2)}, u32[]{:S(2)}) collective-permute-start(bf16[256,1024]{1,0:T(8,128)(2,1)} %get-tuple-element.264), channel_id=1, source_target_pairs={{0,8},{2,10},{4,12},{6,14},{8,0},{10,2},{12,4},{14,6},{16,24},{18,... | collective-permute-start | bytes 1572872 | tf_op jit(solution)/shard_map/ppermute | solution.py:888
  510.9 129.6 %collective-permute-start.21 = (bf16[2048,1024]{1,0:T(8,128)(2,1)}, bf16[2048,1024]{1,0:T(8,128)(2,1)}, u32[]{:S(2)}, u32[]{:S(2)}) collective-permute-start(bf16[2048,1024]{1,0:T(8,128)(2,1)} %unproject.3), channel_id=1, source_target_pairs={{0,1},{1,0},{2,3},{3,2},{4,5},{5,4},{6,7},{7,6},{8,9},{9,8},{10,11... | collective-permute-start | bytes 12582920 | tf_op jit(solution)/shard_map/ppermute | solution.py:1117
  575.1 65.3 %collective-permute-start.20 = (f32[96,128]{1,0:T(8,128)}, f32[96,128]{1,0:T(8,128)S(1)}, u32[]{:S(2)}, u32[]{:S(2)}) collective-permute-start(f32[96,128]{1,0:T(8,128)} %get-tuple-element.368), channel_id=1, source_target_pairs={{0,16},{2,18},{4,20},{6,22},{8,24},{10,26},{12,28},{14,30},{16,0},... | collective-permute-start | bytes 147464 | tf_op jit(solution)/shard_map/ppermute | solution.py:888
  579.1 61.3 %collective-permute-start.19 = (bf16[32,1024]{1,0:T(8,128)(2,1)}, bf16[32,1024]{1,0:T(8,128)(2,1)S(1)}, u32[]{:S(2)}, u32[]{:S(2)}) collective-permute-start(bf16[32,1024]{1,0:T(8,128)(2,1)} %get-tuple-element.282), channel_id=1, source_target_pairs={{0,16},{2,18},{4,20},{6,22},{8,24},{10,26},{12,28},{14,30},{16,0},... | collective-permute-start | bytes 196616 | tf_op jit(solution)/shard_map/ppermute | solution.py:888
  579.2 61.3 %collective-permute-start.17 = (bf16[32,4096]{1,0:T(8,128)(2,1)}, bf16[32,4096]{1,0:T(8,128)(2,1)S(1)}, u32[]{:S(2)}, u32[]{:S(2)}) collective-permute-start(bf16[32,4096]{1,0:T(8,128)(2,1)} %get-tuple-element.278), channel_id=1, source_target_pairs={{0,16},{2,18},{4,20},{6,22},{8,24},{10,26},{12,28},{14,30},{16,0},... | collective-permute-start | bytes 786440 | tf_op jit(solution)/shard_map/ppermute | solution.py:888
  582.0 58.5 %collective-permute-start.18 = (bf16[128,1024]{1,0:T(8,128)(2,1)}, bf16[128,1024]{1,0:T(8,128)(2,1)S(1)}, u32[]{:S(2)}, u32[]{:S(2)}) collective-permute-start(bf16[128,1024]{1,0:T(8,128)(2,1)} %get-tuple-element.280), channel_id=1, source_target_pairs={{0,16},{2,18},{4,20},{6,22},{8,24},{10,26},{12,28},{14,30},{16,0},... | collective-permute-start | bytes 786440 | tf_op jit(solution)/shard_map/ppermute | solution.py:888
  677.2 5.8 collective-permute-start.22
  677.3 5.7 collective-permute-start.23
  689.0 20.0 %collective-permute-start.29 = (f32[40,128]{1,0:T(8,128)}, f32[40,128]{1,0:T(8,128)S(1)}, u32[]{:S(2)}, u32[]{:S(2)}) collective-permute-start(f32[40,128]{1,0:T(8,128)} %get-tuple-element.312.refs_12_), channel_id=1, source_target_pairs={{0,4},{2,6},{4,0},{6,2},{8,12},{10,14},{12,8},{14,10},{16,20},{18,... | collective-permute-start | bytes 61448 | tf_op jit(solution)/shard_map/ppermute | solution.py:888
  689.6 19.3 %collective-permute-start.26 = (bf16[256,1024]{1,0:T(8,128)(2,1)}, bf16[256,1024]{1,0:T(8,128)(2,1)S(1)}, u32[]{:S(2)}, u32[]{:S(2)}) collective-permute-start(bf16[256,1024]{1,0:T(8,128)(2,1)} %get-tuple-element.307), channel_id=1, source_target_pairs={{0,4},{2,6},{4,0},{6,2},{8,12},{10,14},{12,8},{14,10},{16,20},{18,... | collective-permute-start | bytes 1572872 | tf_op jit(solution)/shard_map/ppermute | solution.py:888
  691.0 17.9 %collective-permute-start.27 = (bf16[256,1024]{1,0:T(8,128)(2,1)}, bf16[256,1024]{1,0:T(8,128)(2,1)S(1)}, u32[]{:S(2)}, u32[]{:S(2)}) collective-permute-start(bf16[256,1024]{1,0:T(8,128)(2,1)} %get-tuple-element.309), channel_id=1, source_target_pairs={{0,1},{1,0},{2,3},{3,2},{4,5},{5,4},{6,7},{7,6},{8,9},{9,8},{10,11... | collective-permute-start | bytes 1572872 | tf_op jit(solution)/shard_map/ppermute | solution.py:888
  692.9 16.1 %collective-permute-start.28 = (bf16[256,1024]{1,0:T(8,128)(2,1)}, bf16[256,1024]{1,0:T(8,128)(2,1)S(1)}, u32[]{:S(2)}, u32[]{:S(2)}) collective-permute-start(bf16[256,1024]{1,0:T(8,128)(2,1)} %get-tuple-element.311), channel_id=1, source_target_pairs={{0,8},{2,10},{4,12},{6,14},{8,0},{10,2},{12,4},{14,6},{16,24},{18,... | collective-permute-start | bytes 1572872 | tf_op jit(solution)/shard_map/ppermute | solution.py:888
  713.9 17.0 %collective-permute-start.33 = (f32[40,128]{1,0:T(8,128)}, f32[40,128]{1,0:T(8,128)S(1)}, u32[]{:S(2)}, u32[]{:S(2)}) collective-permute-start(f32[40,128]{1,0:T(8,128)} %get-tuple-element.328.refs_12_), channel_id=1, source_target_pairs={{0,1},{1,0},{2,3},{3,2},{4,5},{5,4},{6,7},{7,6},{8,9},{9,8},{10,11... | collective-permute-start | bytes 61448 | tf_op jit(solution)/shard_map/ppermute | solution.py:888
  714.1 16.8 %collective-permute-start.30 = (bf16[128,1024]{1,0:T(8,128)(2,1)}, bf16[128,1024]{1,0:T(8,128)(2,1)S(1)}, u32[]{:S(2)}, u32[]{:S(2)}) collective-permute-start(bf16[128,1024]{1,0:T(8,128)(2,1)} %get-tuple-element.323), channel_id=1, source_target_pairs={{0,1},{1,0},{2,3},{3,2},{4,5},{5,4},{6,7},{7,6},{8,9},{9,8},{10,11... | collective-permute-start | bytes 786440 | tf_op jit(solution)/shard_map/ppermute | solution.py:888
  716.0 14.9 %collective-permute-start.31 = (bf16[128,1024]{1,0:T(8,128)(2,1)}, bf16[128,1024]{1,0:T(8,128)(2,1)S(1)}, u32[]{:S(2)}, u32[]{:S(2)}) collective-permute-start(bf16[128,1024]{1,0:T(8,128)(2,1)} %get-tuple-element.325), channel_id=1, source_target_pairs={{0,8},{2,10},{4,12},{6,14},{8,0},{10,2},{12,4},{14,6},{16,24},{18,... | collective-permute-start | bytes 786440 | tf_op jit(solution)/shard_map/ppermute | solution.py:888
  716.1 14.8 %collective-permute-start.32 = (bf16[128,1024]{1,0:T(8,128)(2,1)}, bf16[128,1024]{1,0:T(8,128)(2,1)S(1)}, u32[]{:S(2)}, u32[]{:S(2)}) collective-permute-start(bf16[128,1024]{1,0:T(8,128)(2,1)} %get-tuple-element.327), channel_id=1, source_target_pairs={{0,4},{2,6},{4,0},{6,2},{8,12},{10,14},{12,8},{14,10},{16,20},{18,... | collective-permute-start | bytes 786440 | tf_op jit(solution)/shard_map/ppermute | solution.py:888
  746.3 10.8 %collective-permute-start.41 = (f32[40,128]{1,0:T(8,128)}, f32[40,128]{1,0:T(8,128)S(1)}, u32[]{:S(2)}, u32[]{:S(2)}) collective-permute-start(f32[40,128]{1,0:T(8,128)} %get-tuple-element.367), channel_id=1, source_target_pairs={{0,16},{2,18},{4,20},{6,22},{8,24},{10,26},{12,28},{14,30},{16,0},... | collective-permute-start | bytes 61448 | tf_op jit(solution)/shard_map/ppermute | solution.py:888
  754.2 6.0 collective-permute-start.39
  (48 other events, 345.0 us)

commit v4 on v3

--- a/solution.py
+++ b/solution.py
@@ -13,6 +13,7 @@
 LOG2E = 1.4426950408889634
 LN2 = 0.6931471805599453
 NEG = -1e30
+REACH = 60.0
 VMEM = 62 * 1024 * 1024
 SPAN = 1024
 
@@ -26,13 +27,26 @@
     )
 
 
-def fwd_chunk(q0, k0, q_n, k_n, limit, qT, kT, vT, m_ref, l_ref, acc):
+def bounded(qT, kT):
+    worst = None
+    for h in range(2):
+        rows = slice(HEAD_DIM * h, HEAD_DIM * (h + 1))
+        norms = []
+        for item in (qT, kT):
+            values = item[rows, :].astype(f32)
+            norms.append(jnp.max(jnp.sum(values * values, axis=0, keepdims=True)))
+        both = norms[0] * norms[1]
+        worst = both if worst is None else jnp.maximum(worst, both)
+    return worst <= REACH * REACH
+
+
+def fwd_chunk(fast, q0, k0, q_n, k_n, limit, qT, kT, vT, m_ref, l_ref, acc):
     queries = pl.ds(q0, q_n)
     strip = min(256, k_n)
     for h in range(2):
         rows = slice(HEAD_DIM * h, HEAD_DIM * (h + 1))
         old = m_ref[h : h + 1, queries]
-        new = old
+        new = jnp.zeros_like(old) if fast else old
         strips = []
         for j in range(k_n // strip):
             keys = pl.ds(k0 + j * strip, strip)
@@ -41,13 +55,14 @@
                 key_at = lax.broadcasted_iota(jnp.int32, (strip, q_n), 0)
                 scores = jnp.where(key_at < limit - j * strip, scores, NEG)
             strips.append(scores)
-            new = jnp.maximum(new, jnp.max(scores, axis=0, keepdims=True))
+            if not fast:
+                new = jnp.maximum(new, jnp.max(scores, axis=0, keepdims=True))
         factor = jnp.exp2(old - new)
         total = l_ref[h : h + 1, queries] * factor
         value = acc[rows, queries] * factor
         for j in range(k_n // strip):
             keys = pl.ds(k0 + j * strip, strip)
-            weights = jnp.exp2(strips[j] - new)
+            weights = jnp.exp2(strips[j] if fast else strips[j] - new)
             total = total + jnp.sum(weights, axis=0, keepdims=True)
             value = value + dot(vT[rows, keys], weights.astype(bf16), 1, 0)
         m_ref[h : h + 1, queries] = new
@@ -67,7 +82,7 @@
     return jnp.concatenate([values, jnp.zeros((values.shape[0], count), f32)], axis=1)
 
 
-def fwd_diagonal(base, group, limit, qT, kT, vT, m_ref, l_ref, acc):
+def fwd_diagonal(fast, base, group, limit, qT, kT, vT, m_ref, l_ref, acc):
     strip = min(256, group)
     count = group // strip
     for h in range(2):
@@ -84,18 +99,21 @@
                 scores = jnp.where(key_at < limit - j * strip, scores, NEG)
             strips.append(scores)
         peaks = []
-        for g in range(count):
+        for g in range(0 if fast else count):
             peak = None
             for j in range(g + 1):
                 part = strips[j][:, (g - j) * strip : (g - j + 1) * strip]
                 part = jnp.max(part, axis=0, keepdims=True)
                 peak = part if peak is None else jnp.maximum(peak, part)
             peaks.append(peak)
-        peak = jnp.concatenate(peaks, axis=1) if count > 1 else peaks[0]
+        if fast:
+            peak = jnp.zeros((1, group), f32)
+        else:
+            peak = jnp.concatenate(peaks, axis=1) if count > 1 else peaks[0]
         total, value = None, None
         for j in range(count):
             keys = pl.ds(base + j * strip, strip)
-            weights = jnp.exp2(strips[j] - peak[:, j * strip :])
+            weights = jnp.exp2(strips[j] if fast else strips[j] - peak[:, j * strip :])
             part = pad_left(jnp.sum(weights, axis=0, keepdims=True), j * strip)
             term = pad_left(dot(vT[rows, keys], weights.astype(bf16), 1, 0), j * strip)
             total = part if total is None else total + part
@@ -113,30 +131,35 @@
     acc[...] = jnp.zeros(acc.shape, f32)
     refs = (qT, kT, vT, m_ref.at[0], l_ref.at[0], acc)
 
-    def own(i, carry):
-        base = pl.multiple_of(i * group, group)
-        start = info[2 + i]
-
-        @pl.when(start + group <= length)
+    def walk(fast):
+        def own(i, carry):
+            base = pl.multiple_of(i * group, group)
+            start = info[2 + i]
+
+            @pl.when(start + group <= length)
+            def _():
+                fwd_diagonal(fast, base, group, None, *refs)
+
+            @pl.when((start < length) & (start + group > length))
+            def _():
+                fwd_diagonal(fast, base, group, length - start, *refs)
+
+            return carry
+
+        lax.fori_loop(0, 2, own, 0)
+        early = info[2]
+
+        @pl.when(early + group <= length)
         def _():
-            fwd_diagonal(base, group, None, *refs)
-
-        @pl.when((start < length) & (start + group > length))
+            fwd_chunk(fast, group, 0, group, group, None, *refs)
+
+        @pl.when((early < length) & (early + group > length))
         def _():
-            fwd_diagonal(base, group, length - start, *refs)
-
-        return carry
-
-    lax.fori_loop(0, 2, own, 0)
-    early = info[2]
-
-    @pl.when(early + group <= length)
-    def _():
-        fwd_chunk(group, 0, group, group, None, *refs)
-
-    @pl.when((early < length) & (early + group > length))
-    def _():
-        fwd_chunk(group, 0, group, group, length - early, *refs)
+            fwd_chunk(fast, group, 0, group, group, length - early, *refs)
+
+    small = bounded(qT, kT)
+    pl.when(small)(functools.partial(walk, True))
+    pl.when(jnp.logical_not(small))(functools.partial(walk, False))
 
 
 def remote_steps(group, parts, info, full, partial):
@@ -174,13 +197,18 @@
     l_ref[...] = l_in[0]
     refs = (qT, kT, vT, m_ref, l_ref, acc)
 
-    def full(q0, k0):
-        fwd_chunk(q0, k0, group, group, None, *refs)
-
-    def partial(q0, k0, limit):
-        fwd_chunk(q0, k0, group, group, limit, *refs)
-
-    remote_steps(group, parts, info, full, partial)
+    def walk(fast):
+        def full(q0, k0):
+            fwd_chunk(fast, q0, k0, group, group, None, *refs)
+
+        def partial(q0, k0, limit):
+            fwd_chunk(fast, q0, k0, group, group, limit, *refs)
+
+        remote_steps(group, parts, info, full, partial)
+
+    small = bounded(qT, kT) & (jnp.max(m_in[...]) <= 0.0)
+    pl.when(small)(functools.partial(walk, True))
+    pl.when(jnp.logical_not(small))(functools.partial(walk, False))
     for h in range(2):
         rows = slice(HEAD_DIM * h, HEAD_DIM * (h + 1))
         total = l_ref[h : h + 1, :]
@@ -638,7 +666,7 @@
     for section, out in zip(sections, outs):
         for c in range(width // chunk):
             at = section * width + c * chunk
-            mixed = dot(w[:, at : at + chunk], normed, 0, 1) + b[at : at + chunk, :]
+            mixed = dot(w[:, at : at + chunk], normed, 0, 1) + b[:, at : at + chunk].T
             for h in range(chunk // HEAD_DIM):
                 rows = slice(h * HEAD_DIM, (h + 1) * HEAD_DIM)
                 place = slice(c * chunk + h * HEAD_DIM, c * chunk + (h + 1) * HEAD_DIM)
@@ -731,20 +759,24 @@
 
 
 def divide(total, run, levels, near, marks, orders, outs):
-    chunks = [total[at : at + run] for at in range(0, total.shape[0], run)]
     bits = [("narrow", i) for i in range(near)] + [("wide", i) for i in range(levels + 1)]
-    for place, (axis, position) in enumerate(bits):
-        mine = (marks[1 if axis == "narrow" else 0] >> position) & 1
-        chunks = [
-            jnp.where(mine == 1, chunks[k ^ (1 << place)], chunks[k]) for k in range(len(chunks))
-        ]
     cut = run // len(orders)
-    for i, order in enumerate(orders):
-        for k, chunk in enumerate(chunks):
-            value = {bit: (k >> place) & 1 for place, bit in enumerate(bits)}
-            out = outs[2 * i + value["wide", 0]]
-            index = tuple(value.get(bit, 0) for bit in order)
-            out[index] = chunk[i * cut : (i + 1) * cut].astype(bf16)
+
+    def write(core):
+        for at in range(0, total.shape[0], run):
+            number = at // run
+            value = {}
+            for place, (axis, position) in enumerate(bits):
+                mine = (marks[1 if axis == "narrow" else 0] >> position) & 1
+                value[axis, position] = mine ^ ((number >> place) & 1)
+            other = core ^ ((number >> near) & 1)
+            for i, order in enumerate(orders):
+                index = tuple(value.get(bit, 0) for bit in order)
+                part = total[at + i * cut : at + (i + 1) * cut]
+                outs[2 * i + other][index] = part.astype(bf16)
+
+    pl.when((marks[0] & 1) == 0)(functools.partial(write, 0))
+    pl.when((marks[0] & 1) == 1)(functools.partial(write, 1))
 
 
 def divided(orders, levels, run, height, wide, width):
@@ -774,7 +806,7 @@
     rows, height = left.shape
     width = right.shape[1 - right_dim]
     share = height // cores
-    high = max(2 * share, min(512, height))
+    high = max(2 * share, min(1024, height))
     levels = (high // (2 * share)).bit_length() - 1
     wide = min(1024, width)
     if right_dim == 0:
@@ -835,7 +867,7 @@
     far = d_far.shape[1]
     width = normed.shape[1]
     share = height // cores
-    pairs = max(1, 384 // (2 * share))
+    pairs = max(1, 768 // (2 * share))
     levels = pairs.bit_length() - 1
     high = 2 * share * pairs
     first_far = width // high
@@ -1053,11 +1085,10 @@
     turns_far = angles(positions(other))
 
     norm_one = [row(gain_one), row(shift_one)]
-    b_column = b_qkv[:, None]
-    normed, qT, kT, vT = project(tokens, w_qkv, b_column, *norm_one, *turns, (0, 1, 2))
+    normed, qT, kT, vT = project(tokens, w_qkv, row(b_qkv), *norm_one, *turns, (0, 1, 2))
     state = attend_local(info, qT, kT, vT, group)
     normed_far, kT_far, vT_far = project(
-        far_tokens, w_qkv, b_column, *norm_one, *turns_far, (1, 2)
+        far_tokens, w_qkv, row(b_qkv), *norm_one, *turns_far, (1, 2)
     )
     oT, lse = attend_remote(info, qT, kT_far, vT_far, state, group, parts)
 

time: 772 us -> 745 us (0.965)
  Pallas kernels: 676 us -> 634 us
  waiting for transfers between devices: 20.4 us -> 39.3 us
    ppermute x1, waiting for transfers between devices: 0.01 us -> 20.7 us  [body(): lax.ppermute(tokens, 'narrow', [((n + shift) % parts, n) for n in range(p...]
    pallas_call x1, Pallas kernels: 59.7 us -> 39.1 us  [attend_remote(): return call(info, qT, kT, vT, *state)]
    pallas_call x1, Pallas kernels: 63.5 us -> 43.1 us  [attend_local(): return call(info, qT, kT, vT)]
  transfers between devices with their start and end apart: 42 -> 42, of which waited for: 11 -> 12; matrix products, arithmetic and copies ran while one was open for 2% -> 2% of each run, Pallas kernels for 50% -> 49%
where the time goes in v4:
time: 745 us; the launch traced here: 739 us
  Pallas kernels  634 us (85%)
  starting transfers between devices  44.3 us (6%)
  waiting for transfers between devices  39.3 us (5%)
  local copies, waits for them, and re-layouts  12.2 us (2%)
    pallas_call x2, Pallas kernels, back_local(): return call(info, *operands, *turns, *keys, dq, *before)  117 us
    pallas_call x1, Pallas kernels, block_call(): pl.pallas_call(functools.partial(block_kernel, span), grid=(rows // step,...  116 us
    pallas_call x2, Pallas kernels, back_remote(): return call(info, *operands, *turns, *keys, *before)  96.9 us
    pallas_call x3, Pallas kernels, outer_halves(): pl.pallas_call(functools.partial(outer_kernel, run, levels, near, [order]...  59.5 us
    pallas_call x1, Pallas kernels, attend_local(): return call(info, qT, kT, vT)  43.1 us
    pallas_call x3, Pallas kernels, unproject(): pl.pallas_call(functools.partial(unproject_kernel, planes, bool(finish)),...  43.1 us
    ppermute x40, starting transfers between devices, swap(): lax.ppermute(values, axis, [(i, i ^ 1 << position) for i in range(size)])  40.8 us
    pallas_call x2, Pallas kernels, project(): pl.pallas_call(functools.partial(project_kernel, sections), grid=(rows //...  39.3 us
  transfers between devices with their start and end apart: 42, of which 12 were waited for; matrix products, arithmetic and copies ran while one was open for 2% of the time, Pallas kernels for 49%

profile of v4, /device:TPU:0, one launch (start us, length us, event | category | flops | bytes accessed | tf_op | source)
XLA Modules:
  0.0 739.2 jit_solution(10233731410432628143)
XLA Ops:
  0.7 3.0 collective-permute-start
  5.8 2.7 multiply_sine_fusion
  8.6 22.2 %project.2 = (bf16[2048,1024]{1,0:T(8,128)(2,1)}, bf16[1024,2048]{1,0:T(8,128)(2,1)}, bf16[1024,2048]{1,0:T(8,128)(2,1)}, bf16[1024,2048]{1,0:T(8,128)(2,1)}) custom-call(bf16[2048,1024]{1,0:T(8,128)(2,1)} %bitcast.139, bf16[1024,3072]{1,0:T(8,128)(2,1)} %refs_3_.3, f32[1,3072]{1,0:T(1,128)} %bitcast.250, f32[1,1024]{1,0:T(1,128)} %bitcast.229, ...), custom_call_target="tpu_custom_call" | custom-call | flops 12884901888 | bytes 16777216 | tf_op jit(solution)/shard_map/project/pallas_call | solution.py:692
  30.8 43.1 %attend_local.1 = (f32[1024,2048]{1,0:T(8,128)}, f32[8,2,2048]{2,1,0:T(2,128)}, f32[8,2,2048]{2,1,0:T(2,128)}) custom-call(s32[4]{0:T(128)} %pad_add_fusion.info, bf16[1024,2048]{1,0:T(8,128)(2,1)} %get-tuple-element.194.qT, bf16[1024,2048]{1,0:T(8,128)(2,1)} %get-tuple-element.197.kT, bf16[1024,2048]{1,0:T(8,128)(2,1)} %get-tuple-element.198.vT), custom_call_target="tpu_custom_call" | custom-call | flops 34359738368 | bytes 33554432 | tf_op jit(solution)/shard_map/attend_local/pallas_call | solution.py:419
  73.9 20.7 %collective-permute-done.tokens = bf16[2048,1024]{1,0:T(8,128)(2,1)} collective-permute-done((bf16[2048,1024]{1,0:T(8,128)(2,1)}, bf16[2048,1024]{1,0:T(8,128)(2,1)}, u32[]{:S(2)}, u32[]{:S(2)}) %collective-permute-start) | collective-permute-done | bytes 4194336 | tf_op jit(solution)/shard_map/ppermute | solution.py:1075
  94.6 17.1 %project.3 = (bf16[2048,1024]{1,0:T(8,128)(2,1)}, bf16[1024,2048]{1,0:T(8,128)(2,1)}, bf16[1024,2048]{1,0:T(8,128)(2,1)}) custom-call(bf16[2048,1024]{1,0:T(8,128)(2,1)} %collective-permute-done.tokens, bf16[1024,3072]{1,0:T(8,128)(2,1)} %refs_3_.3, f32[1,3072]{1,0:T(1,128)} %bitcast.251, f32[1,1024]{1,0:T(1,128)} %bitcast.230, f32[1,1024]{1,0:T(1,128)} %bitcast.239, ...), custom_call_target="tpu_custom_call" | custom-call | flops 8589934592 | bytes 16777216 | tf_op jit(solution)/shard_map/project/pallas_call | solution.py:692
  111.7 39.1 %attend_remote.1 = (bf16[1024,2048]{1,0:T(8,128)(2,1)}, f32[8,2,2048]{2,1,0:T(2,128)}) custom-call(s32[4]{0:T(128)} %pad_add_fusion.info, bf16[1024,2048]{1,0:T(8,128)(2,1)} %get-tuple-element.194.qT, bf16[1024,2048]{1,0:T(8,128)(2,1)} %get-tuple-element.195.kT, bf16[1024,2048]{1,0:T(8,128)(2,1)} %get-tuple-element.196.vT, ...), custom_call_target="tpu_custom_call" | custom-call | flops 34359738368 | bytes 33554432 | tf_op jit(solution)/shard_map/attend_remote/pallas_call | solution.py:439
  150.8 115.9 %block.1 = (bf16[2048,1024]{1,0:T(8,128)(2,1)}, f32[2048,1024]{1,0:T(8,128)}, bf16[2048,4096]{1,0:T(8,128)(2,1)}, bf16[2048,1024]{1,0:T(8,128)(2,1)}, bf16[2048,...) custom-call(bf16[1024,2048]{1,0:T(8,128)(2,1)} %get-tuple-element.20, ...), custom_call_target="tpu_custom_call" | custom-call | flops 77309411328 | bytes 67108864 | tf_op jit(solution)/shard_map/block/pallas_call | solution.py:627
  266.7 24.6 %outer.3 = (bf16[2,2,2,2,32,4096]{5,4,3,2,1,0:T(8,128)(2,1)}, bf16[2,2,2,2,32,4096]{5,4,3,2,1,0:T(8,128)(2,1)}) custom-call(s32[2]{0:T(128)} %pad_add_fusion.1.marks, bf16[2048,1024]{1,0:T(8,128)(2,1)} %get-tuple-element.205.left, bf16[2048,4096]{1,0:T(8,128)(2,1)} %get-tuple-element.206.right), custom_call_target="tpu_custom_call" | custom-call | flops 17179869184 | bytes 33554432 | tf_op jit(solution)/shard_map/outer/pallas_call | solution.py:819
  291.3 24.6 %outer.4 = (bf16[2,2,2,2,128,1024]{5,4,3,2,1,0:T(8,128)(2,1)}, bf16[2,2,2,2,128,1024]{5,4,3,2,1,0:T(8,128)(2,1)}) custom-call(s32[2]{0:T(128)} %pad_add_fusion.1.marks, bf16[2048,4096]{1,0:T(8,128)(2,1)} %get-tuple-element.209.left, bf16[2048,1024]{1,0:T(8,128)(2,1)} %get-tuple-element.210.right), custom_call_target="tpu_custom_call" | custom-call | flops 17179869184 | bytes 33554432 | tf_op jit(solution)/shard_map/outer/pallas_call | solution.py:819
  316.5 10.3 %outer.5 = (bf16[2,2,2,2,32,1024]{5,4,3,2,1,0:T(8,128)(2,1)}, bf16[2,2,2,2,32,1024]{5,4,3,2,1,0:T(8,128)(2,1)}) custom-call(s32[2]{0:T(128)} %pad_add_fusion.1.marks, bf16[2048,1024]{1,0:T(8,128)(2,1)} %get-tuple-element.213.left, bf16[1024,2048]{1,0:T(8,128)(2,1)} %get-tuple-element.202.oT.right), custom_call_target="tpu_custom_call" | custom-call | flops 4294967296 | bytes 33554432 | tf_op jit(solution)/shard_map/outer/pallas_call | solution.py:819
  330.6 11.2 %halve.8 = (bf16[256,4096]{1,0:T(8,128)(2,1)}, bf16[256,4096]{1,0:T(8,128)(2,1)}, bf16[1024,1024]{1,0:T(8,128)(2,1)}, bf16[1024,1024]{1,0:T(8,128)(2,1)}, bf16[2...) custom-call(bf16[2,256,4096]{2,1,0:T(8,128)(2,1)} %bitcast.144, ...), custom_call_target="tpu_custom_call" | custom-call | tf_op jit(solution)/shard_map/halve/pallas_call | solution.py:966
  347.2 48.3 %back_remote.2 = (f32[1024,2048]{1,0:T(8,128)}, bf16[3,1024,2048]{2,1,0:T(8,128)(2,1)}) custom-call(s32[4]{0:T(128)} %pad_add_fusion.info, bf16[1024,2048]{1,0:T(8,128)(2,1)} %get-tuple-element.194.qT, bf16[1024,2048]{1,0:T(8,128)(2,1)} %get-tuple-element.275.doT, bf16[1024,2048]{1,0:T(8,128)(2,1)} %get-tuple-element.202.oT.right, ...), custom_call_target="tpu_custom_call" | custom-call | flops 42949672960 | bytes 33554432 | tf_op jit(solution)/shard_map/back_remote/pallas_call | solution.py:475
  395.6 7.0 collective-permute-done.6
  402.6 6.6 halve.9
  414.1 48.5 %back_remote.3 = (f32[1024,2048]{1,0:T(8,128)}, bf16[3,1024,2048]{2,1,0:T(8,128)(2,1)}) custom-call(s32[4]{0:T(128)} %pad_add_fusion.info, bf16[1024,2048]{1,0:T(8,128)(2,1)} %get-tuple-element.194.qT, bf16[1024,2048]{1,0:T(8,128)(2,1)} %get-tuple-element.275.doT, ...), custom_call_target="tpu_custom_call", output_to_operand_aliasing={{0}: (9, {}), {1}: (10, {})} | custom-call | flops 42949672960 | bytes 33554432 | tf_op jit(solution)/shard_map/back_remote/pallas_call | solution.py:475
  462.6 14.7 %unproject.3 = bf16[2048,1024]{1,0:T(8,128)(2,1)} custom-call(bf16[3,1024,2048]{2,1,0:T(8,128)(2,1)} %get-tuple-element.244.refs_0_.refs_1_, bf16[3,1024,2048]{2,1,0:T(8,128)(2,1)} %get-tuple-element.244.refs_0_.refs_1_, bf16[1024,3072]{1,0:T(8,128)(2,1)} %refs_3_.3), custom_call_target="tpu_custom_call" | custom-call | flops 8589934592 | bytes 16777216 | tf_op jit(solution)/shard_map/unproject/pallas_call | solution.py:741
  478.4 4.6 halve.10
  487.6 58.5 %back_local.2.rest_0_ = bf16[3,1024,2048]{2,1,0:T(8,128)(2,1)} custom-call(s32[4]{0:T(128)} %pad_add_fusion.info, bf16[1024,2048]{1,0:T(8,128)(2,1)} %get-tuple-element.194.qT, bf16[1024,2048]{1,0:T(8,128)(2,1)} %get-tuple-element.275.doT, bf16[1024,2048]{1,0:T(8,128)(2,1)} %get-tuple-element.202.oT.right, f32[8,2,2048]{2,1,0:T(2,128)} %get-tuple-element.241.lse, ...), custom_call_target="tpu_custom_call" | custom-call | flops 42949672960 | bytes 33554432 | tf_op jit(solution)/shard_map/back_local/pallas_call | solution.py:497
  547.2 2.6 halve.11
  549.8 2.5 collective-permute-start.20
  552.8 2.5 collective-permute-start.17
  555.7 58.3 %back_local.3.refs_0_.refs_1_.refs_2_ = bf16[3,1024,2048]{2,1,0:T(8,128)(2,1)} custom-call(s32[4]{0:T(128)} %pad_add_fusion.info, bf16[1024,2048]{1,0:T(8,128)(2,1)} %get-tuple-element.194.qT, bf16[1024,2048]{1,0:T(8,128)(2,1)} %get-tuple-element.275.doT, bf16[1024,2048]{1,0:T(8,128)(2,1)} %get-tuple-element.202.oT.right, ...), custom_call_target="tpu_custom_call", output_to_operand_aliasing={{}: (10, {})} | custom-call | flops 42949672960 | bytes 33554432 | tf_op jit(solution)/shard_map/back_local/pallas_call | solution.py:497
  614.1 37.5 %mixed.1 = (bf16[2,2,2,2,32,1024]{5,4,3,2,1,0:T(8,128)(2,1)}, bf16[2,2,2,2,32,1024]{5,4,3,2,1,0:T(8,128)(2,1)}, bf16[2,2,2,2,32,1024]{5,4,3,2,1,0:T(8,128)(2,1)}...) custom-call(s32[2]{0:T(128)} %pad_add_fusion.1.marks, ...), custom_call_target="tpu_custom_call" | custom-call | flops 25769803776 | bytes 33554432 | tf_op jit(solution)/shard_map/mixed/pallas_call | solution.py:881
  658.4 5.0 halve.12
  667.5 14.1 %unproject.4.refs_8_ = bf16[2048,1024]{1,0:T(8,128)(2,1)} custom-call(bf16[3,1024,2048]{2,1,0:T(8,128)(2,1)} %back_local.3.refs_0_.refs_1_.refs_2_, bf16[3,1024,2048]{2,1,0:T(8,128)(2,1)} %back_local.3.refs_0_.refs_1_.refs_2_, bf16[3,1024,2048]{2,1,0:T(8,128)(2,1)} %back_local.3.refs_0_.refs_1_.refs_2_, bf16[1024,3072]{1,0:T(8,128)(2,1)} %refs_3_.3, ...), custom_call_target="tpu_custom_call" | custom-call | flops 6442450944 | bytes 16777216 | tf_op jit(solution)/shard_map/unproject/pallas_call | solution.py:741
  682.7 3.8 halve.13
  691.0 14.3 %unproject.5 = bf16[2048,1024]{1,0:T(8,128)(2,1)} custom-call(bf16[3,1024,2048]{2,1,0:T(8,128)(2,1)} %back_local.3.refs_0_.refs_1_.refs_2_, bf16[3,1024,2048]{2,1,0:T(8,128)(2,1)} %back_local.3.refs_0_.refs_1_.refs_2_, bf16[3,1024,2048]{2,1,0:T(8,128)(2,1)} %back_local.3.refs_0_.refs_1_.refs_2_, ...), custom_call_target="tpu_custom_call", output_to_operand_aliasing={{}: (8, {})} | custom-call | flops 6442450944 | bytes 16777216 | tf_op jit(solution)/shard_map/unproject/pallas_call | solution.py:741
  706.2 3.3 halve.14
  714.1 2.4 collective-permute-done.34
  720.7 2.7 collective-permute-start.41
  728.5 2.7 collective-permute-start.39
  (176 shorter events, 62.5 us)
Async XLA Ops:
  0.7 93.9 %collective-permute-start = (bf16[2048,1024]{1,0:T(8,128)(2,1)}, bf16[2048,1024]{1,0:T(8,128)(2,1)}, u32[]{:S(2)}, u32[]{:S(2)}) collective-permute-start(bf16[2048,1024]{1,0:T(8,128)(2,1)} %bitcast.138), channel_id=1, source_target_pairs={{1,0},{0,1},{3,2},{2,3},{5,4},{4,5},{7,6},{6,7},{9,8},{8,9},{11,10... | collective-permute-start | bytes 12582920 | tf_op jit(solution)/shard_map/ppermute | solution.py:1075
  291.3 38.4 %collective-permute-start.1 = (bf16[512,4096]{1,0:T(8,128)(2,1)}, bf16[512,4096]{1,0:T(8,128)(2,1)}, u32[]{:S(2)}, u32[]{:S(2)}) collective-permute-start(bf16[512,4096]{1,0:T(8,128)(2,1)} %bitcast.241), channel_id=1, source_target_pairs={{0,2},{2,0},{4,6},{6,4},{8,10},{10,8},{12,14},{14,12},{16,18},{18,... | collective-permute-start | bytes 12582920 | tf_op jit(solution)/shard_map/ppermute | solution.py:920
  315.9 13.7 %collective-permute-start.2 = (bf16[2048,1024]{1,0:T(8,128)(2,1)}, bf16[2048,1024]{1,0:T(8,128)(2,1)}, u32[]{:S(2)}, u32[]{:S(2)}) collective-permute-start(bf16[2048,1024]{1,0:T(8,128)(2,1)} %bitcast.242), channel_id=1, source_target_pairs={{0,2},{2,0},{4,6},{6,4},{8,10},{10,8},{12,14},{14,12},{16,18},{18,... | collective-permute-start | bytes 12582920 | tf_op jit(solution)/shard_map/ppermute | solution.py:920
  341.9 53.7 %collective-permute-start.8 = (f32[96,128]{1,0:T(8,128)}, f32[96,128]{1,0:T(8,128)S(1)}, u32[]{:S(2)}, u32[]{:S(2)}) collective-permute-start(f32[96,128]{1,0:T(8,128)} %get-tuple-element.232.refs_12_), channel_id=1, source_target_pairs={{0,4},{2,6},{4,0},{6,2},{8,12},{10,14},{12,8},{14,10},{16,20},{18,... | collective-permute-start | bytes 147464 | tf_op jit(solution)/shard_map/ppermute | solution.py:920
  343.6 51.9 %collective-permute-start.7 = (bf16[256,1024]{1,0:T(8,128)(2,1)}, bf16[256,1024]{1,0:T(8,128)(2,1)S(1)}, u32[]{:S(2)}, u32[]{:S(2)}) collective-permute-start(bf16[256,1024]{1,0:T(8,128)(2,1)} %get-tuple-element.231), channel_id=1, source_target_pairs={{0,4},{2,6},{4,0},{6,2},{8,12},{10,14},{12,8},{14,10},{16,20},{18,... | collective-permute-start | bytes 1572872 | tf_op jit(solution)/shard_map/ppermute | solution.py:920
  344.0 51.6 %collective-permute-start.5 = (bf16[256,4096]{1,0:T(8,128)(2,1)}, bf16[256,4096]{1,0:T(8,128)(2,1)}, u32[]{:S(2)}, u32[]{:S(2)}) collective-permute-start(bf16[256,4096]{1,0:T(8,128)(2,1)} %get-tuple-element.227), channel_id=1, source_target_pairs={{0,1},{1,0},{2,3},{3,2},{4,5},{5,4},{6,7},{7,6},{8,9},{9,8},{10,11... | collective-permute-start | bytes 6291464 | tf_op jit(solution)/shard_map/ppermute | solution.py:920
  345.7 56.9 %collective-permute-start.6 = (bf16[1024,1024]{1,0:T(8,128)(2,1)}, bf16[1024,1024]{1,0:T(8,128)(2,1)}, u32[]{:S(2)}, u32[]{:S(2)}) collective-permute-start(bf16[1024,1024]{1,0:T(8,128)(2,1)} %get-tuple-element.229), channel_id=1, source_target_pairs={{0,4},{2,6},{4,0},{6,2},{8,12},{10,14},{12,8},{14,10},{16,20},{18,... | collective-permute-start | bytes 6291464 | tf_op jit(solution)/shard_map/ppermute | solution.py:920
  409.2 68.2 %collective-permute-start.12 = (f32[96,128]{1,0:T(8,128)}, f32[96,128]{1,0:T(8,128)S(1)}, u32[]{:S(2)}, u32[]{:S(2)}) collective-permute-start(f32[96,128]{1,0:T(8,128)} %get-tuple-element.251.refs_12_), channel_id=1, source_target_pairs={{0,1},{1,0},{2,3},{3,2},{4,5},{5,4},{6,7},{7,6},{8,9},{9,8},{10,11... | collective-permute-start | bytes 147464 | tf_op jit(solution)/shard_map/ppermute | solution.py:920
  410.9 66.4 %collective-permute-start.11 = (bf16[128,1024]{1,0:T(8,128)(2,1)}, bf16[128,1024]{1,0:T(8,128)(2,1)S(1)}, u32[]{:S(2)}, u32[]{:S(2)}) collective-permute-start(bf16[128,1024]{1,0:T(8,128)(2,1)} %get-tuple-element.250), channel_id=1, source_target_pairs={{0,1},{1,0},{2,3},{3,2},{4,5},{5,4},{6,7},{7,6},{8,9},{9,8},{10,11... | collective-permute-start | bytes 786440 | tf_op jit(solution)/shard_map/ppermute | solution.py:920
  411.2 66.1 %collective-permute-start.9 = (bf16[128,4096]{1,0:T(8,128)(2,1)}, bf16[128,4096]{1,0:T(8,128)(2,1)S(1)}, u32[]{:S(2)}, u32[]{:S(2)}) collective-permute-start(bf16[128,4096]{1,0:T(8,128)(2,1)} %get-tuple-element.246), channel_id=1, source_target_pairs={{0,4},{2,6},{4,0},{6,2},{8,12},{10,14},{12,8},{14,10},{16,20},{18,... | collective-permute-start | bytes 3145736 | tf_op jit(solution)/shard_map/ppermute | solution.py:920
  412.6 64.8 %collective-permute-start.10 = (bf16[512,1024]{1,0:T(8,128)(2,1)}, bf16[512,1024]{1,0:T(8,128)(2,1)}, u32[]{:S(2)}, u32[]{:S(2)}) collective-permute-start(bf16[512,1024]{1,0:T(8,128)(2,1)} %get-tuple-element.248), channel_id=1, source_target_pairs={{0,1},{1,0},{2,3},{3,2},{4,5},{5,4},{6,7},{7,6},{8,9},{9,8},{10,11... | collective-permute-start | bytes 3145736 | tf_op jit(solution)/shard_map/ppermute | solution.py:920
  483.0 63.2 %collective-permute-start.16 = (f32[96,128]{1,0:T(8,128)}, f32[96,128]{1,0:T(8,128)S(1)}, u32[]{:S(2)}, u32[]{:S(2)}) collective-permute-start(f32[96,128]{1,0:T(8,128)} %get-tuple-element.267.refs_12_), channel_id=1, source_target_pairs={{0,8},{2,10},{4,12},{6,14},{8,0},{10,2},{12,4},{14,6},{16,24},{18,... | collective-permute-start | bytes 147464 | tf_op jit(solution)/shard_map/ppermute | solution.py:920
  483.1 63.1 %collective-permute-start.15 = (bf16[64,1024]{1,0:T(8,128)(2,1)}, bf16[64,1024]{1,0:T(8,128)(2,1)S(1)}, u32[]{:S(2)}, u32[]{:S(2)}) collective-permute-start(bf16[64,1024]{1,0:T(8,128)(2,1)} %get-tuple-element.266), channel_id=1, source_target_pairs={{0,8},{2,10},{4,12},{6,14},{8,0},{10,2},{12,4},{14,6},{16,24},{18,... | collective-permute-start | bytes 393224 | tf_op jit(solution)/shard_map/ppermute | solution.py:920
  485.1 61.1 %collective-permute-start.13 = (bf16[64,4096]{1,0:T(8,128)(2,1)}, bf16[64,4096]{1,0:T(8,128)(2,1)S(1)}, u32[]{:S(2)}, u32[]{:S(2)}) collective-permute-start(bf16[64,4096]{1,0:T(8,128)(2,1)} %get-tuple-element.262), channel_id=1, source_target_pairs={{0,8},{2,10},{4,12},{6,14},{8,0},{10,2},{12,4},{14,6},{16,24},{18,... | collective-permute-start | bytes 1572872 | tf_op jit(solution)/shard_map/ppermute | solution.py:920
  485.1 61.0 %collective-permute-start.14 = (bf16[256,1024]{1,0:T(8,128)(2,1)}, bf16[256,1024]{1,0:T(8,128)(2,1)S(1)}, u32[]{:S(2)}, u32[]{:S(2)}) collective-permute-start(bf16[256,1024]{1,0:T(8,128)(2,1)} %get-tuple-element.264), channel_id=1, source_target_pairs={{0,8},{2,10},{4,12},{6,14},{8,0},{10,2},{12,4},{14,6},{16,24},{18,... | collective-permute-start | bytes 1572872 | tf_op jit(solution)/shard_map/ppermute | solution.py:920
  487.1 127.0 %collective-permute-start.21 = (bf16[2048,1024]{1,0:T(8,128)(2,1)}, bf16[2048,1024]{1,0:T(8,128)(2,1)}, u32[]{:S(2)}, u32[]{:S(2)}) collective-permute-start(bf16[2048,1024]{1,0:T(8,128)(2,1)} %unproject.3), channel_id=1, source_target_pairs={{0,1},{1,0},{2,3},{3,2},{4,5},{5,4},{6,7},{7,6},{8,9},{9,8},{10,11... | collective-permute-start | bytes 12582920 | tf_op jit(solution)/shard_map/ppermute | solution.py:1148
  549.8 64.2 %collective-permute-start.20 = (f32[96,128]{1,0:T(8,128)}, f32[96,128]{1,0:T(8,128)S(1)}, u32[]{:S(2)}, u32[]{:S(2)}) collective-permute-start(f32[96,128]{1,0:T(8,128)} %get-tuple-element.368), channel_id=1, source_target_pairs={{0,16},{2,18},{4,20},{6,22},{8,24},{10,26},{12,28},{14,30},{16,0},... | collective-permute-start | bytes 147464 | tf_op jit(solution)/shard_map/ppermute | solution.py:920
  552.3 61.7 %collective-permute-start.19 = (bf16[32,1024]{1,0:T(8,128)(2,1)}, bf16[32,1024]{1,0:T(8,128)(2,1)S(1)}, u32[]{:S(2)}, u32[]{:S(2)}) collective-permute-start(bf16[32,1024]{1,0:T(8,128)(2,1)} %get-tuple-element.282), channel_id=1, source_target_pairs={{0,16},{2,18},{4,20},{6,22},{8,24},{10,26},{12,28},{14,30},{16,0},... | collective-permute-start | bytes 196616 | tf_op jit(solution)/shard_map/ppermute | solution.py:920
  552.8 61.3 %collective-permute-start.17 = (bf16[32,4096]{1,0:T(8,128)(2,1)}, bf16[32,4096]{1,0:T(8,128)(2,1)S(1)}, u32[]{:S(2)}, u32[]{:S(2)}) collective-permute-start(bf16[32,4096]{1,0:T(8,128)(2,1)} %get-tuple-element.278), channel_id=1, source_target_pairs={{0,16},{2,18},{4,20},{6,22},{8,24},{10,26},{12,28},{14,30},{16,0},... | collective-permute-start | bytes 786440 | tf_op jit(solution)/shard_map/ppermute | solution.py:920
  555.3 58.8 %collective-permute-start.18 = (bf16[128,1024]{1,0:T(8,128)(2,1)}, bf16[128,1024]{1,0:T(8,128)(2,1)S(1)}, u32[]{:S(2)}, u32[]{:S(2)}) collective-permute-start(bf16[128,1024]{1,0:T(8,128)(2,1)} %get-tuple-element.280), channel_id=1, source_target_pairs={{0,16},{2,18},{4,20},{6,22},{8,24},{10,26},{12,28},{14,30},{16,0},... | collective-permute-start | bytes 786440 | tf_op jit(solution)/shard_map/ppermute | solution.py:920
  651.7 5.8 collective-permute-start.22
  651.8 5.7 collective-permute-start.23
  663.5 18.1 %collective-permute-start.29 = (f32[40,128]{1,0:T(8,128)}, f32[40,128]{1,0:T(8,128)S(1)}, u32[]{:S(2)}, u32[]{:S(2)}) collective-permute-start(f32[40,128]{1,0:T(8,128)} %get-tuple-element.312.refs_12_), channel_id=1, source_target_pairs={{0,4},{2,6},{4,0},{6,2},{8,12},{10,14},{12,8},{14,10},{16,20},{18,... | collective-permute-start | bytes 61448 | tf_op jit(solution)/shard_map/ppermute | solution.py:920
  664.2 17.4 %collective-permute-start.26 = (bf16[256,1024]{1,0:T(8,128)(2,1)}, bf16[256,1024]{1,0:T(8,128)(2,1)S(1)}, u32[]{:S(2)}, u32[]{:S(2)}) collective-permute-start(bf16[256,1024]{1,0:T(8,128)(2,1)} %get-tuple-element.307), channel_id=1, source_target_pairs={{0,4},{2,6},{4,0},{6,2},{8,12},{10,14},{12,8},{14,10},{16,20},{18,... | collective-permute-start | bytes 1572872 | tf_op jit(solution)/shard_map/ppermute | solution.py:920
  665.5 16.0 %collective-permute-start.27 = (bf16[256,1024]{1,0:T(8,128)(2,1)}, bf16[256,1024]{1,0:T(8,128)(2,1)S(1)}, u32[]{:S(2)}, u32[]{:S(2)}) collective-permute-start(bf16[256,1024]{1,0:T(8,128)(2,1)} %get-tuple-element.309), channel_id=1, source_target_pairs={{0,1},{1,0},{2,3},{3,2},{4,5},{5,4},{6,7},{7,6},{8,9},{9,8},{10,11... | collective-permute-start | bytes 1572872 | tf_op jit(solution)/shard_map/ppermute | solution.py:920
  667.0 14.6 %collective-permute-start.28 = (bf16[256,1024]{1,0:T(8,128)(2,1)}, bf16[256,1024]{1,0:T(8,128)(2,1)S(1)}, u32[]{:S(2)}, u32[]{:S(2)}) collective-permute-start(bf16[256,1024]{1,0:T(8,128)(2,1)} %get-tuple-element.311), channel_id=1, source_target_pairs={{0,8},{2,10},{4,12},{6,14},{8,0},{10,2},{12,4},{14,6},{16,24},{18,... | collective-permute-start | bytes 1572872 | tf_op jit(solution)/shard_map/ppermute | solution.py:920
  686.5 18.8 %collective-permute-start.33 = (f32[40,128]{1,0:T(8,128)}, f32[40,128]{1,0:T(8,128)S(1)}, u32[]{:S(2)}, u32[]{:S(2)}) collective-permute-start(f32[40,128]{1,0:T(8,128)} %get-tuple-element.328.refs_12_), channel_id=1, source_target_pairs={{0,1},{1,0},{2,3},{3,2},{4,5},{5,4},{6,7},{7,6},{8,9},{9,8},{10,11... | collective-permute-start | bytes 61448 | tf_op jit(solution)/shard_map/ppermute | solution.py:920
  687.2 18.1 %collective-permute-start.30 = (bf16[128,1024]{1,0:T(8,128)(2,1)}, bf16[128,1024]{1,0:T(8,128)(2,1)S(1)}, u32[]{:S(2)}, u32[]{:S(2)}) collective-permute-start(bf16[128,1024]{1,0:T(8,128)(2,1)} %get-tuple-element.323), channel_id=1, source_target_pairs={{0,1},{1,0},{2,3},{3,2},{4,5},{5,4},{6,7},{7,6},{8,9},{9,8},{10,11... | collective-permute-start | bytes 786440 | tf_op jit(solution)/shard_map/ppermute | solution.py:920
  688.6 16.7 %collective-permute-start.31 = (bf16[128,1024]{1,0:T(8,128)(2,1)}, bf16[128,1024]{1,0:T(8,128)(2,1)S(1)}, u32[]{:S(2)}, u32[]{:S(2)}) collective-permute-start(bf16[128,1024]{1,0:T(8,128)(2,1)} %get-tuple-element.325), channel_id=1, source_target_pairs={{0,8},{2,10},{4,12},{6,14},{8,0},{10,2},{12,4},{14,6},{16,24},{18,... | collective-permute-start | bytes 786440 | tf_op jit(solution)/shard_map/ppermute | solution.py:920
  690.2 15.2 %collective-permute-start.32 = (bf16[128,1024]{1,0:T(8,128)(2,1)}, bf16[128,1024]{1,0:T(8,128)(2,1)S(1)}, u32[]{:S(2)}, u32[]{:S(2)}) collective-permute-start(bf16[128,1024]{1,0:T(8,128)(2,1)} %get-tuple-element.327), channel_id=1, source_target_pairs={{0,4},{2,6},{4,0},{6,2},{8,12},{10,14},{12,8},{14,10},{16,20},{18,... | collective-permute-start | bytes 786440 | tf_op jit(solution)/shard_map/ppermute | solution.py:920
  720.7 10.8 %collective-permute-start.41 = (f32[40,128]{1,0:T(8,128)}, f32[40,128]{1,0:T(8,128)S(1)}, u32[]{:S(2)}, u32[]{:S(2)}) collective-permute-start(f32[40,128]{1,0:T(8,128)} %get-tuple-element.367), channel_id=1, source_target_pairs={{0,16},{2,18},{4,20},{6,22},{8,24},{10,26},{12,28},{14,30},{16,0},... | collective-permute-start | bytes 61448 | tf_op jit(solution)/shard_map/ppermute | solution.py:920
  728.5 7.2 collective-permute-start.39
  (48 other events, 347.3 us)

commit v5 on v4

--- a/solution.py
+++ b/solution.py
@@ -40,7 +40,7 @@
     return worst <= REACH * REACH
 
 
-def fwd_chunk(fast, q0, k0, q_n, k_n, limit, qT, kT, vT, m_ref, l_ref, acc):
+def fwd_chunk(fast, q0, k0, q_n, k_n, limit, store, qT, kT, vT, m_ref, l_ref, acc):
     queries = pl.ds(q0, q_n)
     strip = min(256, k_n)
     for h in range(2):
@@ -64,7 +64,10 @@
             keys = pl.ds(k0 + j * strip, strip)
             weights = jnp.exp2(strips[j] if fast else strips[j] - new)
             total = total + jnp.sum(weights, axis=0, keepdims=True)
-            value = value + dot(vT[rows, keys], weights.astype(bf16), 1, 0)
+            weights = weights.astype(bf16)
+            if fast:
+                store(h, j, weights)
+            value = value + dot(vT[rows, keys], weights, 1, 0)
         m_ref[h : h + 1, queries] = new
         l_ref[h : h + 1, queries] = total
         acc[rows, queries] = value
@@ -82,7 +85,7 @@
     return jnp.concatenate([values, jnp.zeros((values.shape[0], count), f32)], axis=1)
 
 
-def fwd_diagonal(fast, base, group, limit, qT, kT, vT, m_ref, l_ref, acc):
+def fwd_diagonal(fast, base, group, limit, store, qT, kT, vT, m_ref, l_ref, acc):
     strip = min(256, group)
     count = group // strip
     for h in range(2):
@@ -115,7 +118,10 @@
             keys = pl.ds(base + j * strip, strip)
             weights = jnp.exp2(strips[j] if fast else strips[j] - peak[:, j * strip :])
             part = pad_left(jnp.sum(weights, axis=0, keepdims=True), j * strip)
-            term = pad_left(dot(vT[rows, keys], weights.astype(bf16), 1, 0), j * strip)
+            weights = weights.astype(bf16)
+            if fast:
+                store(h, j, weights)
+            term = pad_left(dot(vT[rows, keys], weights, 1, 0), j * strip)
             total = part if total is None else total + part
             value = term if value is None else value + term
         queries = pl.ds(base, group)
@@ -124,7 +130,24 @@
         acc[rows, queries] = value
 
 
-def fwd_local_kernel(group, info, qT, kT, vT, acc, m_ref, l_ref):
+def triangle_slot(i, j, group):
+    strip = min(256, group)
+    count = group // strip
+    row = jnp.where(i == 0, j, count - j) * strip
+    column = jnp.where(i == 0, j * strip, 0)
+    wide = group - j * strip
+    return (
+        pl.ds(pl.multiple_of(row, strip), strip),
+        pl.ds(pl.multiple_of(column, strip), wide),
+    )
+
+
+def square_slot(j, group):
+    strip = min(256, group)
+    return pl.ds(group + strip + j * strip, strip), slice(None)
+
+
+def fwd_local_kernel(group, info, qT, kT, vT, acc, m_ref, l_ref, kept, flags):
     length = info[1]
     m_ref[...] = jnp.full(m_ref.shape, NEG, f32)
     l_ref[...] = jnp.zeros(l_ref.shape, f32)
@@ -136,28 +159,37 @@
             base = pl.multiple_of(i * group, group)
             start = info[2 + i]
 
+            def store(h, j, weights):
+                rows, columns = triangle_slot(i, j, group)
+                kept[h, rows, columns] = weights
+
             @pl.when(start + group <= length)
             def _():
-                fwd_diagonal(fast, base, group, None, *refs)
+                fwd_diagonal(fast, base, group, None, store, *refs)
 
             @pl.when((start < length) & (start + group > length))
             def _():
-                fwd_diagonal(fast, base, group, length - start, *refs)
+                fwd_diagonal(fast, base, group, length - start, store, *refs)
 
             return carry
 
         lax.fori_loop(0, 2, own, 0)
         early = info[2]
 
+        def store(h, j, weights):
+            rows, columns = square_slot(j, group)
+            kept[h, rows, columns] = weights
+
         @pl.when(early + group <= length)
         def _():
-            fwd_chunk(fast, group, 0, group, group, None, *refs)
+            fwd_chunk(fast, group, 0, group, group, None, store, *refs)
 
         @pl.when((early < length) & (early + group > length))
         def _():
-            fwd_chunk(fast, group, 0, group, group, length - early, *refs)
+            fwd_chunk(fast, group, 0, group, group, length - early, store, *refs)
 
     small = bounded(qT, kT)
+    flags[pl.program_id(0)] = small.astype(jnp.int32)
     pl.when(small)(functools.partial(walk, True))
     pl.when(jnp.logical_not(small))(functools.partial(walk, False))
 
@@ -174,15 +206,16 @@
         wanted = jnp.where(turn_at == 0, before, jnp.where(late_key, 1 - before, 1)) == 1
         q0 = pl.multiple_of(jnp.where(turn_at == 0, 0, group), group)
         k0 = pl.multiple_of((2 * j + jnp.where(late_key, 1, 0)) * group, group)
+        slot = pl.multiple_of((2 * j + turn_at - (1 - before)) * group, group)
         start = block * group
 
         @pl.when(wanted & (start + group <= length))
         def _():
-            full(q0, k0)
+            full(q0, k0, slot)
 
         @pl.when(wanted & (start < length) & (start + group > length))
         def _():
-            partial(q0, k0, length - start)
+            partial(q0, k0, slot, length - start)
 
         return carry
 
@@ -190,23 +223,28 @@
 
 
 def fwd_remote_kernel(
-    group, parts, info, qT, kT, vT, acc_in, m_in, l_in, out, lse, acc, m_ref, l_ref
+    group, parts, info, qT, kT, vT, acc_in, m_in, l_in, out, lse, kept, flags, acc, m_ref, l_ref
 ):
     acc[...] = acc_in[...]
     m_ref[...] = m_in[0]
     l_ref[...] = l_in[0]
     refs = (qT, kT, vT, m_ref, l_ref, acc)
+    strip = min(256, group)
 
     def walk(fast):
-        def full(q0, k0):
-            fwd_chunk(fast, q0, k0, group, group, None, *refs)
-
-        def partial(q0, k0, limit):
-            fwd_chunk(fast, q0, k0, group, group, limit, *refs)
+        def partial(q0, k0, slot, limit):
+            def store(h, j, weights):
+                kept[h, pl.ds(pl.multiple_of(slot + j * strip, strip), strip), :] = weights
+
+            fwd_chunk(fast, q0, k0, group, group, limit, store, *refs)
+
+        def full(q0, k0, slot):
+            partial(q0, k0, slot, None)
 
         remote_steps(group, parts, info, full, partial)
 
     small = bounded(qT, kT) & (jnp.max(m_in[...]) <= 0.0)
+    flags[pl.program_id(0)] = small.astype(jnp.int32)
     pl.when(small)(functools.partial(walk, True))
     pl.when(jnp.logical_not(small))(functools.partial(walk, False))
     for h in range(2):
@@ -289,6 +327,24 @@
         dv[rows, here] += d_values
 
 
+def stored_prepare(doT, oT, lse, scaled, delta):
+    for h in range(2):
+        rows = slice(HEAD_DIM * h, HEAD_DIM * (h + 1))
+        grad = (doT[rows, :].astype(f32) * jnp.exp2(-lse[0, h : h + 1, :])).astype(bf16)
+        scaled[rows, :] = grad
+        delta[h : h + 1, :] = column_sum(grad.astype(f32) * oT[rows, :].astype(f32))
+
+
+def stored_chunk(h, weights, queries, keys, qT, kT, vT, scaled, delta, dq, dk, dv):
+    rows = slice(HEAD_DIM * h, HEAD_DIM * (h + 1))
+    d_probs = dot(vT[rows, keys], scaled[rows, queries], 0, 0)
+    d_scores = weights.astype(f32) * (d_probs - delta[h : h + 1, queries])
+    d_scores = d_scores.astype(bf16)
+    dv[rows, keys] += dot(scaled[rows, queries], weights, 1, 1)
+    dk[rows, keys] += dot(qT[rows, queries], d_scores, 1, 1)
+    dq[rows, queries] += dot(kT[rows, keys], d_scores, 1, 0)
+
+
 def turn_back(values, cosine, sine):
     half = HEAD_DIM // 2
     first, second = values[:half], values[half:]
@@ -297,22 +353,43 @@
     )
 
 
-def bwd_remote_kernel(group, parts, info, qT, doT, oT, lse, cosine, sine, kT, vT, *rest):
-    dq, dkv, *scratch = rest[-8:]
-    qa, da, ka, va, dk, dv = scratch
-    bwd_prepare(qT, kT, vT, doT, oT, lse, qa, da, ka, va)
+def bwd_remote_kernel(
+    group, parts, first, info, flags, qT, doT, oT, lse, cosine, sine, kT, vT, kept, *rest
+):
+    dq, dkv, qa, da, ka, va, dk, dv, scaled, delta = rest[-10:]
     dq[...] = jnp.zeros(dq.shape, f32)
     dk[...] = jnp.zeros(dk.shape, f32)
     dv[...] = jnp.zeros(dv.shape, f32)
-    refs = (qT, doT, qa, da, ka, va, dq, dk, dv)
-
-    def full(q0, k0):
-        bwd_chunk(q0, k0, group, group, None, *refs)
-
-    def partial(q0, k0, limit):
-        bwd_chunk(q0, k0, group, group, limit, *refs)
-
-    remote_steps(group, parts, info, full, partial)
+    fast = flags[first + pl.program_id(0)] == 1
+
+    @pl.when(fast)
+    def _():
+        stored_prepare(doT, oT, lse, scaled, delta)
+
+        def full(q0, k0, slot):
+            for h in range(2):
+                weights = kept[h, pl.ds(slot, group), :]
+                queries, keys = pl.ds(q0, group), pl.ds(k0, group)
+                stored_chunk(h, weights, queries, keys, qT, kT, vT, scaled, delta, dq, dk, dv)
+
+        def partial(q0, k0, slot, limit):
+            full(q0, k0, slot)
+
+        remote_steps(group, parts, info, full, partial)
+
+    @pl.when(jnp.logical_not(fast))
+    def _():
+        bwd_prepare(qT, kT, vT, doT, oT, lse, qa, da, ka, va)
+        refs = (qT, doT, qa, da, ka, va, dq, dk, dv)
+
+        def full(q0, k0, slot):
+            bwd_chunk(q0, k0, group, group, None, *refs)
+
+        def partial(q0, k0, slot, limit):
+            bwd_chunk(q0, k0, group, group, limit, *refs)
+
+        remote_steps(group, parts, info, full, partial)
+
     for h in range(2):
         rows = slice(HEAD_DIM * h, HEAD_DIM * (h + 1))
         dkv[1, rows, :] = turn_back(dk[rows, :] * LN2, cosine[...], sine[...]).astype(bf16)
@@ -320,40 +397,65 @@
     dkv[2] = dv[...].astype(bf16)
 
 
-def bwd_local_kernel(group, info, qT, doT, oT, lse, cosine, sine, kT, vT, dq_in, *rest):
-    dqkv, *scratch = rest[-8:]
-    qa, da, ka, va, dq, dk, dv = scratch
+def bwd_local_kernel(
+    group, first, info, flags, qT, doT, oT, lse, cosine, sine, kT, vT, dq_in, kept, *rest
+):
+    dqkv, qa, da, ka, va, dk, dv, scaled, delta, dq = rest[-10:]
     length = info[1]
-    bwd_prepare(qT, kT, vT, doT, oT, lse, qa, da, ka, va)
     dq[...] = dq_in[...]
     dk[...] = jnp.zeros(dk.shape, f32)
     dv[...] = jnp.zeros(dv.shape, f32)
-    refs = (qT, doT, qa, da, ka, va, dq, dk, dv)
-
-    def own(i, carry):
-        base = pl.multiple_of(i * group, group)
-        start = info[2 + i]
-
-        @pl.when(start + group <= length)
+    early = info[2]
+    strip = min(256, group)
+    fast = flags[first + pl.program_id(0)] == 1
+
+    @pl.when(fast)
+    def _():
+        stored_prepare(doT, oT, lse, scaled, delta)
+        refs = (qT, kT, vT, scaled, delta, dq, dk, dv)
+
+        def own(i, carry):
+            base = pl.multiple_of(i * group, group)
+
+            @pl.when(info[2 + i] < length)
+            def _():
+                for h in range(2):
+                    for j in range(group // strip):
+                        rows, columns = triangle_slot(i, j, group)
+                        queries = pl.ds(base + j * strip, group - j * strip)
+                        keys = pl.ds(base + j * strip, strip)
+                        stored_chunk(h, kept[h, rows, columns], queries, keys, *refs)
+
+            return carry
+
+        lax.fori_loop(0, 2, own, 0)
+
+        @pl.when(early < length)
         def _():
-            bwd_diagonal(base, group, None, *refs)
-
-        @pl.when((start < length) & (start + group > length))
+            for h in range(2):
+                weights = kept[h, group + strip :, :]
+                stored_chunk(h, weights, pl.ds(group, group), pl.ds(0, group), *refs)
+
+    @pl.when(jnp.logical_not(fast))
+    def _():
+        bwd_prepare(qT, kT, vT, doT, oT, lse, qa, da, ka, va)
+        refs = (qT, doT, qa, da, ka, va, dq, dk, dv)
+
+        def own(i, carry):
+            base = pl.multiple_of(i * group, group)
+            start = info[2 + i]
+
+            @pl.when(start < length)
+            def _():
+                bwd_diagonal(base, group, length - start, *refs)
+
+            return carry
+
+        lax.fori_loop(0, 2, own, 0)
+
+        @pl.when(early < length)
         def _():
-            bwd_diagonal(base, group, length - start, *refs)
-
-        return carry
-
-    lax.fori_loop(0, 2, own, 0)
-    early = info[2]
-
-    @pl.when(early + group <= length)
-    def _():
-        bwd_chunk(group, 0, group, group, None, *refs)
-
-    @pl.when((early < length) & (early + group > length))
-    def _():
-        bwd_chunk(group, 0, group, group, length - early, *refs)
+            bwd_chunk(group, 0, group, group, length - early, *refs)
 
     for h in range(2):
         rows = slice(HEAD_DIM * h, HEAD_DIM * (h + 1))
@@ -364,26 +466,34 @@
 
 
 def rows_of(count, first=0):
-    return pl.BlockSpec((PAIR, count), lambda i, info: (first + i, 0))
+    return pl.BlockSpec((PAIR, count), lambda i, *info: (first + i, 0))
 
 
 def stats_of(count, first=0):
-    return pl.BlockSpec((1, 2, count), lambda i, info: (first + i, 0, 0))
+    return pl.BlockSpec((1, 2, count), lambda i, *info: (first + i, 0, 0))
 
 
 def planes_of(planes, count, first=0):
-    return pl.BlockSpec((planes, PAIR, count), lambda i, info: (0, first + i, 0))
+    return pl.BlockSpec((planes, PAIR, count), lambda i, *info: (0, first + i, 0))
+
+
+def kept_of(rows, group, first=0):
+    return pl.BlockSpec((2, rows, group), lambda i, *info: (first + i, 0, 0))
+
+
+def scalars():
+    return pl.BlockSpec(memory_space=pltpu.SMEM)
 
 
 def whole(shape):
-    return pl.BlockSpec(shape, lambda i, info: (0,) * len(shape))
-
-
-def attention_call(kernel, pairs, in_specs, out_specs, out_shape, scratch, flops, name, alias={}):
+    return pl.BlockSpec(shape, lambda i, *info: (0,) * len(shape))
+
+
+def attention_call(kernel, pairs, in_specs, out_specs, out_shape, scratch, flops, name, alias={}, prefetch=1):
     return pl.pallas_call(
         kernel,
         grid_spec=pltpu.PrefetchScalarGridSpec(
-            num_scalar_prefetch=1,
+            num_scalar_prefetch=prefetch,
             grid=(pairs,),
             in_specs=in_specs,
             out_specs=out_specs,
@@ -402,21 +512,25 @@
 def attend_local(info, qT, kT, vT, group):
     width, n_q = qT.shape
     pairs = width // PAIR
+    kept_rows = 2 * group + min(256, group)
     call = attention_call(
         functools.partial(fwd_local_kernel, group),
         pairs,
         [rows_of(n_q)] * 3,
-        [rows_of(n_q), stats_of(n_q), stats_of(n_q)],
+        [rows_of(n_q), stats_of(n_q), stats_of(n_q), kept_of(kept_rows, group), scalars()],
         [
             jax.ShapeDtypeStruct((width, n_q), f32),
             jax.ShapeDtypeStruct((pairs, 2, n_q), f32),
             jax.ShapeDtypeStruct((pairs, 2, n_q), f32),
+            jax.ShapeDtypeStruct((2 * pairs, kept_rows, group), bf16),
+            jax.ShapeDtypeStruct((pairs,), jnp.int32),
         ],
         [],
         4 * width * 2 * group * group * 4,
         "attend_local",
     )
-    return call(info, qT, kT, vT)
+    *state, kept, flags = call(info, qT, kT, vT)
+    return state, kept, flags
 
 
 def attend_remote(info, qT, kT, vT, state, group, parts):
@@ -427,10 +541,12 @@
         functools.partial(fwd_remote_kernel, group, parts),
         pairs,
         [rows_of(n_q), rows_of(n_k), rows_of(n_k), rows_of(n_q), stats_of(n_q), stats_of(n_q)],
-        [rows_of(n_q), stats_of(n_q)],
+        [rows_of(n_q), stats_of(n_q), kept_of(n_k, group), scalars()],
         [
             jax.ShapeDtypeStruct((width, n_q), bf16),
             jax.ShapeDtypeStruct((pairs, 2, n_q), f32),
+            jax.ShapeDtypeStruct((2 * pairs, n_k, group), bf16),
+            jax.ShapeDtypeStruct((pairs,), jnp.int32),
         ],
         [pltpu.VMEM((PAIR, n_q), f32)] + [pltpu.VMEM((2, n_q), f32)] * 2,
         4 * width * 2 * group * group * 4,
@@ -441,60 +557,64 @@
 
 def back_scratch(n_q, n_k):
     rows = HEAD_DIM + 16
-    return [
-        pltpu.VMEM((2, rows, n_q), bf16),
-        pltpu.VMEM((2, rows, n_q), bf16),
-        pltpu.VMEM((2, rows, n_k), bf16),
-        pltpu.VMEM((2, rows, n_k), bf16),
-    ]
-
-
-def back_remote(info, operands, turns, keys, group, parts, first, count, before):
+    return (
+        [pltpu.VMEM((2, rows, n_q), bf16)] * 2
+        + [pltpu.VMEM((2, rows, n_k), bf16)] * 2
+        + [pltpu.VMEM((PAIR, n_k), f32)] * 2
+        + [pltpu.VMEM((PAIR, n_q), bf16), pltpu.VMEM((2, n_q), f32)]
+    )
+
+
+def back_remote(info, flags, operands, turns, keys, kept, group, parts, first, count, before):
     width, n_q = operands[0].shape
     n_k = keys[0].shape[1]
     half = HEAD_DIM // 2
-    n_in = 1 + len(operands) + len(turns) + len(keys)
+    n_in = 2 + len(operands) + len(turns) + len(keys) + 1
     call = attention_call(
-        functools.partial(bwd_remote_kernel, group, parts),
+        functools.partial(bwd_remote_kernel, group, parts, first),
         count,
         [rows_of(n_q, first)] * 3
         + [stats_of(n_q, first)]
         + [whole((half, n_k))] * 2
         + [rows_of(n_k, first)] * 2
+        + [kept_of(kept.shape[1], group, first)]
         + [pl.BlockSpec(memory_space=pl.ANY)] * len(before),
         [rows_of(n_q, first), planes_of(3, n_k, first)],
         [
             jax.ShapeDtypeStruct((width, n_q), f32),
             jax.ShapeDtypeStruct((3, width, n_k), bf16),
         ],
-        back_scratch(n_q, n_k) + [pltpu.VMEM((PAIR, n_k), f32)] * 2,
+        back_scratch(n_q, n_k),
         10 * count * PAIR * 2 * group * group * 4,
         "back_remote",
         {n_in + i: i for i in range(len(before))},
-    )
-    return call(info, *operands, *turns, *keys, *before)
-
-
-def back_local(info, operands, turns, keys, dq, group, first, count, before):
+        2,
+    )
+    return call(info, flags, *operands, *turns, *keys, kept, *before)
+
+
+def back_local(info, flags, operands, turns, keys, dq, kept, group, first, count, before):
     width, n_q = operands[0].shape
     half = HEAD_DIM // 2
-    n_in = 1 + len(operands) + len(turns) + len(keys) + 1
+    n_in = 2 + len(operands) + len(turns) + len(keys) + 2
     call = attention_call(
-        functools.partial(bwd_local_kernel, group),
+        functools.partial(bwd_local_kernel, group, first),
         count,
         [rows_of(n_q, first)] * 3
         + [stats_of(n_q, first)]
         + [whole((half, n_q))] * 2
         + [rows_of(n_q, first)] * 3
+        + [kept_of(kept.shape[1], group, first)]
         + [pl.BlockSpec(memory_space=pl.ANY)] * len(before),
         planes_of(3, n_q, first),
         jax.ShapeDtypeStruct((3, width, n_q), bf16),
-        back_scratch(n_q, n_q) + [pltpu.VMEM((PAIR, n_q), f32)] * 3,
+        back_scratch(n_q, n_q) + [pltpu.VMEM((PAIR, n_q), f32)],
         10 * count * PAIR * 2 * group * group * 4,
         "back_local",
         {n_in + i: i for i in range(len(before))},
-    )
-    return call(info, *operands, *turns, *keys, dq, *before)
+        2,
+    )
+    return call(info, flags, *operands, *turns, *keys, dq, kept, *before)
 
 
 def normalize(values):
@@ -1018,6 +1138,107 @@
     )(*operands)
 
 
+def read_small(ref, at, rows):
+    parts = [ref[at + i * rows : at + (i + 1) * rows, :].astype(f32) for i in range(3)]
+    return parts[0] + parts[1] + parts[2]
+
+
+def joint_kernel(plan, last, *refs):
+    count, buffers, from_at, small_from, to_at, small_to, rows = plan
+    arrays, refs = refs[:count], refs[count:]
+    received, refs = refs[:buffers], refs[buffers:]
+    small, refs = refs[0], refs[1:]
+    if small_from is None:
+        total = small[...] + refs[0][...]
+        refs = refs[1:]
+    else:
+        total = small[...] + read_small(received[small_from[0]], small_from[1], rows)
+    if last:
+        out, small_out = refs
+        for i in range(count):
+            which, at = from_at[i]
+            height = arrays[i].shape[0]
+            part = received[which][at : at + height, :].astype(f32)
+            out[i * height : (i + 1) * height, :] = arrays[i][...].astype(f32) + part
+        small_out[...] = total
+        return
+    outs, sent, small_out = refs[:count], refs[count:-1], refs[-1]
+    for i in range(count):
+        which, at = from_at[i]
+        height = arrays[i].shape[0] // 2
+        for half in range(2):
+            here = slice(half * height, (half + 1) * height)
+            there = slice(at + half * height, at + (half + 1) * height)
+            part = arrays[i][here, :].astype(f32) + received[which][there, :].astype(f32)
+            if half:
+                which_out, at_out = to_at[i]
+                sent[which_out][at_out : at_out + height, :] = part.astype(bf16)
+            else:
+                outs[i][...] = part.astype(bf16)
+    small_out[...] = total
+    which_out, at_out = small_to
+    for part in split_three(total):
+        sent[which_out][at_out : at_out + rows, :] = part.astype(bf16)
+        at_out += rows
+
+
+class Joint:
+    def __init__(self, halves, orders, small):
+        self.arrays = [kept for kept, _ in halves]
+        self.received = [swap(given, "wide", 0) for _, given in halves]
+        self.from_at = [(i, 0) for i in range(len(halves))]
+        self.orders = [list(order) for order in orders]
+        self.small, self.small_from = small, None
+        self.extra = [swap(small, "wide", 0)]
+
+    def call(self, plan, last, shapes):
+        return pl.pallas_call(
+            functools.partial(joint_kernel, plan, last),
+            out_shape=shapes,
+            compiler_params=pltpu.CompilerParams(vmem_limit_bytes=VMEM),
+            name="joint",
+        )(*self.arrays, *self.received, self.small, *self.extra)
+
+    def plan(self, to_at, small_to):
+        buffers, rows = len(self.received), self.small.shape[0]
+        count = len(self.arrays)
+        return count, buffers, self.from_at, self.small_from, to_at, small_to, rows
+
+    def step(self, lead, *others):
+        bits, heights, to_at = [], [], []
+        width = self.arrays[0].shape[1]
+        for array, order in zip(self.arrays, self.orders):
+            bit = order.pop(0)
+            if bit not in bits:
+                bits.append(bit)
+                heights.append(0)
+            which = bits.index(bit)
+            to_at.append((which, heights[which]))
+            heights[which] += array.shape[0] // 2
+        small_to = (0, heights[0])
+        heights[0] += 3 * self.small.shape[0]
+        shapes = [
+            jax.ShapeDtypeStruct((array.shape[0] // 2, width), bf16) for array in self.arrays
+        ]
+        shapes += [jax.ShapeDtypeStruct((height, width), bf16) for height in heights]
+        shapes += [jax.ShapeDtypeStruct(self.small.shape, f32)]
+        outs = self.call(self.plan(to_at, small_to), False, shapes)
+        lead, others, outs = lax.optimization_barrier((lead, others, outs))
+        count = len(self.arrays)
+        self.arrays, sent, self.small = outs[:count], outs[count:-1], outs[-1]
+        self.received = [swap(item, *bit) for item, bit in zip(sent, bits)]
+        self.from_at, self.small_from, self.extra = to_at, small_to, []
+        return (lead, *others)
+
+    def result(self):
+        height = sum(array.shape[0] for array in self.arrays)
+        shapes = [
+            jax.ShapeDtypeStruct((height, self.arrays[0].shape[1]), f32),
+            jax.ShapeDtypeStruct(self.small.shape, f32),
+        ]
+        return self.call(self.plan([], None), True, shapes)
+
+
 def angles(positions):
     half = HEAD_DIM // 2
     freqs = jnp.power(10000.0, -jnp.arange(half, dtype=f32) / half)
@@ -1086,11 +1307,13 @@
 
     norm_one = [row(gain_one), row(shift_one)]
     normed, qT, kT, vT = project(tokens, w_qkv, row(b_qkv), *norm_one, *turns, (0, 1, 2))
-    state = attend_local(info, qT, kT, vT, group)
+    state, kept_own, flags_own = attend_local(info, qT, kT, vT, group)
     normed_far, kT_far, vT_far = project(
         far_tokens, w_qkv, row(b_qkv), *norm_one, *turns_far, (1, 2)
     )
-    oT, lse = attend_remote(info, qT, kT_far, vT_far, state, group, parts)
+    oT, lse, kept_far, flags_far = attend_remote(
+        info, qT, kT_far, vT_far, state, group, parts
+    )
 
     blocks = block_call(
         oT,
@@ -1129,9 +1352,11 @@
         (doT,) = launch(doT, sums, early)
         far = back_remote(
             info,
+            flags_far,
             [qT, doT, oT, lse],
             turns_far,
             [kT_far, vT_far],
+            kept_far,
             group,
             parts,
             portion * count,
@@ -1155,10 +1380,12 @@
         d_mixed = [
             back_local(
                 info,
+                flags_own,
                 [qT, doT, oT, lse],
                 turns,
                 [kT, vT],
                 dq_far,
+                kept_own,
                 group,
                 portion * count,
                 count,
@@ -1185,29 +1412,32 @@
         parts,
         orders,
     )
-    pieces = [Halving(halves, order) for halves, order in zip(pieces, orders)]
     part_shift = weighted[1]
     part_gain = (weighted[0] - shift_one * part_shift) / gain_one
-    flat = jnp.concatenate([bias.reshape(-1), part_gain, part_shift])
-    late = Adding(flat.reshape(-1, PAIR), small_order)
-    sum_w_down, sum_w_up, sum_w_out = collect([[item] for item in sums])
-    (d_mixed,) = launch(d_mixed, pieces, late)
+    flat = jnp.concatenate(
+        [bias.reshape(-1), part_gain, part_shift, jnp.zeros((11 * width,), f32)]
+    )
+    tail = Joint(pieces, orders, flat.reshape(16, width))
+    (d_mixed,) = tail.step(d_mixed)
     d_tokens = []
     for i in range(2):
         finish = (returned[0], tokens, d_middle, row(gain_one))
         d_tokens = [
             unproject(d_mixed, w_qkv, (0, 1, 2), i * group, group, finish, d_tokens)
         ]
-        if late.order:
-            d_mixed, d_tokens[0] = launch(d_mixed, pieces, late, d_tokens[0])
-    while late.order:
-        (d_tokens[0],) = launch(d_tokens[0], pieces, late)
-
-    (sum_w_qkv,) = collect([pieces])
+        if tail.orders[0]:
+            d_mixed, d_tokens[0] = tail.step(d_mixed, d_tokens[0])
+    while tail.orders[0]:
+        d_tokens[0], *terms = tail.step(d_tokens[0], *[item.terms for item in sums])
+        for item, arrays in zip(sums, terms):
+            item.terms = list(arrays)
+
+    sum_w_down, sum_w_up, sum_w_out = collect([[item] for item in sums])
+    sum_w_qkv, late_small = tail.result()
+    late_small = late_small.reshape(-1)[: 5 * width]
     early_small = (early.terms[0] + early.terms[1]).reshape(-1)
     small = early_small[: 8 * width].reshape(8, width)
     small_up = early_small[8 * width :]
-    late_small = (late.terms[0] + late.terms[1]).reshape(-1)
     shape = inputs.shape
     return (
         result.reshape(shape),

time: 745 us -> 731 us (0.981)
  Pallas kernels: 634 us -> 556 us
  starting transfers between devices: 44.3 us -> 85.7 us
  waiting for transfers between devices: 39.3 us -> 58.2 us
    pallas_call x5 -> x10, Pallas kernels: 257 us -> 199 us  [the longest x2 80.5 us: back_local(): return call(info, flags, *operands, *turns, *keys, dq, kept, *before)]
    ppermute x40 -> x34, waiting for transfers between devices: 18.6 us -> 42.8 us  [swap(): lax.ppermute(values, axis, [(i, i ^ 1 << position) for i in range(size)])]
    ppermute x40 -> x34, starting transfers between devices: 40.8 us -> 63.5 us  [swap(): lax.ppermute(values, axis, [(i, i ^ 1 << position) for i in range(size)])]
    ppermute x1, starting transfers between devices: 0.53 us -> 19.1 us  [body(): lax.ppermute(d_back[j * rows:(j + 1) * rows] if others > 1 else d_back, '...]
    pallas_call x8 -> x4, Pallas kernels: 39.1 us -> 24.6 us  [halve(): pl.pallas_call(functools.partial(halve_kernel, len(sums)), grid=(grid,),...]
  transfers between devices with their start and end apart: 42 -> 36, of which waited for: 12 -> 9; matrix products, arithmetic and copies ran while one was open for 2% -> 1% of each run, Pallas kernels for 49% -> 40%
where the time goes in v5:
time: 731 us; the launch traced here: 725 us
  Pallas kernels  556 us (76%)
  starting transfers between devices  85.7 us (12%)
  waiting for transfers between devices  58.2 us (8%)
  local copies, waits for them, and re-layouts  16.7 us (2%)
    pallas_call x1, Pallas kernels, block_call(): pl.pallas_call(functools.partial(block_kernel, span), grid=(rows // step,...  116 us
    pallas_call x2, Pallas kernels, back_local(): return call(info, flags, *operands, *turns, *keys, dq, kept, *before)  80.5 us
    ppermute x34, starting transfers between devices, swap(): lax.ppermute(values, axis, [(i, i ^ 1 << position) for i in range(size)])  63.5 us
    pallas_call x3, Pallas kernels, outer_halves(): pl.pallas_call(functools.partial(outer_kernel, run, levels, near, [order]...  59.5 us
    pallas_call x2, Pallas kernels, back_remote(): return call(info, flags, *operands, *turns, *keys, kept, *before)  56.4 us
    pallas_call x1, Pallas kernels, attend_local(): *state, kept, flags = call(info, qT, kT, vT)  48.3 us
    pallas_call x3, Pallas kernels, unproject(): pl.pallas_call(functools.partial(unproject_kernel, planes, bool(finish)),...  43 us
    ppermute x34, waiting for transfers between devices, swap(): lax.ppermute(values, axis, [(i, i ^ 1 << position) for i in range(size)])  42.8 us
  transfers between devices with their start and end apart: 36, of which 9 were waited for; matrix products, arithmetic and copies ran while one was open for 1% of the time, Pallas kernels for 40%

profile of v5, /device:TPU:0, one launch (start us, length us, event | category | flops | bytes accessed | tf_op | source)
XLA Modules:
  0.0 725.0 jit_solution(8212803508987818204)
XLA Ops:
  0.7 3.0 collective-permute-start
  8.6 22.3 %project.2 = (bf16[2048,1024]{1,0:T(8,128)(2,1)}, bf16[1024,2048]{1,0:T(8,128)(2,1)}, bf16[1024,2048]{1,0:T(8,128)(2,1)}, bf16[1024,2048]{1,0:T(8,128)(2,1)}) custom-call(bf16[2048,1024]{1,0:T(8,128)(2,1)} %bitcast.112, bf16[1024,3072]{1,0:T(8,128)(2,1)} %refs_3_.3, f32[1,3072]{1,0:T(1,128)} %bitcast.184, f32[1,1024]{1,0:T(1,128)} %bitcast.160, ...), custom_call_target="tpu_custom_call" | custom-call | flops 12884901888 | bytes 16777216 | tf_op jit(solution)/shard_map/project/pallas_call | solution.py:812
  30.8 48.3 %attend_local.1 = (f32[1024,2048]{1,0:T(8,128)}, f32[8,2,2048]{2,1,0:T(2,128)}, f32[8,2,2048]{2,1,0:T(2,128)}, bf16[16,2304,1024]{2,1,0:T(8,128)(2,1)}, s32[8]{0:T(128)}) custom-call(s32[4]{0:T(128)} %pad_add_fusion.info, bf16[1024,2048]{1,0:T(8,128)(2,1)} %get-tuple-element.202.qT, bf16[1024,2048]{1,0:T(8,128)(2,1)} %get-tuple-element.205.kT, ...), custom_call_target="tpu_custom_call" | custom-call | flops 34359738368 | bytes 33554432 | tf_op jit(solution)/shard_map/attend_local/pallas_call | solution.py:532
  79.1 15.5 %collective-permute-done.tokens = bf16[2048,1024]{1,0:T(8,128)(2,1)} collective-permute-done((bf16[2048,1024]{1,0:T(8,128)(2,1)}, bf16[2048,1024]{1,0:T(8,128)(2,1)}, u32[]{:S(2)}, u32[]{:S(2)}) %collective-permute-start) | collective-permute-done | bytes 4194336 | tf_op jit(solution)/shard_map/ppermute | solution.py:1296
  94.6 17.1 %project.3 = (bf16[2048,1024]{1,0:T(8,128)(2,1)}, bf16[1024,2048]{1,0:T(8,128)(2,1)}, bf16[1024,2048]{1,0:T(8,128)(2,1)}) custom-call(bf16[2048,1024]{1,0:T(8,128)(2,1)} %collective-permute-done.tokens, bf16[1024,3072]{1,0:T(8,128)(2,1)} %refs_3_.3, f32[1,3072]{1,0:T(1,128)} %bitcast.185, f32[1,1024]{1,0:T(1,128)} %bitcast.161, f32[1,1024]{1,0:T(1,128)} %bitcast.170, ...), custom_call_target="tpu_custom_call" | custom-call | flops 8589934592 | bytes 16777216 | tf_op jit(solution)/shard_map/project/pallas_call | solution.py:812
  111.7 34.4 %attend_remote.1 = (bf16[1024,2048]{1,0:T(8,128)(2,1)}, f32[8,2,2048]{2,1,0:T(2,128)}, bf16[16,2048,1024]{2,1,0:T(8,128)(2,1)}, s32[8]{0:T(128)}) custom-call(s32[4]{0:T(128)} %pad_add_fusion.info, bf16[1024,2048]{1,0:T(8,128)(2,1)} %get-tuple-element.202.qT, bf16[1024,2048]{1,0:T(8,128)(2,1)} %get-tuple-element.203.kT, ...), custom_call_target="tpu_custom_call" | custom-call | flops 34359738368 | bytes 33554432 | tf_op jit(solution)/shard_map/attend_remote/pallas_call | solution.py:555
  146.0 116.2 %block.1 = (bf16[2048,1024]{1,0:T(8,128)(2,1)}, f32[2048,1024]{1,0:T(8,128)}, bf16[2048,4096]{1,0:T(8,128)(2,1)}, bf16[2048,1024]{1,0:T(8,128)(2,1)}, bf16[2048,...) custom-call(bf16[1024,2048]{1,0:T(8,128)(2,1)} %get-tuple-element.21, ...), custom_call_target="tpu_custom_call" | custom-call | flops 77309411328 | bytes 67108864 | tf_op jit(solution)/shard_map/block/pallas_call | solution.py:747
  262.2 24.6 %outer.4 = (bf16[2,2,2,2,128,1024]{5,4,3,2,1,0:T(8,128)(2,1)}, bf16[2,2,2,2,128,1024]{5,4,3,2,1,0:T(8,128)(2,1)}) custom-call(s32[2]{0:T(128)} %pad_add_fusion.1.marks, bf16[2048,4096]{1,0:T(8,128)(2,1)} %get-tuple-element.218.left, bf16[2048,1024]{1,0:T(8,128)(2,1)} %get-tuple-element.219.right), custom_call_target="tpu_custom_call" | custom-call | flops 17179869184 | bytes 33554432 | tf_op jit(solution)/shard_map/outer/pallas_call | solution.py:939
  286.8 7.3 %collective-permute-start.2 = (bf16[2048,1024]{1,0:T(8,128)(2,1)}, bf16[2048,1024]{1,0:T(8,128)(2,1)}, u32[]{:S(2)}, u32[]{:S(2)}) collective-permute-start(bf16[2048,1024]{1,0:T(8,128)(2,1)} %bitcast.174), channel_id=1, source_target_pairs={{0,2},{2,0},{4,6},{6,4},{8,10},{10,8},{12,14},{14,12},{16,18},{18,... | collective-permute-start | bytes 12582920 | tf_op jit(solution)/shard_map/ppermute | solution.py:1040
  294.2 24.6 %outer.3 = (bf16[2,2,2,2,32,4096]{5,4,3,2,1,0:T(8,128)(2,1)}, bf16[2,2,2,2,32,4096]{5,4,3,2,1,0:T(8,128)(2,1)}) custom-call(s32[2]{0:T(128)} %pad_add_fusion.1.marks, bf16[2048,1024]{1,0:T(8,128)(2,1)} %get-tuple-element.214.left, bf16[2048,4096]{1,0:T(8,128)(2,1)} %get-tuple-element.215.right), custom_call_target="tpu_custom_call" | custom-call | flops 17179869184 | bytes 33554432 | tf_op jit(solution)/shard_map/outer/pallas_call | solution.py:939
  318.8 10.3 %outer.5 = (bf16[2,2,2,2,32,1024]{5,4,3,2,1,0:T(8,128)(2,1)}, bf16[2,2,2,2,32,1024]{5,4,3,2,1,0:T(8,128)(2,1)}) custom-call(s32[2]{0:T(128)} %pad_add_fusion.1.marks, bf16[2048,1024]{1,0:T(8,128)(2,1)} %get-tuple-element.222.left, bf16[1024,2048]{1,0:T(8,128)(2,1)} %get-tuple-element.210.oT.right), custom_call_target="tpu_custom_call" | custom-call | flops 4294967296 | bytes 33554432 | tf_op jit(solution)/shard_map/outer/pallas_call | solution.py:939
  333.1 10.8 %halve.4 = (bf16[256,4096]{1,0:T(8,128)(2,1)}, bf16[256,4096]{1,0:T(8,128)(2,1)}, bf16[1024,1024]{1,0:T(8,128)(2,1)}, bf16[1024,1024]{1,0:T(8,128)(2,1)}, bf16[2...) custom-call(bf16[2,256,4096]{2,1,0:T(8,128)(2,1)} %bitcast.119, ...), custom_call_target="tpu_custom_call" | custom-call | tf_op jit(solution)/shard_map/halve/pallas_call | solution.py:1086
  343.9 2.9 collective-permute-start.5
  350.3 28.1 %back_remote.2 = (f32[1024,2048]{1,0:T(8,128)}, bf16[3,1024,2048]{2,1,0:T(8,128)(2,1)}) custom-call(s32[4]{0:T(128)} %pad_add_fusion.info, s32[8]{0:T(128)} %get-tuple-element.250.flags, bf16[1024,2048]{1,0:T(8,128)(2,1)} %get-tuple-element.202.qT, bf16[1024,2048]{1,0:T(8,128)(2,1)} %get-tuple-element.286.doT, ...), custom_call_target="tpu_custom_call" | custom-call | flops 42949672960 | bytes 33554432 | tf_op jit(solution)/shard_map/back_remote/pallas_call | solution.py:593
  378.5 28.2 %collective-permute-done.8.refs_13_ = f32[96,128]{1,0:T(8,128)S(1)} collective-permute-done((f32[96,128]{1,0:T(8,128)}, f32[96,128]{1,0:T(8,128)S(1)}, u32[]{:S(2)}, u32[]{:S(2)}) %collective-permute-start.8) | collective-permute-done | bytes 49184 | tf_op jit(solution)/shard_map/ppermute | solution.py:1040
  407.5 6.6 halve.5
  418.2 28.3 %back_remote.3 = (f32[1024,2048]{1,0:T(8,128)}, bf16[3,1024,2048]{2,1,0:T(8,128)(2,1)}) custom-call(s32[4]{0:T(128)} %pad_add_fusion.info, s32[8]{0:T(128)} %get-tuple-element.250.flags, bf16[1024,2048]{1,0:T(8,128)(2,1)} %get-tuple-element.202.qT, bf16[1024,2048]{1,0:T(8,128)(2,1)} %get-tuple-element.286.doT, ...), custom_call_target="tpu_custom_call", output_to_operand_aliasing={{0}: (11, {}), {1}: (12, {})} | custom-call | flops 42949672960 | bytes 33554432 | tf_op jit(solution)/shard_map/back_remote/pallas_call | solution.py:593
  446.5 14.7 %unproject.3 = bf16[2048,1024]{1,0:T(8,128)(2,1)} custom-call(bf16[3,1024,2048]{2,1,0:T(8,128)(2,1)} %get-tuple-element.255.refs_0_.refs_1_, bf16[3,1024,2048]{2,1,0:T(8,128)(2,1)} %get-tuple-element.255.refs_0_.refs_1_, bf16[1024,3072]{1,0:T(8,128)(2,1)} %refs_3_.3), custom_call_target="tpu_custom_call" | custom-call | flops 8589934592 | bytes 16777216 | tf_op jit(solution)/shard_map/unproject/pallas_call | solution.py:861
  462.2 4.6 halve.6
  470.9 19.1 %collective-permute-start.21 = (bf16[2048,1024]{1,0:T(8,128)(2,1)}, bf16[2048,1024]{1,0:T(8,128)(2,1)}, u32[]{:S(2)}, u32[]{:S(2)}) collective-permute-start(bf16[2048,1024]{1,0:T(8,128)(2,1)} %unproject.3), channel_id=1, source_target_pairs={{0,1},{1,0},{2,3},{3,2},{4,5},{5,4},{6,7},{7,6},{8,9},{9,8},{10,11... | collective-permute-start | bytes 12582920 | tf_op jit(solution)/shard_map/ppermute | solution.py:1373
  490.0 40.1 %back_local.2.rest_0_ = bf16[3,1024,2048]{2,1,0:T(8,128)(2,1)} custom-call(s32[4]{0:T(128)} %pad_add_fusion.info, s32[8]{0:T(128)} %get-tuple-element.212.flags, bf16[1024,2048]{1,0:T(8,128)(2,1)} %get-tuple-element.202.qT, bf16[1024,2048]{1,0:T(8,128)(2,1)} %get-tuple-element.286.doT, bf16[1024,2048]{1,0:T(8,128)(2,1)} %get-tuple-element.210.oT.right, ...), custom_call_target="tpu_custom_call" | custom-call | flops 42949672960 | bytes 33554432 | tf_op jit(solution)/shard_map/back_local/pallas_call | solution.py:617
  533.8 13.6 %collective-permute-start.17 = (bf16[32,4096]{1,0:T(8,128)(2,1)}, bf16[32,4096]{1,0:T(8,128)(2,1)S(1)}, u32[]{:S(2)}, u32[]{:S(2)}) collective-permute-start(bf16[32,4096]{1,0:T(8,128)(2,1)} %get-tuple-element.290), channel_id=1, source_target_pairs={{0,16},{2,18},{4,20},{6,22},{8,24},{10,26},{12,28},{14,30},{16,0},... | collective-permute-start | bytes 786440 | tf_op jit(solution)/shard_map/ppermute | solution.py:1040
  550.4 40.4 %back_local.3.refs_0_.refs_1_.refs_2_ = bf16[3,1024,2048]{2,1,0:T(8,128)(2,1)} custom-call(s32[4]{0:T(128)} %pad_add_fusion.info, s32[8]{0:T(128)} %get-tuple-element.212.flags, bf16[1024,2048]{1,0:T(8,128)(2,1)} %get-tuple-element.202.qT, bf16[1024,2048]{1,0:T(8,128)(2,1)} %get-tuple-element.286.doT, ...), custom_call_target="tpu_custom_call", output_to_operand_aliasing={{}: (12, {})} | custom-call | flops 42949672960 | bytes 33554432 | tf_op jit(solution)/shard_map/back_local/pallas_call | solution.py:617
  590.9 37.5 %mixed.1 = (bf16[2,2,2,2,32,1024]{5,4,3,2,1,0:T(8,128)(2,1)}, bf16[2,2,2,2,32,1024]{5,4,3,2,1,0:T(8,128)(2,1)}, bf16[2,2,2,2,32,1024]{5,4,3,2,1,0:T(8,128)(2,1)}...) custom-call(s32[2]{0:T(128)} %pad_add_fusion.1.marks, ...), custom_call_target="tpu_custom_call" | custom-call | flops 25769803776 | bytes 33554432 | tf_op jit(solution)/shard_map/mixed/pallas_call | solution.py:1001
  628.5 6.6 collective-permute-start.22
  641.5 4.8 joint.5
  646.3 6.1 collective-permute-start.26
  654.3 14.3 %unproject.4.refs_8_ = bf16[2048,1024]{1,0:T(8,128)(2,1)} custom-call(bf16[3,1024,2048]{2,1,0:T(8,128)(2,1)} %back_local.3.refs_0_.refs_1_.refs_2_, bf16[3,1024,2048]{2,1,0:T(8,128)(2,1)} %back_local.3.refs_0_.refs_1_.refs_2_, bf16[3,1024,2048]{2,1,0:T(8,128)(2,1)} %back_local.3.refs_0_.refs_1_.refs_2_, bf16[1024,3072]{1,0:T(8,128)(2,1)} %refs_3_.3, ...), custom_call_target="tpu_custom_call" | custom-call | flops 6442450944 | bytes 16777216 | tf_op jit(solution)/shard_map/unproject/pallas_call | solution.py:861
  670.4 3.2 joint.6
  675.9 14.1 %unproject.5 = bf16[2048,1024]{1,0:T(8,128)(2,1)} custom-call(bf16[3,1024,2048]{2,1,0:T(8,128)(2,1)} %back_local.3.refs_0_.refs_1_.refs_2_, bf16[3,1024,2048]{2,1,0:T(8,128)(2,1)} %back_local.3.refs_0_.refs_1_.refs_2_, bf16[3,1024,2048]{2,1,0:T(8,128)(2,1)} %back_local.3.refs_0_.refs_1_.refs_2_, ...), custom_call_target="tpu_custom_call", output_to_operand_aliasing={{}: (8, {})} | custom-call | flops 6442450944 | bytes 16777216 | tf_op jit(solution)/shard_map/unproject/pallas_call | solution.py:861
  706.0 2.9 collective-permute-start.35
  714.4 5.1 collective-permute-done.35.refs_3_
  (160 shorter events, 67.5 us)
Async XLA Ops:
  0.7 93.9 %collective-permute-start = (bf16[2048,1024]{1,0:T(8,128)(2,1)}, bf16[2048,1024]{1,0:T(8,128)(2,1)}, u32[]{:S(2)}, u32[]{:S(2)}) collective-permute-start(bf16[2048,1024]{1,0:T(8,128)(2,1)} %bitcast.111), channel_id=1, source_target_pairs={{1,0},{0,1},{3,2},{2,3},{5,4},{4,5},{7,6},{6,7},{9,8},{8,9},{11,10... | collective-permute-start | bytes 12582920 | tf_op jit(solution)/shard_map/ppermute | solution.py:1296
  286.8 45.4 %collective-permute-start.2 = (bf16[2048,1024]{1,0:T(8,128)(2,1)}, bf16[2048,1024]{1,0:T(8,128)(2,1)}, u32[]{:S(2)}, u32[]{:S(2)}) collective-permute-start(bf16[2048,1024]{1,0:T(8,128)(2,1)} %bitcast.174), channel_id=1, source_target_pairs={{0,2},{2,0},{4,6},{6,4},{8,10},{10,8},{12,14},{14,12},{16,18},{18,... | collective-permute-start | bytes 12582920 | tf_op jit(solution)/shard_map/ppermute | solution.py:1040
  318.8 13.4 %collective-permute-start.1 = (bf16[512,4096]{1,0:T(8,128)(2,1)}, bf16[512,4096]{1,0:T(8,128)(2,1)}, u32[]{:S(2)}, u32[]{:S(2)}) collective-permute-start(bf16[512,4096]{1,0:T(8,128)(2,1)} %bitcast.175), channel_id=1, source_target_pairs={{0,2},{2,0},{4,6},{6,4},{8,10},{10,8},{12,14},{14,12},{16,18},{18,... | collective-permute-start | bytes 12582920 | tf_op jit(solution)/shard_map/ppermute | solution.py:1040
  343.9 62.8 %collective-permute-start.5 = (bf16[256,4096]{1,0:T(8,128)(2,1)}, bf16[256,4096]{1,0:T(8,128)(2,1)}, u32[]{:S(2)}, u32[]{:S(2)}) collective-permute-start(bf16[256,4096]{1,0:T(8,128)(2,1)} %get-tuple-element.236), channel_id=1, source_target_pairs={{0,1},{1,0},{2,3},{3,2},{4,5},{5,4},{6,7},{7,6},{8,9},{9,8},{10,11... | collective-permute-start | bytes 6291464 | tf_op jit(solution)/shard_map/ppermute | solution.py:1040
  346.8 59.9 %collective-permute-start.6 = (bf16[1024,1024]{1,0:T(8,128)(2,1)}, bf16[1024,1024]{1,0:T(8,128)(2,1)}, u32[]{:S(2)}, u32[]{:S(2)}) collective-permute-start(bf16[1024,1024]{1,0:T(8,128)(2,1)} %get-tuple-element.238), channel_id=1, source_target_pairs={{0,4},{2,6},{4,0},{6,2},{8,12},{10,14},{12,8},{14,10},{16,20},{18,... | collective-permute-start | bytes 6291464 | tf_op jit(solution)/shard_map/ppermute | solution.py:1040
  348.3 58.4 %collective-permute-start.7 = (bf16[256,1024]{1,0:T(8,128)(2,1)}, bf16[256,1024]{1,0:T(8,128)(2,1)S(1)}, u32[]{:S(2)}, u32[]{:S(2)}) collective-permute-start(bf16[256,1024]{1,0:T(8,128)(2,1)} %get-tuple-element.240), channel_id=1, source_target_pairs={{0,4},{2,6},{4,0},{6,2},{8,12},{10,14},{12,8},{14,10},{16,20},{18,... | collective-permute-start | bytes 1572872 | tf_op jit(solution)/shard_map/ppermute | solution.py:1040
  348.8 57.9 %collective-permute-start.8 = (f32[96,128]{1,0:T(8,128)}, f32[96,128]{1,0:T(8,128)S(1)}, u32[]{:S(2)}, u32[]{:S(2)}) collective-permute-start(f32[96,128]{1,0:T(8,128)} %get-tuple-element.241.refs_12_), channel_id=1, source_target_pairs={{0,4},{2,6},{4,0},{6,2},{8,12},{10,14},{12,8},{14,10},{16,20},{18,... | collective-permute-start | bytes 147464 | tf_op jit(solution)/shard_map/ppermute | solution.py:1040
  414.1 47.1 %collective-permute-start.9 = (bf16[128,4096]{1,0:T(8,128)(2,1)}, bf16[128,4096]{1,0:T(8,128)(2,1)S(1)}, u32[]{:S(2)}, u32[]{:S(2)}) collective-permute-start(bf16[128,4096]{1,0:T(8,128)(2,1)} %get-tuple-element.257), channel_id=1, source_target_pairs={{0,4},{2,6},{4,0},{6,2},{8,12},{10,14},{12,8},{14,10},{16,20},{18,... | collective-permute-start | bytes 3145736 | tf_op jit(solution)/shard_map/ppermute | solution.py:1040
  415.7 45.5 %collective-permute-start.10 = (bf16[512,1024]{1,0:T(8,128)(2,1)}, bf16[512,1024]{1,0:T(8,128)(2,1)}, u32[]{:S(2)}, u32[]{:S(2)}) collective-permute-start(bf16[512,1024]{1,0:T(8,128)(2,1)} %get-tuple-element.259), channel_id=1, source_target_pairs={{0,1},{1,0},{2,3},{3,2},{4,5},{5,4},{6,7},{7,6},{8,9},{9,8},{10,11... | collective-permute-start | bytes 3145736 | tf_op jit(solution)/shard_map/ppermute | solution.py:1040
  416.2 45.0 %collective-permute-start.11 = (bf16[128,1024]{1,0:T(8,128)(2,1)}, bf16[128,1024]{1,0:T(8,128)(2,1)S(1)}, u32[]{:S(2)}, u32[]{:S(2)}) collective-permute-start(bf16[128,1024]{1,0:T(8,128)(2,1)} %get-tuple-element.261), channel_id=1, source_target_pairs={{0,1},{1,0},{2,3},{3,2},{4,5},{5,4},{6,7},{7,6},{8,9},{9,8},{10,11... | collective-permute-start | bytes 786440 | tf_op jit(solution)/shard_map/ppermute | solution.py:1040
  417.7 43.4 %collective-permute-start.12 = (f32[96,128]{1,0:T(8,128)}, f32[96,128]{1,0:T(8,128)S(1)}, u32[]{:S(2)}, u32[]{:S(2)}) collective-permute-start(f32[96,128]{1,0:T(8,128)} %get-tuple-element.262.refs_12_), channel_id=1, source_target_pairs={{0,1},{1,0},{2,3},{3,2},{4,5},{5,4},{6,7},{7,6},{8,9},{9,8},{10,11... | collective-permute-start | bytes 147464 | tf_op jit(solution)/shard_map/ppermute | solution.py:1040
  466.8 63.4 %collective-permute-start.13 = (bf16[64,4096]{1,0:T(8,128)(2,1)}, bf16[64,4096]{1,0:T(8,128)(2,1)S(1)}, u32[]{:S(2)}, u32[]{:S(2)}) collective-permute-start(bf16[64,4096]{1,0:T(8,128)(2,1)} %get-tuple-element.273), channel_id=1, source_target_pairs={{0,8},{2,10},{4,12},{6,14},{8,0},{10,2},{12,4},{14,6},{16,24},{18,... | collective-permute-start | bytes 1572872 | tf_op jit(solution)/shard_map/ppermute | solution.py:1040
  468.5 61.8 %collective-permute-start.14 = (bf16[256,1024]{1,0:T(8,128)(2,1)}, bf16[256,1024]{1,0:T(8,128)(2,1)S(1)}, u32[]{:S(2)}, u32[]{:S(2)}) collective-permute-start(bf16[256,1024]{1,0:T(8,128)(2,1)} %get-tuple-element.275), channel_id=1, source_target_pairs={{0,8},{2,10},{4,12},{6,14},{8,0},{10,2},{12,4},{14,6},{16,24},{18,... | collective-permute-start | bytes 1572872 | tf_op jit(solution)/shard_map/ppermute | solution.py:1040
  468.9 61.3 %collective-permute-start.15 = (bf16[64,1024]{1,0:T(8,128)(2,1)}, bf16[64,1024]{1,0:T(8,128)(2,1)S(1)}, u32[]{:S(2)}, u32[]{:S(2)}) collective-permute-start(bf16[64,1024]{1,0:T(8,128)(2,1)} %get-tuple-element.277), channel_id=1, source_target_pairs={{0,8},{2,10},{4,12},{6,14},{8,0},{10,2},{12,4},{14,6},{16,24},{18,... | collective-permute-start | bytes 393224 | tf_op jit(solution)/shard_map/ppermute | solution.py:1040
  470.5 59.7 %collective-permute-start.16 = (f32[96,128]{1,0:T(8,128)}, f32[96,128]{1,0:T(8,128)S(1)}, u32[]{:S(2)}, u32[]{:S(2)}) collective-permute-start(f32[96,128]{1,0:T(8,128)} %get-tuple-element.278.refs_12_), channel_id=1, source_target_pairs={{0,8},{2,10},{4,12},{6,14},{8,0},{10,2},{12,4},{14,6},{16,24},{18,... | collective-permute-start | bytes 147464 | tf_op jit(solution)/shard_map/ppermute | solution.py:1040
  470.9 120.0 %collective-permute-start.21 = (bf16[2048,1024]{1,0:T(8,128)(2,1)}, bf16[2048,1024]{1,0:T(8,128)(2,1)}, u32[]{:S(2)}, u32[]{:S(2)}) collective-permute-start(bf16[2048,1024]{1,0:T(8,128)(2,1)} %unproject.3), channel_id=1, source_target_pairs={{0,1},{1,0},{2,3},{3,2},{4,5},{5,4},{6,7},{7,6},{8,9},{9,8},{10,11... | collective-permute-start | bytes 12582920 | tf_op jit(solution)/shard_map/ppermute | solution.py:1373
  533.8 57.0 %collective-permute-start.17 = (bf16[32,4096]{1,0:T(8,128)(2,1)}, bf16[32,4096]{1,0:T(8,128)(2,1)S(1)}, u32[]{:S(2)}, u32[]{:S(2)}) collective-permute-start(bf16[32,4096]{1,0:T(8,128)(2,1)} %get-tuple-element.290), channel_id=1, source_target_pairs={{0,16},{2,18},{4,20},{6,22},{8,24},{10,26},{12,28},{14,30},{16,0},... | collective-permute-start | bytes 786440 | tf_op jit(solution)/shard_map/ppermute | solution.py:1040
  547.4 43.4 %collective-permute-start.18 = (bf16[128,1024]{1,0:T(8,128)(2,1)}, bf16[128,1024]{1,0:T(8,128)(2,1)S(1)}, u32[]{:S(2)}, u32[]{:S(2)}) collective-permute-start(bf16[128,1024]{1,0:T(8,128)(2,1)} %get-tuple-element.292), channel_id=1, source_target_pairs={{0,16},{2,18},{4,20},{6,22},{8,24},{10,26},{12,28},{14,30},{16,0},... | collective-permute-start | bytes 786440 | tf_op jit(solution)/shard_map/ppermute | solution.py:1040
  547.5 43.3 %collective-permute-start.19 = (bf16[32,1024]{1,0:T(8,128)(2,1)}, bf16[32,1024]{1,0:T(8,128)(2,1)S(1)}, u32[]{:S(2)}, u32[]{:S(2)}) collective-permute-start(bf16[32,1024]{1,0:T(8,128)(2,1)} %get-tuple-element.294), channel_id=1, source_target_pairs={{0,16},{2,18},{4,20},{6,22},{8,24},{10,26},{12,28},{14,30},{16,0},... | collective-permute-start | bytes 196616 | tf_op jit(solution)/shard_map/ppermute | solution.py:1040
  550.4 40.4 %collective-permute-start.20 = (f32[96,128]{1,0:T(8,128)}, f32[96,128]{1,0:T(8,128)S(1)}, u32[]{:S(2)}, u32[]{:S(2)}) collective-permute-start(f32[96,128]{1,0:T(8,128)} %get-tuple-element.384), channel_id=1, source_target_pairs={{0,16},{2,18},{4,20},{6,22},{8,24},{10,26},{12,28},{14,30},{16,0},... | collective-permute-start | bytes 147464 | tf_op jit(solution)/shard_map/ppermute | solution.py:1040
  628.5 12.0 %collective-permute-start.22 = (bf16[512,1024]{1,0:T(8,128)(2,1)}, bf16[512,1024]{1,0:T(8,128)(2,1)S(1)}, u32[]{:S(2)}, u32[]{:S(2)}) collective-permute-start(bf16[512,1024]{1,0:T(8,128)(2,1)} %bitcast.178), channel_id=1, source_target_pairs={{0,2},{2,0},{4,6},{6,4},{8,10},{10,8},{12,14},{14,12},{16,18},{18,... | collective-permute-start | bytes 3145736 | tf_op jit(solution)/shard_map/ppermute | solution.py:1040
  635.1 5.4 collective-permute-start.23
  635.2 5.5 collective-permute-start.24
  646.3 22.3 %collective-permute-start.26 = (bf16[304,1024]{1,0:T(8,128)(2,1)}, bf16[304,1024]{1,0:T(8,128)(2,1)S(1)}, u32[]{:S(2)}, u32[]{:S(2)}) collective-permute-start(bf16[304,1024]{1,0:T(8,128)(2,1)} %get-tuple-element.321), channel_id=1, source_target_pairs={{0,4},{2,6},{4,0},{6,2},{8,12},{10,14},{12,8},{14,10},{16,20},{18,... | collective-permute-start | bytes 1867784 | tf_op jit(solution)/shard_map/ppermute | solution.py:1040
  652.4 16.2 %collective-permute-start.27 = (bf16[256,1024]{1,0:T(8,128)(2,1)}, bf16[256,1024]{1,0:T(8,128)(2,1)S(1)}, u32[]{:S(2)}, u32[]{:S(2)}) collective-permute-start(bf16[256,1024]{1,0:T(8,128)(2,1)} %get-tuple-element.322), channel_id=1, source_target_pairs={{0,1},{1,0},{2,3},{3,2},{4,5},{5,4},{6,7},{7,6},{8,9},{9,8},{10,11... | collective-permute-start | bytes 1572872 | tf_op jit(solution)/shard_map/ppermute | solution.py:1040
  652.7 15.8 %collective-permute-start.28 = (bf16[256,1024]{1,0:T(8,128)(2,1)}, bf16[256,1024]{1,0:T(8,128)(2,1)S(1)}, u32[]{:S(2)}, u32[]{:S(2)}) collective-permute-start(bf16[256,1024]{1,0:T(8,128)(2,1)} %get-tuple-element.323), channel_id=1, source_target_pairs={{0,8},{2,10},{4,12},{6,14},{8,0},{10,2},{12,4},{14,6},{16,24},{18,... | collective-permute-start | bytes 1572872 | tf_op jit(solution)/shard_map/ppermute | solution.py:1040
  673.6 16.4 %collective-permute-start.29 = (bf16[176,1024]{1,0:T(8,128)(2,1)}, bf16[176,1024]{1,0:T(8,128)(2,1)S(1)}, u32[]{:S(2)}, u32[]{:S(2)}) collective-permute-start(bf16[176,1024]{1,0:T(8,128)(2,1)} %get-tuple-element.337), channel_id=1, source_target_pairs={{0,1},{1,0},{2,3},{3,2},{4,5},{5,4},{6,7},{7,6},{8,9},{9,8},{10,11... | collective-permute-start | bytes 1081352 | tf_op jit(solution)/shard_map/ppermute | solution.py:1040
  675.3 14.6 %collective-permute-start.30 = (bf16[128,1024]{1,0:T(8,128)(2,1)}, bf16[128,1024]{1,0:T(8,128)(2,1)S(1)}, u32[]{:S(2)}, u32[]{:S(2)}) collective-permute-start(bf16[128,1024]{1,0:T(8,128)(2,1)} %get-tuple-element.338), channel_id=1, source_target_pairs={{0,8},{2,10},{4,12},{6,14},{8,0},{10,2},{12,4},{14,6},{16,24},{18,... | collective-permute-start | bytes 786440 | tf_op jit(solution)/shard_map/ppermute | solution.py:1040
  675.8 14.2 %collective-permute-start.31 = (bf16[128,1024]{1,0:T(8,128)(2,1)}, bf16[128,1024]{1,0:T(8,128)(2,1)S(1)}, u32[]{:S(2)}, u32[]{:S(2)}) collective-permute-start(bf16[128,1024]{1,0:T(8,128)(2,1)} %get-tuple-element.339), channel_id=1, source_target_pairs={{0,4},{2,6},{4,0},{6,2},{8,12},{10,14},{12,8},{14,10},{16,20},{18,... | collective-permute-start | bytes 786440 | tf_op jit(solution)/shard_map/ppermute | solution.py:1040
  693.8 8.7 %collective-permute-start.32 = (bf16[112,1024]{1,0:T(8,128)(2,1)}, bf16[112,1024]{1,0:T(8,128)(2,1)S(1)}, u32[]{:S(2)}, u32[]{:S(2)}) collective-permute-start(bf16[112,1024]{1,0:T(8,128)(2,1)} %get-tuple-element.358), channel_id=1, source_target_pairs={{0,8},{2,10},{4,12},{6,14},{8,0},{10,2},{12,4},{14,6},{16,24},{18,... | collective-permute-start | bytes 688136 | tf_op jit(solution)/shard_map/ppermute | solution.py:1040
  695.4 5.2 collective-permute-start.33
  706.0 13.5 %collective-permute-start.35 = (bf16[144,1024]{1,0:T(8,128)(2,1)}, bf16[144,1024]{1,0:T(8,128)(2,1)S(1)}, u32[]{:S(2)}, u32[]{:S(2)}) collective-permute-start(bf16[144,1024]{1,0:T(8,128)(2,1)} %get-tuple-element.371), channel_id=1, source_target_pairs={{0,16},{2,18},{4,20},{6,22},{8,24},{10,26},{12,28},{14,30},{16,0},... | collective-permute-start | bytes 884744 | tf_op jit(solution)/shard_map/ppermute | solution.py:1040
  (39 other events, 351.5 us)

commit v6 on v5

--- a/solution.py
+++ b/solution.py
@@ -786,7 +786,7 @@
     for section, out in zip(sections, outs):
         for c in range(width // chunk):
             at = section * width + c * chunk
-            mixed = dot(w[:, at : at + chunk], normed, 0, 1) + b[:, at : at + chunk].T
+            mixed = (dot(normed, w[:, at : at + chunk], 1, 0) + b[:, at : at + chunk]).T
             for h in range(chunk // HEAD_DIM):
                 rows = slice(h * HEAD_DIM, (h + 1) * HEAD_DIM)
                 place = slice(c * chunk + h * HEAD_DIM, c * chunk + (h + 1) * HEAD_DIM)
@@ -955,22 +955,38 @@
 
 
 def mixed_kernel(
-    run, levels, near, orders, first_far, marks, d_own, d_far, normed, normed_far, w, *outs
+    run,
+    levels,
+    near,
+    orders,
+    first_far,
+    marks,
+    d_own,
+    d_far,
+    normed,
+    normed_far,
+    w,
+    gain,
+    shift,
+    *outs,
 ):
-    *halves, bias, sums = outs
-    step = pl.program_id(1)
+    *halves, small, sums, bias = outs
+    step, last = pl.program_id(1), pl.num_programs(1) - 1
     total = dot(d_own[...], normed[...], 1, 0)
     bias[...] = jnp.sum(d_own[...].astype(f32), axis=1, keepdims=True)
 
     @pl.when(step == 0)
     def _():
         sums[...] = jnp.zeros(sums.shape, f32)
+        small[...] = jnp.zeros(small.shape, f32)
 
     def finish(value):
         divide(value, run, levels, near, marks, orders, halves)
         weights = w[...].astype(f32).T
         sums[0:1, :] += column_sum(weights * value)
         sums[1:2, :] += column_sum(weights * bias[...])
+        wide = jnp.broadcast_to(bias[...], (bias.shape[0], PAIR)).T
+        small[pl.ds(step, 1), : bias.shape[0]] = wide[0:1, :]
 
     @pl.when(step < first_far)
     def _():
@@ -981,8 +997,13 @@
         bias[...] += jnp.sum(d_far[...].astype(f32), axis=1, keepdims=True)
         finish(total + dot(d_far[...], normed_far[...], 1, 0))
 
-
-def mixed_halves(marks, d_own, d_far, normed, normed_far, w, cores, parts, orders):
+    @pl.when(step == last)
+    def _():
+        small[pl.ds(last + 1, 1), :] = (sums[0:1, :] - shift[...] * sums[1:2, :]) / gain[...]
+        small[pl.ds(last + 2, 1), :] = sums[1:2, :]
+
+
+def mixed_halves(marks, d_own, d_far, normed, normed_far, w, gain, shift, cores, parts, orders):
     height, rows = d_own.shape
     far = d_far.shape[1]
     width = normed.shape[1]
@@ -993,42 +1014,38 @@
     first_far = width // high
     run = share // parts
     near = parts.bit_length() - 1
+    steps = height // high
 
     def fixed(shape):
         return pl.BlockSpec(shape, lambda j, i, marks: (0, 0), pipeline_mode=pl.Buffered(1))
 
     specs, shapes = divided(orders, levels, run, height, width, width)
-    *halves, bias, sums = pl.pallas_call(
+    *halves, small = pl.pallas_call(
         functools.partial(mixed_kernel, run, levels, near, orders, first_far),
         grid_spec=pltpu.PrefetchScalarGridSpec(
             num_scalar_prefetch=1,
-            grid=(1, height // high),
+            grid=(1, steps),
             in_specs=[
                 pl.BlockSpec((high, rows), lambda j, i, marks: (i, 0)),
                 pl.BlockSpec((high, far), lambda j, i, marks: (jnp.maximum(i, first_far), 0)),
                 fixed(normed.shape),
                 fixed(normed_far.shape),
                 pl.BlockSpec((width, high), lambda j, i, marks: (0, i)),
+                fixed(gain.shape),
+                fixed(shift.shape),
             ],
-            out_specs=specs
-            + [
-                pl.BlockSpec((high, 1), lambda j, i, marks: (i, 0)),
-                pl.BlockSpec((2, width), lambda j, i, marks: (0, 0)),
-            ],
+            out_specs=specs + [pl.BlockSpec((16, width), lambda j, i, marks: (0, 0))],
+            scratch_shapes=[pltpu.VMEM((2, width), f32), pltpu.VMEM((high, 1), f32)],
         ),
-        out_shape=shapes
-        + [
-            jax.ShapeDtypeStruct((height, 1), f32),
-            jax.ShapeDtypeStruct((2, width), f32),
-        ],
+        out_shape=shapes + [jax.ShapeDtypeStruct((16, width), f32)],
         compiler_params=pltpu.CompilerParams(vmem_limit_bytes=VMEM),
         cost_estimate=pl.CostEstimate(
             flops=2 * (rows + far) * height * width, bytes_accessed=1 << 25, transcendentals=0
         ),
         name="mixed",
-    )(marks, d_own, d_far, normed, normed_far, w)
+    )(marks, d_own, d_far, normed, normed_far, w, gain, shift)
     halves = [item.reshape(-1, width) for item in halves]
-    return [halves[i : i + 2] for i in range(0, len(halves), 2)], bias, sums
+    return [halves[i : i + 2] for i in range(0, len(halves), 2)], small, steps
 
 
 def bit_of(axis, position):
@@ -1044,10 +1061,17 @@
     def __init__(self, halves, order):
         self.order = list(order)
         kept, given = halves
+        self.height = kept.shape[0]
         self.terms = [kept, swap(given, "wide", 0)]
 
-    def send(self, array, away):
-        self.terms = [array, swap(away, *self.order.pop(0))]
+    def send(self, away):
+        self.terms = self.terms + [swap(away, *self.order.pop(0))]
+        self.height //= 2
+
+    def blocks(self, height, grid, which):
+        width = self.terms[0].shape[1]
+        spec = pl.BlockSpec((1, height // grid, width), lambda i: (which, i, 0))
+        return [term.reshape(-1, height, width) for term in self.terms], [spec] * len(self.terms)
 
 
 class Adding:
@@ -1059,32 +1083,30 @@
         self.terms = [total, swap(total, *self.order.pop(0))]
 
 
-def halve_kernel(count, *refs):
-    ins, outs = refs[: 4 * count + 2], refs[4 * count + 2 :]
-    for i in range(count):
-        one, two = ins[4 * i : 4 * i + 2], ins[4 * i + 2 : 4 * i + 4]
-        for half in range(2):
-            total = one[half][0].astype(f32) + two[half][0].astype(f32)
-            outs[2 * i + half][...] = total.astype(bf16)
+def halve_kernel(counts, *refs):
+    ins, outs = refs[: sum(counts) + 2], refs[sum(counts) + 2 :]
+    at = 0
+    for count, out in zip(counts, outs):
+        parts = [ref[0].astype(f32) for ref in ins[at : at + count]]
+        out[...] = functools.reduce(jnp.add, parts).astype(bf16)
+        at += count
     outs[-1][...] = ins[-2][...] + ins[-1][...]
 
 
 def halve(sums, small):
-    heights = [item.terms[0].shape[0] // 2 for item in sums]
+    heights = [item.height // 2 for item in sums]
     grid = 4 if all(height % 64 == 0 for height in heights) else 1
     operands, in_specs, out_specs, out_shape = [], [], [], []
     for item, height in zip(sums, heights):
-        width = item.terms[0].shape[1]
-        block = (height // grid, width)
-        for term in item.terms:
-            for half in range(2):
-                operands.append(term.reshape(2, height, width))
-                in_specs.append(pl.BlockSpec((1, *block), lambda i, half=half: (half, i, 0)))
-        out_specs += [pl.BlockSpec(block, lambda i: (i, 0))] * 2
-        out_shape += [jax.ShapeDtypeStruct((height, width), bf16)] * 2
+        arrays, specs = item.blocks(height, grid, 1)
+        operands += arrays
+        in_specs += specs
+        width = arrays[0].shape[2]
+        out_specs.append(pl.BlockSpec((height // grid, width), lambda i: (i, 0)))
+        out_shape.append(jax.ShapeDtypeStruct((height, width), bf16))
     whole_small = pl.BlockSpec(small.terms[0].shape, lambda i: (0, 0))
     return pl.pallas_call(
-        functools.partial(halve_kernel, len(sums)),
+        functools.partial(halve_kernel, [len(item.terms) for item in sums]),
         grid=(grid,),
         in_specs=in_specs + [whole_small] * 2,
         out_specs=out_specs + [whole_small],
@@ -1096,8 +1118,8 @@
 
 def launch(lead, sums, small, *others):
     lead, others, halves = lax.optimization_barrier((lead, others, halve(sums, small)))
-    for i, item in enumerate(sums):
-        item.send(halves[2 * i], halves[2 * i + 1])
+    for item, away in zip(sums, halves):
+        item.send(away)
     small.send(halves[-1])
     return (lead, *others)
 
@@ -1110,29 +1132,28 @@
     return lead
 
 
-def collect_kernel(groups, *refs):
+def collect_kernel(counts, *refs):
     at = 0
-    for out, count in zip(refs[-len(groups) :], groups):
-        parts = [
-            refs[at + 2 * i][...].astype(f32) + refs[at + 2 * i + 1][...].astype(f32)
-            for i in range(count)
-        ]
-        at += 2 * count
-        height = parts[0].shape[0]
-        for i, part in enumerate(parts):
-            out[i * height : (i + 1) * height, :] = part
-
-
-def collect(groups):
-    operands = [term for group in groups for item in group for term in item.terms]
+    for count, out in zip(counts, refs[sum(counts) :]):
+        out[...] = functools.reduce(jnp.add, [ref[0].astype(f32) for ref in refs[at : at + count]])
+        at += count
+
+
+def collect(sums):
+    operands, in_specs, out_specs, out_shape = [], [], [], []
+    for item in sums:
+        arrays, specs = item.blocks(item.height, 1, 0)
+        operands += arrays
+        in_specs += specs
+        shape = arrays[0].shape[1:]
+        out_specs.append(pl.BlockSpec(shape, lambda i: (0, 0)))
+        out_shape.append(jax.ShapeDtypeStruct(shape, f32))
     return pl.pallas_call(
-        functools.partial(collect_kernel, [len(group) for group in groups]),
-        out_shape=[
-            jax.ShapeDtypeStruct(
-                (sum(item.terms[0].shape[0] for item in group), group[0].terms[0].shape[1]), f32
-            )
-            for group in groups
-        ],
+        functools.partial(collect_kernel, [len(item.terms) for item in sums]),
+        grid=(1,),
+        in_specs=in_specs,
+        out_specs=out_specs,
+        out_shape=out_shape,
         compiler_params=pltpu.CompilerParams(vmem_limit_bytes=VMEM),
         name="collect",
     )(*operands)
@@ -1339,7 +1360,7 @@
 
     sum_up = outer(d_inner, normed_two, 0, first_order)
     sum_down = outer(d_outer, hidden, 0, second_order)
-    sum_out = outer(d_branch, oT, 1, first_order)
+    sum_out = outer(d_branch, oT, 1, fourth_order)
     flat = jnp.concatenate([small.reshape(-1), small_up.reshape(-1)])
     early = Adding(flat.reshape(-1, PAIR), small_order)
     sums = [sum_down, sum_up, sum_out]
@@ -1401,23 +1422,19 @@
         returned = [functools.reduce(jnp.add, [item.astype(f32) for item in returned])]
 
     orders = [first_order, third_order, fourth_order]
-    pieces, bias, weighted = mixed_halves(
+    pieces, late, steps = mixed_halves(
         marks,
         d_mixed.reshape(3 * width, rows),
         d_far.reshape(3 * width, -1),
         normed,
         normed_far,
         w_qkv,
+        *norm_one,
         cores,
         parts,
         orders,
     )
-    part_shift = weighted[1]
-    part_gain = (weighted[0] - shift_one * part_shift) / gain_one
-    flat = jnp.concatenate(
-        [bias.reshape(-1), part_gain, part_shift, jnp.zeros((11 * width,), f32)]
-    )
-    tail = Joint(pieces, orders, flat.reshape(16, width))
+    tail = Joint(pieces, orders, late)
     (d_mixed,) = tail.step(d_mixed)
     d_tokens = []
     for i in range(2):
@@ -1432,9 +1449,9 @@
         for item, arrays in zip(sums, terms):
             item.terms = list(arrays)
 
-    sum_w_down, sum_w_up, sum_w_out = collect([[item] for item in sums])
+    sum_w_down, sum_w_up, sum_w_out = collect(sums)
     sum_w_qkv, late_small = tail.result()
-    late_small = late_small.reshape(-1)[: 5 * width]
+    grad_b_qkv = late_small[:steps, : 3 * width // steps].reshape(-1)
     early_small = (early.terms[0] + early.terms[1]).reshape(-1)
     small = early_small[: 8 * width].reshape(8, width)
     small_up = early_small[8 * width :]
@@ -1446,12 +1463,12 @@
         sum_w_out.T,
         sum_w_up.T,
         sum_w_down.T,
-        late_small[: 3 * width],
+        grad_b_qkv,
         small[7],
         small_up,
         small[2],
-        late_small[3 * width : 4 * width],
-        late_small[4 * width :],
+        late_small[steps],
+        late_small[steps + 1],
         small[5],
         small[6],
         small[3],

time: 731 us -> 712 us (0.974)
  Pallas kernels: 556 us -> 594 us
  starting transfers between devices: 85.7 us -> 58.2 us
  waiting for transfers between devices: 58.2 us -> 33.8 us
    pallas_call x2, Pallas kernels: 56.4 us -> 91.6 us  [back_remote(): return call(info, flags, *operands, *turns, *keys, kept, *before)]
    ppermute x34, waiting for transfers between devices: 42.8 us -> 16.7 us  [swap(): lax.ppermute(values, axis, [(i, i ^ 1 << position) for i in range(size)])]
    ppermute x1, starting transfers between devices: 19.1 us -> 1.94 us  [body(): lax.ppermute(d_back[j * rows:(j + 1) * rows] if others > 1 else d_back, '...]
    ppermute x34, starting transfers between devices: 63.5 us -> 53.2 us  [swap(): lax.ppermute(values, axis, [(i, i ^ 1 << position) for i in range(size)])]
    pallas_call x1, Pallas kernels: 34.4 us -> 43.4 us  [attend_remote(): return call(info, qT, kT, vT, *state)]
  transfers between devices with their start and end apart: 36 -> 36, of which waited for: 9 -> 10; matrix products, arithmetic and copies ran while one was open for 1% -> 1% of each run, Pallas kernels for 40% -> 46%
where the time goes in v6:
time: 712 us; the launch traced here: 707 us
  Pallas kernels  594 us (83%)
  starting transfers between devices  58.2 us (8%)
  waiting for transfers between devices  33.8 us (5%)
  local copies, waits for them, and re-layouts  15.3 us (2%)
    pallas_call x1, Pallas kernels, block_call(): pl.pallas_call(functools.partial(block_kernel, span), grid=(rows // step,...  116 us
    pallas_call x2, Pallas kernels, back_remote(): return call(info, flags, *operands, *turns, *keys, kept, *before)  91.6 us
    pallas_call x2, Pallas kernels, back_local(): return call(info, flags, *operands, *turns, *keys, dq, kept, *before)  80.4 us
    pallas_call x3, Pallas kernels, outer_halves(): pl.pallas_call(functools.partial(outer_kernel, run, levels, near, [order]...  59.6 us
    ppermute x34, starting transfers between devices, swap(): lax.ppermute(values, axis, [(i, i ^ 1 << position) for i in range(size)])  53.2 us
    pallas_call x1, Pallas kernels, attend_local(): *state, kept, flags = call(info, qT, kT, vT)  48.3 us
    pallas_call x1, Pallas kernels, attend_remote(): return call(info, qT, kT, vT, *state)  43.4 us
    pallas_call x3, Pallas kernels, unproject(): pl.pallas_call(functools.partial(unproject_kernel, planes, bool(finish)),...  43 us
  transfers between devices with their start and end apart: 36, of which 10 were waited for; matrix products, arithmetic and copies ran while one was open for 1% of the time, Pallas kernels for 46%

profile of v6, /device:TPU:0, one launch (start us, length us, event | category | flops | bytes accessed | tf_op | source)
XLA Modules:
  0.0 707.1 jit_solution(8198729150474528081)
XLA Ops:
  0.7 3.0 collective-permute-start
  8.6 20.7 %project.2 = (bf16[2048,1024]{1,0:T(8,128)(2,1)}, bf16[1024,2048]{1,0:T(8,128)(2,1)}, bf16[1024,2048]{1,0:T(8,128)(2,1)}, bf16[1024,2048]{1,0:T(8,128)(2,1)}) custom-call(bf16[2048,1024]{1,0:T(8,128)(2,1)} %bitcast.169, bf16[1024,3072]{1,0:T(8,128)(2,1)} %refs_3_.3, f32[1,3072]{1,0:T(1,128)} %bitcast.218, f32[1,1024]{1,0:T(1,128)} %bitcast.199, ...), custom_call_target="tpu_custom_call" | custom-call | flops 12884901888 | bytes 16777216 | tf_op jit(solution)/shard_map/project/pallas_call | solution.py:812
  29.3 48.3 %attend_local.1 = (f32[1024,2048]{1,0:T(8,128)}, f32[8,2,2048]{2,1,0:T(2,128)}, f32[8,2,2048]{2,1,0:T(2,128)}, bf16[16,2304,1024]{2,1,0:T(8,128)(2,1)}, s32[8]{0:T(128)}) custom-call(s32[4]{0:T(128)} %pad_add_fusion.info, bf16[1024,2048]{1,0:T(8,128)(2,1)} %get-tuple-element.201.qT, bf16[1024,2048]{1,0:T(8,128)(2,1)} %get-tuple-element.204.kT, ...), custom_call_target="tpu_custom_call" | custom-call | flops 34359738368 | bytes 33554432 | tf_op jit(solution)/shard_map/attend_local/pallas_call | solution.py:532
  77.6 17.0 %collective-permute-done.tokens = bf16[2048,1024]{1,0:T(8,128)(2,1)} collective-permute-done((bf16[2048,1024]{1,0:T(8,128)(2,1)}, bf16[2048,1024]{1,0:T(8,128)(2,1)}, u32[]{:S(2)}, u32[]{:S(2)}) %collective-permute-start) | collective-permute-done | bytes 4194336 | tf_op jit(solution)/shard_map/ppermute | solution.py:1317
  94.6 16.2 %project.3 = (bf16[2048,1024]{1,0:T(8,128)(2,1)}, bf16[1024,2048]{1,0:T(8,128)(2,1)}, bf16[1024,2048]{1,0:T(8,128)(2,1)}) custom-call(bf16[2048,1024]{1,0:T(8,128)(2,1)} %collective-permute-done.tokens, bf16[1024,3072]{1,0:T(8,128)(2,1)} %refs_3_.3, f32[1,3072]{1,0:T(1,128)} %bitcast.219, f32[1,1024]{1,0:T(1,128)} %bitcast.200, f32[1,1024]{1,0:T(1,128)} %bitcast.229, ...), custom_call_target="tpu_custom_call" | custom-call | flops 8589934592 | bytes 16777216 | tf_op jit(solution)/shard_map/project/pallas_call | solution.py:812
  110.8 43.4 %attend_remote.1 = (bf16[1024,2048]{1,0:T(8,128)(2,1)}, f32[8,2,2048]{2,1,0:T(2,128)}, bf16[16,2048,1024]{2,1,0:T(8,128)(2,1)}, s32[8]{0:T(128)}) custom-call(s32[4]{0:T(128)} %pad_add_fusion.info, bf16[1024,2048]{1,0:T(8,128)(2,1)} %get-tuple-element.201.qT, bf16[1024,2048]{1,0:T(8,128)(2,1)} %get-tuple-element.202.kT, ...), custom_call_target="tpu_custom_call" | custom-call | flops 34359738368 | bytes 33554432 | tf_op jit(solution)/shard_map/attend_remote/pallas_call | solution.py:555
  154.2 116.2 %block.1 = (bf16[2048,1024]{1,0:T(8,128)(2,1)}, f32[2048,1024]{1,0:T(8,128)}, bf16[2048,4096]{1,0:T(8,128)(2,1)}, bf16[2048,1024]{1,0:T(8,128)(2,1)}, bf16[2048,...) custom-call(bf16[1024,2048]{1,0:T(8,128)(2,1)} %get-tuple-element.20, ...), custom_call_target="tpu_custom_call" | custom-call | flops 77309411328 | bytes 67108864 | tf_op jit(solution)/shard_map/block/pallas_call | solution.py:747
  270.5 24.6 %outer.3 = (bf16[2,2,2,2,32,4096]{5,4,3,2,1,0:T(8,128)(2,1)}, bf16[2,2,2,2,32,4096]{5,4,3,2,1,0:T(8,128)(2,1)}) custom-call(s32[2]{0:T(128)} %pad_add_fusion.1.marks, bf16[2048,1024]{1,0:T(8,128)(2,1)} %get-tuple-element.213.left, bf16[2048,4096]{1,0:T(8,128)(2,1)} %get-tuple-element.214.right), custom_call_target="tpu_custom_call" | custom-call | flops 17179869184 | bytes 33554432 | tf_op jit(solution)/shard_map/outer/pallas_call | solution.py:939
  295.1 24.6 %outer.4 = (bf16[2,2,2,2,128,1024]{5,4,3,2,1,0:T(8,128)(2,1)}, bf16[2,2,2,2,128,1024]{5,4,3,2,1,0:T(8,128)(2,1)}) custom-call(s32[2]{0:T(128)} %pad_add_fusion.1.marks, bf16[2048,4096]{1,0:T(8,128)(2,1)} %get-tuple-element.217.left, bf16[2048,1024]{1,0:T(8,128)(2,1)} %get-tuple-element.218.right), custom_call_target="tpu_custom_call" | custom-call | flops 17179869184 | bytes 33554432 | tf_op jit(solution)/shard_map/outer/pallas_call | solution.py:939
  320.2 10.4 %outer.5 = (bf16[2,2,2,2,32,1024]{5,4,3,2,1,0:T(8,128)(2,1)}, bf16[2,2,2,2,32,1024]{5,4,3,2,1,0:T(8,128)(2,1)}) custom-call(s32[2]{0:T(128)} %pad_add_fusion.1.marks, bf16[2048,1024]{1,0:T(8,128)(2,1)} %get-tuple-element.221.left, bf16[1024,2048]{1,0:T(8,128)(2,1)} %get-tuple-element.209.oT.right), custom_call_target="tpu_custom_call" | custom-call | flops 4294967296 | bytes 33554432 | tf_op jit(solution)/shard_map/outer/pallas_call | solution.py:939
  334.5 6.6 halve.4
  341.9 3.5 collective-permute-start.6
  345.6 45.7 %back_remote.2 = (f32[1024,2048]{1,0:T(8,128)}, bf16[3,1024,2048]{2,1,0:T(8,128)(2,1)}) custom-call(s32[4]{0:T(128)} %pad_add_fusion.info, s32[8]{0:T(128)} %get-tuple-element.240.flags, bf16[1024,2048]{1,0:T(8,128)(2,1)} %get-tuple-element.201.qT, bf16[1024,2048]{1,0:T(8,128)(2,1)} %get-tuple-element.264.doT, ...), custom_call_target="tpu_custom_call" | custom-call | flops 42949672960 | bytes 33554432 | tf_op jit(solution)/shard_map/back_remote/pallas_call | solution.py:593
  393.2 5.3 halve.5
  402.6 45.9 %back_remote.3 = (f32[1024,2048]{1,0:T(8,128)}, bf16[3,1024,2048]{2,1,0:T(8,128)(2,1)}) custom-call(s32[4]{0:T(128)} %pad_add_fusion.info, s32[8]{0:T(128)} %get-tuple-element.240.flags, bf16[1024,2048]{1,0:T(8,128)(2,1)} %get-tuple-element.201.qT, bf16[1024,2048]{1,0:T(8,128)(2,1)} %get-tuple-element.264.doT, ...), custom_call_target="tpu_custom_call", output_to_operand_aliasing={{0}: (11, {}), {1}: (12, {})} | custom-call | flops 42949672960 | bytes 33554432 | tf_op jit(solution)/shard_map/back_remote/pallas_call | solution.py:593
  448.4 14.7 %unproject.3 = bf16[2048,1024]{1,0:T(8,128)(2,1)} custom-call(bf16[3,1024,2048]{2,1,0:T(8,128)(2,1)} %get-tuple-element.245.refs_0_.refs_1_, bf16[3,1024,2048]{2,1,0:T(8,128)(2,1)} %get-tuple-element.245.refs_0_.refs_1_, bf16[1024,3072]{1,0:T(8,128)(2,1)} %refs_3_.3), custom_call_target="tpu_custom_call" | custom-call | flops 8589934592 | bytes 16777216 | tf_op jit(solution)/shard_map/unproject/pallas_call | solution.py:861
  464.2 4.2 halve.6
  473.5 40.1 %back_local.2.rest_0_ = bf16[3,1024,2048]{2,1,0:T(8,128)(2,1)} custom-call(s32[4]{0:T(128)} %pad_add_fusion.info, s32[8]{0:T(128)} %get-tuple-element.211.flags, bf16[1024,2048]{1,0:T(8,128)(2,1)} %get-tuple-element.201.qT, bf16[1024,2048]{1,0:T(8,128)(2,1)} %get-tuple-element.264.doT, bf16[1024,2048]{1,0:T(8,128)(2,1)} %get-tuple-element.209.oT.right, ...), custom_call_target="tpu_custom_call" | custom-call | flops 42949672960 | bytes 33554432 | tf_op jit(solution)/shard_map/back_local/pallas_call | solution.py:617
  517.5 12.6 %collective-permute-start.17 = (bf16[32,4096]{1,0:T(8,128)(2,1)}, bf16[32,4096]{1,0:T(8,128)(2,1)S(1)}, u32[]{:S(2)}, u32[]{:S(2)}) collective-permute-start(bf16[32,4096]{1,0:T(8,128)(2,1)} %get-tuple-element.267), channel_id=1, source_target_pairs={{0,16},{2,18},{4,20},{6,22},{8,24},{10,26},{12,28},{14,30},{16,0},... | collective-permute-start | bytes 786440 | tf_op jit(solution)/shard_map/ppermute | solution.py:1057
  530.1 2.8 collective-permute-start.19
  533.0 40.3 %back_local.3.refs_0_.refs_1_.refs_2_ = bf16[3,1024,2048]{2,1,0:T(8,128)(2,1)} custom-call(s32[4]{0:T(128)} %pad_add_fusion.info, s32[8]{0:T(128)} %get-tuple-element.211.flags, bf16[1024,2048]{1,0:T(8,128)(2,1)} %get-tuple-element.201.qT, bf16[1024,2048]{1,0:T(8,128)(2,1)} %get-tuple-element.264.doT, ...), custom_call_target="tpu_custom_call", output_to_operand_aliasing={{}: (12, {})} | custom-call | flops 42949672960 | bytes 33554432 | tf_op jit(solution)/shard_map/back_local/pallas_call | solution.py:617
  573.5 37.9 %mixed.1 = (bf16[2,2,2,2,32,1024]{5,4,3,2,1,0:T(8,128)(2,1)}, bf16[2,2,2,2,32,1024]{5,4,3,2,1,0:T(8,128)(2,1)}, bf16[2,2,2,2,32,1024]{5,4,3,2,1,0:T(8,128)(2,1)}...) custom-call(s32[2]{0:T(128)} %pad_add_fusion.1.marks, ...), custom_call_target="tpu_custom_call" | custom-call | flops 25769803776 | bytes 33554432 | tf_op jit(solution)/shard_map/mixed/pallas_call | solution.py:1023
  611.4 8.0 %collective-permute-start.22 = (bf16[512,1024]{1,0:T(8,128)(2,1)}, bf16[512,1024]{1,0:T(8,128)(2,1)S(1)}, u32[]{:S(2)}, u32[]{:S(2)}) collective-permute-start(bf16[512,1024]{1,0:T(8,128)(2,1)} %bitcast.212), channel_id=1, source_target_pairs={{0,2},{2,0},{4,6},{6,4},{8,10},{10,8},{12,14},{14,12},{16,18},{18,... | collective-permute-start | bytes 3145736 | tf_op jit(solution)/shard_map/ppermute | solution.py:1057
  625.1 4.8 joint.5
  630.8 3.8 collective-permute-start.27
  634.7 3.0 collective-permute-start.28
  637.7 14.1 %unproject.4.refs_8_ = bf16[2048,1024]{1,0:T(8,128)(2,1)} custom-call(bf16[3,1024,2048]{2,1,0:T(8,128)(2,1)} %back_local.3.refs_0_.refs_1_.refs_2_, bf16[3,1024,2048]{2,1,0:T(8,128)(2,1)} %back_local.3.refs_0_.refs_1_.refs_2_, bf16[3,1024,2048]{2,1,0:T(8,128)(2,1)} %back_local.3.refs_0_.refs_1_.refs_2_, bf16[1024,3072]{1,0:T(8,128)(2,1)} %refs_3_.3, ...), custom_call_target="tpu_custom_call" | custom-call | flops 6442450944 | bytes 16777216 | tf_op jit(solution)/shard_map/unproject/pallas_call | solution.py:861
  653.7 3.2 joint.6
  658.9 14.3 %unproject.5 = bf16[2048,1024]{1,0:T(8,128)(2,1)} custom-call(bf16[3,1024,2048]{2,1,0:T(8,128)(2,1)} %back_local.3.refs_0_.refs_1_.refs_2_, bf16[3,1024,2048]{2,1,0:T(8,128)(2,1)} %back_local.3.refs_0_.refs_1_.refs_2_, bf16[3,1024,2048]{2,1,0:T(8,128)(2,1)} %back_local.3.refs_0_.refs_1_.refs_2_, ...), custom_call_target="tpu_custom_call", output_to_operand_aliasing={{}: (8, {})} | custom-call | flops 6442450944 | bytes 16777216 | tf_op jit(solution)/shard_map/unproject/pallas_call | solution.py:861
  681.2 3.1 collective-permute-done.33.refs_4_
  692.1 3.1 collect.1
  697.2 4.3 collective-permute-done.35.refs_3_
  (148 shorter events, 59.4 us)
Async XLA Ops:
  0.7 93.9 %collective-permute-start = (bf16[2048,1024]{1,0:T(8,128)(2,1)}, bf16[2048,1024]{1,0:T(8,128)(2,1)}, u32[]{:S(2)}, u32[]{:S(2)}) collective-permute-start(bf16[2048,1024]{1,0:T(8,128)(2,1)} %bitcast.168), channel_id=1, source_target_pairs={{1,0},{0,1},{3,2},{2,3},{5,4},{4,5},{7,6},{6,7},{9,8},{8,9},{11,10... | collective-permute-start | bytes 12582920 | tf_op jit(solution)/shard_map/ppermute | solution.py:1317
  295.1 38.4 %collective-permute-start.1 = (bf16[512,4096]{1,0:T(8,128)(2,1)}, bf16[512,4096]{1,0:T(8,128)(2,1)}, u32[]{:S(2)}, u32[]{:S(2)}) collective-permute-start(bf16[512,4096]{1,0:T(8,128)(2,1)} %bitcast.208), channel_id=1, source_target_pairs={{0,2},{2,0},{4,6},{6,4},{8,10},{10,8},{12,14},{14,12},{16,18},{18,... | collective-permute-start | bytes 12582920 | tf_op jit(solution)/shard_map/ppermute | solution.py:1057
  319.7 13.8 %collective-permute-start.2 = (bf16[2048,1024]{1,0:T(8,128)(2,1)}, bf16[2048,1024]{1,0:T(8,128)(2,1)}, u32[]{:S(2)}, u32[]{:S(2)}) collective-permute-start(bf16[2048,1024]{1,0:T(8,128)(2,1)} %bitcast.209), channel_id=1, source_target_pairs={{0,2},{2,0},{4,6},{6,4},{8,10},{10,8},{12,14},{14,12},{16,18},{18,... | collective-permute-start | bytes 12582920 | tf_op jit(solution)/shard_map/ppermute | solution.py:1057
  341.1 51.3 %collective-permute-start.5 = (bf16[256,4096]{1,0:T(8,128)(2,1)}, bf16[256,4096]{1,0:T(8,128)(2,1)}, u32[]{:S(2)}, u32[]{:S(2)}) collective-permute-start(bf16[256,4096]{1,0:T(8,128)(2,1)} %get-tuple-element.231), channel_id=1, source_target_pairs={{0,1},{1,0},{2,3},{3,2},{4,5},{5,4},{6,7},{7,6},{8,9},{9,8},{10,11... | collective-permute-start | bytes 6291464 | tf_op jit(solution)/shard_map/ppermute | solution.py:1057
  341.9 50.5 %collective-permute-start.6 = (bf16[1024,1024]{1,0:T(8,128)(2,1)}, bf16[1024,1024]{1,0:T(8,128)(2,1)}, u32[]{:S(2)}, u32[]{:S(2)}) collective-permute-start(bf16[1024,1024]{1,0:T(8,128)(2,1)} %get-tuple-element.232), channel_id=1, source_target_pairs={{0,4},{2,6},{4,0},{6,2},{8,12},{10,14},{12,8},{14,10},{16,20},{18,... | collective-permute-start | bytes 6291464 | tf_op jit(solution)/shard_map/ppermute | solution.py:1057
  345.4 46.9 %collective-permute-start.7 = (bf16[256,1024]{1,0:T(8,128)(2,1)}, bf16[256,1024]{1,0:T(8,128)(2,1)S(1)}, u32[]{:S(2)}, u32[]{:S(2)}) collective-permute-start(bf16[256,1024]{1,0:T(8,128)(2,1)} %get-tuple-element.233), channel_id=1, source_target_pairs={{0,8},{2,10},{4,12},{6,14},{8,0},{10,2},{12,4},{14,6},{16,24},{18,... | collective-permute-start | bytes 1572872 | tf_op jit(solution)/shard_map/ppermute | solution.py:1057
  345.4 46.9 %collective-permute-start.8 = (f32[96,128]{1,0:T(8,128)}, f32[96,128]{1,0:T(8,128)S(1)}, u32[]{:S(2)}, u32[]{:S(2)}) collective-permute-start(f32[96,128]{1,0:T(8,128)} %get-tuple-element.234.refs_9_), channel_id=1, source_target_pairs={{0,4},{2,6},{4,0},{6,2},{8,12},{10,14},{12,8},{14,10},{16,20},{18,... | collective-permute-start | bytes 147464 | tf_op jit(solution)/shard_map/ppermute | solution.py:1057
  398.4 64.7 %collective-permute-start.9 = (bf16[128,4096]{1,0:T(8,128)(2,1)}, bf16[128,4096]{1,0:T(8,128)(2,1)S(1)}, u32[]{:S(2)}, u32[]{:S(2)}) collective-permute-start(bf16[128,4096]{1,0:T(8,128)(2,1)} %get-tuple-element.246), channel_id=1, source_target_pairs={{0,4},{2,6},{4,0},{6,2},{8,12},{10,14},{12,8},{14,10},{16,20},{18,... | collective-permute-start | bytes 3145736 | tf_op jit(solution)/shard_map/ppermute | solution.py:1057
  400.2 62.9 %collective-permute-start.10 = (bf16[512,1024]{1,0:T(8,128)(2,1)}, bf16[512,1024]{1,0:T(8,128)(2,1)}, u32[]{:S(2)}, u32[]{:S(2)}) collective-permute-start(bf16[512,1024]{1,0:T(8,128)(2,1)} %get-tuple-element.247), channel_id=1, source_target_pairs={{0,1},{1,0},{2,3},{3,2},{4,5},{5,4},{6,7},{7,6},{8,9},{9,8},{10,11... | collective-permute-start | bytes 3145736 | tf_op jit(solution)/shard_map/ppermute | solution.py:1057
  400.6 62.5 %collective-permute-start.11 = (bf16[128,1024]{1,0:T(8,128)(2,1)}, bf16[128,1024]{1,0:T(8,128)(2,1)S(1)}, u32[]{:S(2)}, u32[]{:S(2)}) collective-permute-start(bf16[128,1024]{1,0:T(8,128)(2,1)} %get-tuple-element.248), channel_id=1, source_target_pairs={{0,4},{2,6},{4,0},{6,2},{8,12},{10,14},{12,8},{14,10},{16,20},{18,... | collective-permute-start | bytes 786440 | tf_op jit(solution)/shard_map/ppermute | solution.py:1057
  400.9 62.2 %collective-permute-start.12 = (f32[96,128]{1,0:T(8,128)}, f32[96,128]{1,0:T(8,128)S(1)}, u32[]{:S(2)}, u32[]{:S(2)}) collective-permute-start(f32[96,128]{1,0:T(8,128)} %get-tuple-element.249.refs_12_), channel_id=1, source_target_pairs={{0,1},{1,0},{2,3},{3,2},{4,5},{5,4},{6,7},{7,6},{8,9},{9,8},{10,11... | collective-permute-start | bytes 147464 | tf_op jit(solution)/shard_map/ppermute | solution.py:1057
  468.5 45.2 %collective-permute-start.13 = (bf16[64,4096]{1,0:T(8,128)(2,1)}, bf16[64,4096]{1,0:T(8,128)(2,1)S(1)}, u32[]{:S(2)}, u32[]{:S(2)}) collective-permute-start(bf16[64,4096]{1,0:T(8,128)(2,1)} %get-tuple-element.256), channel_id=1, source_target_pairs={{0,8},{2,10},{4,12},{6,14},{8,0},{10,2},{12,4},{14,6},{16,24},{18,... | collective-permute-start | bytes 1572872 | tf_op jit(solution)/shard_map/ppermute | solution.py:1057
  469.4 44.2 %collective-permute-start.14 = (bf16[256,1024]{1,0:T(8,128)(2,1)}, bf16[256,1024]{1,0:T(8,128)(2,1)S(1)}, u32[]{:S(2)}, u32[]{:S(2)}) collective-permute-start(bf16[256,1024]{1,0:T(8,128)(2,1)} %get-tuple-element.257), channel_id=1, source_target_pairs={{0,8},{2,10},{4,12},{6,14},{8,0},{10,2},{12,4},{14,6},{16,24},{18,... | collective-permute-start | bytes 1572872 | tf_op jit(solution)/shard_map/ppermute | solution.py:1057
  470.5 43.0 %collective-permute-start.15 = (bf16[64,1024]{1,0:T(8,128)(2,1)}, bf16[64,1024]{1,0:T(8,128)(2,1)S(1)}, u32[]{:S(2)}, u32[]{:S(2)}) collective-permute-start(bf16[64,1024]{1,0:T(8,128)(2,1)} %get-tuple-element.258), channel_id=1, source_target_pairs={{0,1},{1,0},{2,3},{3,2},{4,5},{5,4},{6,7},{7,6},{8,9},{9,8},{10,11... | collective-permute-start | bytes 393224 | tf_op jit(solution)/shard_map/ppermute | solution.py:1057
  470.9 42.7 %collective-permute-start.16 = (f32[96,128]{1,0:T(8,128)}, f32[96,128]{1,0:T(8,128)S(1)}, u32[]{:S(2)}, u32[]{:S(2)}) collective-permute-start(f32[96,128]{1,0:T(8,128)} %get-tuple-element.259.refs_15_), channel_id=1, source_target_pairs={{0,8},{2,10},{4,12},{6,14},{8,0},{10,2},{12,4},{14,6},{16,24},{18,... | collective-permute-start | bytes 147464 | tf_op jit(solution)/shard_map/ppermute | solution.py:1057
  471.6 101.9 %collective-permute-start.21 = (bf16[2048,1024]{1,0:T(8,128)(2,1)}, bf16[2048,1024]{1,0:T(8,128)(2,1)}, u32[]{:S(2)}, u32[]{:S(2)}) collective-permute-start(bf16[2048,1024]{1,0:T(8,128)(2,1)} %unproject.3), channel_id=1, source_target_pairs={{0,1},{1,0},{2,3},{3,2},{4,5},{5,4},{6,7},{7,6},{8,9},{9,8},{10,11... | collective-permute-start | bytes 12582920 | tf_op jit(solution)/shard_map/ppermute | solution.py:1394
  517.5 55.9 %collective-permute-start.17 = (bf16[32,4096]{1,0:T(8,128)(2,1)}, bf16[32,4096]{1,0:T(8,128)(2,1)S(1)}, u32[]{:S(2)}, u32[]{:S(2)}) collective-permute-start(bf16[32,4096]{1,0:T(8,128)(2,1)} %get-tuple-element.267), channel_id=1, source_target_pairs={{0,16},{2,18},{4,20},{6,22},{8,24},{10,26},{12,28},{14,30},{16,0},... | collective-permute-start | bytes 786440 | tf_op jit(solution)/shard_map/ppermute | solution.py:1057
  530.0 43.4 %collective-permute-start.18 = (bf16[128,1024]{1,0:T(8,128)(2,1)}, bf16[128,1024]{1,0:T(8,128)(2,1)S(1)}, u32[]{:S(2)}, u32[]{:S(2)}) collective-permute-start(bf16[128,1024]{1,0:T(8,128)(2,1)} %get-tuple-element.268), channel_id=1, source_target_pairs={{0,16},{2,18},{4,20},{6,22},{8,24},{10,26},{12,28},{14,30},{16,0},... | collective-permute-start | bytes 786440 | tf_op jit(solution)/shard_map/ppermute | solution.py:1057
  530.1 43.3 %collective-permute-start.19 = (bf16[32,1024]{1,0:T(8,128)(2,1)}, bf16[32,1024]{1,0:T(8,128)(2,1)S(1)}, u32[]{:S(2)}, u32[]{:S(2)}) collective-permute-start(bf16[32,1024]{1,0:T(8,128)(2,1)} %get-tuple-element.269), channel_id=1, source_target_pairs={{0,16},{2,18},{4,20},{6,22},{8,24},{10,26},{12,28},{14,30},{16,0},... | collective-permute-start | bytes 196616 | tf_op jit(solution)/shard_map/ppermute | solution.py:1057
  532.9 40.4 %collective-permute-start.20 = (f32[96,128]{1,0:T(8,128)}, f32[96,128]{1,0:T(8,128)S(1)}, u32[]{:S(2)}, u32[]{:S(2)}) collective-permute-start(f32[96,128]{1,0:T(8,128)} %get-tuple-element.382), channel_id=1, source_target_pairs={{0,16},{2,18},{4,20},{6,22},{8,24},{10,26},{12,28},{14,30},{16,0},... | collective-permute-start | bytes 147464 | tf_op jit(solution)/shard_map/ppermute | solution.py:1057
  611.4 11.4 %collective-permute-start.22 = (bf16[512,1024]{1,0:T(8,128)(2,1)}, bf16[512,1024]{1,0:T(8,128)(2,1)S(1)}, u32[]{:S(2)}, u32[]{:S(2)}) collective-permute-start(bf16[512,1024]{1,0:T(8,128)(2,1)} %bitcast.212), channel_id=1, source_target_pairs={{0,2},{2,0},{4,6},{6,4},{8,10},{10,8},{12,14},{14,12},{16,18},{18,... | collective-permute-start | bytes 3145736 | tf_op jit(solution)/shard_map/ppermute | solution.py:1057
  619.4 5.6 collective-permute-start.24
  629.8 22.0 %collective-permute-start.26 = (bf16[304,1024]{1,0:T(8,128)(2,1)}, bf16[304,1024]{1,0:T(8,128)(2,1)S(1)}, u32[]{:S(2)}, u32[]{:S(2)}) collective-permute-start(bf16[304,1024]{1,0:T(8,128)(2,1)} %get-tuple-element.295), channel_id=1, source_target_pairs={{0,4},{2,6},{4,0},{6,2},{8,12},{10,14},{12,8},{14,10},{16,20},{18,... | collective-permute-start | bytes 1867784 | tf_op jit(solution)/shard_map/ppermute | solution.py:1057
  630.8 20.9 %collective-permute-start.27 = (bf16[256,1024]{1,0:T(8,128)(2,1)}, bf16[256,1024]{1,0:T(8,128)(2,1)S(1)}, u32[]{:S(2)}, u32[]{:S(2)}) collective-permute-start(bf16[256,1024]{1,0:T(8,128)(2,1)} %get-tuple-element.296), channel_id=1, source_target_pairs={{0,1},{1,0},{2,3},{3,2},{4,5},{5,4},{6,7},{7,6},{8,9},{9,8},{10,11... | collective-permute-start | bytes 1572872 | tf_op jit(solution)/shard_map/ppermute | solution.py:1057
  634.7 17.1 %collective-permute-start.28 = (bf16[256,1024]{1,0:T(8,128)(2,1)}, bf16[256,1024]{1,0:T(8,128)(2,1)S(1)}, u32[]{:S(2)}, u32[]{:S(2)}) collective-permute-start(bf16[256,1024]{1,0:T(8,128)(2,1)} %get-tuple-element.297), channel_id=1, source_target_pairs={{0,8},{2,10},{4,12},{6,14},{8,0},{10,2},{12,4},{14,6},{16,24},{18,... | collective-permute-start | bytes 1572872 | tf_op jit(solution)/shard_map/ppermute | solution.py:1057
  656.9 16.3 %collective-permute-start.29 = (bf16[176,1024]{1,0:T(8,128)(2,1)}, bf16[176,1024]{1,0:T(8,128)(2,1)S(1)}, u32[]{:S(2)}, u32[]{:S(2)}) collective-permute-start(bf16[176,1024]{1,0:T(8,128)(2,1)} %get-tuple-element.311), channel_id=1, source_target_pairs={{0,1},{1,0},{2,3},{3,2},{4,5},{5,4},{6,7},{7,6},{8,9},{9,8},{10,11... | collective-permute-start | bytes 1081352 | tf_op jit(solution)/shard_map/ppermute | solution.py:1057
  657.8 15.4 %collective-permute-start.30 = (bf16[128,1024]{1,0:T(8,128)(2,1)}, bf16[128,1024]{1,0:T(8,128)(2,1)S(1)}, u32[]{:S(2)}, u32[]{:S(2)}) collective-permute-start(bf16[128,1024]{1,0:T(8,128)(2,1)} %get-tuple-element.312), channel_id=1, source_target_pairs={{0,8},{2,10},{4,12},{6,14},{8,0},{10,2},{12,4},{14,6},{16,24},{18,... | collective-permute-start | bytes 786440 | tf_op jit(solution)/shard_map/ppermute | solution.py:1057
  657.8 15.4 %collective-permute-start.31 = (bf16[128,1024]{1,0:T(8,128)(2,1)}, bf16[128,1024]{1,0:T(8,128)(2,1)S(1)}, u32[]{:S(2)}, u32[]{:S(2)}) collective-permute-start(bf16[128,1024]{1,0:T(8,128)(2,1)} %get-tuple-element.313), channel_id=1, source_target_pairs={{0,4},{2,6},{4,0},{6,2},{8,12},{10,14},{12,8},{14,10},{16,20},{18,... | collective-permute-start | bytes 786440 | tf_op jit(solution)/shard_map/ppermute | solution.py:1057
  677.1 8.1 %collective-permute-start.32 = (bf16[112,1024]{1,0:T(8,128)(2,1)}, bf16[112,1024]{1,0:T(8,128)(2,1)S(1)}, u32[]{:S(2)}, u32[]{:S(2)}) collective-permute-start(bf16[112,1024]{1,0:T(8,128)(2,1)} %get-tuple-element.344), channel_id=1, source_target_pairs={{0,8},{2,10},{4,12},{6,14},{8,0},{10,2},{12,4},{14,6},{16,24},{18,... | collective-permute-start | bytes 688136 | tf_op jit(solution)/shard_map/ppermute | solution.py:1057
  679.1 5.2 collective-permute-start.33
  680.0 5.2 collective-permute-start.34
  688.6 12.9 %collective-permute-start.35 = (bf16[144,1024]{1,0:T(8,128)(2,1)}, bf16[144,1024]{1,0:T(8,128)(2,1)S(1)}, u32[]{:S(2)}, u32[]{:S(2)}) collective-permute-start(bf16[144,1024]{1,0:T(8,128)(2,1)} %get-tuple-element.357), channel_id=1, source_target_pairs={{0,16},{2,18},{4,20},{6,22},{8,24},{10,26},{12,28},{14,30},{16,0},... | collective-permute-start | bytes 884744 | tf_op jit(solution)/shard_map/ppermute | solution.py:1057
  (36 other events, 258.0 us)

commit v7 on v6

--- a/solution.py
+++ b/solution.py
@@ -327,18 +327,10 @@
         dv[rows, here] += d_values
 
 
-def stored_prepare(doT, oT, lse, scaled, delta):
-    for h in range(2):
-        rows = slice(HEAD_DIM * h, HEAD_DIM * (h + 1))
-        grad = (doT[rows, :].astype(f32) * jnp.exp2(-lse[0, h : h + 1, :])).astype(bf16)
-        scaled[rows, :] = grad
-        delta[h : h + 1, :] = column_sum(grad.astype(f32) * oT[rows, :].astype(f32))
-
-
 def stored_chunk(h, weights, queries, keys, qT, kT, vT, scaled, delta, dq, dk, dv):
     rows = slice(HEAD_DIM * h, HEAD_DIM * (h + 1))
     d_probs = dot(vT[rows, keys], scaled[rows, queries], 0, 0)
-    d_scores = weights.astype(f32) * (d_probs - delta[h : h + 1, queries])
+    d_scores = weights.astype(f32) * (d_probs - delta[0, h : h + 1, queries])
     d_scores = d_scores.astype(bf16)
     dv[rows, keys] += dot(scaled[rows, queries], weights, 1, 1)
     dk[rows, keys] += dot(qT[rows, queries], d_scores, 1, 1)
@@ -354,9 +346,25 @@
 
 
 def bwd_remote_kernel(
-    group, parts, first, info, flags, qT, doT, oT, lse, cosine, sine, kT, vT, kept, *rest
+    group,
+    parts,
+    first,
+    info,
+    flags,
+    qT,
+    doT,
+    oT,
+    lse,
+    scaled,
+    delta,
+    cosine,
+    sine,
+    kT,
+    vT,
+    kept,
+    *rest,
 ):
-    dq, dkv, qa, da, ka, va, dk, dv, scaled, delta = rest[-10:]
+    dq, dkv, qa, da, ka, va, dk, dv = rest[-8:]
     dq[...] = jnp.zeros(dq.shape, f32)
     dk[...] = jnp.zeros(dk.shape, f32)
     dv[...] = jnp.zeros(dv.shape, f32)
@@ -364,8 +372,6 @@
 
     @pl.when(fast)
     def _():
-        stored_prepare(doT, oT, lse, scaled, delta)
-
         def full(q0, k0, slot):
             for h in range(2):
                 weights = kept[h, pl.ds(slot, group), :]
@@ -398,9 +404,25 @@
 
 
 def bwd_local_kernel(
-    group, first, info, flags, qT, doT, oT, lse, cosine, sine, kT, vT, dq_in, kept, *rest
+    group,
+    first,
+    info,
+    flags,
+    qT,
+    doT,
+    oT,
+    lse,
+    scaled,
+    delta,
+    cosine,
+    sine,
+    kT,
+    vT,
+    dq_in,
+    kept,
+    *rest,
 ):
-    dqkv, qa, da, ka, va, dk, dv, scaled, delta, dq = rest[-10:]
+    dqkv, qa, da, ka, va, dk, dv, dq = rest[-8:]
     length = info[1]
     dq[...] = dq_in[...]
     dk[...] = jnp.zeros(dk.shape, f32)
@@ -411,7 +433,6 @@
 
     @pl.when(fast)
     def _():
-        stored_prepare(doT, oT, lse, scaled, delta)
         refs = (qT, kT, vT, scaled, delta, dq, dk, dv)
 
         def own(i, carry):
@@ -561,7 +582,6 @@
         [pltpu.VMEM((2, rows, n_q), bf16)] * 2
         + [pltpu.VMEM((2, rows, n_k), bf16)] * 2
         + [pltpu.VMEM((PAIR, n_k), f32)] * 2
-        + [pltpu.VMEM((PAIR, n_q), bf16), pltpu.VMEM((2, n_q), f32)]
     )
 
 
@@ -574,7 +594,7 @@
         functools.partial(bwd_remote_kernel, group, parts, first),
         count,
         [rows_of(n_q, first)] * 3
-        + [stats_of(n_q, first)]
+        + [stats_of(n_q, first), rows_of(n_q, first), stats_of(n_q, first)]
         + [whole((half, n_k))] * 2
         + [rows_of(n_k, first)] * 2
         + [kept_of(kept.shape[1], group, first)]
@@ -601,7 +621,7 @@
         functools.partial(bwd_local_kernel, group, first),
         count,
         [rows_of(n_q, first)] * 3
-        + [stats_of(n_q, first)]
+        + [stats_of(n_q, first), rows_of(n_q, first), stats_of(n_q, first)]
         + [whole((half, n_q))] * 2
         + [rows_of(n_q, first)] * 3
         + [kept_of(kept.shape[1], group, first)]
@@ -642,6 +662,7 @@
 def block_kernel(
     span,
     oT,
+    lse,
     tokens,
     cotangent,
     w_out,
@@ -664,6 +685,8 @@
     d_inner_out,
     d_branch_out,
     doT,
+    scaled,
+    delta,
     small,
     small_up,
     slope,
@@ -723,10 +746,17 @@
     d_branch = norm_back(d_middle, unit_two, rate_two, gain_two[...]).astype(bf16)
     d_branch_out[...] = d_branch
     small[7:8, :] += column_sum(d_branch.astype(f32))
-    doT[...] = dot(w_out[...], d_branch, 1, 1).astype(bf16)
-
-
-def block_call(oT, tokens, cotangent, weights, vectors):
+    d_attended = dot(w_out[...], d_branch, 1, 1).astype(bf16)
+    doT[...] = d_attended
+    for h in range(oT.shape[0] // HEAD_DIM):
+        rows = slice(HEAD_DIM * h, HEAD_DIM * (h + 1))
+        at = slice(h % 2, h % 2 + 1)
+        part = (d_attended[rows].astype(f32) * jnp.exp2(-lse[h // 2, at, :])).astype(bf16)
+        scaled[rows, :] = part
+        delta[h // 2, at, :] = column_sum(part.astype(f32) * oT[rows, :].astype(f32))
+
+
+def block_call(oT, lse, tokens, cotangent, weights, vectors):
     width, rows = oT.shape
     wide = weights[1].shape[1]
     step = min(256, rows)
@@ -742,19 +772,22 @@
         return pl.BlockSpec(shape, lambda i: (0, 0))
 
     features = pl.BlockSpec((width, step), lambda i: (0, i))
+    stats = pl.BlockSpec((*lse.shape[:2], step), lambda i: (0, 0, i))
     sizes = [width, width, wide, width, width, wide, width]
     kinds = [bf16, f32, bf16, bf16, bf16, bf16, bf16]
     return pl.pallas_call(
         functools.partial(block_kernel, span),
         grid=(rows // step,),
-        in_specs=[features, lines(width), lines(width)]
+        in_specs=[features, stats, lines(width), lines(width)]
         + [fixed(item.shape) for item in weights]
         + [fixed(item.shape) for item in vectors],
         out_specs=[lines(size) for size in sizes]
-        + [features, total((8, width)), total((1, wide))],
+        + [features, features, stats, total((8, width)), total((1, wide))],
         out_shape=[jax.ShapeDtypeStruct((rows, size), kind) for size, kind in zip(sizes, kinds)]
         + [
             jax.ShapeDtypeStruct((width, rows), bf16),
+            jax.ShapeDtypeStruct((width, rows), bf16),
+            jax.ShapeDtypeStruct(lse.shape, f32),
             jax.ShapeDtypeStruct((8, width), f32),
             jax.ShapeDtypeStruct((1, wide), f32),
         ],
@@ -766,7 +799,7 @@
             transcendentals=rows * wide,
         ),
         name="block",
-    )(oT, tokens, cotangent, *weights, *vectors)
+    )(oT, lse, tokens, cotangent, *weights, *vectors)
 
 
 def turn(values, cosine, sine):
@@ -1338,6 +1371,7 @@
 
     blocks = block_call(
         oT,
+        lse,
         tokens,
         cotangent.reshape(rows, width),
         [w_out, w_up, w_down],
@@ -1345,7 +1379,8 @@
         + [row(item) for item in (gain_two, shift_two, gain_three, shift_three)]
         + [row(item) for item in (gain_four, shift_four)],
     )
-    result, d_middle, hidden, d_outer, normed_two, d_inner, d_branch, doT, small, small_up = blocks
+    result, d_middle, hidden, d_outer, normed_two, d_inner, d_branch = blocks[:7]
+    doT, scaled, delta, small, small_up = blocks[7:]
 
     wide_bits = axis_bits("wide")
     narrow_bits = axis_bits("narrow")
@@ -1368,23 +1403,20 @@
     heads = width // PAIR
     portions = 2 if heads % 2 == 0 else 1
     count = heads // portions
-    far = []
-    for portion in range(portions):
-        (doT,) = launch(doT, sums, early)
-        far = back_remote(
-            info,
-            flags_far,
-            [qT, doT, oT, lse],
-            turns_far,
-            [kT_far, vT_far],
-            kept_far,
-            group,
-            parts,
-            portion * count,
-            count,
-            far,
-        )
-    dq_far, d_far = far
+    (doT,) = launch(doT, sums, early)
+    dq_far, d_far = back_remote(
+        info,
+        flags_far,
+        [qT, doT, oT, lse, scaled, delta],
+        turns_far,
+        [kT_far, vT_far],
+        kept_far,
+        group,
+        parts,
+        0,
+        heads,
+        [],
+    )
     d_back = unproject(d_far, w_qkv, (1, 2), 0, others * rows)
     d_mixed = []
     for portion in range(portions):
@@ -1402,7 +1434,7 @@
             back_local(
                 info,
                 flags_own,
-                [qT, doT, oT, lse],
+                [qT, doT, oT, lse, scaled, delta],
                 turns,
                 [kT, vT],
                 dq_far,
@@ -1416,7 +1448,6 @@
     d_mixed = d_mixed[0]
     while early.order:
         (d_mixed,) = launch(d_mixed, sums, early)
-    d_mixed = settle(d_mixed, sums, early)
     d_mixed, returned = lax.optimization_barrier((d_mixed, returned))
     if others > 1:
         returned = [functools.reduce(jnp.add, [item.astype(f32) for item in returned])]
@@ -1434,6 +1465,7 @@
         parts,
         orders,
     )
+    late, pieces = settle((late, pieces), sums, early)
     tail = Joint(pieces, orders, late)
     (d_mixed,) = tail.step(d_mixed)
     d_tokens = []

time: 712 us -> 707 us (level)
  starting transfers between devices: 58.2 us -> 37.2 us
  Pallas kernels: 594 us -> 604 us
    pallas_call x2, Pallas kernels: 80.4 us -> 100 us  [back_local(): return call(info, flags, *operands, *turns, *keys, dq, kept, *before)]
    ppermute x34, starting transfers between devices: 53.2 us -> 34.1 us  [swap(): lax.ppermute(values, axis, [(i, i ^ 1 << position) for i in range(size)])]
    pallas_call x2 -> x1, Pallas kernels: 91.6 us -> 83.2 us  [back_remote(): return call(info, flags, *operands, *turns, *keys, kept, *before)]
  transfers between devices with their start and end apart: 36 -> 36, of which waited for: 10 -> 10; matrix products, arithmetic and copies ran while one was open for 1% -> 1% of each run, Pallas kernels for 46% -> 54%
where the time goes in v7:
time: 707 us; the launch traced here: 703 us
  Pallas kernels  604 us (85%)
  waiting for transfers between devices  39.8 us (6%)
  starting transfers between devices  37.2 us (5%)
  local copies, waits for them, and re-layouts  15.7 us (2%)
    pallas_call x1, Pallas kernels, block_call(): pl.pallas_call(functools.partial(block_kernel, span), grid=(rows // step,...  117 us
    pallas_call x2, Pallas kernels, back_local(): return call(info, flags, *operands, *turns, *keys, dq, kept, *before)  100 us
    pallas_call x1, Pallas kernels, back_remote(): return call(info, flags, *operands, *turns, *keys, kept, *before)  83.2 us
    pallas_call x3, Pallas kernels, outer_halves(): pl.pallas_call(functools.partial(outer_kernel, run, levels, near, [order]...  59.5 us
    pallas_call x1, Pallas kernels, attend_local(): *state, kept, flags = call(info, qT, kT, vT)  47.3 us
    pallas_call x3, Pallas kernels, unproject(): pl.pallas_call(functools.partial(unproject_kernel, planes, bool(finish)),...  43.1 us
    pallas_call x1, Pallas kernels, attend_remote(): return call(info, qT, kT, vT, *state)  42.4 us
    pallas_call x1, Pallas kernels, mixed_halves(): pl.pallas_call(functools.partial(mixed_kernel, run, levels, near, orders,...  37.9 us
  transfers between devices with their start and end apart: 36, of which 10 were waited for; matrix products, arithmetic and copies ran while one was open for 1% of the time, Pallas kernels for 54%

profile of v7, /device:TPU:0, one launch (start us, length us, event | category | flops | bytes accessed | tf_op | source)
XLA Modules:
  0.0 702.6 jit_solution(14086454944694513591)
XLA Ops:
  0.7 3.0 collective-permute-start
  5.8 2.7 multiply_sine_fusion
  8.6 20.7 %project.2 = (bf16[2048,1024]{1,0:T(8,128)(2,1)}, bf16[1024,2048]{1,0:T(8,128)(2,1)}, bf16[1024,2048]{1,0:T(8,128)(2,1)}, bf16[1024,2048]{1,0:T(8,128)(2,1)}) custom-call(bf16[2048,1024]{1,0:T(8,128)(2,1)} %bitcast.169, bf16[1024,3072]{1,0:T(8,128)(2,1)} %refs_3_.3, f32[1,3072]{1,0:T(1,128)} %bitcast.218, f32[1,1024]{1,0:T(1,128)} %bitcast.199, ...), custom_call_target="tpu_custom_call" | custom-call | flops 12884901888 | bytes 16777216 | tf_op jit(solution)/shard_map/project/pallas_call | solution.py:845
  29.3 47.3 %attend_local.1 = (f32[1024,2048]{1,0:T(8,128)}, f32[8,2,2048]{2,1,0:T(2,128)}, f32[8,2,2048]{2,1,0:T(2,128)}, bf16[16,2304,1024]{2,1,0:T(8,128)(2,1)}, s32[8]{0:T(128)}) custom-call(s32[4]{0:T(128)} %pad_add_fusion.info, bf16[1024,2048]{1,0:T(8,128)(2,1)} %get-tuple-element.207.qT, bf16[1024,2048]{1,0:T(8,128)(2,1)} %get-tuple-element.210.kT, ...), custom_call_target="tpu_custom_call" | custom-call | flops 34359738368 | bytes 33554432 | tf_op jit(solution)/shard_map/attend_local/pallas_call | solution.py:553
  76.6 17.9 %collective-permute-done.tokens = bf16[2048,1024]{1,0:T(8,128)(2,1)} collective-permute-done((bf16[2048,1024]{1,0:T(8,128)(2,1)}, bf16[2048,1024]{1,0:T(8,128)(2,1)}, u32[]{:S(2)}, u32[]{:S(2)}) %collective-permute-start) | collective-permute-done | bytes 4194336 | tf_op jit(solution)/shard_map/ppermute | solution.py:1350
  94.6 16.2 %project.3 = (bf16[2048,1024]{1,0:T(8,128)(2,1)}, bf16[1024,2048]{1,0:T(8,128)(2,1)}, bf16[1024,2048]{1,0:T(8,128)(2,1)}) custom-call(bf16[2048,1024]{1,0:T(8,128)(2,1)} %collective-permute-done.tokens, bf16[1024,3072]{1,0:T(8,128)(2,1)} %refs_3_.3, f32[1,3072]{1,0:T(1,128)} %bitcast.219, f32[1,1024]{1,0:T(1,128)} %bitcast.200, f32[1,1024]{1,0:T(1,128)} %bitcast.229, ...), custom_call_target="tpu_custom_call" | custom-call | flops 8589934592 | bytes 16777216 | tf_op jit(solution)/shard_map/project/pallas_call | solution.py:845
  110.8 42.4 %attend_remote.1 = (bf16[1024,2048]{1,0:T(8,128)(2,1)}, f32[8,2,2048]{2,1,0:T(2,128)}, bf16[16,2048,1024]{2,1,0:T(8,128)(2,1)}, s32[8]{0:T(128)}) custom-call(s32[4]{0:T(128)} %pad_add_fusion.info, bf16[1024,2048]{1,0:T(8,128)(2,1)} %get-tuple-element.207.qT, bf16[1024,2048]{1,0:T(8,128)(2,1)} %get-tuple-element.208.kT, ...), custom_call_target="tpu_custom_call" | custom-call | flops 34359738368 | bytes 33554432 | tf_op jit(solution)/shard_map/attend_remote/pallas_call | solution.py:576
  153.2 117.3 %block.1 = (bf16[2048,1024]{1,0:T(8,128)(2,1)}, f32[2048,1024]{1,0:T(8,128)}, bf16[2048,4096]{1,0:T(8,128)(2,1)}, bf16[2048,1024]{1,0:T(8,128)(2,1)}, bf16[2048,...) custom-call(bf16[1024,2048]{1,0:T(8,128)(2,1)} %get-tuple-element.21, ...), custom_call_target="tpu_custom_call" | custom-call | flops 77309411328 | bytes 67108864 | tf_op jit(solution)/shard_map/block/pallas_call | solution.py:778
  270.5 24.5 %outer.3 = (bf16[2,2,2,2,32,4096]{5,4,3,2,1,0:T(8,128)(2,1)}, bf16[2,2,2,2,32,4096]{5,4,3,2,1,0:T(8,128)(2,1)}) custom-call(s32[2]{0:T(128)} %pad_add_fusion.1.marks, bf16[2048,1024]{1,0:T(8,128)(2,1)} %get-tuple-element.220.left, bf16[2048,4096]{1,0:T(8,128)(2,1)} %get-tuple-element.221.right), custom_call_target="tpu_custom_call" | custom-call | flops 17179869184 | bytes 33554432 | tf_op jit(solution)/shard_map/outer/pallas_call | solution.py:972
  295.1 24.6 %outer.4 = (bf16[2,2,2,2,128,1024]{5,4,3,2,1,0:T(8,128)(2,1)}, bf16[2,2,2,2,128,1024]{5,4,3,2,1,0:T(8,128)(2,1)}) custom-call(s32[2]{0:T(128)} %pad_add_fusion.1.marks, bf16[2048,4096]{1,0:T(8,128)(2,1)} %get-tuple-element.224.left, bf16[2048,1024]{1,0:T(8,128)(2,1)} %get-tuple-element.225.right), custom_call_target="tpu_custom_call" | custom-call | flops 17179869184 | bytes 33554432 | tf_op jit(solution)/shard_map/outer/pallas_call | solution.py:972
  320.2 10.4 %outer.5 = (bf16[2,2,2,2,32,1024]{5,4,3,2,1,0:T(8,128)(2,1)}, bf16[2,2,2,2,32,1024]{5,4,3,2,1,0:T(8,128)(2,1)}) custom-call(s32[2]{0:T(128)} %pad_add_fusion.1.marks, bf16[2048,1024]{1,0:T(8,128)(2,1)} %get-tuple-element.228.left, bf16[1024,2048]{1,0:T(8,128)(2,1)} %get-tuple-element.215.oT.right), custom_call_target="tpu_custom_call" | custom-call | flops 4294967296 | bytes 33554432 | tf_op jit(solution)/shard_map/outer/pallas_call | solution.py:972
  334.4 6.6 halve.4
  344.4 2.1 collective-permute-start.5
  348.5 83.2 %back_remote.1 = (f32[1024,2048]{1,0:T(8,128)}, bf16[3,1024,2048]{2,1,0:T(8,128)(2,1)}) custom-call(s32[4]{0:T(128)} %pad_add_fusion.info, s32[8]{0:T(128)} %get-tuple-element.238.flags, bf16[1024,2048]{1,0:T(8,128)(2,1)} %get-tuple-element.207.qT, bf16[1024,2048]{1,0:T(8,128)(2,1)} %get-tuple-element.261.doT, ...), custom_call_target="tpu_custom_call" | custom-call | flops 85899345920 | bytes 33554432 | tf_op jit(solution)/shard_map/back_remote/pallas_call | solution.py:613
  431.7 14.7 %unproject.3 = bf16[2048,1024]{1,0:T(8,128)(2,1)} custom-call(bf16[3,1024,2048]{2,1,0:T(8,128)(2,1)} %get-tuple-element.242.refs_0_.refs_1_, bf16[3,1024,2048]{2,1,0:T(8,128)(2,1)} %get-tuple-element.242.refs_0_.refs_1_, bf16[1024,3072]{1,0:T(8,128)(2,1)} %refs_3_.3), custom_call_target="tpu_custom_call" | custom-call | flops 8589934592 | bytes 16777216 | tf_op jit(solution)/shard_map/unproject/pallas_call | solution.py:894
  447.2 5.2 halve.5
  456.7 49.9 %back_local.2.rest_0_ = bf16[3,1024,2048]{2,1,0:T(8,128)(2,1)} custom-call(s32[4]{0:T(128)} %pad_add_fusion.info, s32[8]{0:T(128)} %get-tuple-element.218.flags, bf16[1024,2048]{1,0:T(8,128)(2,1)} %get-tuple-element.207.qT, bf16[1024,2048]{1,0:T(8,128)(2,1)} %get-tuple-element.261.doT, bf16[1024,2048]{1,0:T(8,128)(2,1)} %get-tuple-element.215.oT.right, ...), custom_call_target="tpu_custom_call" | custom-call | flops 42949672960 | bytes 33554432 | tf_op jit(solution)/shard_map/back_local/pallas_call | solution.py:637
  507.7 4.2 halve.6
  516.0 50.0 %back_local.3.refs_0_.refs_1_.refs_2_ = bf16[3,1024,2048]{2,1,0:T(8,128)(2,1)} custom-call(s32[4]{0:T(128)} %pad_add_fusion.info, s32[8]{0:T(128)} %get-tuple-element.218.flags, bf16[1024,2048]{1,0:T(8,128)(2,1)} %get-tuple-element.207.qT, bf16[1024,2048]{1,0:T(8,128)(2,1)} %get-tuple-element.261.doT, ...), custom_call_target="tpu_custom_call", output_to_operand_aliasing={{}: (14, {})} | custom-call | flops 42949672960 | bytes 33554432 | tf_op jit(solution)/shard_map/back_local/pallas_call | solution.py:637
  566.1 5.5 collective-permute-done.15
  572.7 2.8 halve.7
  581.4 37.9 %mixed.1 = (bf16[2,2,2,2,32,1024]{5,4,3,2,1,0:T(8,128)(2,1)}, bf16[2,2,2,2,32,1024]{5,4,3,2,1,0:T(8,128)(2,1)}, bf16[2,2,2,2,32,1024]{5,4,3,2,1,0:T(8,128)(2,1)}...) custom-call(s32[2]{0:T(128)} %pad_add_fusion.1.marks, ...), custom_call_target="tpu_custom_call" | custom-call | flops 25769803776 | bytes 33554432 | tf_op jit(solution)/shard_map/mixed/pallas_call | solution.py:1056
  621.1 3.5 collective-permute-done.25.refs_7_
  626.1 4.8 joint.5
  632.8 14.3 %unproject.4.refs_8_ = bf16[2048,1024]{1,0:T(8,128)(2,1)} custom-call(bf16[3,1024,2048]{2,1,0:T(8,128)(2,1)} %back_local.3.refs_0_.refs_1_.refs_2_, bf16[3,1024,2048]{2,1,0:T(8,128)(2,1)} %back_local.3.refs_0_.refs_1_.refs_2_, bf16[3,1024,2048]{2,1,0:T(8,128)(2,1)} %back_local.3.refs_0_.refs_1_.refs_2_, bf16[1024,3072]{1,0:T(8,128)(2,1)} %refs_3_.3, ...), custom_call_target="tpu_custom_call" | custom-call | flops 6442450944 | bytes 16777216 | tf_op jit(solution)/shard_map/unproject/pallas_call | solution.py:894
  649.0 3.2 joint.6
  656.4 14.1 %unproject.5 = bf16[2048,1024]{1,0:T(8,128)(2,1)} custom-call(bf16[3,1024,2048]{2,1,0:T(8,128)(2,1)} %back_local.3.refs_0_.refs_1_.refs_2_, bf16[3,1024,2048]{2,1,0:T(8,128)(2,1)} %back_local.3.refs_0_.refs_1_.refs_2_, bf16[3,1024,2048]{2,1,0:T(8,128)(2,1)} %back_local.3.refs_0_.refs_1_.refs_2_, ...), custom_call_target="tpu_custom_call", output_to_operand_aliasing={{}: (8, {})} | custom-call | flops 6442450944 | bytes 16777216 | tf_op jit(solution)/shard_map/unproject/pallas_call | solution.py:894
  672.0 2.4 joint.7
  676.3 3.3 collective-permute-done.33.refs_4_
  683.7 2.3 collective-permute-start.35
  687.3 3.1 collect.1
  692.4 4.6 collective-permute-done.35.refs_3_
  (147 shorter events, 55.7 us)
Async XLA Ops:
  0.7 93.9 %collective-permute-start = (bf16[2048,1024]{1,0:T(8,128)(2,1)}, bf16[2048,1024]{1,0:T(8,128)(2,1)}, u32[]{:S(2)}, u32[]{:S(2)}) collective-permute-start(bf16[2048,1024]{1,0:T(8,128)(2,1)} %bitcast.168), channel_id=1, source_target_pairs={{1,0},{0,1},{3,2},{2,3},{5,4},{4,5},{7,6},{6,7},{9,8},{8,9},{11,10... | collective-permute-start | bytes 12582920 | tf_op jit(solution)/shard_map/ppermute | solution.py:1350
  295.1 38.4 %collective-permute-start.1 = (bf16[512,4096]{1,0:T(8,128)(2,1)}, bf16[512,4096]{1,0:T(8,128)(2,1)}, u32[]{:S(2)}, u32[]{:S(2)}) collective-permute-start(bf16[512,4096]{1,0:T(8,128)(2,1)} %bitcast.208), channel_id=1, source_target_pairs={{0,2},{2,0},{4,6},{6,4},{8,10},{10,8},{12,14},{14,12},{16,18},{18,... | collective-permute-start | bytes 12582920 | tf_op jit(solution)/shard_map/ppermute | solution.py:1090
  319.6 13.8 %collective-permute-start.2 = (bf16[2048,1024]{1,0:T(8,128)(2,1)}, bf16[2048,1024]{1,0:T(8,128)(2,1)}, u32[]{:S(2)}, u32[]{:S(2)}) collective-permute-start(bf16[2048,1024]{1,0:T(8,128)(2,1)} %bitcast.209), channel_id=1, source_target_pairs={{0,2},{2,0},{4,6},{6,4},{8,10},{10,8},{12,14},{14,12},{16,18},{18,... | collective-permute-start | bytes 12582920 | tf_op jit(solution)/shard_map/ppermute | solution.py:1090
  341.0 105.4 %collective-permute-start.8 = (f32[96,128]{1,0:T(8,128)}, f32[96,128]{1,0:T(8,128)S(1)}, u32[]{:S(2)}, u32[]{:S(2)}) collective-permute-start(f32[96,128]{1,0:T(8,128)} %get-tuple-element.246.refs_9_), channel_id=1, source_target_pairs={{0,4},{2,6},{4,0},{6,2},{8,12},{10,14},{12,8},{14,10},{16,20},{18,... | collective-permute-start | bytes 147464 | tf_op jit(solution)/shard_map/ppermute | solution.py:1090
  342.8 103.6 %collective-permute-start.7 = (bf16[256,1024]{1,0:T(8,128)(2,1)}, bf16[256,1024]{1,0:T(8,128)(2,1)S(1)}, u32[]{:S(2)}, u32[]{:S(2)}) collective-permute-start(bf16[256,1024]{1,0:T(8,128)(2,1)} %get-tuple-element.245), channel_id=1, source_target_pairs={{0,8},{2,10},{4,12},{6,14},{8,0},{10,2},{12,4},{14,6},{16,24},{18,... | collective-permute-start | bytes 1572872 | tf_op jit(solution)/shard_map/ppermute | solution.py:1090
  344.4 102.1 %collective-permute-start.5 = (bf16[256,4096]{1,0:T(8,128)(2,1)}, bf16[256,4096]{1,0:T(8,128)(2,1)}, u32[]{:S(2)}, u32[]{:S(2)}) collective-permute-start(bf16[256,4096]{1,0:T(8,128)(2,1)} %get-tuple-element.243), channel_id=1, source_target_pairs={{0,1},{1,0},{2,3},{3,2},{4,5},{5,4},{6,7},{7,6},{8,9},{9,8},{10,11... | collective-permute-start | bytes 6291464 | tf_op jit(solution)/shard_map/ppermute | solution.py:1090
  346.5 100.0 %collective-permute-start.6 = (bf16[1024,1024]{1,0:T(8,128)(2,1)}, bf16[1024,1024]{1,0:T(8,128)(2,1)}, u32[]{:S(2)}, u32[]{:S(2)}) collective-permute-start(bf16[1024,1024]{1,0:T(8,128)(2,1)} %get-tuple-element.244), channel_id=1, source_target_pairs={{0,4},{2,6},{4,0},{6,2},{8,12},{10,14},{12,8},{14,10},{16,20},{18,... | collective-permute-start | bytes 6291464 | tf_op jit(solution)/shard_map/ppermute | solution.py:1090
  452.5 54.1 %collective-permute-start.12 = (f32[96,128]{1,0:T(8,128)}, f32[96,128]{1,0:T(8,128)S(1)}, u32[]{:S(2)}, u32[]{:S(2)}) collective-permute-start(f32[96,128]{1,0:T(8,128)} %get-tuple-element.256.refs_12_), channel_id=1, source_target_pairs={{0,1},{1,0},{2,3},{3,2},{4,5},{5,4},{6,7},{7,6},{8,9},{9,8},{10,11... | collective-permute-start | bytes 147464 | tf_op jit(solution)/shard_map/ppermute | solution.py:1090
  452.5 54.1 %collective-permute-start.11 = (bf16[128,1024]{1,0:T(8,128)(2,1)}, bf16[128,1024]{1,0:T(8,128)(2,1)S(1)}, u32[]{:S(2)}, u32[]{:S(2)}) collective-permute-start(bf16[128,1024]{1,0:T(8,128)(2,1)} %get-tuple-element.255), channel_id=1, source_target_pairs={{0,4},{2,6},{4,0},{6,2},{8,12},{10,14},{12,8},{14,10},{16,20},{18,... | collective-permute-start | bytes 786440 | tf_op jit(solution)/shard_map/ppermute | solution.py:1090
  452.7 54.0 %collective-permute-start.9 = (bf16[128,4096]{1,0:T(8,128)(2,1)}, bf16[128,4096]{1,0:T(8,128)(2,1)S(1)}, u32[]{:S(2)}, u32[]{:S(2)}) collective-permute-start(bf16[128,4096]{1,0:T(8,128)(2,1)} %get-tuple-element.253), channel_id=1, source_target_pairs={{0,4},{2,6},{4,0},{6,2},{8,12},{10,14},{12,8},{14,10},{16,20},{18,... | collective-permute-start | bytes 3145736 | tf_op jit(solution)/shard_map/ppermute | solution.py:1090
  454.6 52.0 %collective-permute-start.10 = (bf16[512,1024]{1,0:T(8,128)(2,1)}, bf16[512,1024]{1,0:T(8,128)(2,1)}, u32[]{:S(2)}, u32[]{:S(2)}) collective-permute-start(bf16[512,1024]{1,0:T(8,128)(2,1)} %get-tuple-element.254), channel_id=1, source_target_pairs={{0,1},{1,0},{2,3},{3,2},{4,5},{5,4},{6,7},{7,6},{8,9},{9,8},{10,11... | collective-permute-start | bytes 3145736 | tf_op jit(solution)/shard_map/ppermute | solution.py:1090
  456.6 124.8 %collective-permute-start.17 = (bf16[2048,1024]{1,0:T(8,128)(2,1)}, bf16[2048,1024]{1,0:T(8,128)(2,1)}, u32[]{:S(2)}, u32[]{:S(2)}) collective-permute-start(bf16[2048,1024]{1,0:T(8,128)(2,1)} %unproject.3), channel_id=1, source_target_pairs={{0,1},{1,0},{2,3},{3,2},{4,5},{5,4},{6,7},{7,6},{8,9},{9,8},{10,11... | collective-permute-start | bytes 12582920 | tf_op jit(solution)/shard_map/ppermute | solution.py:1426
  511.9 54.2 %collective-permute-start.16 = (f32[96,128]{1,0:T(8,128)}, f32[96,128]{1,0:T(8,128)S(1)}, u32[]{:S(2)}, u32[]{:S(2)}) collective-permute-start(f32[96,128]{1,0:T(8,128)} %get-tuple-element.267.refs_15_), channel_id=1, source_target_pairs={{0,8},{2,10},{4,12},{6,14},{8,0},{10,2},{12,4},{14,6},{16,24},{18,... | collective-permute-start | bytes 147464 | tf_op jit(solution)/shard_map/ppermute | solution.py:1090
  512.0 59.6 %collective-permute-start.15 = (bf16[64,1024]{1,0:T(8,128)(2,1)}, bf16[64,1024]{1,0:T(8,128)(2,1)S(1)}, u32[]{:S(2)}, u32[]{:S(2)}) collective-permute-start(bf16[64,1024]{1,0:T(8,128)(2,1)} %get-tuple-element.266), channel_id=1, source_target_pairs={{0,1},{1,0},{2,3},{3,2},{4,5},{5,4},{6,7},{7,6},{8,9},{9,8},{10,11... | collective-permute-start | bytes 393224 | tf_op jit(solution)/shard_map/ppermute | solution.py:1090
  514.0 57.6 %collective-permute-start.13 = (bf16[64,4096]{1,0:T(8,128)(2,1)}, bf16[64,4096]{1,0:T(8,128)(2,1)S(1)}, u32[]{:S(2)}, u32[]{:S(2)}) collective-permute-start(bf16[64,4096]{1,0:T(8,128)(2,1)} %get-tuple-element.264), channel_id=1, source_target_pairs={{0,8},{2,10},{4,12},{6,14},{8,0},{10,2},{12,4},{14,6},{16,24},{18,... | collective-permute-start | bytes 1572872 | tf_op jit(solution)/shard_map/ppermute | solution.py:1090
  515.9 55.6 %collective-permute-start.14 = (bf16[256,1024]{1,0:T(8,128)(2,1)}, bf16[256,1024]{1,0:T(8,128)(2,1)S(1)}, u32[]{:S(2)}, u32[]{:S(2)}) collective-permute-start(bf16[256,1024]{1,0:T(8,128)(2,1)} %get-tuple-element.265), channel_id=1, source_target_pairs={{0,8},{2,10},{4,12},{6,14},{8,0},{10,2},{12,4},{14,6},{16,24},{18,... | collective-permute-start | bytes 1572872 | tf_op jit(solution)/shard_map/ppermute | solution.py:1090
  575.5 43.8 %collective-permute-start.21 = (f32[96,128]{1,0:T(8,128)}, f32[96,128]{1,0:T(8,128)S(1)}, u32[]{:S(2)}, u32[]{:S(2)}) collective-permute-start(f32[96,128]{1,0:T(8,128)} %get-tuple-element.394), channel_id=1, source_target_pairs={{0,16},{2,18},{4,20},{6,22},{8,24},{10,26},{12,28},{14,30},{16,0},... | collective-permute-start | bytes 147464 | tf_op jit(solution)/shard_map/ppermute | solution.py:1090
  576.6 42.6 %collective-permute-start.20 = (bf16[32,1024]{1,0:T(8,128)(2,1)}, bf16[32,1024]{1,0:T(8,128)(2,1)S(1)}, u32[]{:S(2)}, u32[]{:S(2)}) collective-permute-start(bf16[32,1024]{1,0:T(8,128)(2,1)} %get-tuple-element.285), channel_id=1, source_target_pairs={{0,16},{2,18},{4,20},{6,22},{8,24},{10,26},{12,28},{14,30},{16,0},... | collective-permute-start | bytes 196616 | tf_op jit(solution)/shard_map/ppermute | solution.py:1090
  578.4 40.8 %collective-permute-start.18 = (bf16[32,4096]{1,0:T(8,128)(2,1)}, bf16[32,4096]{1,0:T(8,128)(2,1)S(1)}, u32[]{:S(2)}, u32[]{:S(2)}) collective-permute-start(bf16[32,4096]{1,0:T(8,128)(2,1)} %get-tuple-element.283), channel_id=1, source_target_pairs={{0,16},{2,18},{4,20},{6,22},{8,24},{10,26},{12,28},{14,30},{16,0},... | collective-permute-start | bytes 786440 | tf_op jit(solution)/shard_map/ppermute | solution.py:1090
  579.6 39.7 %collective-permute-start.19 = (bf16[128,1024]{1,0:T(8,128)(2,1)}, bf16[128,1024]{1,0:T(8,128)(2,1)S(1)}, u32[]{:S(2)}, u32[]{:S(2)}) collective-permute-start(bf16[128,1024]{1,0:T(8,128)(2,1)} %get-tuple-element.284), channel_id=1, source_target_pairs={{0,16},{2,18},{4,20},{6,22},{8,24},{10,26},{12,28},{14,30},{16,0},... | collective-permute-start | bytes 786440 | tf_op jit(solution)/shard_map/ppermute | solution.py:1090
  620.0 4.5 collective-permute-start.23
  620.5 5.6 collective-permute-start.24
  630.9 16.3 %collective-permute-start.26 = (bf16[304,1024]{1,0:T(8,128)(2,1)}, bf16[304,1024]{1,0:T(8,128)(2,1)S(1)}, u32[]{:S(2)}, u32[]{:S(2)}) collective-permute-start(bf16[304,1024]{1,0:T(8,128)(2,1)} %get-tuple-element.307), channel_id=1, source_target_pairs={{0,4},{2,6},{4,0},{6,2},{8,12},{10,14},{12,8},{14,10},{16,20},{18,... | collective-permute-start | bytes 1867784 | tf_op jit(solution)/shard_map/ppermute | solution.py:1090
  631.3 15.9 %collective-permute-start.27 = (bf16[256,1024]{1,0:T(8,128)(2,1)}, bf16[256,1024]{1,0:T(8,128)(2,1)S(1)}, u32[]{:S(2)}, u32[]{:S(2)}) collective-permute-start(bf16[256,1024]{1,0:T(8,128)(2,1)} %get-tuple-element.308), channel_id=1, source_target_pairs={{0,1},{1,0},{2,3},{3,2},{4,5},{5,4},{6,7},{7,6},{8,9},{9,8},{10,11... | collective-permute-start | bytes 1572872 | tf_op jit(solution)/shard_map/ppermute | solution.py:1090
  632.4 14.8 %collective-permute-start.28 = (bf16[256,1024]{1,0:T(8,128)(2,1)}, bf16[256,1024]{1,0:T(8,128)(2,1)S(1)}, u32[]{:S(2)}, u32[]{:S(2)}) collective-permute-start(bf16[256,1024]{1,0:T(8,128)(2,1)} %get-tuple-element.309), channel_id=1, source_target_pairs={{0,8},{2,10},{4,12},{6,14},{8,0},{10,2},{12,4},{14,6},{16,24},{18,... | collective-permute-start | bytes 1572872 | tf_op jit(solution)/shard_map/ppermute | solution.py:1090
  652.1 18.3 %collective-permute-start.30 = (bf16[128,1024]{1,0:T(8,128)(2,1)}, bf16[128,1024]{1,0:T(8,128)(2,1)S(1)}, u32[]{:S(2)}, u32[]{:S(2)}) collective-permute-start(bf16[128,1024]{1,0:T(8,128)(2,1)} %get-tuple-element.324), channel_id=1, source_target_pairs={{0,8},{2,10},{4,12},{6,14},{8,0},{10,2},{12,4},{14,6},{16,24},{18,... | collective-permute-start | bytes 786440 | tf_op jit(solution)/shard_map/ppermute | solution.py:1090
  653.8 16.7 %collective-permute-start.31 = (bf16[128,1024]{1,0:T(8,128)(2,1)}, bf16[128,1024]{1,0:T(8,128)(2,1)S(1)}, u32[]{:S(2)}, u32[]{:S(2)}) collective-permute-start(bf16[128,1024]{1,0:T(8,128)(2,1)} %get-tuple-element.325), channel_id=1, source_target_pairs={{0,4},{2,6},{4,0},{6,2},{8,12},{10,14},{12,8},{14,10},{16,20},{18,... | collective-permute-start | bytes 786440 | tf_op jit(solution)/shard_map/ppermute | solution.py:1090
  655.5 15.0 %collective-permute-start.29 = (bf16[176,1024]{1,0:T(8,128)(2,1)}, bf16[176,1024]{1,0:T(8,128)(2,1)S(1)}, u32[]{:S(2)}, u32[]{:S(2)}) collective-permute-start(bf16[176,1024]{1,0:T(8,128)(2,1)} %get-tuple-element.323), channel_id=1, source_target_pairs={{0,1},{1,0},{2,3},{3,2},{4,5},{5,4},{6,7},{7,6},{8,9},{9,8},{10,11... | collective-permute-start | bytes 1081352 | tf_op jit(solution)/shard_map/ppermute | solution.py:1090
  674.3 6.2 collective-permute-start.32
  674.4 5.2 collective-permute-start.33
  675.1 5.2 collective-permute-start.34
  683.7 13.3 %collective-permute-start.35 = (bf16[144,1024]{1,0:T(8,128)(2,1)}, bf16[144,1024]{1,0:T(8,128)(2,1)S(1)}, u32[]{:S(2)}, u32[]{:S(2)}) collective-permute-start(bf16[144,1024]{1,0:T(8,128)(2,1)} %get-tuple-element.369), channel_id=1, source_target_pairs={{0,16},{2,18},{4,20},{6,22},{8,24},{10,26},{12,28},{14,30},{16,0},... | collective-permute-start | bytes 884744 | tf_op jit(solution)/shard_map/ppermute | solution.py:1090
  (36 other events, 167.5 us)

commit v8 on v7

--- a/solution.py
+++ b/solution.py
@@ -959,7 +959,7 @@
     rows, height = left.shape
     width = right.shape[1 - right_dim]
     share = height // cores
-    high = max(2 * share, min(1024, height))
+    high = max(2 * share, min(512 if right_dim else 1024, height))
     levels = (high // (2 * share)).bit_length() - 1
     wide = min(1024, width)
     if right_dim == 0:
@@ -1388,6 +1388,7 @@
     second_order = narrow_bits + wide_bits[1:]
     third_order = narrow_bits + wide_bits[2:3] + wide_bits[1:2] + wide_bits[3:]
     fourth_order = wide_bits[2:3] + wide_bits[1:2] + narrow_bits + wide_bits[3:]
+    fifth_order = wide_bits[2:3] + narrow_bits + wide_bits[1:2] + wide_bits[3:]
     small_order = wide_bits[:1] + first_order
 
     def outer(left, right, right_dim, order):
@@ -1395,7 +1396,7 @@
 
     sum_up = outer(d_inner, normed_two, 0, first_order)
     sum_down = outer(d_outer, hidden, 0, second_order)
-    sum_out = outer(d_branch, oT, 1, fourth_order)
+    sum_out = outer(d_branch, oT, 1, fifth_order)
     flat = jnp.concatenate([small.reshape(-1), small_up.reshape(-1)])
     early = Adding(flat.reshape(-1, PAIR), small_order)
     sums = [sum_down, sum_up, sum_out]

time: 707 us -> 701 us (level)
  Pallas kernels: 604 us -> 572 us
  starting transfers between devices: 37.2 us -> 58.3 us
    pallas_call x2, Pallas kernels: 100 us -> 78.3 us  [back_local(): return call(info, flags, *operands, *turns, *keys, dq, kept, *before)]
    ppermute x34, starting transfers between devices: 34.1 us -> 53.7 us  [swap(): lax.ppermute(values, axis, [(i, i ^ 1 << position) for i in range(size)])]
    pallas_call x1, Pallas kernels: 47.3 us -> 37.2 us  [attend_local(): *state, kept, flags = call(info, qT, kT, vT)]
    ppermute x1, waiting for transfers between devices: 17.9 us -> 28.1 us  [body(): lax.ppermute(tokens, 'narrow', [((n + shift) % parts, n) for n in range(p...]
  transfers between devices with their start and end apart: 36 -> 36, of which waited for: 10 -> 8; matrix products, arithmetic and copies ran while one was open for 1% -> 1% of each run, Pallas kernels for 54% -> 50%
where the time goes in v8:
time: 701 us; the launch traced here: 696 us
  Pallas kernels  572 us (82%)
  starting transfers between devices  58.3 us (8%)
  waiting for transfers between devices  43.4 us (6%)
  local copies, waits for them, and re-layouts  15.9 us (2%)
    pallas_call x1, Pallas kernels, block_call(): pl.pallas_call(functools.partial(block_kernel, span), grid=(rows // step,...  117 us
    pallas_call x1, Pallas kernels, back_remote(): return call(info, flags, *operands, *turns, *keys, kept, *before)  83.3 us
    pallas_call x2, Pallas kernels, back_local(): return call(info, flags, *operands, *turns, *keys, dq, kept, *before)  78.3 us
    pallas_call x3, Pallas kernels, outer_halves(): pl.pallas_call(functools.partial(outer_kernel, run, levels, near, [order]...  58.7 us
    ppermute x34, starting transfers between devices, swap(): lax.ppermute(values, axis, [(i, i ^ 1 << position) for i in range(size)])  53.7 us
    pallas_call x1, Pallas kernels, attend_remote(): return call(info, qT, kT, vT, *state)  43.4 us
    pallas_call x3, Pallas kernels, unproject(): pl.pallas_call(functools.partial(unproject_kernel, planes, bool(finish)),...  43 us
    pallas_call x1, Pallas kernels, mixed_halves(): pl.pallas_call(functools.partial(mixed_kernel, run, levels, near, orders,...  37.9 us
  transfers between devices with their start and end apart: 36, of which 8 were waited for; matrix products, arithmetic and copies ran while one was open for 1% of the time, Pallas kernels for 50%

profile of v8, /device:TPU:0, one launch (start us, length us, event | category | flops | bytes accessed | tf_op | source)
XLA Modules:
  0.0 695.8 jit_solution(7247459955385068894)
XLA Ops:
  0.7 3.0 collective-permute-start
  5.8 2.7 multiply_sine_fusion
  8.6 20.7 %project.2 = (bf16[2048,1024]{1,0:T(8,128)(2,1)}, bf16[1024,2048]{1,0:T(8,128)(2,1)}, bf16[1024,2048]{1,0:T(8,128)(2,1)}, bf16[1024,2048]{1,0:T(8,128)(2,1)}) custom-call(bf16[2048,1024]{1,0:T(8,128)(2,1)} %bitcast.169, bf16[1024,3072]{1,0:T(8,128)(2,1)} %refs_3_.3, f32[1,3072]{1,0:T(1,128)} %bitcast.218, f32[1,1024]{1,0:T(1,128)} %bitcast.199, ...), custom_call_target="tpu_custom_call" | custom-call | flops 12884901888 | bytes 16777216 | tf_op jit(solution)/shard_map/project/pallas_call | solution.py:845
  29.3 37.2 %attend_local.1 = (f32[1024,2048]{1,0:T(8,128)}, f32[8,2,2048]{2,1,0:T(2,128)}, f32[8,2,2048]{2,1,0:T(2,128)}, bf16[16,2304,1024]{2,1,0:T(8,128)(2,1)}, s32[8]{0:T(128)}) custom-call(s32[4]{0:T(128)} %pad_add_fusion.info, bf16[1024,2048]{1,0:T(8,128)(2,1)} %get-tuple-element.207.qT, bf16[1024,2048]{1,0:T(8,128)(2,1)} %get-tuple-element.210.kT, ...), custom_call_target="tpu_custom_call" | custom-call | flops 34359738368 | bytes 33554432 | tf_op jit(solution)/shard_map/attend_local/pallas_call | solution.py:553
  66.5 28.1 %collective-permute-done.tokens = bf16[2048,1024]{1,0:T(8,128)(2,1)} collective-permute-done((bf16[2048,1024]{1,0:T(8,128)(2,1)}, bf16[2048,1024]{1,0:T(8,128)(2,1)}, u32[]{:S(2)}, u32[]{:S(2)}) %collective-permute-start) | collective-permute-done | bytes 4194336 | tf_op jit(solution)/shard_map/ppermute | solution.py:1350
  94.6 16.2 %project.3 = (bf16[2048,1024]{1,0:T(8,128)(2,1)}, bf16[1024,2048]{1,0:T(8,128)(2,1)}, bf16[1024,2048]{1,0:T(8,128)(2,1)}) custom-call(bf16[2048,1024]{1,0:T(8,128)(2,1)} %collective-permute-done.tokens, bf16[1024,3072]{1,0:T(8,128)(2,1)} %refs_3_.3, f32[1,3072]{1,0:T(1,128)} %bitcast.219, f32[1,1024]{1,0:T(1,128)} %bitcast.200, f32[1,1024]{1,0:T(1,128)} %bitcast.229, ...), custom_call_target="tpu_custom_call" | custom-call | flops 8589934592 | bytes 16777216 | tf_op jit(solution)/shard_map/project/pallas_call | solution.py:845
  110.8 43.4 %attend_remote.1 = (bf16[1024,2048]{1,0:T(8,128)(2,1)}, f32[8,2,2048]{2,1,0:T(2,128)}, bf16[16,2048,1024]{2,1,0:T(8,128)(2,1)}, s32[8]{0:T(128)}) custom-call(s32[4]{0:T(128)} %pad_add_fusion.info, bf16[1024,2048]{1,0:T(8,128)(2,1)} %get-tuple-element.207.qT, bf16[1024,2048]{1,0:T(8,128)(2,1)} %get-tuple-element.208.kT, ...), custom_call_target="tpu_custom_call" | custom-call | flops 34359738368 | bytes 33554432 | tf_op jit(solution)/shard_map/attend_remote/pallas_call | solution.py:576
  154.2 117.1 %block.1 = (bf16[2048,1024]{1,0:T(8,128)(2,1)}, f32[2048,1024]{1,0:T(8,128)}, bf16[2048,4096]{1,0:T(8,128)(2,1)}, bf16[2048,1024]{1,0:T(8,128)(2,1)}, bf16[2048,...) custom-call(bf16[1024,2048]{1,0:T(8,128)(2,1)} %get-tuple-element.21, ...), custom_call_target="tpu_custom_call" | custom-call | flops 77309411328 | bytes 67108864 | tf_op jit(solution)/shard_map/block/pallas_call | solution.py:778
  271.3 24.5 %outer.3 = (bf16[2,2,2,2,32,4096]{5,4,3,2,1,0:T(8,128)(2,1)}, bf16[2,2,2,2,32,4096]{5,4,3,2,1,0:T(8,128)(2,1)}) custom-call(s32[2]{0:T(128)} %pad_add_fusion.1.marks, bf16[2048,1024]{1,0:T(8,128)(2,1)} %get-tuple-element.220.left, bf16[2048,4096]{1,0:T(8,128)(2,1)} %get-tuple-element.221.right), custom_call_target="tpu_custom_call" | custom-call | flops 17179869184 | bytes 33554432 | tf_op jit(solution)/shard_map/outer/pallas_call | solution.py:972
  295.8 24.6 %outer.4 = (bf16[2,2,2,2,128,1024]{5,4,3,2,1,0:T(8,128)(2,1)}, bf16[2,2,2,2,128,1024]{5,4,3,2,1,0:T(8,128)(2,1)}) custom-call(s32[2]{0:T(128)} %pad_add_fusion.1.marks, bf16[2048,4096]{1,0:T(8,128)(2,1)} %get-tuple-element.224.left, bf16[2048,1024]{1,0:T(8,128)(2,1)} %get-tuple-element.225.right), custom_call_target="tpu_custom_call" | custom-call | flops 17179869184 | bytes 33554432 | tf_op jit(solution)/shard_map/outer/pallas_call | solution.py:972
  320.9 9.6 %outer.5 = (bf16[2,2,2,2,32,1024]{5,4,3,2,1,0:T(8,128)(2,1)}, bf16[2,2,2,2,32,1024]{5,4,3,2,1,0:T(8,128)(2,1)}) custom-call(s32[2]{0:T(128)} %pad_add_fusion.1.marks, bf16[2048,1024]{1,0:T(8,128)(2,1)} %get-tuple-element.228.left, bf16[1024,2048]{1,0:T(8,128)(2,1)} %get-tuple-element.215.oT.right), custom_call_target="tpu_custom_call" | custom-call | flops 4294967296 | bytes 33554432 | tf_op jit(solution)/shard_map/outer/pallas_call | solution.py:972
  334.4 6.6 halve.4
  346.1 83.3 %back_remote.1 = (f32[1024,2048]{1,0:T(8,128)}, bf16[3,1024,2048]{2,1,0:T(8,128)(2,1)}) custom-call(s32[4]{0:T(128)} %pad_add_fusion.info, s32[8]{0:T(128)} %get-tuple-element.238.flags, bf16[1024,2048]{1,0:T(8,128)(2,1)} %get-tuple-element.207.qT, bf16[1024,2048]{1,0:T(8,128)(2,1)} %get-tuple-element.261.doT, ...), custom_call_target="tpu_custom_call" | custom-call | flops 85899345920 | bytes 33554432 | tf_op jit(solution)/shard_map/back_remote/pallas_call | solution.py:613
  429.4 14.7 %unproject.3 = bf16[2048,1024]{1,0:T(8,128)(2,1)} custom-call(bf16[3,1024,2048]{2,1,0:T(8,128)(2,1)} %get-tuple-element.242.refs_0_.refs_1_, bf16[3,1024,2048]{2,1,0:T(8,128)(2,1)} %get-tuple-element.242.refs_0_.refs_1_, bf16[1024,3072]{1,0:T(8,128)(2,1)} %refs_3_.3), custom_call_target="tpu_custom_call" | custom-call | flops 8589934592 | bytes 16777216 | tf_op jit(solution)/shard_map/unproject/pallas_call | solution.py:894
  444.9 5.2 halve.5
  455.1 39.0 %back_local.2.rest_0_ = bf16[3,1024,2048]{2,1,0:T(8,128)(2,1)} custom-call(s32[4]{0:T(128)} %pad_add_fusion.info, s32[8]{0:T(128)} %get-tuple-element.218.flags, bf16[1024,2048]{1,0:T(8,128)(2,1)} %get-tuple-element.207.qT, bf16[1024,2048]{1,0:T(8,128)(2,1)} %get-tuple-element.261.doT, bf16[1024,2048]{1,0:T(8,128)(2,1)} %get-tuple-element.215.oT.right, ...), custom_call_target="tpu_custom_call" | custom-call | flops 42949672960 | bytes 33554432 | tf_op jit(solution)/shard_map/back_local/pallas_call | solution.py:637
  495.2 4.2 halve.6
  499.4 11.5 %collective-permute-start.16 = (f32[96,128]{1,0:T(8,128)}, f32[96,128]{1,0:T(8,128)S(1)}, u32[]{:S(2)}, u32[]{:S(2)}) collective-permute-start(f32[96,128]{1,0:T(8,128)} %get-tuple-element.267.refs_15_), channel_id=1, source_target_pairs={{0,8},{2,10},{4,12},{6,14},{8,0},{10,2},{12,4},{14,6},{16,24},{18,... | collective-permute-start | bytes 147464 | tf_op jit(solution)/shard_map/ppermute | solution.py:1090
  513.6 39.3 %back_local.3.refs_0_.refs_1_.refs_2_ = bf16[3,1024,2048]{2,1,0:T(8,128)(2,1)} custom-call(s32[4]{0:T(128)} %pad_add_fusion.info, s32[8]{0:T(128)} %get-tuple-element.218.flags, bf16[1024,2048]{1,0:T(8,128)(2,1)} %get-tuple-element.207.qT, bf16[1024,2048]{1,0:T(8,128)(2,1)} %get-tuple-element.261.doT, ...), custom_call_target="tpu_custom_call", output_to_operand_aliasing={{}: (14, {})} | custom-call | flops 42949672960 | bytes 33554432 | tf_op jit(solution)/shard_map/back_local/pallas_call | solution.py:637
  554.1 2.8 halve.7
  556.8 13.4 %collective-permute-start.21 = (f32[96,128]{1,0:T(8,128)}, f32[96,128]{1,0:T(8,128)S(1)}, u32[]{:S(2)}, u32[]{:S(2)}) collective-permute-start(f32[96,128]{1,0:T(8,128)} %get-tuple-element.394), channel_id=1, source_target_pairs={{0,16},{2,18},{4,20},{6,22},{8,24},{10,26},{12,28},{14,30},{16,0},... | collective-permute-start | bytes 147464 | tf_op jit(solution)/shard_map/ppermute | solution.py:1090
  570.3 2.8 collective-permute-start.18
  573.3 37.9 %mixed.1 = (bf16[2,2,2,2,32,1024]{5,4,3,2,1,0:T(8,128)(2,1)}, bf16[2,2,2,2,32,1024]{5,4,3,2,1,0:T(8,128)(2,1)}, bf16[2,2,2,2,32,1024]{5,4,3,2,1,0:T(8,128)(2,1)}...) custom-call(s32[2]{0:T(128)} %pad_add_fusion.1.marks, ...), custom_call_target="tpu_custom_call" | custom-call | flops 25769803776 | bytes 33554432 | tf_op jit(solution)/shard_map/mixed/pallas_call | solution.py:1056
  613.0 3.5 collective-permute-done.25.refs_7_
  618.0 4.8 joint.5
  622.8 3.2 collective-permute-start.27
  626.5 14.3 %unproject.4.refs_8_ = bf16[2048,1024]{1,0:T(8,128)(2,1)} custom-call(bf16[3,1024,2048]{2,1,0:T(8,128)(2,1)} %back_local.3.refs_0_.refs_1_.refs_2_, bf16[3,1024,2048]{2,1,0:T(8,128)(2,1)} %back_local.3.refs_0_.refs_1_.refs_2_, bf16[3,1024,2048]{2,1,0:T(8,128)(2,1)} %back_local.3.refs_0_.refs_1_.refs_2_, bf16[1024,3072]{1,0:T(8,128)(2,1)} %refs_3_.3, ...), custom_call_target="tpu_custom_call" | custom-call | flops 6442450944 | bytes 16777216 | tf_op jit(solution)/shard_map/unproject/pallas_call | solution.py:894
  642.6 3.2 joint.6
  648.2 14.1 %unproject.5 = bf16[2048,1024]{1,0:T(8,128)(2,1)} custom-call(bf16[3,1024,2048]{2,1,0:T(8,128)(2,1)} %back_local.3.refs_0_.refs_1_.refs_2_, bf16[3,1024,2048]{2,1,0:T(8,128)(2,1)} %back_local.3.refs_0_.refs_1_.refs_2_, bf16[3,1024,2048]{2,1,0:T(8,128)(2,1)} %back_local.3.refs_0_.refs_1_.refs_2_, ...), custom_call_target="tpu_custom_call", output_to_operand_aliasing={{}: (8, {})} | custom-call | flops 6442450944 | bytes 16777216 | tf_op jit(solution)/shard_map/unproject/pallas_call | solution.py:894
  676.6 2.7 collective-permute-start.35
  680.5 3.1 collect.1
  685.6 4.6 collective-permute-done.35.refs_3_
  (147 shorter events, 52.5 us)
Async XLA Ops:
  0.7 93.9 %collective-permute-start = (bf16[2048,1024]{1,0:T(8,128)(2,1)}, bf16[2048,1024]{1,0:T(8,128)(2,1)}, u32[]{:S(2)}, u32[]{:S(2)}) collective-permute-start(bf16[2048,1024]{1,0:T(8,128)(2,1)} %bitcast.168), channel_id=1, source_target_pairs={{1,0},{0,1},{3,2},{2,3},{5,4},{4,5},{7,6},{6,7},{9,8},{8,9},{11,10... | collective-permute-start | bytes 12582920 | tf_op jit(solution)/shard_map/ppermute | solution.py:1350
  295.8 37.7 %collective-permute-start.1 = (bf16[512,4096]{1,0:T(8,128)(2,1)}, bf16[512,4096]{1,0:T(8,128)(2,1)}, u32[]{:S(2)}, u32[]{:S(2)}) collective-permute-start(bf16[512,4096]{1,0:T(8,128)(2,1)} %bitcast.208), channel_id=1, source_target_pairs={{0,2},{2,0},{4,6},{6,4},{8,10},{10,8},{12,14},{14,12},{16,18},{18,... | collective-permute-start | bytes 12582920 | tf_op jit(solution)/shard_map/ppermute | solution.py:1090
  320.4 13.1 %collective-permute-start.2 = (bf16[2048,1024]{1,0:T(8,128)(2,1)}, bf16[2048,1024]{1,0:T(8,128)(2,1)}, u32[]{:S(2)}, u32[]{:S(2)}) collective-permute-start(bf16[2048,1024]{1,0:T(8,128)(2,1)} %bitcast.209), channel_id=1, source_target_pairs={{0,2},{2,0},{4,6},{6,4},{8,10},{10,8},{12,14},{14,12},{16,18},{18,... | collective-permute-start | bytes 12582920 | tf_op jit(solution)/shard_map/ppermute | solution.py:1090
  341.0 103.1 %collective-permute-start.8 = (f32[96,128]{1,0:T(8,128)}, f32[96,128]{1,0:T(8,128)S(1)}, u32[]{:S(2)}, u32[]{:S(2)}) collective-permute-start(f32[96,128]{1,0:T(8,128)} %get-tuple-element.246.refs_9_), channel_id=1, source_target_pairs={{0,4},{2,6},{4,0},{6,2},{8,12},{10,14},{12,8},{14,10},{16,20},{18,... | collective-permute-start | bytes 147464 | tf_op jit(solution)/shard_map/ppermute | solution.py:1090
  342.8 101.3 %collective-permute-start.7 = (bf16[256,1024]{1,0:T(8,128)(2,1)}, bf16[256,1024]{1,0:T(8,128)(2,1)S(1)}, u32[]{:S(2)}, u32[]{:S(2)}) collective-permute-start(bf16[256,1024]{1,0:T(8,128)(2,1)} %get-tuple-element.245), channel_id=1, source_target_pairs={{0,8},{2,10},{4,12},{6,14},{8,0},{10,2},{12,4},{14,6},{16,24},{18,... | collective-permute-start | bytes 1572872 | tf_op jit(solution)/shard_map/ppermute | solution.py:1090
  343.4 100.8 %collective-permute-start.5 = (bf16[256,4096]{1,0:T(8,128)(2,1)}, bf16[256,4096]{1,0:T(8,128)(2,1)}, u32[]{:S(2)}, u32[]{:S(2)}) collective-permute-start(bf16[256,4096]{1,0:T(8,128)(2,1)} %get-tuple-element.243), channel_id=1, source_target_pairs={{0,1},{1,0},{2,3},{3,2},{4,5},{5,4},{6,7},{7,6},{8,9},{9,8},{10,11... | collective-permute-start | bytes 6291464 | tf_op jit(solution)/shard_map/ppermute | solution.py:1090
  344.9 99.3 %collective-permute-start.6 = (bf16[1024,1024]{1,0:T(8,128)(2,1)}, bf16[1024,1024]{1,0:T(8,128)(2,1)}, u32[]{:S(2)}, u32[]{:S(2)}) collective-permute-start(bf16[1024,1024]{1,0:T(8,128)(2,1)} %get-tuple-element.244), channel_id=1, source_target_pairs={{0,4},{2,6},{4,0},{6,2},{8,12},{10,14},{12,8},{14,10},{16,20},{18,... | collective-permute-start | bytes 6291464 | tf_op jit(solution)/shard_map/ppermute | solution.py:1090
  450.2 43.9 %collective-permute-start.12 = (f32[96,128]{1,0:T(8,128)}, f32[96,128]{1,0:T(8,128)S(1)}, u32[]{:S(2)}, u32[]{:S(2)}) collective-permute-start(f32[96,128]{1,0:T(8,128)} %get-tuple-element.256.refs_12_), channel_id=1, source_target_pairs={{0,1},{1,0},{2,3},{3,2},{4,5},{5,4},{6,7},{7,6},{8,9},{9,8},{10,11... | collective-permute-start | bytes 147464 | tf_op jit(solution)/shard_map/ppermute | solution.py:1090
  450.2 43.9 %collective-permute-start.11 = (bf16[128,1024]{1,0:T(8,128)(2,1)}, bf16[128,1024]{1,0:T(8,128)(2,1)S(1)}, u32[]{:S(2)}, u32[]{:S(2)}) collective-permute-start(bf16[128,1024]{1,0:T(8,128)(2,1)} %get-tuple-element.255), channel_id=1, source_target_pairs={{0,1},{1,0},{2,3},{3,2},{4,5},{5,4},{6,7},{7,6},{8,9},{9,8},{10,11... | collective-permute-start | bytes 786440 | tf_op jit(solution)/shard_map/ppermute | solution.py:1090
  452.3 41.9 %collective-permute-start.9 = (bf16[128,4096]{1,0:T(8,128)(2,1)}, bf16[128,4096]{1,0:T(8,128)(2,1)S(1)}, u32[]{:S(2)}, u32[]{:S(2)}) collective-permute-start(bf16[128,4096]{1,0:T(8,128)(2,1)} %get-tuple-element.253), channel_id=1, source_target_pairs={{0,4},{2,6},{4,0},{6,2},{8,12},{10,14},{12,8},{14,10},{16,20},{18,... | collective-permute-start | bytes 3145736 | tf_op jit(solution)/shard_map/ppermute | solution.py:1090
  453.1 41.1 %collective-permute-start.10 = (bf16[512,1024]{1,0:T(8,128)(2,1)}, bf16[512,1024]{1,0:T(8,128)(2,1)}, u32[]{:S(2)}, u32[]{:S(2)}) collective-permute-start(bf16[512,1024]{1,0:T(8,128)(2,1)} %get-tuple-element.254), channel_id=1, source_target_pairs={{0,1},{1,0},{2,3},{3,2},{4,5},{5,4},{6,7},{7,6},{8,9},{9,8},{10,11... | collective-permute-start | bytes 3145736 | tf_op jit(solution)/shard_map/ppermute | solution.py:1090
  453.6 119.7 %collective-permute-start.17 = (bf16[2048,1024]{1,0:T(8,128)(2,1)}, bf16[2048,1024]{1,0:T(8,128)(2,1)}, u32[]{:S(2)}, u32[]{:S(2)}) collective-permute-start(bf16[2048,1024]{1,0:T(8,128)(2,1)} %unproject.3), channel_id=1, source_target_pairs={{0,1},{1,0},{2,3},{3,2},{4,5},{5,4},{6,7},{7,6},{8,9},{9,8},{10,11... | collective-permute-start | bytes 12582920 | tf_op jit(solution)/shard_map/ppermute | solution.py:1427
  499.4 53.6 %collective-permute-start.16 = (f32[96,128]{1,0:T(8,128)}, f32[96,128]{1,0:T(8,128)S(1)}, u32[]{:S(2)}, u32[]{:S(2)}) collective-permute-start(f32[96,128]{1,0:T(8,128)} %get-tuple-element.267.refs_15_), channel_id=1, source_target_pairs={{0,8},{2,10},{4,12},{6,14},{8,0},{10,2},{12,4},{14,6},{16,24},{18,... | collective-permute-start | bytes 147464 | tf_op jit(solution)/shard_map/ppermute | solution.py:1090
  510.9 42.1 %collective-permute-start.15 = (bf16[64,1024]{1,0:T(8,128)(2,1)}, bf16[64,1024]{1,0:T(8,128)(2,1)S(1)}, u32[]{:S(2)}, u32[]{:S(2)}) collective-permute-start(bf16[64,1024]{1,0:T(8,128)(2,1)} %get-tuple-element.266), channel_id=1, source_target_pairs={{0,4},{2,6},{4,0},{6,2},{8,12},{10,14},{12,8},{14,10},{16,20},{18,... | collective-permute-start | bytes 393224 | tf_op jit(solution)/shard_map/ppermute | solution.py:1090
  511.6 41.4 %collective-permute-start.13 = (bf16[64,4096]{1,0:T(8,128)(2,1)}, bf16[64,4096]{1,0:T(8,128)(2,1)S(1)}, u32[]{:S(2)}, u32[]{:S(2)}) collective-permute-start(bf16[64,4096]{1,0:T(8,128)(2,1)} %get-tuple-element.264), channel_id=1, source_target_pairs={{0,8},{2,10},{4,12},{6,14},{8,0},{10,2},{12,4},{14,6},{16,24},{18,... | collective-permute-start | bytes 1572872 | tf_op jit(solution)/shard_map/ppermute | solution.py:1090
  511.7 41.3 %collective-permute-start.14 = (bf16[256,1024]{1,0:T(8,128)(2,1)}, bf16[256,1024]{1,0:T(8,128)(2,1)S(1)}, u32[]{:S(2)}, u32[]{:S(2)}) collective-permute-start(bf16[256,1024]{1,0:T(8,128)(2,1)} %get-tuple-element.265), channel_id=1, source_target_pairs={{0,8},{2,10},{4,12},{6,14},{8,0},{10,2},{12,4},{14,6},{16,24},{18,... | collective-permute-start | bytes 1572872 | tf_op jit(solution)/shard_map/ppermute | solution.py:1090
  556.8 54.3 %collective-permute-start.21 = (f32[96,128]{1,0:T(8,128)}, f32[96,128]{1,0:T(8,128)S(1)}, u32[]{:S(2)}, u32[]{:S(2)}) collective-permute-start(f32[96,128]{1,0:T(8,128)} %get-tuple-element.394), channel_id=1, source_target_pairs={{0,16},{2,18},{4,20},{6,22},{8,24},{10,26},{12,28},{14,30},{16,0},... | collective-permute-start | bytes 147464 | tf_op jit(solution)/shard_map/ppermute | solution.py:1090
  570.2 40.9 %collective-permute-start.20 = (bf16[32,1024]{1,0:T(8,128)(2,1)}, bf16[32,1024]{1,0:T(8,128)(2,1)S(1)}, u32[]{:S(2)}, u32[]{:S(2)}) collective-permute-start(bf16[32,1024]{1,0:T(8,128)(2,1)} %get-tuple-element.285), channel_id=1, source_target_pairs={{0,16},{2,18},{4,20},{6,22},{8,24},{10,26},{12,28},{14,30},{16,0},... | collective-permute-start | bytes 196616 | tf_op jit(solution)/shard_map/ppermute | solution.py:1090
  570.3 40.8 %collective-permute-start.18 = (bf16[32,4096]{1,0:T(8,128)(2,1)}, bf16[32,4096]{1,0:T(8,128)(2,1)S(1)}, u32[]{:S(2)}, u32[]{:S(2)}) collective-permute-start(bf16[32,4096]{1,0:T(8,128)(2,1)} %get-tuple-element.283), channel_id=1, source_target_pairs={{0,16},{2,18},{4,20},{6,22},{8,24},{10,26},{12,28},{14,30},{16,0},... | collective-permute-start | bytes 786440 | tf_op jit(solution)/shard_map/ppermute | solution.py:1090
  573.2 38.0 %collective-permute-start.19 = (bf16[128,1024]{1,0:T(8,128)(2,1)}, bf16[128,1024]{1,0:T(8,128)(2,1)S(1)}, u32[]{:S(2)}, u32[]{:S(2)}) collective-permute-start(bf16[128,1024]{1,0:T(8,128)(2,1)} %get-tuple-element.284), channel_id=1, source_target_pairs={{0,16},{2,18},{4,20},{6,22},{8,24},{10,26},{12,28},{14,30},{16,0},... | collective-permute-start | bytes 786440 | tf_op jit(solution)/shard_map/ppermute | solution.py:1090
  611.9 4.5 collective-permute-start.23
  612.4 5.6 collective-permute-start.24
  622.8 18.1 %collective-permute-start.26 = (bf16[304,1024]{1,0:T(8,128)(2,1)}, bf16[304,1024]{1,0:T(8,128)(2,1)S(1)}, u32[]{:S(2)}, u32[]{:S(2)}) collective-permute-start(bf16[304,1024]{1,0:T(8,128)(2,1)} %get-tuple-element.307), channel_id=1, source_target_pairs={{0,4},{2,6},{4,0},{6,2},{8,12},{10,14},{12,8},{14,10},{16,20},{18,... | collective-permute-start | bytes 1867784 | tf_op jit(solution)/shard_map/ppermute | solution.py:1090
  622.8 18.0 %collective-permute-start.27 = (bf16[256,1024]{1,0:T(8,128)(2,1)}, bf16[256,1024]{1,0:T(8,128)(2,1)S(1)}, u32[]{:S(2)}, u32[]{:S(2)}) collective-permute-start(bf16[256,1024]{1,0:T(8,128)(2,1)} %get-tuple-element.308), channel_id=1, source_target_pairs={{0,1},{1,0},{2,3},{3,2},{4,5},{5,4},{6,7},{7,6},{8,9},{9,8},{10,11... | collective-permute-start | bytes 1572872 | tf_op jit(solution)/shard_map/ppermute | solution.py:1090
  626.0 14.9 %collective-permute-start.28 = (bf16[256,1024]{1,0:T(8,128)(2,1)}, bf16[256,1024]{1,0:T(8,128)(2,1)S(1)}, u32[]{:S(2)}, u32[]{:S(2)}) collective-permute-start(bf16[256,1024]{1,0:T(8,128)(2,1)} %get-tuple-element.309), channel_id=1, source_target_pairs={{0,8},{2,10},{4,12},{6,14},{8,0},{10,2},{12,4},{14,6},{16,24},{18,... | collective-permute-start | bytes 1572872 | tf_op jit(solution)/shard_map/ppermute | solution.py:1090
  645.8 16.5 %collective-permute-start.30 = (bf16[128,1024]{1,0:T(8,128)(2,1)}, bf16[128,1024]{1,0:T(8,128)(2,1)S(1)}, u32[]{:S(2)}, u32[]{:S(2)}) collective-permute-start(bf16[128,1024]{1,0:T(8,128)(2,1)} %get-tuple-element.324), channel_id=1, source_target_pairs={{0,8},{2,10},{4,12},{6,14},{8,0},{10,2},{12,4},{14,6},{16,24},{18,... | collective-permute-start | bytes 786440 | tf_op jit(solution)/shard_map/ppermute | solution.py:1090
  647.3 15.0 %collective-permute-start.31 = (bf16[128,1024]{1,0:T(8,128)(2,1)}, bf16[128,1024]{1,0:T(8,128)(2,1)S(1)}, u32[]{:S(2)}, u32[]{:S(2)}) collective-permute-start(bf16[128,1024]{1,0:T(8,128)(2,1)} %get-tuple-element.325), channel_id=1, source_target_pairs={{0,4},{2,6},{4,0},{6,2},{8,12},{10,14},{12,8},{14,10},{16,20},{18,... | collective-permute-start | bytes 786440 | tf_op jit(solution)/shard_map/ppermute | solution.py:1090
  647.7 14.7 %collective-permute-start.29 = (bf16[176,1024]{1,0:T(8,128)(2,1)}, bf16[176,1024]{1,0:T(8,128)(2,1)S(1)}, u32[]{:S(2)}, u32[]{:S(2)}) collective-permute-start(bf16[176,1024]{1,0:T(8,128)(2,1)} %get-tuple-element.323), channel_id=1, source_target_pairs={{0,1},{1,0},{2,3},{3,2},{4,5},{5,4},{6,7},{7,6},{8,9},{9,8},{10,11... | collective-permute-start | bytes 1081352 | tf_op jit(solution)/shard_map/ppermute | solution.py:1090
  666.2 7.0 %collective-permute-start.32 = (bf16[112,1024]{1,0:T(8,128)(2,1)}, bf16[112,1024]{1,0:T(8,128)(2,1)S(1)}, u32[]{:S(2)}, u32[]{:S(2)}) collective-permute-start(bf16[112,1024]{1,0:T(8,128)(2,1)} %get-tuple-element.356), channel_id=1, source_target_pairs={{0,8},{2,10},{4,12},{6,14},{8,0},{10,2},{12,4},{14,6},{16,24},{18,... | collective-permute-start | bytes 688136 | tf_op jit(solution)/shard_map/ppermute | solution.py:1090
  666.7 5.2 collective-permute-start.33
  668.0 5.2 collective-permute-start.34
  676.6 13.6 %collective-permute-start.35 = (bf16[144,1024]{1,0:T(8,128)(2,1)}, bf16[144,1024]{1,0:T(8,128)(2,1)S(1)}, u32[]{:S(2)}, u32[]{:S(2)}) collective-permute-start(bf16[144,1024]{1,0:T(8,128)(2,1)} %get-tuple-element.369), channel_id=1, source_target_pairs={{0,16},{2,18},{4,20},{6,22},{8,24},{10,26},{12,28},{14,30},{16,0},... | collective-permute-start | bytes 884744 | tf_op jit(solution)/shard_map/ppermute | solution.py:1090
  (36 other events, 165.0 us)

commit v9 on v8

--- a/solution.py
+++ b/solution.py
@@ -878,7 +878,7 @@
 
 def unproject(d_mixed, w, planes, start, count, finish=(), before=()):
     _, width, total = d_mixed.shape
-    step = min(256, count)
+    step = min(256 if finish else 512, count)
     first = start // step
 
     def fixed(shape):
@@ -1128,7 +1128,7 @@
 
 def halve(sums, small):
     heights = [item.height // 2 for item in sums]
-    grid = 4 if all(height % 64 == 0 for height in heights) else 1
+    grid = max(n for n in (1, 4, 8) if n == 1 or all(item % (16 * n) == 0 for item in heights))
     operands, in_specs, out_specs, out_shape = [], [], [], []
     for item, height in zip(sums, heights):
         arrays, specs = item.blocks(height, grid, 1)

time: 701 us -> 704 us (level)
  starting transfers between devices: 58.3 us -> 101 us
  Pallas kernels: 572 us -> 530 us
    ppermute x34, starting transfers between devices: 53.7 us -> 96.9 us  [swap(): lax.ppermute(values, axis, [(i, i ^ 1 << position) for i in range(size)])]
    pallas_call x1, Pallas kernels: 83.3 us -> 48 us  [back_remote(): return call(info, flags, *operands, *turns, *keys, kept, *before)]
    pallas_call x1, Pallas kernels: 43.4 us -> 34.4 us  [attend_remote(): return call(info, qT, kT, vT, *state)]
  transfers between devices with their start and end apart: 36 -> 36, of which waited for: 8 -> 8; matrix products, arithmetic and copies ran while one was open for 1% -> 1% of each run, Pallas kernels for 50% -> 44%
where the time goes in v9:
time: 704 us; the launch traced here: 698 us
  Pallas kernels  530 us (75%)
  starting transfers between devices  101 us (14%)
  waiting for transfers between devices  44.5 us (6%)
  local copies, waits for them, and re-layouts  15.9 us (2%)
    pallas_call x1, Pallas kernels, block_call(): pl.pallas_call(functools.partial(block_kernel, span), grid=(rows // step,...  117 us
    ppermute x34, starting transfers between devices, swap(): lax.ppermute(values, axis, [(i, i ^ 1 << position) for i in range(size)])  96.9 us
    pallas_call x2, Pallas kernels, back_local(): return call(info, flags, *operands, *turns, *keys, dq, kept, *before)  78.3 us
    pallas_call x3, Pallas kernels, outer_halves(): pl.pallas_call(functools.partial(outer_kernel, run, levels, near, [order]...  58.7 us
    pallas_call x1, Pallas kernels, back_remote(): return call(info, flags, *operands, *turns, *keys, kept, *before)  48 us
    pallas_call x3, Pallas kernels, unproject(): pl.pallas_call(functools.partial(unproject_kernel, planes, bool(finish)),...  42.4 us
    pallas_call x1, Pallas kernels, mixed_halves(): pl.pallas_call(functools.partial(mixed_kernel, run, levels, near, orders,...  37.9 us
    pallas_call x1, Pallas kernels, attend_local(): *state, kept, flags = call(info, qT, kT, vT)  37.2 us
  transfers between devices with their start and end apart: 36, of which 8 were waited for; matrix products, arithmetic and copies ran while one was open for 1% of the time, Pallas kernels for 44%

profile of v9, /device:TPU:0, one launch (start us, length us, event | category | flops | bytes accessed | tf_op | source)
XLA Modules:
  0.0 698.1 jit_solution(11787182817186799021)
XLA Ops:
  0.7 3.0 collective-permute-start
  8.6 20.7 %project.2 = (bf16[2048,1024]{1,0:T(8,128)(2,1)}, bf16[1024,2048]{1,0:T(8,128)(2,1)}, bf16[1024,2048]{1,0:T(8,128)(2,1)}, bf16[1024,2048]{1,0:T(8,128)(2,1)}) custom-call(bf16[2048,1024]{1,0:T(8,128)(2,1)} %bitcast.169, bf16[1024,3072]{1,0:T(8,128)(2,1)} %refs_3_.3, f32[1,3072]{1,0:T(1,128)} %bitcast.218, f32[1,1024]{1,0:T(1,128)} %bitcast.199, ...), custom_call_target="tpu_custom_call" | custom-call | flops 12884901888 | bytes 16777216 | tf_op jit(solution)/shard_map/project/pallas_call | solution.py:845
  29.3 37.2 %attend_local.1 = (f32[1024,2048]{1,0:T(8,128)}, f32[8,2,2048]{2,1,0:T(2,128)}, f32[8,2,2048]{2,1,0:T(2,128)}, bf16[16,2304,1024]{2,1,0:T(8,128)(2,1)}, s32[8]{0:T(128)}) custom-call(s32[4]{0:T(128)} %pad_add_fusion.info, bf16[1024,2048]{1,0:T(8,128)(2,1)} %get-tuple-element.207.qT, bf16[1024,2048]{1,0:T(8,128)(2,1)} %get-tuple-element.210.kT, ...), custom_call_target="tpu_custom_call" | custom-call | flops 34359738368 | bytes 33554432 | tf_op jit(solution)/shard_map/attend_local/pallas_call | solution.py:553
  66.5 28.1 %collective-permute-done.tokens = bf16[2048,1024]{1,0:T(8,128)(2,1)} collective-permute-done((bf16[2048,1024]{1,0:T(8,128)(2,1)}, bf16[2048,1024]{1,0:T(8,128)(2,1)}, u32[]{:S(2)}, u32[]{:S(2)}) %collective-permute-start) | collective-permute-done | bytes 4194336 | tf_op jit(solution)/shard_map/ppermute | solution.py:1350
  94.6 16.2 %project.3 = (bf16[2048,1024]{1,0:T(8,128)(2,1)}, bf16[1024,2048]{1,0:T(8,128)(2,1)}, bf16[1024,2048]{1,0:T(8,128)(2,1)}) custom-call(bf16[2048,1024]{1,0:T(8,128)(2,1)} %collective-permute-done.tokens, bf16[1024,3072]{1,0:T(8,128)(2,1)} %refs_3_.3, f32[1,3072]{1,0:T(1,128)} %bitcast.219, f32[1,1024]{1,0:T(1,128)} %bitcast.200, f32[1,1024]{1,0:T(1,128)} %bitcast.229, ...), custom_call_target="tpu_custom_call" | custom-call | flops 8589934592 | bytes 16777216 | tf_op jit(solution)/shard_map/project/pallas_call | solution.py:845
  110.8 34.4 %attend_remote.1 = (bf16[1024,2048]{1,0:T(8,128)(2,1)}, f32[8,2,2048]{2,1,0:T(2,128)}, bf16[16,2048,1024]{2,1,0:T(8,128)(2,1)}, s32[8]{0:T(128)}) custom-call(s32[4]{0:T(128)} %pad_add_fusion.info, bf16[1024,2048]{1,0:T(8,128)(2,1)} %get-tuple-element.207.qT, bf16[1024,2048]{1,0:T(8,128)(2,1)} %get-tuple-element.208.kT, ...), custom_call_target="tpu_custom_call" | custom-call | flops 34359738368 | bytes 33554432 | tf_op jit(solution)/shard_map/attend_remote/pallas_call | solution.py:576
  145.2 117.1 %block.1 = (bf16[2048,1024]{1,0:T(8,128)(2,1)}, f32[2048,1024]{1,0:T(8,128)}, bf16[2048,4096]{1,0:T(8,128)(2,1)}, bf16[2048,1024]{1,0:T(8,128)(2,1)}, bf16[2048,...) custom-call(bf16[1024,2048]{1,0:T(8,128)(2,1)} %get-tuple-element.21, ...), custom_call_target="tpu_custom_call" | custom-call | flops 77309411328 | bytes 67108864 | tf_op jit(solution)/shard_map/block/pallas_call | solution.py:778
  262.3 24.5 %outer.3 = (bf16[2,2,2,2,32,4096]{5,4,3,2,1,0:T(8,128)(2,1)}, bf16[2,2,2,2,32,4096]{5,4,3,2,1,0:T(8,128)(2,1)}) custom-call(s32[2]{0:T(128)} %pad_add_fusion.1.marks, bf16[2048,1024]{1,0:T(8,128)(2,1)} %get-tuple-element.220.left, bf16[2048,4096]{1,0:T(8,128)(2,1)} %get-tuple-element.221.right), custom_call_target="tpu_custom_call" | custom-call | flops 17179869184 | bytes 33554432 | tf_op jit(solution)/shard_map/outer/pallas_call | solution.py:972
  286.8 7.4 %collective-permute-start.1 = (bf16[512,4096]{1,0:T(8,128)(2,1)}, bf16[512,4096]{1,0:T(8,128)(2,1)}, u32[]{:S(2)}, u32[]{:S(2)}) collective-permute-start(bf16[512,4096]{1,0:T(8,128)(2,1)} %bitcast.208), channel_id=1, source_target_pairs={{0,2},{2,0},{4,6},{6,4},{8,10},{10,8},{12,14},{14,12},{16,18},{18,... | collective-permute-start | bytes 12582920 | tf_op jit(solution)/shard_map/ppermute | solution.py:1090
  294.1 24.6 %outer.4 = (bf16[2,2,2,2,128,1024]{5,4,3,2,1,0:T(8,128)(2,1)}, bf16[2,2,2,2,128,1024]{5,4,3,2,1,0:T(8,128)(2,1)}) custom-call(s32[2]{0:T(128)} %pad_add_fusion.1.marks, bf16[2048,4096]{1,0:T(8,128)(2,1)} %get-tuple-element.224.left, bf16[2048,1024]{1,0:T(8,128)(2,1)} %get-tuple-element.225.right), custom_call_target="tpu_custom_call" | custom-call | flops 17179869184 | bytes 33554432 | tf_op jit(solution)/shard_map/outer/pallas_call | solution.py:972
  318.7 9.6 %outer.5 = (bf16[2,2,2,2,32,1024]{5,4,3,2,1,0:T(8,128)(2,1)}, bf16[2,2,2,2,32,1024]{5,4,3,2,1,0:T(8,128)(2,1)}) custom-call(s32[2]{0:T(128)} %pad_add_fusion.1.marks, bf16[2048,1024]{1,0:T(8,128)(2,1)} %get-tuple-element.228.left, bf16[1024,2048]{1,0:T(8,128)(2,1)} %get-tuple-element.215.oT.right), custom_call_target="tpu_custom_call" | custom-call | flops 4294967296 | bytes 33554432 | tf_op jit(solution)/shard_map/outer/pallas_call | solution.py:972
  332.4 7.9 %halve.4 = (bf16[256,4096]{1,0:T(8,128)(2,1)}, bf16[1024,1024]{1,0:T(8,128)(2,1)}, bf16[256,1024]{1,0:T(8,128)(2,1)}, f32[96,128]{1,0:T(8,128)}) custom-call(bf16[2,256,4096]{2,1,0:T(8,128)(2,1)} %bitcast.147, bf16[2,256,4096]{2,1,0:T(8,128)(2,1)} %bitcast.29.refs_1_, bf16[2,1024,1024]{2,1,0:T(8,128)(2,1)} %bitcast.152, ...), custom_call_target="tpu_custom_call" | custom-call | tf_op jit(solution)/shard_map/halve/pallas_call | solution.py:1141
  340.3 2.9 collective-permute-start.8
  346.7 48.0 %back_remote.1 = (f32[1024,2048]{1,0:T(8,128)}, bf16[3,1024,2048]{2,1,0:T(8,128)(2,1)}) custom-call(s32[4]{0:T(128)} %pad_add_fusion.info, s32[8]{0:T(128)} %get-tuple-element.238.flags, bf16[1024,2048]{1,0:T(8,128)(2,1)} %get-tuple-element.207.qT, bf16[1024,2048]{1,0:T(8,128)(2,1)} %get-tuple-element.261.doT, ...), custom_call_target="tpu_custom_call" | custom-call | flops 85899345920 | bytes 33554432 | tf_op jit(solution)/shard_map/back_remote/pallas_call | solution.py:613
  394.7 14.1 %unproject.3 = bf16[2048,1024]{1,0:T(8,128)(2,1)} custom-call(bf16[3,1024,2048]{2,1,0:T(8,128)(2,1)} %get-tuple-element.242.refs_0_.refs_1_, bf16[3,1024,2048]{2,1,0:T(8,128)(2,1)} %get-tuple-element.242.refs_0_.refs_1_, bf16[1024,3072]{1,0:T(8,128)(2,1)} %refs_3_.3), custom_call_target="tpu_custom_call" | custom-call | flops 8589934592 | bytes 16777216 | tf_op jit(solution)/shard_map/unproject/pallas_call | solution.py:894
  409.6 6.9 halve.5
  416.5 35.9 %collective-permute-start.12 = (f32[96,128]{1,0:T(8,128)}, f32[96,128]{1,0:T(8,128)S(1)}, u32[]{:S(2)}, u32[]{:S(2)}) collective-permute-start(f32[96,128]{1,0:T(8,128)} %get-tuple-element.256.refs_12_), channel_id=1, source_target_pairs={{0,1},{1,0},{2,3},{3,2},{4,5},{5,4},{6,7},{7,6},{8,9},{9,8},{10,11... | collective-permute-start | bytes 147464 | tf_op jit(solution)/shard_map/ppermute | solution.py:1090
  452.5 2.9 collective-permute-start.9
  457.4 39.0 %back_local.2.rest_0_ = bf16[3,1024,2048]{2,1,0:T(8,128)(2,1)} custom-call(s32[4]{0:T(128)} %pad_add_fusion.info, s32[8]{0:T(128)} %get-tuple-element.218.flags, bf16[1024,2048]{1,0:T(8,128)(2,1)} %get-tuple-element.207.qT, bf16[1024,2048]{1,0:T(8,128)(2,1)} %get-tuple-element.261.doT, bf16[1024,2048]{1,0:T(8,128)(2,1)} %get-tuple-element.215.oT.right, ...), custom_call_target="tpu_custom_call" | custom-call | flops 42949672960 | bytes 33554432 | tf_op jit(solution)/shard_map/back_local/pallas_call | solution.py:637
  497.5 4.2 halve.6
  501.8 11.5 %collective-permute-start.16 = (f32[96,128]{1,0:T(8,128)}, f32[96,128]{1,0:T(8,128)S(1)}, u32[]{:S(2)}, u32[]{:S(2)}) collective-permute-start(f32[96,128]{1,0:T(8,128)} %get-tuple-element.267.refs_15_), channel_id=1, source_target_pairs={{0,8},{2,10},{4,12},{6,14},{8,0},{10,2},{12,4},{14,6},{16,24},{18,... | collective-permute-start | bytes 147464 | tf_op jit(solution)/shard_map/ppermute | solution.py:1090
  515.8 39.3 %back_local.3.refs_0_.refs_1_.refs_2_ = bf16[3,1024,2048]{2,1,0:T(8,128)(2,1)} custom-call(s32[4]{0:T(128)} %pad_add_fusion.info, s32[8]{0:T(128)} %get-tuple-element.218.flags, bf16[1024,2048]{1,0:T(8,128)(2,1)} %get-tuple-element.207.qT, bf16[1024,2048]{1,0:T(8,128)(2,1)} %get-tuple-element.261.doT, ...), custom_call_target="tpu_custom_call", output_to_operand_aliasing={{}: (14, {})} | custom-call | flops 42949672960 | bytes 33554432 | tf_op jit(solution)/shard_map/back_local/pallas_call | solution.py:637
  559.0 13.2 %collective-permute-start.21 = (f32[96,128]{1,0:T(8,128)}, f32[96,128]{1,0:T(8,128)S(1)}, u32[]{:S(2)}, u32[]{:S(2)}) collective-permute-start(f32[96,128]{1,0:T(8,128)} %get-tuple-element.394), channel_id=1, source_target_pairs={{0,16},{2,18},{4,20},{6,22},{8,24},{10,26},{12,28},{14,30},{16,0},... | collective-permute-start | bytes 147464 | tf_op jit(solution)/shard_map/ppermute | solution.py:1090
  575.2 37.9 %mixed.1 = (bf16[2,2,2,2,32,1024]{5,4,3,2,1,0:T(8,128)(2,1)}, bf16[2,2,2,2,32,1024]{5,4,3,2,1,0:T(8,128)(2,1)}, bf16[2,2,2,2,32,1024]{5,4,3,2,1,0:T(8,128)(2,1)}...) custom-call(s32[2]{0:T(128)} %pad_add_fusion.1.marks, ...), custom_call_target="tpu_custom_call" | custom-call | flops 25769803776 | bytes 33554432 | tf_op jit(solution)/shard_map/mixed/pallas_call | solution.py:1056
  614.9 3.5 collective-permute-done.25.refs_7_
  620.0 4.8 joint.5
  628.3 14.3 %unproject.4.refs_8_ = bf16[2048,1024]{1,0:T(8,128)(2,1)} custom-call(bf16[3,1024,2048]{2,1,0:T(8,128)(2,1)} %back_local.3.refs_0_.refs_1_.refs_2_, bf16[3,1024,2048]{2,1,0:T(8,128)(2,1)} %back_local.3.refs_0_.refs_1_.refs_2_, bf16[3,1024,2048]{2,1,0:T(8,128)(2,1)} %back_local.3.refs_0_.refs_1_.refs_2_, bf16[1024,3072]{1,0:T(8,128)(2,1)} %refs_3_.3, ...), custom_call_target="tpu_custom_call" | custom-call | flops 6442450944 | bytes 16777216 | tf_op jit(solution)/shard_map/unproject/pallas_call | solution.py:894
  644.4 3.2 joint.6
  650.3 14.1 %unproject.5 = bf16[2048,1024]{1,0:T(8,128)(2,1)} custom-call(bf16[3,1024,2048]{2,1,0:T(8,128)(2,1)} %back_local.3.refs_0_.refs_1_.refs_2_, bf16[3,1024,2048]{2,1,0:T(8,128)(2,1)} %back_local.3.refs_0_.refs_1_.refs_2_, bf16[3,1024,2048]{2,1,0:T(8,128)(2,1)} %back_local.3.refs_0_.refs_1_.refs_2_, ...), custom_call_target="tpu_custom_call", output_to_operand_aliasing={{}: (8, {})} | custom-call | flops 6442450944 | bytes 16777216 | tf_op jit(solution)/shard_map/unproject/pallas_call | solution.py:894
  671.7 3.2 collective-permute-done.33.refs_4_
  682.4 3.1 collect.1
  687.5 5.0 collective-permute-done.35.refs_3_
  (147 shorter events, 58.6 us)
Async XLA Ops:
  0.7 93.9 %collective-permute-start = (bf16[2048,1024]{1,0:T(8,128)(2,1)}, bf16[2048,1024]{1,0:T(8,128)(2,1)}, u32[]{:S(2)}, u32[]{:S(2)}) collective-permute-start(bf16[2048,1024]{1,0:T(8,128)(2,1)} %bitcast.168), channel_id=1, source_target_pairs={{1,0},{0,1},{3,2},{2,3},{5,4},{4,5},{7,6},{6,7},{9,8},{8,9},{11,10... | collective-permute-start | bytes 12582920 | tf_op jit(solution)/shard_map/ppermute | solution.py:1350
  286.8 44.6 %collective-permute-start.1 = (bf16[512,4096]{1,0:T(8,128)(2,1)}, bf16[512,4096]{1,0:T(8,128)(2,1)}, u32[]{:S(2)}, u32[]{:S(2)}) collective-permute-start(bf16[512,4096]{1,0:T(8,128)(2,1)} %bitcast.208), channel_id=1, source_target_pairs={{0,2},{2,0},{4,6},{6,4},{8,10},{10,8},{12,14},{14,12},{16,18},{18,... | collective-permute-start | bytes 12582920 | tf_op jit(solution)/shard_map/ppermute | solution.py:1090
  318.7 12.7 %collective-permute-start.2 = (bf16[2048,1024]{1,0:T(8,128)(2,1)}, bf16[2048,1024]{1,0:T(8,128)(2,1)}, u32[]{:S(2)}, u32[]{:S(2)}) collective-permute-start(bf16[2048,1024]{1,0:T(8,128)(2,1)} %bitcast.209), channel_id=1, source_target_pairs={{0,2},{2,0},{4,6},{6,4},{8,10},{10,8},{12,14},{14,12},{16,18},{18,... | collective-permute-start | bytes 12582920 | tf_op jit(solution)/shard_map/ppermute | solution.py:1090
  340.3 68.5 %collective-permute-start.8 = (f32[96,128]{1,0:T(8,128)}, f32[96,128]{1,0:T(8,128)S(1)}, u32[]{:S(2)}, u32[]{:S(2)}) collective-permute-start(f32[96,128]{1,0:T(8,128)} %get-tuple-element.246.refs_9_), channel_id=1, source_target_pairs={{0,4},{2,6},{4,0},{6,2},{8,12},{10,14},{12,8},{14,10},{16,20},{18,... | collective-permute-start | bytes 147464 | tf_op jit(solution)/shard_map/ppermute | solution.py:1090
  343.1 65.7 %collective-permute-start.7 = (bf16[256,1024]{1,0:T(8,128)(2,1)}, bf16[256,1024]{1,0:T(8,128)(2,1)S(1)}, u32[]{:S(2)}, u32[]{:S(2)}) collective-permute-start(bf16[256,1024]{1,0:T(8,128)(2,1)} %get-tuple-element.245), channel_id=1, source_target_pairs={{0,8},{2,10},{4,12},{6,14},{8,0},{10,2},{12,4},{14,6},{16,24},{18,... | collective-permute-start | bytes 1572872 | tf_op jit(solution)/shard_map/ppermute | solution.py:1090
  344.7 64.2 %collective-permute-start.5 = (bf16[256,4096]{1,0:T(8,128)(2,1)}, bf16[256,4096]{1,0:T(8,128)(2,1)}, u32[]{:S(2)}, u32[]{:S(2)}) collective-permute-start(bf16[256,4096]{1,0:T(8,128)(2,1)} %get-tuple-element.243), channel_id=1, source_target_pairs={{0,1},{1,0},{2,3},{3,2},{4,5},{5,4},{6,7},{7,6},{8,9},{9,8},{10,11... | collective-permute-start | bytes 6291464 | tf_op jit(solution)/shard_map/ppermute | solution.py:1090
  346.2 62.7 %collective-permute-start.6 = (bf16[1024,1024]{1,0:T(8,128)(2,1)}, bf16[1024,1024]{1,0:T(8,128)(2,1)}, u32[]{:S(2)}, u32[]{:S(2)}) collective-permute-start(bf16[1024,1024]{1,0:T(8,128)(2,1)} %get-tuple-element.244), channel_id=1, source_target_pairs={{0,4},{2,6},{4,0},{6,2},{8,12},{10,14},{12,8},{14,10},{16,20},{18,... | collective-permute-start | bytes 6291464 | tf_op jit(solution)/shard_map/ppermute | solution.py:1090
  416.5 79.9 %collective-permute-start.12 = (f32[96,128]{1,0:T(8,128)}, f32[96,128]{1,0:T(8,128)S(1)}, u32[]{:S(2)}, u32[]{:S(2)}) collective-permute-start(f32[96,128]{1,0:T(8,128)} %get-tuple-element.256.refs_12_), channel_id=1, source_target_pairs={{0,1},{1,0},{2,3},{3,2},{4,5},{5,4},{6,7},{7,6},{8,9},{9,8},{10,11... | collective-permute-start | bytes 147464 | tf_op jit(solution)/shard_map/ppermute | solution.py:1090
  452.4 44.1 %collective-permute-start.11 = (bf16[128,1024]{1,0:T(8,128)(2,1)}, bf16[128,1024]{1,0:T(8,128)(2,1)S(1)}, u32[]{:S(2)}, u32[]{:S(2)}) collective-permute-start(bf16[128,1024]{1,0:T(8,128)(2,1)} %get-tuple-element.255), channel_id=1, source_target_pairs={{0,1},{1,0},{2,3},{3,2},{4,5},{5,4},{6,7},{7,6},{8,9},{9,8},{10,11... | collective-permute-start | bytes 786440 | tf_op jit(solution)/shard_map/ppermute | solution.py:1090
  452.5 44.0 %collective-permute-start.9 = (bf16[128,4096]{1,0:T(8,128)(2,1)}, bf16[128,4096]{1,0:T(8,128)(2,1)S(1)}, u32[]{:S(2)}, u32[]{:S(2)}) collective-permute-start(bf16[128,4096]{1,0:T(8,128)(2,1)} %get-tuple-element.253), channel_id=1, source_target_pairs={{0,4},{2,6},{4,0},{6,2},{8,12},{10,14},{12,8},{14,10},{16,20},{18,... | collective-permute-start | bytes 3145736 | tf_op jit(solution)/shard_map/ppermute | solution.py:1090
  455.4 41.1 %collective-permute-start.10 = (bf16[512,1024]{1,0:T(8,128)(2,1)}, bf16[512,1024]{1,0:T(8,128)(2,1)}, u32[]{:S(2)}, u32[]{:S(2)}) collective-permute-start(bf16[512,1024]{1,0:T(8,128)(2,1)} %get-tuple-element.254), channel_id=1, source_target_pairs={{0,1},{1,0},{2,3},{3,2},{4,5},{5,4},{6,7},{7,6},{8,9},{9,8},{10,11... | collective-permute-start | bytes 3145736 | tf_op jit(solution)/shard_map/ppermute | solution.py:1090
  455.9 119.3 %collective-permute-start.17 = (bf16[2048,1024]{1,0:T(8,128)(2,1)}, bf16[2048,1024]{1,0:T(8,128)(2,1)}, u32[]{:S(2)}, u32[]{:S(2)}) collective-permute-start(bf16[2048,1024]{1,0:T(8,128)(2,1)} %unproject.3), channel_id=1, source_target_pairs={{0,1},{1,0},{2,3},{3,2},{4,5},{5,4},{6,7},{7,6},{8,9},{9,8},{10,11... | collective-permute-start | bytes 12582920 | tf_op jit(solution)/shard_map/ppermute | solution.py:1427
  501.8 53.4 %collective-permute-start.16 = (f32[96,128]{1,0:T(8,128)}, f32[96,128]{1,0:T(8,128)S(1)}, u32[]{:S(2)}, u32[]{:S(2)}) collective-permute-start(f32[96,128]{1,0:T(8,128)} %get-tuple-element.267.refs_15_), channel_id=1, source_target_pairs={{0,8},{2,10},{4,12},{6,14},{8,0},{10,2},{12,4},{14,6},{16,24},{18,... | collective-permute-start | bytes 147464 | tf_op jit(solution)/shard_map/ppermute | solution.py:1090
  513.2 41.9 %collective-permute-start.15 = (bf16[64,1024]{1,0:T(8,128)(2,1)}, bf16[64,1024]{1,0:T(8,128)(2,1)S(1)}, u32[]{:S(2)}, u32[]{:S(2)}) collective-permute-start(bf16[64,1024]{1,0:T(8,128)(2,1)} %get-tuple-element.266), channel_id=1, source_target_pairs={{0,4},{2,6},{4,0},{6,2},{8,12},{10,14},{12,8},{14,10},{16,20},{18,... | collective-permute-start | bytes 393224 | tf_op jit(solution)/shard_map/ppermute | solution.py:1090
  513.8 41.4 %collective-permute-start.13 = (bf16[64,4096]{1,0:T(8,128)(2,1)}, bf16[64,4096]{1,0:T(8,128)(2,1)S(1)}, u32[]{:S(2)}, u32[]{:S(2)}) collective-permute-start(bf16[64,4096]{1,0:T(8,128)(2,1)} %get-tuple-element.264), channel_id=1, source_target_pairs={{0,8},{2,10},{4,12},{6,14},{8,0},{10,2},{12,4},{14,6},{16,24},{18,... | collective-permute-start | bytes 1572872 | tf_op jit(solution)/shard_map/ppermute | solution.py:1090
  514.8 40.4 %collective-permute-start.14 = (bf16[256,1024]{1,0:T(8,128)(2,1)}, bf16[256,1024]{1,0:T(8,128)(2,1)S(1)}, u32[]{:S(2)}, u32[]{:S(2)}) collective-permute-start(bf16[256,1024]{1,0:T(8,128)(2,1)} %get-tuple-element.265), channel_id=1, source_target_pairs={{0,8},{2,10},{4,12},{6,14},{8,0},{10,2},{12,4},{14,6},{16,24},{18,... | collective-permute-start | bytes 1572872 | tf_op jit(solution)/shard_map/ppermute | solution.py:1090
  559.0 54.1 %collective-permute-start.21 = (f32[96,128]{1,0:T(8,128)}, f32[96,128]{1,0:T(8,128)S(1)}, u32[]{:S(2)}, u32[]{:S(2)}) collective-permute-start(f32[96,128]{1,0:T(8,128)} %get-tuple-element.394), channel_id=1, source_target_pairs={{0,16},{2,18},{4,20},{6,22},{8,24},{10,26},{12,28},{14,30},{16,0},... | collective-permute-start | bytes 147464 | tf_op jit(solution)/shard_map/ppermute | solution.py:1090
  572.2 40.9 %collective-permute-start.20 = (bf16[32,1024]{1,0:T(8,128)(2,1)}, bf16[32,1024]{1,0:T(8,128)(2,1)S(1)}, u32[]{:S(2)}, u32[]{:S(2)}) collective-permute-start(bf16[32,1024]{1,0:T(8,128)(2,1)} %get-tuple-element.285), channel_id=1, source_target_pairs={{0,16},{2,18},{4,20},{6,22},{8,24},{10,26},{12,28},{14,30},{16,0},... | collective-permute-start | bytes 196616 | tf_op jit(solution)/shard_map/ppermute | solution.py:1090
  572.3 40.8 %collective-permute-start.18 = (bf16[32,4096]{1,0:T(8,128)(2,1)}, bf16[32,4096]{1,0:T(8,128)(2,1)S(1)}, u32[]{:S(2)}, u32[]{:S(2)}) collective-permute-start(bf16[32,4096]{1,0:T(8,128)(2,1)} %get-tuple-element.283), channel_id=1, source_target_pairs={{0,16},{2,18},{4,20},{6,22},{8,24},{10,26},{12,28},{14,30},{16,0},... | collective-permute-start | bytes 786440 | tf_op jit(solution)/shard_map/ppermute | solution.py:1090
  575.1 38.0 %collective-permute-start.19 = (bf16[128,1024]{1,0:T(8,128)(2,1)}, bf16[128,1024]{1,0:T(8,128)(2,1)S(1)}, u32[]{:S(2)}, u32[]{:S(2)}) collective-permute-start(bf16[128,1024]{1,0:T(8,128)(2,1)} %get-tuple-element.284), channel_id=1, source_target_pairs={{0,16},{2,18},{4,20},{6,22},{8,24},{10,26},{12,28},{14,30},{16,0},... | collective-permute-start | bytes 786440 | tf_op jit(solution)/shard_map/ppermute | solution.py:1090
  613.9 4.5 collective-permute-start.23
  614.4 5.6 collective-permute-start.24
  624.8 17.8 %collective-permute-start.26 = (bf16[304,1024]{1,0:T(8,128)(2,1)}, bf16[304,1024]{1,0:T(8,128)(2,1)S(1)}, u32[]{:S(2)}, u32[]{:S(2)}) collective-permute-start(bf16[304,1024]{1,0:T(8,128)(2,1)} %get-tuple-element.307), channel_id=1, source_target_pairs={{0,4},{2,6},{4,0},{6,2},{8,12},{10,14},{12,8},{14,10},{16,20},{18,... | collective-permute-start | bytes 1867784 | tf_op jit(solution)/shard_map/ppermute | solution.py:1090
  626.9 15.7 %collective-permute-start.27 = (bf16[256,1024]{1,0:T(8,128)(2,1)}, bf16[256,1024]{1,0:T(8,128)(2,1)S(1)}, u32[]{:S(2)}, u32[]{:S(2)}) collective-permute-start(bf16[256,1024]{1,0:T(8,128)(2,1)} %get-tuple-element.308), channel_id=1, source_target_pairs={{0,1},{1,0},{2,3},{3,2},{4,5},{5,4},{6,7},{7,6},{8,9},{9,8},{10,11... | collective-permute-start | bytes 1572872 | tf_op jit(solution)/shard_map/ppermute | solution.py:1090
  627.4 15.2 %collective-permute-start.28 = (bf16[256,1024]{1,0:T(8,128)(2,1)}, bf16[256,1024]{1,0:T(8,128)(2,1)S(1)}, u32[]{:S(2)}, u32[]{:S(2)}) collective-permute-start(bf16[256,1024]{1,0:T(8,128)(2,1)} %get-tuple-element.309), channel_id=1, source_target_pairs={{0,8},{2,10},{4,12},{6,14},{8,0},{10,2},{12,4},{14,6},{16,24},{18,... | collective-permute-start | bytes 1572872 | tf_op jit(solution)/shard_map/ppermute | solution.py:1090
  647.5 16.9 %collective-permute-start.30 = (bf16[128,1024]{1,0:T(8,128)(2,1)}, bf16[128,1024]{1,0:T(8,128)(2,1)S(1)}, u32[]{:S(2)}, u32[]{:S(2)}) collective-permute-start(bf16[128,1024]{1,0:T(8,128)(2,1)} %get-tuple-element.324), channel_id=1, source_target_pairs={{0,8},{2,10},{4,12},{6,14},{8,0},{10,2},{12,4},{14,6},{16,24},{18,... | collective-permute-start | bytes 786440 | tf_op jit(solution)/shard_map/ppermute | solution.py:1090
  648.7 15.7 %collective-permute-start.31 = (bf16[128,1024]{1,0:T(8,128)(2,1)}, bf16[128,1024]{1,0:T(8,128)(2,1)S(1)}, u32[]{:S(2)}, u32[]{:S(2)}) collective-permute-start(bf16[128,1024]{1,0:T(8,128)(2,1)} %get-tuple-element.325), channel_id=1, source_target_pairs={{0,4},{2,6},{4,0},{6,2},{8,12},{10,14},{12,8},{14,10},{16,20},{18,... | collective-permute-start | bytes 786440 | tf_op jit(solution)/shard_map/ppermute | solution.py:1090
  649.6 14.8 %collective-permute-start.29 = (bf16[176,1024]{1,0:T(8,128)(2,1)}, bf16[176,1024]{1,0:T(8,128)(2,1)S(1)}, u32[]{:S(2)}, u32[]{:S(2)}) collective-permute-start(bf16[176,1024]{1,0:T(8,128)(2,1)} %get-tuple-element.323), channel_id=1, source_target_pairs={{0,1},{1,0},{2,3},{3,2},{4,5},{5,4},{6,7},{7,6},{8,9},{9,8},{10,11... | collective-permute-start | bytes 1081352 | tf_op jit(solution)/shard_map/ppermute | solution.py:1090
  668.3 7.2 %collective-permute-start.32 = (bf16[112,1024]{1,0:T(8,128)(2,1)}, bf16[112,1024]{1,0:T(8,128)(2,1)S(1)}, u32[]{:S(2)}, u32[]{:S(2)}) collective-permute-start(bf16[112,1024]{1,0:T(8,128)(2,1)} %get-tuple-element.356), channel_id=1, source_target_pairs={{0,8},{2,10},{4,12},{6,14},{8,0},{10,2},{12,4},{14,6},{16,24},{18,... | collective-permute-start | bytes 688136 | tf_op jit(solution)/shard_map/ppermute | solution.py:1090
  669.7 5.2 collective-permute-start.33
  670.3 5.2 collective-permute-start.34
  678.9 13.7 %collective-permute-start.35 = (bf16[144,1024]{1,0:T(8,128)(2,1)}, bf16[144,1024]{1,0:T(8,128)(2,1)S(1)}, u32[]{:S(2)}, u32[]{:S(2)}) collective-permute-start(bf16[144,1024]{1,0:T(8,128)(2,1)} %get-tuple-element.369), channel_id=1, source_target_pairs={{0,16},{2,18},{4,20},{6,22},{8,24},{10,26},{12,28},{14,30},{16,0},... | collective-permute-start | bytes 884744 | tf_op jit(solution)/shard_map/ppermute | solution.py:1090
  (36 other events, 164.1 us)
